TPU v7x, 32 devices: a whole 2x2x4 slice. The times are simulated.
32 devices in a mesh: dp: 4 (over y, core), ctx: 8 (over z, x).
Axes of the slice: x: 2, y: 2, z: 4, core: 2. Of those that a mesh axis runs over, the one named last changes fastest.
Arguments:
- queries: bfloat16 [4, 1024, 1152], P('dp', 'ctx')
- key_states: bfloat16 [4, 1024, 1152], P('dp', 'ctx')
- value_states: bfloat16 [4, 1024, 1152], P('dp', 'ctx'), may hold values from -6 to 6
- out_cotangent: bfloat16 [4, 1024, 1024], P('dp', 'ctx'), may hold values from -0.875 to 0.875
- out_weight: bfloat16 [1024, 1152], replicated, may hold values from -3 to 3
- block_clip: int32 [4, 8], P('dp', 'ctx'), may hold values from 0 to 1, never falling along the last dimension, each value on 1 to 7 neighbouring positions
Outputs:
- sublayer_out: bfloat16 [4, 1024, 1024], P('dp', 'ctx')
- query_grad: bfloat16 [4, 1024, 1152], P('dp', 'ctx')
- key_grad: bfloat16 [4, 1024, 1152], P('dp', 'ctx')
- value_grad: bfloat16 [4, 1024, 1152], P('dp', 'ctx')
- weight_grad: float32 [1024, 1152], P('ctx', 'dp')
All inputs are finite; a program needn't handle non-finite values.
Results may differ from a plain program's by a relative error of at most 0.034.
Values may be sent and summed in bfloat16 or wider, within the bound.
No kernel may reach another device: no remote copies, remote signals or barrier semaphores. Data moves between devices by JAX's collectives and lax.ppermute only.
A program may use at most 64 MiB of HBM per device.

v0:
```python
import math

import jax
import jax.numpy as jnp
from jax import lax
from jax.sharding import PartitionSpec as P

HEADS = 18
HDIM = 64
BLOCK = 128
WIN = 256


big_negative = -1e30


def passed_along(value, axis, steps):
    count = lax.axis_size(axis)
    first, last = (max(0, -steps), min(count, count - steps))
    return lax.ppermute(value, axis, [(source, source + steps) for source in range(first, last)])


def grouped_heads(matrix, head_count, group):
    rows = matrix.shape[0]
    stacked = matrix.reshape(rows, head_count, -1).transpose(1, 0, 2)
    return stacked.reshape(head_count // group, group, rows, stacked.shape[2])


def merge_groups(grouped):
    heads = grouped.reshape(grouped.shape[0] * grouped.shape[1], grouped.shape[2], grouped.shape[3])
    return heads.transpose(1, 0, 2).reshape(heads.shape[1], -1)


def rounded_back(values):
    return lax.optimization_barrier(values.astype(jnp.bfloat16)).astype(jnp.float32)


def allowed(query_pos, key_pos, query_clip, key_clip, window):
    causal = key_pos[None, :] <= query_pos[:, None]
    inside = query_pos[:, None] - key_pos[None, :] < window
    present = key_pos[None, :] >= 0
    same_clip = query_clip[:, None] == key_clip[None, :]
    return causal & inside & present & same_clip


def forward_block(query_rows, key_rows, value_rows, visible, head_count, scaling):
    group = math.gcd(head_count, 8)

    def forward_one_group(triple):
        query_head, key_head, value_head = triple
        scores = (
            jnp.einsum("hqd,hkd->hqk", query_head, key_head, preferred_element_type=jnp.float32)
            * scaling
        )
        scores = jnp.where(visible[None], scores, big_negative)
        maximum = jnp.max(scores, axis=2, keepdims=True)
        log_total = maximum[:, :, 0] + jnp.log(jnp.sum(jnp.exp(scores - maximum), axis=2))
        weights = jnp.exp(scores - log_total[:, :, None]).astype(jnp.bfloat16)
        mixed = jnp.einsum(
            "hqk,hkd->hqd", weights, value_head, preferred_element_type=jnp.float32
        ).astype(jnp.bfloat16)
        return (mixed, log_total)

    stacked = (
        grouped_heads(query_rows, head_count, group),
        grouped_heads(key_rows, head_count, group),
        grouped_heads(value_rows, head_count, group),
    )
    mixed, log_total = lax.map(forward_one_group, stacked)
    return (merge_groups(mixed), log_total.reshape(head_count, -1))


def backward_block(
    query_rows, key_rows, value_rows, d_rows, log_total, delta, visible, head_count, scaling
):
    group = math.gcd(head_count, 8)

    def backward_one_group(inputs):
        query_head, key_head, value_head, d_head, total_head, delta_head = inputs
        scores = (
            jnp.einsum("hqd,hkd->hqk", query_head, key_head, preferred_element_type=jnp.float32)
            * scaling
        )
        scores = jnp.where(visible[None], scores, big_negative)
        probs = jnp.exp(scores - total_head[:, :, None])
        d_weights = jnp.einsum(
            "hqd,hkd->hqk", d_head, value_head, preferred_element_type=jnp.float32
        )
        d_scores = (probs * (d_weights - delta_head[:, :, None]) * scaling).astype(jnp.bfloat16)
        query_part = jnp.einsum(
            "hqk,hkd->hqd", d_scores, key_head, preferred_element_type=jnp.float32
        )
        key_part = jnp.einsum(
            "hqk,hqd->hkd", d_scores, query_head, preferred_element_type=jnp.float32
        )
        value_part = jnp.einsum(
            "hqk,hqd->hkd", probs.astype(jnp.bfloat16), d_head, preferred_element_type=jnp.float32
        )
        return (query_part, key_part, value_part)

    rows = log_total.shape[1]
    stacked = (
        grouped_heads(query_rows, head_count, group),
        grouped_heads(key_rows, head_count, group),
        grouped_heads(value_rows, head_count, group),
        grouped_heads(d_rows, head_count, group),
        log_total.reshape(head_count // group, group, rows),
        delta.reshape(head_count // group, group, rows),
    )
    query_part, key_part, value_part = lax.map(backward_one_group, stacked)
    return (merge_groups(query_part), merge_groups(key_part), merge_groups(value_part))


def per_device(queries, key_states, value_states, out_cotangent, out_weight, block_clip):
    row_count = queries.shape[1]
    width = queries.shape[2]
    head_count = HEADS
    scaling = 1.0 / math.sqrt(HDIM)
    window = WIN
    query_own = queries[0]
    key_own = key_states[0]
    value_own = value_states[0]
    cotangent_own = out_cotangent[0]
    clip_steps = jnp.repeat(block_clip[0], BLOCK)
    reach = min(row_count, window)
    hop_count = min(window // reach, lax.axis_size("ctx") - 1)
    anchor = lax.axis_index("ctx") * row_count
    tail_rows = (key_own, value_own, clip_steps)
    received = []
    for hop_index in range(1, hop_count + 1):
        received.append(passed_along((tail_rows[0], tail_rows[1], tail_rows[2]), "ctx", hop_index))
    front_rows = window - hop_count * reach
    earlier = list(reversed(received))
    key_cat = jnp.concatenate(
        [jnp.zeros((front_rows, width), jnp.bfloat16)]
        + [piece[0] for piece in earlier]
        + [key_own],
        axis=0,
    )
    value_cat = jnp.concatenate(
        [jnp.zeros((front_rows, width), jnp.bfloat16)]
        + [piece[1] for piece in earlier]
        + [value_own],
        axis=0,
    )
    clip_cat = jnp.concatenate(
        [jnp.full((front_rows,), -1, jnp.int32)] + [piece[2] for piece in earlier] + [clip_steps],
        axis=0,
    )
    key_positions = anchor - window + jnp.arange(window + row_count, dtype=jnp.int32)
    block_rows = min(row_count, 512)
    block_start = 0
    query_pos = anchor + block_start + jnp.arange(block_rows, dtype=jnp.int32)
    visible = allowed(query_pos, key_positions, clip_steps, clip_cat, window)
    masks = [visible]
    mixed, log_total = forward_block(query_own, key_cat, value_cat, visible, head_count, scaling)
    sublayer_out = lax.dot_general(
        mixed, out_weight, (((1,), (1,)), ((), ())), preferred_element_type=jnp.float32
    ).astype(jnp.bfloat16)
    d_attended = jnp.dot(cotangent_own, out_weight, preferred_element_type=jnp.float32).astype(
        jnp.bfloat16
    )
    delta = jnp.sum(
        (d_attended.astype(jnp.float32) * mixed.astype(jnp.float32)).reshape(
            row_count, head_count, -1
        ),
        axis=2,
    ).T
    query_parts = []
    key_acc = jnp.zeros((window + row_count, width), jnp.float32)
    value_acc = jnp.zeros((window + row_count, width), jnp.float32)
    for number, block_start in enumerate(range(0, row_count, block_rows)):
        stop = block_start + block_rows
        query_part, key_part, value_part = backward_block(
            query_own,
            key_cat,
            value_cat,
            d_attended,
            log_total,
            delta,
            masks[number],
            head_count,
            scaling,
        )
        query_parts.append(query_part.astype(jnp.bfloat16))
        key_acc = key_acc.at[block_start : stop + window].add(key_part)
        value_acc = value_acc.at[block_start : stop + window].add(value_part)
    query_grad = query_parts[0]
    key_total = rounded_back(key_acc[window:])
    value_total = rounded_back(value_acc[window:])
    key_tail = jnp.zeros((reach, width), jnp.float32)
    value_tail = jnp.zeros((reach, width), jnp.float32)
    for hop_index in range(1, hop_count + 1):
        lower = window - hop_index * reach
        outgoing = (
            key_acc[lower : lower + reach].astype(jnp.bfloat16),
            value_acc[lower : lower + reach].astype(jnp.bfloat16),
        )
        incoming = passed_along((outgoing[0], outgoing[1]), "ctx", -hop_index)
        key_tail = key_tail + incoming[0].astype(jnp.float32)
        value_tail = value_tail + incoming[1].astype(jnp.float32)
    key_total = key_total.at[row_count - reach :].add(key_tail)
    value_total = value_total.at[row_count - reach :].add(value_tail)
    piece = cotangent_own
    sequence_grad = lax.psum_scatter(
        lax.dot_general(
            piece, mixed, (((0,), (0,)), ((), ())), preferred_element_type=jnp.float32
        ).astype(jnp.bfloat16),
        "ctx",
        scatter_dimension=0,
        tiled=True,
    ).astype(jnp.float32)
    weight_grad = lax.psum_scatter(sequence_grad, "dp", scatter_dimension=1, tiled=True)
    return (
        sublayer_out[None],
        query_grad[None],
        key_total.astype(jnp.bfloat16)[None],
        value_total.astype(jnp.bfloat16)[None],
        weight_grad,
    )


def solution(mesh):
    return jax.shard_map(
        per_device,
        mesh=mesh,
        in_specs=(
            P("dp", "ctx", None),
            P("dp", "ctx", None),
            P("dp", "ctx", None),
            P("dp", "ctx", None),
            P(),
            P("dp", "ctx"),
        ),
        out_specs=(
            P("dp", "ctx", None),
            P("dp", "ctx", None),
            P("dp", "ctx", None),
            P("dp", "ctx", None),
            P("ctx", "dp"),
        ),
        check_vma=False,
    )
```

profile of v0, /device:TPU:0, one launch (start us, length us, event | category | flops | bytes accessed | tf_op | source)
XLA Modules:
  0.0 208.4 jit_solution(7753396169929459784)
XLA Ops:
  8.5 5.6 %collective-permute-start.4 = (bf16[128,1152]{0,1:T(8,128)(2,1)S(1)}, bf16[128,1152]{0,1:T(8,128)(2,1)}, u32[]{:S(2)}, u32[]{:S(2)}) collective-permute-start(bf16[128,1152]{0,1:T(8,128)(2,1)S(1)} %bitcast.173), channel_id=1, source_target_pairs={{0,2},{1,3},{2,4},{3,5},{4,6},{5,7},{8,10},{9,11},{10,12},{11,13},... | collective-permute-start | bytes 884744 | tf_op jit(solution)/shard_map/ppermute | solution.py:20
  14.2 4.1 %collective-permute-start.5 = (bf16[128,1152]{0,1:T(8,128)(2,1)S(1)}, bf16[128,1152]{0,1:T(8,128)(2,1)}, u32[]{:S(2)}, u32[]{:S(2)}) collective-permute-start(bf16[128,1152]{0,1:T(8,128)(2,1)S(1)} %bitcast.174), channel_id=1, source_target_pairs={{0,1},{1,2},{2,3},{3,4},{4,5},{5,6},{6,7},{8,9},{9,10},{10,11},{11... | collective-permute-start | bytes 884744 | tf_op jit(solution)/shard_map/ppermute | solution.py:20
  19.5 2.1 %collective-permute-start.2 = (bf16[128,1152]{0,1:T(8,128)(2,1)S(1)}, bf16[128,1152]{0,1:T(8,128)(2,1)S(1)}, u32[]{:S(2)}, u32[]{:S(2)}) collective-permute-start(bf16[128,1152]{0,1:T(8,128)(2,1)S(1)} %bitcast.170), channel_id=1, source_target_pairs={{0,2},{1,3},{2,4},{3,5},{4,6},{5,7},{8,10},{9,11},{10,12},{11,13},... | collective-permute-start | bytes 884744 | tf_op jit(solution)/shard_map/ppermute | solution.py:20
  21.6 4.2 %collective-permute-start.3 = (bf16[128,1152]{0,1:T(8,128)(2,1)S(1)}, bf16[128,1152]{0,1:T(8,128)(2,1)}, u32[]{:S(2)}, u32[]{:S(2)}) collective-permute-start(bf16[128,1152]{0,1:T(8,128)(2,1)S(1)} %bitcast.171), channel_id=1, source_target_pairs={{0,1},{1,2},{2,3},{3,4},{4,5},{5,6},{6,7},{8,9},{9,10},{10,11},{11... | collective-permute-start | bytes 884744 | tf_op jit(solution)/shard_map/ppermute | solution.py:20
  29.5 13.7 %collective-permute-start.1 = (s32[128]{0:T(128)S(1)}, s32[128]{0:T(128)}, u32[]{:S(2)}, u32[]{:S(2)}) collective-permute-start(s32[128]{0:T(128)S(1)} %reshape.235), channel_id=1, source_target_pairs={{0,1},{1,2},{2,3},{3,4},{4,5},{5,6},{6,7},{8,9},{9,10},{10,11},{11... | collective-permute-start | bytes 1544 | tf_op jit(solution)/shard_map/ppermute | solution.py:20
  43.2 1.8 copy.34
  45.8 2.1 %pad_maximum_fusion.1 = bf16[384,18,64]{0,2,1:T(8,128)(2,1)} fusion(bf16[128,18,64]{0,2,1:T(8,128)(2,1)S(1)} %bitcast.175, bf16[128,18,64]{0,2,1:T(8,128)(2,1)} %bitcast.11, bf16[128,18,64]{0,2,1:T(8,128)(2,1)} %bitcast.10), kind=kLoop, calls=%fused_computation.72 | loop fusion | flops 2654208 | bytes 1769472 | tf_op jit(solution)/shard_map/concatenate | solution.py:140
  49.9 29.1 %while.36 = (s32[]{:T(128)}, bf16[9,2,128,64]{2,3,1,0:T(8,128)(2,1)S(1)}, f32[9,2,128]{2,1,0:T(2,128)}, bf16[9,2,128,64]{2,3,1,0:T(8,128)(2,1)}, bf16[9,2,384,64...) while((s32[]{:T(128)}, ...), condition=%wide.region_3.4_spmd.clone, body=%wide.region_0.3_spmd.clone.sunk | while | flops 26164992 | bytes 1553773 | solution.py:69
  79.9 3.2 %fusion.53 = bf16[1024,1152]{0,1:T(8,128)(2,1)} fusion(bf16[128,1152]{0,1:T(8,128)(2,1)S(1)} %bitcast.165, bf16[1,128,1024]{2,1,0:T(8,128)(2,1)} %param.29), kind=kOutput, calls=%fused_computation.67 | convolution fusion | flops 303169536 | bytes 2916352 | tf_op jit(solution)/shard_map/dot_general | solution.py:206
  84.6 2.1 %copy.41 = f32[128,1152]{0,1:T(8,128)} copy(f32[128,1152]{1,0:T(8,128)} %get-tuple-element.317) | data formatting | bytes 1179648 | tf_op jit(solution)/shard_map/mul | solution.py:164
  86.7 1.7 reduce_sum.18
  89.7 1.8 copy.39
  91.5 4.3 %copy.45 = bf16[1024,1152]{1,0:T(8,128)(2,1)} copy(bf16[1024,1152]{0,1:T(8,128)(2,1)} %fusion.53) | data formatting | bytes 4718592
  95.9 63.1 %while.37 = (s32[]{:T(128)}, bf16[9,2,128,64]{2,3,1,0:T(8,128)(2,1)}, bf16[9,2,384,64]{2,3,1,0:T(8,128)(2,1)}, bf16[9,2,384,64]{2,3,1,0:T(8,128)(2,1)}, bf16[9,2...) while((s32[]{:T(128)}, ...), condition=%wide.region_6.7_spmd.clone, body=%wide.region_5.6_spmd.clone.sunk | while | flops 63995904 | bytes 2766737 | solution.py:110
  113.0 1.6 fusion.108
  120.1 1.6 fusion.108
  134.0 1.6 fusion.108
  148.1 1.6 fusion.108
  159.0 2.1 %fusion.60 = (bf16[128,18,64]{0,2,1:T(8,128)(2,1)S(1)}, bf16[128,18,64]{0,2,1:T(8,128)(2,1)}, bf16[128,18,64]{0,2,1:T(8,128)(2,1)}) fusion(bf16[384,18,64]{0,2,1:T(8,128)(2,1)} %bitcast.179), kind=kLoop, calls=%fused_computation.85 | loop fusion | bytes 1769472 | tf_op jit(solution)/shard_map/slice | solution.py:190
  167.4 1.8 copy.42
  171.3 1.6 fusion.54
  172.9 7.2 %collective-permute-done.9 = bf16[128,1152]{0,1:T(8,128)(2,1)} collective-permute-done((bf16[128,1152]{0,1:T(8,128)(2,1)}, bf16[128,1152]{0,1:T(8,128)(2,1)}, u32[]{:S(2)}, u32[]{:S(2)}) %collective-permute-start.9) | collective-permute-done | bytes 294944 | tf_op jit(solution)/shard_map/ppermute | solution.py:20
  182.2 8.4 %collective-permute-done.7 = bf16[128,1152]{0,1:T(8,128)(2,1)} collective-permute-done((bf16[128,1152]{0,1:T(8,128)(2,1)}, bf16[128,1152]{0,1:T(8,128)(2,1)}, u32[]{:S(2)}, u32[]{:S(2)}) %collective-permute-start.7) | collective-permute-done | bytes 294944 | tf_op jit(solution)/shard_map/ppermute | solution.py:20
  192.7 8.8 %reduce-scatter.5.cloned.1.call-done = f32[128,288]{0,1:T(8,128)} async-done(((f32[128,1152]{0,1:T(8,128)}), f32[128,288]{0,1:T(8,128)}) %reduce-scatter.5.cloned.1.call-update) | async-done | bytes 147472 | tf_op jit(solution)/shard_map/reduce_scatter | solution.py:213
  (161 shorter events, 109.8 us)
Async XLA Ops:
  7.2 75.9 %copy-start = (bf16[1024,1152]{1,0:T(8,128)(2,1)S(1)}, bf16[1024,1152]{1,0:T(8,128)(2,1)}, u32[]{:S(2)}) copy-start(bf16[1024,1152]{1,0:T(8,128)(2,1)} %param.30) | copy-start | bytes 7077892
  7.2 162.0 %reduce-scatter.7.cloned.1.call-start = ((), (), s32[]{:S(2)}) async-start(), calls=%async_computation.3 | async-start | bytes 2654208
  8.5 37.2 %collective-permute-start.4 = (bf16[128,1152]{0,1:T(8,128)(2,1)S(1)}, bf16[128,1152]{0,1:T(8,128)(2,1)}, u32[]{:S(2)}, u32[]{:S(2)}) collective-permute-start(bf16[128,1152]{0,1:T(8,128)(2,1)S(1)} %bitcast.173), channel_id=1, source_target_pairs={{0,2},{1,3},{2,4},{3,5},{4,6},{5,7},{8,10},{9,11},{10,12},{11,13},... | collective-permute-start | bytes 884744 | tf_op jit(solution)/shard_map/ppermute | solution.py:20
  14.2 31.6 %collective-permute-start.5 = (bf16[128,1152]{0,1:T(8,128)(2,1)S(1)}, bf16[128,1152]{0,1:T(8,128)(2,1)}, u32[]{:S(2)}, u32[]{:S(2)}) collective-permute-start(bf16[128,1152]{0,1:T(8,128)(2,1)S(1)} %bitcast.174), channel_id=1, source_target_pairs={{0,1},{1,2},{2,3},{3,4},{4,5},{5,6},{6,7},{8,9},{9,10},{10,11},{11... | collective-permute-start | bytes 884744 | tf_op jit(solution)/shard_map/ppermute | solution.py:20
  19.4 28.5 %copy-start.1 = (bf16[1,128,1152]{1,2,0:T(8,128)(2,1)}, bf16[1,128,1152]{1,2,0:T(8,128)(2,1)S(1)}, u32[]{:S(2)}) copy-start(bf16[1,128,1152]{1,2,0:T(8,128)(2,1)S(1)} %copy.35) | copy-start | bytes 884740
  19.5 28.4 %collective-permute-start.2 = (bf16[128,1152]{0,1:T(8,128)(2,1)S(1)}, bf16[128,1152]{0,1:T(8,128)(2,1)S(1)}, u32[]{:S(2)}, u32[]{:S(2)}) collective-permute-start(bf16[128,1152]{0,1:T(8,128)(2,1)S(1)} %bitcast.170), channel_id=1, source_target_pairs={{0,2},{1,3},{2,4},{3,5},{4,6},{5,7},{8,10},{9,11},{10,12},{11,13},... | collective-permute-start | bytes 884744 | tf_op jit(solution)/shard_map/ppermute | solution.py:20
  21.6 26.3 %collective-permute-start.3 = (bf16[128,1152]{0,1:T(8,128)(2,1)S(1)}, bf16[128,1152]{0,1:T(8,128)(2,1)}, u32[]{:S(2)}, u32[]{:S(2)}) collective-permute-start(bf16[128,1152]{0,1:T(8,128)(2,1)S(1)} %bitcast.171), channel_id=1, source_target_pairs={{0,1},{1,2},{2,3},{3,4},{4,5},{5,6},{6,7},{8,9},{9,10},{10,11},{11... | collective-permute-start | bytes 884744 | tf_op jit(solution)/shard_map/ppermute | solution.py:20
  26.4 18.7 %copy-start.6 = (s32[128]{0:T(128)}, s32[128]{0:T(128)S(1)}, u32[]{:S(2)}) copy-start(s32[128]{0:T(128)S(1)} %reshape.235) | copy-start | bytes 1540
  26.4 2.6 %collective-permute-start = (s32[128]{0:T(128)S(1)}, s32[128]{0:T(128)S(1)}, u32[]{:S(2)}, u32[]{:S(2)}) collective-permute-start(s32[128]{0:T(128)S(1)} %reshape.235), channel_id=1, source_target_pairs={{0,2},{1,3},{2,4},{3,5},{4,6},{5,7},{8,10},{9,11},{10,12},{11,13},... | collective-permute-start | bytes 1544 | tf_op jit(solution)/shard_map/ppermute | solution.py:20
  29.0 0.5 copy-start.7
  29.5 15.5 %collective-permute-start.1 = (s32[128]{0:T(128)S(1)}, s32[128]{0:T(128)}, u32[]{:S(2)}, u32[]{:S(2)}) collective-permute-start(s32[128]{0:T(128)S(1)} %reshape.235), channel_id=1, source_target_pairs={{0,1},{1,2},{2,3},{3,4},{4,5},{5,6},{6,7},{8,9},{9,10},{10,11},{11... | collective-permute-start | bytes 1544 | tf_op jit(solution)/shard_map/ppermute | solution.py:20
  47.9 0.7 copy-start.5
  79.9 3.2 %copy-start.2 = (bf16[128,1152]{1,0:T(8,128)(2,1)S(1)}, bf16[128,1152]{1,0:T(8,128)(2,1)}, u32[]{:S(2)}) copy-start(bf16[128,1152]{1,0:T(8,128)(2,1)} %copy.40) | copy-start | bytes 884740
  79.9 3.2 %copy-start.3 = (bf16[1,128,1024]{2,1,0:T(8,128)(2,1)S(1)}, bf16[1,128,1024]{2,1,0:T(8,128)(2,1)}, u32[]{:S(2)}) copy-start(bf16[1,128,1024]{2,1,0:T(8,128)(2,1)} %param.29) | copy-start | bytes 786436
  95.9 105.6 %reduce-scatter.5.cloned.1.call-start = ((), (), s32[]{:S(2)}) async-start(), calls=%async_computation.2 | async-start | bytes 737280 | tf_op jit(solution)/shard_map/reduce_scatter | solution.py:213
  159.0 4.7 %copy-start.4 = (bf16[9,2,384,64]{2,3,1,0:T(8,128)(2,1)S(1)}, bf16[9,2,384,64]{2,3,1,0:T(8,128)(2,1)}, u32[]{:S(2)}) copy-start(bf16[9,2,384,64]{2,3,1,0:T(8,128)(2,1)} %get-tuple-element.185) | copy-start | bytes 2654212
  161.1 11.8 %collective-permute-start.8 = (bf16[128,1152]{0,1:T(8,128)(2,1)}, bf16[128,1152]{0,1:T(8,128)(2,1)}, u32[]{:S(2)}, u32[]{:S(2)}) collective-permute-start(bf16[128,1152]{0,1:T(8,128)(2,1)} %bitcast.46), channel_id=1, source_target_pairs={{1,0},{2,1},{3,2},{4,3},{5,4},{6,5},{7,6},{9,8},{10,9},{11,10},{12... | collective-permute-start | bytes 884744 | tf_op jit(solution)/shard_map/ppermute | solution.py:20
  162.4 17.7 %collective-permute-start.9 = (bf16[128,1152]{0,1:T(8,128)(2,1)}, bf16[128,1152]{0,1:T(8,128)(2,1)}, u32[]{:S(2)}, u32[]{:S(2)}) collective-permute-start(bf16[128,1152]{0,1:T(8,128)(2,1)} %bitcast.47), channel_id=1, source_target_pairs={{2,0},{3,1},{4,2},{5,3},{6,4},{7,5},{10,8},{11,9},{12,10},{13,11},... | collective-permute-start | bytes 884744 | tf_op jit(solution)/shard_map/ppermute | solution.py:20
  164.8 17.4 %collective-permute-start.6 = (bf16[128,1152]{0,1:T(8,128)(2,1)}, bf16[128,1152]{0,1:T(8,128)(2,1)}, u32[]{:S(2)}, u32[]{:S(2)}) collective-permute-start(bf16[128,1152]{0,1:T(8,128)(2,1)} %bitcast.39), channel_id=1, source_target_pairs={{1,0},{2,1},{3,2},{4,3},{5,4},{6,5},{7,6},{9,8},{10,9},{11,10},{12... | collective-permute-start | bytes 884744 | tf_op jit(solution)/shard_map/ppermute | solution.py:20
  166.1 24.6 %collective-permute-start.7 = (bf16[128,1152]{0,1:T(8,128)(2,1)}, bf16[128,1152]{0,1:T(8,128)(2,1)}, u32[]{:S(2)}, u32[]{:S(2)}) collective-permute-start(bf16[128,1152]{0,1:T(8,128)(2,1)} %bitcast.40), channel_id=1, source_target_pairs={{2,0},{3,1},{4,2},{5,3},{6,4},{7,5},{10,8},{11,9},{12,10},{13,11},... | collective-permute-start | bytes 884744 | tf_op jit(solution)/shard_map/ppermute | solution.py:20
Sparse Core Ops, SparseCore 0:
  96.0 70.7 reduce-scatter.6
  171.4 30.0 reduce-scatter.4
where the time goes:
time: 212 us; the launch traced here: 208 us
  matrix products  82.3 us (39%)
  starting transfers between devices  36.2 us (17%)
  local copies, waits for them, and re-layouts  30.2 us (14%)
  waiting for transfers between devices  25.8 us (12%)
  other arithmetic  18.4 us (9%)
  between operations  14.9 us (7%)
    ppermute x10, starting transfers between devices, passed_along(): lax.ppermute(value, axis, [(source, source + steps) for source in range(f...  36.1 us
    ppermute x10, waiting for transfers between devices, passed_along(): lax.ppermute(value, axis, [(source, source + steps) for source in range(f...  16.9 us
    unnamed x24, local copies, waits for them, and re-layouts  14.7 us
    dot_general x9, matrix products, backward_one_group(): jnp.einsum('hqk,hqd->hkd', d_scores, query_head, preferred_element_type=j...  14.2 us
    dot_general x9, matrix products, backward_one_group(): jnp.einsum('hqk,hqd->hkd', probs.astype(jnp.bfloat16), d_head, preferred_...  14.1 us
    dot_general x9, matrix products, forward_one_group(): jnp.einsum('hqk,hkd->hqd', weights, value_head, preferred_element_type=jn...  10.6 us
    dot_general x9, matrix products, backward_one_group(): jnp.einsum('hqd,hkd->hqk', d_head, value_head, preferred_element_type=jnp...  10.6 us
    dot_general x9, matrix products, forward_one_group(): jnp.einsum('hqd,hkd->hqk', query_head, key_head, preferred_element_type=j...  9.93 us
  transfers between devices with their start and end apart: 12, of which 4 were waited for; matrix products, arithmetic and copies ran while one was open for 39% of the time, Pallas kernels for 0%

commit v1 on v0

v1 whole, which is shorter than its diff:
```python
import functools
import math

import jax
import jax.numpy as jnp
from jax import lax
from jax.experimental import pallas as pl
from jax.experimental.pallas import tpu as pltpu
from jax.sharding import PartitionSpec as P

HEADS = 18
HDIM = 64
BLOCK = 128
WIN = 256
PAIR = 2 * HDIM
WIDTH = HEADS * HDIM
PAIRS = (HEADS + 2) // 4
PART = PAIRS * PAIR
START = WIDTH - PART
REST = WIDTH - PART
CLIP_ROWS = 16
PAYLOAD = 2 * BLOCK + CLIP_ROWS
SCALING = 1.0 / math.sqrt(HDIM)
VMEM_LIMIT = 48 * 1024 * 1024

big_negative = -1e30
bf16 = jnp.bfloat16
f32 = jnp.float32

SMEM = pl.BlockSpec(memory_space=pltpu.SMEM)
VMEM = pl.BlockSpec(memory_space=pltpu.VMEM)


def shaped(shape, dtype):
    return jax.ShapeDtypeStruct(shape, dtype)


def estimate(flops, moved):
    return pl.CostEstimate(flops=flops, bytes_accessed=moved, transcendentals=0)


def params():
    return pltpu.CompilerParams(vmem_limit_bytes=VMEM_LIMIT)


def at(index, size):
    return pl.ds(pl.multiple_of(index * size, size), size)


def span(start, size, unit):
    return pl.ds(pl.multiple_of(start, unit), size)


def times(a, b, dims):
    return lax.dot_general(a, b, (dims, ((), ())), preferred_element_type=f32)


def pack_kernel(where, clip, query, key, value, swap_kv, own_kv, swap_query):
    half = where[0]
    mine = span(half * START, PART, 128)
    other = span((1 - half) * START, PART, 128)
    clip_rows = jnp.full((CLIP_ROWS, PART), clip[0, 0].astype(f32), f32).astype(bf16)
    swap_kv[0:BLOCK] = key[:, other]
    swap_kv[BLOCK : 2 * BLOCK] = value[:, other]
    swap_kv[2 * BLOCK :] = clip_rows
    own_kv[0:BLOCK] = key[:, mine]
    own_kv[BLOCK : 2 * BLOCK] = value[:, mine]
    own_kv[2 * BLOCK :] = clip_rows
    swap_query[...] = query[:, other]


def pack(where, clip, query, key, value):
    return pl.pallas_call(
        pack_kernel,
        out_shape=(
            shaped((PAYLOAD, PART), bf16),
            shaped((PAYLOAD, PART), bf16),
            shaped((BLOCK, PART), bf16),
        ),
        in_specs=[SMEM, SMEM, VMEM, VMEM, VMEM],
        out_specs=(VMEM, VMEM, VMEM),
        compiler_params=params(),
        cost_estimate=estimate(0, 3_000_000),
        name="pack",
    )(where, clip, query, key, value)


def gather_rows(target, half, offset, own, partner, own_at):
    target[at(offset + half, BLOCK)] = own[own_at : own_at + BLOCK]
    target[at(offset + 1 - half, BLOCK)] = partner[own_at : own_at + BLOCK]


def doubled(rows):
    lane = lax.broadcasted_iota(jnp.int32, (1, PAIR), 1)
    first = jnp.where(lane < HDIM, 1.0, 0.0).astype(bf16)
    second = jnp.where(lane < HDIM, 0.0, 1.0).astype(bf16)
    return jnp.concatenate([rows * first, rows * second], axis=0)


def diagonal(pair):
    return jnp.concatenate([pair[:HDIM, :BLOCK], pair[HDIM:, BLOCK:]], axis=0)


def fill_mask(where, clips, mask):
    row = lax.broadcasted_iota(jnp.int32, (BLOCK, BLOCK), 0)
    lane = lax.broadcasted_iota(jnp.int32, (BLOCK, BLOCK), 1)
    older = jnp.where(row > lane, 1.0, 0.0)
    every = jnp.ones((BLOCK, BLOCK), f32)
    causal = jnp.where(row <= lane, 1.0, 0.0)
    for query_block in range(2):
        at_query = (2 + query_block) * CLIP_ROWS
        query_clip = clips[at_query : at_query + CLIP_ROWS].astype(f32)[0:1]
        for step, shape in enumerate((older, every, causal)):
            block = query_block + step
            key_clip = clips[block * CLIP_ROWS : (block + 1) * CLIP_ROWS].astype(f32)[0:1]
            same = jnp.where(key_clip == query_clip, 1.0, 0.0)
            present = jnp.where(2 * where[1] - 2 + block >= 0, 1.0, 0.0)
            mask[query_block, step * BLOCK : (step + 1) * BLOCK] = shape * same * present


def forward_kernel(
    pieces_wanted,
    where,
    own,
    partner,
    halo,
    halo_other,
    query_own,
    query_partner,
    weights_out,
    att_own,
    att_swap,
    *rest,
):
    pieces = rest[:pieces_wanted]
    att, mask, key_all, value_all, query_all, clips = rest[pieces_wanted:]
    pair = pl.program_id(0)
    half = where[0]
    for target, start in ((key_all, 0), (value_all, BLOCK)):
        gather_rows(target, half, 0, halo, halo_other, start)
        gather_rows(target, half, 2, own, partner, start)
    gather_rows(query_all, half, 0, query_own, query_partner, 0)

    @pl.when(pair == 0)
    def _():
        for offset, mine, theirs in ((0, halo, halo_other), (2, own, partner)):
            clips[at(offset + half, CLIP_ROWS)] = mine[2 * BLOCK :]
            clips[at(offset + 1 - half, CLIP_ROWS)] = theirs[2 * BLOCK :]
        fill_mask(where, clips, mask)

    for query_block in range(2):
        keys = slice(query_block * BLOCK, query_block * BLOCK + WIN + BLOCK)
        steps = slice(query_block * BLOCK, (query_block + 1) * BLOCK)
        scores = times(key_all[keys], doubled(query_all[steps]), ((1,), (1,))) * SCALING
        visible = mask[query_block]
        visible = jnp.concatenate([visible, visible], axis=1)
        scores = jnp.where(visible > 0.5, scores, big_negative)
        maximum = jnp.max(scores, axis=0, keepdims=True)
        powers = jnp.exp(scores - maximum)
        total = jnp.sum(powers, axis=0, keepdims=True)
        weights = (powers * (1.0 / total)).astype(bf16)
        weights_out[0, query_block] = weights
        mixed = times(value_all[keys], weights, ((0,), (0,)))
        att[at(pair, PAIR), steps] = diagonal(mixed).astype(bf16)

    @pl.when(pair == PAIRS - 1)
    def _():
        att_own[...] = att[:, at(half, BLOCK)]
        att_swap[...] = att[span(half * PAIR, REST, PAIR), at(1 - half, BLOCK)]
        if pieces_wanted:
            rows = pieces[0].shape[0]
            for number, piece in enumerate(pieces):
                begin = half * HDIM + rows * jnp.bitwise_xor(where[2], number)
                piece[...] = att[span(begin, rows, 16), :]


def column(rows):
    return pl.BlockSpec((rows, PAIR), lambda pair, where: (0, pair))


def shifted_column(rows):
    return pl.BlockSpec((rows, PAIR), lambda pair, where: (0, where[0] * (START // PAIR) + pair))


def whole(shape):
    return pl.BlockSpec(shape, lambda pair, where: (0,) * len(shape))


def forward(where, pieces_wanted, own, partner, halo, halo_other, query, query_partner):
    piece = (WIDTH // 2 // max(pieces_wanted, 1), 2 * BLOCK)
    return pl.pallas_call(
        functools.partial(forward_kernel, pieces_wanted),
        out_shape=(
            shaped((PAIRS, 2, WIN + BLOCK, 2 * BLOCK), bf16),
            shaped((PART, BLOCK), bf16),
            shaped((REST, BLOCK), bf16),
        )
        + (shaped(piece, bf16),) * pieces_wanted,
        grid_spec=pltpu.PrefetchScalarGridSpec(
            num_scalar_prefetch=1,
            grid=(PAIRS,),
            in_specs=[column(PAYLOAD)] * 4 + [shifted_column(BLOCK), column(BLOCK)],
            out_specs=(
                pl.BlockSpec(
                    (1, 2, WIN + BLOCK, 2 * BLOCK), lambda pair, where: (pair, 0, 0, 0)
                ),
                whole((PART, BLOCK)),
                whole((REST, BLOCK)),
            )
            + (whole(piece),) * pieces_wanted,
            scratch_shapes=[
                pltpu.VMEM((PART, 2 * BLOCK), bf16),
                pltpu.VMEM((2, WIN + BLOCK, BLOCK), f32),
                pltpu.VMEM((4 * BLOCK, PAIR), bf16),
                pltpu.VMEM((4 * BLOCK, PAIR), bf16),
                pltpu.VMEM((2 * BLOCK, PAIR), bf16),
                pltpu.VMEM((4 * CLIP_ROWS, PAIR), bf16),
            ],
        ),
        compiler_params=params(),
        cost_estimate=estimate(2_000_000_000, 6_000_000),
        name="forward",
    )(where, own, partner, halo, halo_other, query, query_partner)


def cotangent_kernel(where, own, partner, weight, d_attended, both):
    half = where[0]

    @pl.when(pl.program_id(0) == 0)
    def _():
        gather_rows(both, half, 0, own, partner, 0)

    d_attended[...] = times(both[...], weight[...], ((1,), (0,))).astype(bf16)


def cotangents(where, own, partner, weight):
    outs = own.shape[1]
    return pl.pallas_call(
        cotangent_kernel,
        out_shape=(shaped((2 * BLOCK, PART), bf16), shaped((2 * BLOCK, outs), bf16)),
        grid_spec=pltpu.PrefetchScalarGridSpec(
            num_scalar_prefetch=1,
            grid=(PAIRS,),
            in_specs=[whole((BLOCK, outs)), whole((BLOCK, outs)), shifted_column(outs)],
            out_specs=(column(2 * BLOCK), whole((2 * BLOCK, outs))),
        ),
        compiler_params=params(),
        cost_estimate=estimate(700_000_000, 3_000_000),
        name="cotangents",
    )(where, own, partner, weight)


def backward_kernel(
    where,
    own,
    partner,
    halo,
    halo_other,
    query_own,
    query_partner,
    weights_in,
    d_attended,
    dq_own,
    dq_swap,
    halo_grads,
    halo_other_grads,
    own_grads,
    partner_grads,
    key_all,
    value_all,
    query_all,
    dq_all,
    dk_all,
    dv_all,
):
    pair = pl.program_id(0)
    half = where[0]
    for target, start in ((key_all, 0), (value_all, BLOCK)):
        gather_rows(target, half, 0, halo, halo_other, start)
        gather_rows(target, half, 2, own, partner, start)
    gather_rows(query_all, half, 0, query_own, query_partner, 0)
    for query_block in range(2):
        keys = slice(query_block * BLOCK, query_block * BLOCK + WIN + BLOCK)
        steps = slice(query_block * BLOCK, (query_block + 1) * BLOCK)
        d_rows = doubled(d_attended[steps])
        query_rows = doubled(query_all[steps])
        weights = weights_in[0, query_block]
        d_weights = times(value_all[keys], d_rows, ((1,), (1,)))
        wide = weights.astype(f32)
        delta = jnp.sum(wide * d_weights, axis=0, keepdims=True)
        d_scores = (wide * (d_weights - delta) * SCALING).astype(bf16)
        dv = times(weights, d_rows, ((1,), (0,)))
        dk = times(d_scores, query_rows, ((1,), (0,)))
        dq = diagonal(times(key_all[keys], d_scores, ((0,), (0,))))
        dq_all[steps] = dq.T
        if query_block == 0:
            dk_all[: WIN + BLOCK] = dk
            dv_all[: WIN + BLOCK] = dv
        else:
            dk_all[BLOCK : WIN + BLOCK] += dk[:WIN]
            dv_all[BLOCK : WIN + BLOCK] += dv[:WIN]
            dk_all[WIN + BLOCK :] = dk[WIN:]
            dv_all[WIN + BLOCK :] = dv[WIN:]
    dq_own[...] = dq_all[at(half, BLOCK)].astype(bf16)

    @pl.when((pair >= half) & (pair - half < REST // PAIR))
    def _():
        dq_swap[...] = dq_all[at(1 - half, BLOCK)].astype(bf16)

    for start, grads in ((0, dk_all), (BLOCK, dv_all)):
        rows = slice(start, start + BLOCK)
        halo_grads[rows] = grads[at(half, BLOCK)].astype(bf16)
        halo_other_grads[rows] = grads[at(1 - half, BLOCK)].astype(bf16)
        own_grads[rows] = grads[at(2 + half, BLOCK)]
        partner_grads[rows] = grads[at(3 - half, BLOCK)]


def backward(where, own, partner, halo, halo_other, query, query_partner, weights, d_attended):
    return pl.pallas_call(
        backward_kernel,
        out_shape=(
            shaped((BLOCK, PART), bf16),
            shaped((BLOCK, REST), bf16),
            shaped((2 * BLOCK, PART), bf16),
            shaped((2 * BLOCK, PART), bf16),
            shaped((2 * BLOCK, PART), f32),
            shaped((2 * BLOCK, PART), f32),
        ),
        grid_spec=pltpu.PrefetchScalarGridSpec(
            num_scalar_prefetch=1,
            grid=(PAIRS,),
            in_specs=[column(PAYLOAD)] * 4
            + [
                shifted_column(BLOCK),
                column(BLOCK),
                pl.BlockSpec(
                    (1, 2, WIN + BLOCK, 2 * BLOCK), lambda pair, where: (pair, 0, 0, 0)
                ),
                column(2 * BLOCK),
            ],
            out_specs=(
                column(BLOCK),
                pl.BlockSpec(
                    (BLOCK, PAIR),
                    lambda pair, where: (0, jnp.clip(pair - where[0], 0, REST // PAIR - 1)),
                ),
                column(2 * BLOCK),
                column(2 * BLOCK),
                column(2 * BLOCK),
                column(2 * BLOCK),
            ),
            scratch_shapes=[
                pltpu.VMEM((4 * BLOCK, PAIR), bf16),
                pltpu.VMEM((4 * BLOCK, PAIR), bf16),
                pltpu.VMEM((2 * BLOCK, PAIR), bf16),
                pltpu.VMEM((2 * BLOCK, PAIR), f32),
                pltpu.VMEM((4 * BLOCK, PAIR), f32),
                pltpu.VMEM((4 * BLOCK, PAIR), f32),
            ],
        ),
        compiler_params=params(),
        cost_estimate=estimate(4_000_000_000, 8_000_000),
        name="backward",
    )(where, own, partner, halo, halo_other, query, query_partner, weights, d_attended)


def output_kernel(where, att_own, att_rest, weight, out, full):
    half = where[0]

    @pl.when(pl.program_id(0) == 0)
    def _():
        full[span(half * START, PART, 128)] = att_own[...]
        full[span((1 - half) * PART, REST, 128)] = att_rest[...]

    out[...] = times(weight[...], full[...], ((1,), (0,))).T.astype(bf16)


def output_rows(where, att_own, att_rest, weight):
    outs = weight.shape[0]
    rows = 256
    return pl.pallas_call(
        output_kernel,
        out_shape=(shaped((BLOCK, outs), bf16), shaped((WIDTH, BLOCK), bf16)),
        grid_spec=pltpu.PrefetchScalarGridSpec(
            num_scalar_prefetch=1,
            grid=(outs // rows,),
            in_specs=[
                whole((PART, BLOCK)),
                whole((REST, BLOCK)),
                pl.BlockSpec((rows, WIDTH), lambda step, where: (step, 0)),
            ],
            out_specs=(
                pl.BlockSpec((BLOCK, rows), lambda step, where: (0, step)),
                whole((WIDTH, BLOCK)),
            ),
        ),
        compiler_params=params(),
        cost_estimate=estimate(300_000_000, 3_000_000),
        name="output",
    )(where, att_own, att_rest, weight)


def add_partner_kernel(where, partner_grads, received, out):
    columns = span(where[0] * PAIR, REST, PAIR)
    out[...] = (partner_grads[:, columns] + received[:, columns].astype(f32)).astype(bf16)


def add_partner(where, partner_grads, received):
    return pl.pallas_call(
        add_partner_kernel,
        out_shape=shaped((2 * BLOCK, REST), bf16),
        in_specs=[SMEM, VMEM, VMEM],
        out_specs=VMEM,
        compiler_params=params(),
        cost_estimate=estimate(0, 1_000_000),
        name="add_partner",
    )(where, partner_grads, received)


def place_query_kernel(where, mine, theirs, out):
    half = where[0]
    out[:, span(half * START, PART, 128)] = mine[...]
    out[:, span((1 - half) * PART, REST, 128)] = theirs[...]


def place_query(where, mine, theirs):
    return pl.pallas_call(
        place_query_kernel,
        out_shape=shaped((BLOCK, WIDTH), bf16),
        in_specs=[SMEM, VMEM, VMEM],
        out_specs=VMEM,
        compiler_params=params(),
        cost_estimate=estimate(0, 600_000),
        name="place_query",
    )(where, mine, theirs)


def place_keys_kernel(where, mine, received, theirs, key_out, value_out):
    half = where[0]
    total = (mine[...] + received[...].astype(f32)).astype(bf16)
    for rows, out in ((slice(0, BLOCK), key_out), (slice(BLOCK, 2 * BLOCK), value_out)):
        out[:, span(half * START, PART, 128)] = total[rows]
        out[:, span((1 - half) * PART, REST, 128)] = theirs[rows]


def place_keys(where, mine, received, theirs):
    return pl.pallas_call(
        place_keys_kernel,
        out_shape=(shaped((BLOCK, WIDTH), bf16),) * 2,
        in_specs=[SMEM, VMEM, VMEM, VMEM],
        out_specs=(VMEM, VMEM),
        compiler_params=params(),
        cost_estimate=estimate(0, 2_000_000),
        name="place_keys",
    )(where, mine, received, theirs)


def weight_kernel(where, piece0, piece1, piece2, piece3, cot0, cot1, cot2, cot3, kept, *sent):
    products = None
    for piece, cot in ((piece0, cot0), (piece1, cot1), (piece2, cot2), (piece3, cot3)):
        product = times(piece[...], cot[...], ((1,), (0,)))
        products = product if products is None else products + product
    total = sent[-1]
    total[...] = products
    group = where[1]
    lanes = kept.shape[1]
    kept[...] = total[:, at(group, lanes)]
    for number, out in enumerate(sent[:-1]):
        target = jnp.bitwise_xor(group, number + 1)
        out[...] = total[:, at(target, lanes)].astype(bf16)


def weight_products(where, pieces, cots, groups):
    rows = pieces[0].shape[0]
    outs = cots[0].shape[1]
    part = (rows, outs // groups)
    return pl.pallas_call(
        weight_kernel,
        out_shape=(shaped(part, f32),) + (shaped(part, bf16),) * (groups - 1),
        in_specs=[SMEM] + [VMEM] * 8,
        out_specs=(VMEM,) * groups,
        scratch_shapes=[pltpu.VMEM((rows, outs), f32)],
        compiler_params=params(),
        cost_estimate=estimate(300_000_000, 3_000_000),
        name="weight_products",
    )(where, *pieces, *cots)


def weight_sum_kernel(where, kept, *rest):
    received, (first, second, total) = rest[:-3], rest[-3:]
    value = kept[...]
    for part in received:
        value = value + part[...].astype(f32)
    total[...] = value
    lanes = first.shape[1]
    odd = jnp.bitwise_and(where[2], 1)
    first[...] = total[:, at(odd, lanes)]
    second[...] = total[:, at(1 - odd, lanes)]


def weight_sum(where, kept, received):
    rows, lanes = kept.shape
    return pl.pallas_call(
        weight_sum_kernel,
        out_shape=(shaped((rows, lanes // 2), f32),) * 2,
        in_specs=[SMEM, VMEM] + [VMEM] * len(received),
        out_specs=(VMEM, VMEM),
        scratch_shapes=[pltpu.VMEM((rows, lanes), f32)],
        compiler_params=params(),
        cost_estimate=estimate(0, 800_000),
        name="weight_sum",
    )(where, kept, *received)


def weight_place_kernel(where, first, second, out, stacked):
    half = where[0]
    rows = first.shape[0]
    stacked[span(half * rows, rows, 16)] = first[...]
    stacked[span((1 - half) * rows, rows, 16)] = second[...]
    out[...] = stacked[...].T


def weight_place(where, first, second):
    rows, lanes = first.shape
    return pl.pallas_call(
        weight_place_kernel,
        out_shape=shaped((lanes, 2 * rows), f32),
        in_specs=[SMEM, VMEM, VMEM],
        out_specs=VMEM,
        scratch_shapes=[pltpu.VMEM((2 * rows, lanes), f32)],
        compiler_params=params(),
        cost_estimate=estimate(0, 400_000),
        name="weight_place",
    )(where, first, second)


def swapped(value, axis, bits):
    count = lax.axis_size(axis)
    return lax.ppermute(value, axis, [(source, source ^ bits) for source in range(count)])


def moved(value, axis, steps):
    count = lax.axis_size(axis)
    first, last = (max(0, -steps), min(count, count - steps))
    return lax.ppermute(value, axis, [(source, source + steps) for source in range(first, last)])


def placed(value, flip):
    lanes = lax.axis_size("ctx")
    moves = []
    for source in range(lax.axis_size("dp")):
        for index in range(lanes):
            group, half = index // 2, index % 2
            target_half = (source % 2) ^ flip
            target = 2 * half + source // 2
            moves.append((source * lanes + index, target * lanes + 2 * group + target_half))
    return lax.ppermute(value, ("dp", "ctx"), moves)


def per_device(queries, key_states, value_states, out_cotangent, out_weight, block_clip):
    sequences = lax.axis_size("dp")
    groups = lax.axis_size("ctx") // 2
    short = sequences == 4 and groups in (2, 4)
    index = lax.axis_index("ctx")
    where = jnp.stack([index % 2, index // 2, lax.axis_index("dp")]).astype(jnp.int32)
    query, cotangent = queries[0], out_cotangent[0]

    swap_kv, own, swap_query = pack(where, block_clip, query, key_states[0], value_states[0])
    partner = swapped(swap_kv, "ctx", 1)
    halo = moved(own, "ctx", 2)
    cot_partner = swapped(cotangent, "ctx", 1)
    halo_other = moved(partner, "ctx", 2)
    query_partner = swapped(swap_query, "ctx", 1)
    d_attended, cot_pair = cotangents(where, cotangent, cot_partner, out_weight)
    sources = (own, partner, halo, halo_other, query, query_partner)

    weights, att_own, att_swap, *pieces = forward(where, 4 if short else 0, *sources)
    if short:
        cot_y = swapped(cot_pair, "dp", 2)
        cots = (cot_pair, swapped(cot_pair, "dp", 1), cot_y, swapped(cot_y, "dp", 1))
        received = [pieces[0]] + [swapped(pieces[n], "dp", n) for n in (1, 2, 3)]
    att_rest = swapped(att_swap, "ctx", 1)
    dq_own, dq_swap, halo_grads, halo_other_grads, own_grads, partner_grads = backward(
        where, *sources, weights, d_attended
    )
    partner_late = moved(halo_other_grads, "ctx", -2)
    own_late = moved(halo_grads, "ctx", -2)
    dq_rest = swapped(dq_swap, "ctx", 1)
    sublayer_out, att_full = output_rows(where, att_own, att_rest, out_weight)
    if short:
        kept, *sent = weight_products(where, received, cots, groups)
        arrived = [swapped(part, "ctx", 2 * (n + 1)) for n, part in enumerate(sent)]
        first, second = weight_sum(where, kept, arrived)
        weight_grad = weight_place(where, placed(first, 0), placed(second, 1))
    else:
        product = lax.dot_general(
            cotangent, att_full, (((0,), (1,)), ((), ())), preferred_element_type=f32
        ).astype(bf16)
        sequence_grad = lax.psum_scatter(product, "ctx", scatter_dimension=0, tiled=True)
        weight_grad = lax.psum_scatter(
            sequence_grad.astype(f32), "dp", scatter_dimension=1, tiled=True
        )
    query_grad = place_query(where, dq_own, dq_rest)
    kv_rest = swapped(add_partner(where, partner_grads, partner_late), "ctx", 1)
    key_grad, value_grad = place_keys(where, own_grads, own_late, kv_rest)
    return (
        sublayer_out[None],
        query_grad[None],
        key_grad[None],
        value_grad[None],
        weight_grad,
    )


def solution(mesh):
    return jax.shard_map(
        per_device,
        mesh=mesh,
        in_specs=(
            P("dp", "ctx", None),
            P("dp", "ctx", None),
            P("dp", "ctx", None),
            P("dp", "ctx", None),
            P(),
            P("dp", "ctx"),
        ),
        out_specs=(
            P("dp", "ctx", None),
            P("dp", "ctx", None),
            P("dp", "ctx", None),
            P("dp", "ctx", None),
            P("ctx", "dp"),
        ),
        check_vma=False,
    )
```

time: 212 us -> 96 us (0.45); the launches traced: 208 us -> 95.6 us
  matrix products: 82.3 us -> 0 us
  Pallas kernels: 0 us -> 26.1 us
  local copies, waits for them, and re-layouts: 30.2 us -> 7.58 us
  other arithmetic: 18.4 us -> 0.08 us
  between operations: 14.9 us -> 1.45 us
  starting transfers between devices: 36.2 us -> 32.1 us
  waiting for transfers between devices: 25.8 us -> 28.3 us
    dot_general x66 -> x0, matrix products: 82.3 us -> none  [the longest x9 14.2 us: backward_one_group(): jnp.einsum('hqk,hqd->hkd', d_scores, query_head, preferred_element_type=j...]
    pallas_call x0 -> x11, Pallas kernels: none -> 26.1 us  [the longest x1 8.09 us: backward(): pl.pallas_call(backward_kernel, out_shape=(shaped((BLOCK, PART), bf16), s...]
    ppermute x10 -> x21, waiting for transfers between devices: 16.9 us -> 28.3 us  [the longest x15 19.6 us: swapped(): lax.ppermute(value, axis, [(source, source ^ bits) for source in range(co...]
    reduce_scatter x1 -> x0, waiting for transfers between devices: 8.83 us -> none  [per_device(): lax.psum_scatter(sequence_grad, 'dp', scatter_dimension=1, tiled=True)]
    unnamed x24 -> x17, local copies, waits for them, and re-layouts: 14.7 us -> 7.58 us
    sub x9 -> x0, local copies, waits for them, and re-layouts: 6.21 us -> none  [backward_one_group(): probs = jnp.exp(scores - total_head[:, :, None])]
    dynamic_update_slice x9 -> x0, other arithmetic: 5.2 us -> none  [forward_block(): mixed, log_total = lax.map(forward_one_group, stacked)]
    ppermute x10 -> x21, starting transfers between devices: 36.1 us -> 32.1 us  [the longest x15 17.4 us: swapped(): lax.ppermute(value, axis, [(source, source ^ bits) for source in range(co...]
  transfers between devices with their start and end apart: 12 -> 21, of which waited for: 4 -> 7; matrix products, arithmetic and copies ran while one was open for 39% -> 0% of each run, Pallas kernels for 0% -> 26%
where the time goes in v1:
time: 96 us; the launch traced here: 95.6 us
  starting transfers between devices  32.1 us (33%)
  waiting for transfers between devices  28.3 us (29%)
  Pallas kernels  26.1 us (27%)
  local copies, waits for them, and re-layouts  7.58 us (8%)
  between operations  1.45 us (2%)
    ppermute x15, waiting for transfers between devices, swapped(): lax.ppermute(value, axis, [(source, source ^ bits) for source in range(co...  19.6 us
    ppermute x15, starting transfers between devices, swapped(): lax.ppermute(value, axis, [(source, source ^ bits) for source in range(co...  17.4 us
    ppermute x4, starting transfers between devices, moved(): lax.ppermute(value, axis, [(source, source + steps) for source in range(f...  10.7 us
    ppermute x4, waiting for transfers between devices, moved(): lax.ppermute(value, axis, [(source, source + steps) for source in range(f...  8.72 us
    pallas_call x1, Pallas kernels, backward(): pl.pallas_call(backward_kernel, out_shape=(shaped((BLOCK, PART), bf16), s...  8.09 us
    unnamed x17, local copies, waits for them, and re-layouts  7.58 us
    pallas_call x1, Pallas kernels, forward(): pl.pallas_call(functools.partial(forward_kernel, pieces_wanted), out_shap...  6.36 us
    ppermute x2, starting transfers between devices, placed(): return lax.ppermute(value, ('dp', 'ctx'), moves)  3.9 us
  transfers between devices with their start and end apart: 21, of which 7 were waited for; matrix products, arithmetic and copies ran while one was open for 0% of the time, Pallas kernels for 26%

profile of v1, /device:TPU:0, one launch (start us, length us, event | category | flops | bytes accessed | tf_op | source)
XLA Modules:
  0.0 95.6 jit_solution(1717981261464749855)
XLA Ops:
  4.9 3.0 %collective-permute-start = (bf16[272,640]{1,0:T(8,128)(2,1)S(1)}, bf16[272,640]{1,0:T(8,128)(2,1)S(1)}, u32[]{:S(2)}, u32[]{:S(2)}) collective-permute-start(bf16[272,640]{1,0:T(8,128)(2,1)S(1)} %get-tuple-element.33), channel_id=1, source_target_pairs={{0,1},{1,0},{2,3},{3,2},{4,5},{5,4},{6,7},{7,6},{8,9},{9,8},{10,11... | collective-permute-start | bytes 1044488 | tf_op jit(solution)/shard_map/ppermute | solution.py:539
  8.0 3.9 %collective-permute-start.1 = (bf16[272,640]{1,0:T(8,128)(2,1)S(1)}, bf16[272,640]{1,0:T(8,128)(2,1)S(1)}, u32[]{:S(2)}, u32[]{:S(2)}) collective-permute-start(bf16[272,640]{1,0:T(8,128)(2,1)S(1)} %get-tuple-element.32.own), channel_id=1, source_target_pairs={{0,2},{1,3},{2,4},{3,5},{4,6},{5,7},{8,10},{9,11},{10,12},{11,13},... | collective-permute-start | bytes 1044488 | tf_op jit(solution)/shard_map/ppermute | solution.py:545
  11.9 4.9 %collective-permute-done.partner = bf16[272,640]{1,0:T(8,128)(2,1)S(1)} collective-permute-done((bf16[272,640]{1,0:T(8,128)(2,1)S(1)}, bf16[272,640]{1,0:T(8,128)(2,1)S(1)}, u32[]{:S(2)}, u32[]{:S(2)}) %collective-permute-start) | collective-permute-done | bytes 348192 | tf_op jit(solution)/shard_map/ppermute | solution.py:539
  16.9 4.1 %collective-permute-start.2 = (bf16[272,640]{1,0:T(8,128)(2,1)S(1)}, bf16[272,640]{1,0:T(8,128)(2,1)S(1)}, u32[]{:S(2)}, u32[]{:S(2)}) collective-permute-start(bf16[272,640]{1,0:T(8,128)(2,1)S(1)} %collective-permute-done.partner), channel_id=1, source_target_pairs={{0,2},{1,3},{2,4},{3,5},{4,6},{5,7},{8,10},{9,11},{10,12},{11,13},... | collective-permute-start | bytes 1044488 | tf_op jit(solution)/shard_map/ppermute | solution.py:545
  21.7 1.7 %copy-done = bf16[1024,1152]{1,0:T(8,128)(2,1)S(1)} copy-done((bf16[1024,1152]{1,0:T(8,128)(2,1)S(1)}, bf16[1024,1152]{1,0:T(8,128)(2,1)}, u32[]{:S(2)}) %copy-start) | copy-done | bytes 2359320
  24.3 2.4 %cotangents.1 = (bf16[256,640]{1,0:T(8,128)(2,1)S(1)}, bf16[256,1024]{1,0:T(8,128)(2,1)S(1)}) custom-call(s32[3]{0:T(128)S(1)} %pad_add_fusion.where, bf16[128,1024]{1,0:T(8,128)(2,1)S(1)} %bitcast.17, bf16[128,1024]{1,0:T(8,128)(2,1)S(1)} %collective-permute-done.5.partner, bf16[1024,1152]{1,0:T(8,128)(2,1)S(1)} %copy-done), custom_call_target="tpu_custom_call" | custom-call | flops 700000000 | bytes 3000000 | tf_op jit(solution)/shard_map/cotangents/pallas_call | solution.py:238
  26.7 1.8 %collective-permute-start.14 = (bf16[256,1024]{1,0:T(8,128)(2,1)S(1)}, bf16[256,1024]{1,0:T(8,128)(2,1)S(1)}, u32[]{:S(2)}, u32[]{:S(2)}) collective-permute-start(bf16[256,1024]{1,0:T(8,128)(2,1)S(1)} %get-tuple-element.52.cot0), channel_id=1, source_target_pairs={{0,16},{8,24},{16,0},{24,8},{1,17},{9,25},{17,1},{25,9},{2,18},{10... | collective-permute-start | bytes 1572872 | tf_op jit(solution)/shard_map/ppermute | solution.py:539
  28.5 1.5 %collective-permute-start.3 = (bf16[128,640]{1,0:T(8,128)(2,1)S(1)}, bf16[128,640]{1,0:T(8,128)(2,1)S(1)}, u32[]{:S(2)}, u32[]{:S(2)}) collective-permute-start(bf16[128,640]{1,0:T(8,128)(2,1)S(1)} %get-tuple-element.34), channel_id=1, source_target_pairs={{0,1},{1,0},{2,3},{3,2},{4,5},{5,4},{6,7},{7,6},{8,9},{9,8},{10,11... | collective-permute-start | bytes 491528 | tf_op jit(solution)/shard_map/ppermute | solution.py:539
  30.0 3.8 %collective-permute-done.3.query_partner = bf16[128,640]{1,0:T(8,128)(2,1)S(1)} collective-permute-done((bf16[128,640]{1,0:T(8,128)(2,1)S(1)}, bf16[128,640]{1,0:T(8,128)(2,1)S(1)}, u32[]{:S(2)}, u32[]{:S(2)}) %collective-permute-start.3) | collective-permute-done | bytes 163872 | tf_op jit(solution)/shard_map/ppermute | solution.py:539
  33.9 6.4 %forward.1 = (bf16[5,2,384,256]{3,2,1,0:T(8,128)(2,1)S(1)}, bf16[640,128]{1,0:T(8,128)(2,1)S(1)}, bf16[512,128]{1,0:T(8,128)(2,1)S(1)}, bf16[144,256]{1,0:T(8,12...) custom-call(s32[3]{0:T(128)S(1)} %pad_add_fusion.where, ...), custom_call_target="tpu_custom_call" | custom-call | flops 2000000000 | bytes 6000000 | tf_op jit(solution)/shard_map/forward/pallas_call | solution.py:191
  40.2 1.3 %copy-done.7 = bf16[5,2,384,256]{3,2,1,0:T(8,128)(2,1)} copy-done((bf16[5,2,384,256]{3,2,1,0:T(8,128)(2,1)}, bf16[5,2,384,256]{3,2,1,0:T(8,128)(2,1)S(1)}, u32[]{:S(2)}) %copy-start.7) | copy-done | bytes 1966104
  41.5 8.1 %backward.1 = (bf16[128,640]{1,0:T(8,128)(2,1)S(1)}, bf16[128,512]{1,0:T(8,128)(2,1)S(1)}, bf16[256,640]{1,0:T(8,128)(2,1)S(1)}, bf16[256,640]{1,0:T(8,128)(2,1)...) custom-call(s32[3]{0:T(128)S(1)} %pad_add_fusion.where, bf16[272,640]{1,0:T(8,128)(2,1)S(1)} %get-tuple-element.32.own, ...), custom_call_target="tpu_custom_call" | custom-call | flops 4000000000 | bytes 8000000 | tf_op jit(solution)/shard_map/backward/pallas_call | solution.py:319
  49.7 1.4 %collective-permute-start.8 = (bf16[256,640]{1,0:T(8,128)(2,1)S(1)}, bf16[256,640]{1,0:T(8,128)(2,1)S(1)}, u32[]{:S(2)}, u32[]{:S(2)}) collective-permute-start(bf16[256,640]{1,0:T(8,128)(2,1)S(1)} %get-tuple-element.45), channel_id=1, source_target_pairs={{2,0},{3,1},{4,2},{5,3},{6,4},{7,5},{10,8},{11,9},{12,10},{13,11},... | collective-permute-start | bytes 983048 | tf_op jit(solution)/shard_map/ppermute | solution.py:545
  53.1 8.7 %collective-permute-done.8.received = bf16[256,640]{1,0:T(8,128)(2,1)S(1)} collective-permute-done((bf16[256,640]{1,0:T(8,128)(2,1)S(1)}, bf16[256,640]{1,0:T(8,128)(2,1)S(1)}, u32[]{:S(2)}, u32[]{:S(2)}) %collective-permute-start.8) | collective-permute-done | bytes 327712 | tf_op jit(solution)/shard_map/ppermute | solution.py:545
  61.8 1.3 %collective-permute-start.7 = (bf16[256,640]{1,0:T(8,128)(2,1)S(1)}, bf16[256,640]{1,0:T(8,128)(2,1)S(1)}, u32[]{:S(2)}, u32[]{:S(2)}) collective-permute-start(bf16[256,640]{1,0:T(8,128)(2,1)S(1)} %get-tuple-element.43), channel_id=1, source_target_pairs={{2,0},{3,1},{4,2},{5,3},{6,4},{7,5},{10,8},{11,9},{12,10},{13,11},... | collective-permute-start | bytes 983048 | tf_op jit(solution)/shard_map/ppermute | solution.py:545
  63.7 1.6 %collective-permute-start.9 = (bf16[256,512]{1,0:T(8,128)(2,1)S(1)}, bf16[256,512]{1,0:T(8,128)(2,1)S(1)}, u32[]{:S(2)}, u32[]{:S(2)}) collective-permute-start(bf16[256,512]{1,0:T(8,128)(2,1)S(1)} %add_partner.1), channel_id=1, source_target_pairs={{0,1},{1,0},{2,3},{3,2},{4,5},{5,4},{6,7},{7,6},{8,9},{9,8},{10,11... | collective-permute-start | bytes 786440 | tf_op jit(solution)/shard_map/ppermute | solution.py:539
  66.4 2.7 %collective-permute-start.16 = (bf16[144,256]{1,0:T(8,128)(2,1)S(1)}, bf16[144,256]{1,0:T(8,128)(2,1)S(1)}, u32[]{:S(2)}, u32[]{:S(2)}) collective-permute-start(bf16[144,256]{1,0:T(8,128)(2,1)S(1)} %get-tuple-element.54), channel_id=1, source_target_pairs={{0,2},{1,3},{2,0},{3,1},{4,6},{5,7},{6,4},{7,5},{8,10},{9,11},{10,... | collective-permute-start | bytes 221192 | tf_op jit(solution)/shard_map/ppermute | solution.py:539
  69.1 2.6 %collective-permute-start.17 = (bf16[144,256]{1,0:T(8,128)(2,1)S(1)}, bf16[144,256]{1,0:T(8,128)(2,1)S(1)}, u32[]{:S(2)}, u32[]{:S(2)}) collective-permute-start(bf16[144,256]{1,0:T(8,128)(2,1)S(1)} %get-tuple-element.55), channel_id=1, source_target_pairs={{0,4},{1,5},{2,6},{3,7},{4,0},{5,1},{6,2},{7,3},{8,12},{9,13},{10,... | collective-permute-start | bytes 221192 | tf_op jit(solution)/shard_map/ppermute | solution.py:539
  72.2 4.0 %collective-permute-done.16.rest_0_ = bf16[144,256]{1,0:T(8,128)(2,1)S(1)} collective-permute-done((bf16[144,256]{1,0:T(8,128)(2,1)S(1)}, bf16[144,256]{1,0:T(8,128)(2,1)S(1)}, u32[]{:S(2)}, u32[]{:S(2)}) %collective-permute-start.16) | collective-permute-done | bytes 73760 | tf_op jit(solution)/shard_map/ppermute | solution.py:539
  76.2 1.5 %collective-permute-start.4 = (bf16[512,128]{1,0:T(8,128)(2,1)S(1)}, bf16[512,128]{1,0:T(8,128)(2,1)S(1)}, u32[]{:S(2)}, u32[]{:S(2)}) collective-permute-start(bf16[512,128]{1,0:T(8,128)(2,1)S(1)} %get-tuple-element.36), channel_id=1, source_target_pairs={{0,1},{1,0},{2,3},{3,2},{4,5},{5,4},{6,7},{7,6},{8,9},{9,8},{10,11... | collective-permute-start | bytes 393224 | tf_op jit(solution)/shard_map/ppermute | solution.py:539
  78.5 5.4 %collective-permute-done.18.rest_2_ = bf16[144,256]{1,0:T(8,128)(2,1)S(1)} collective-permute-done((bf16[144,256]{1,0:T(8,128)(2,1)S(1)}, bf16[144,256]{1,0:T(8,128)(2,1)S(1)}, u32[]{:S(2)}, u32[]{:S(2)}) %collective-permute-start.18) | collective-permute-done | bytes 73760 | tf_op jit(solution)/shard_map/ppermute | solution.py:539
  85.2 3.2 %collective-permute-start.20 = (f32[144,128]{1,0:T(8,128)S(1)}, f32[144,128]{1,0:T(8,128)S(1)}, u32[]{:S(2)}, u32[]{:S(2)}) collective-permute-start(f32[144,128]{1,0:T(8,128)S(1)} %get-tuple-element.58), channel_id=1, source_target_pairs={{0,1},{1,17},{2,3},{3,19},{4,5},{5,21},{6,7},{7,23},{8,0},{9,16},{... | collective-permute-start | bytes 221192 | tf_op jit(solution)/shard_map/ppermute | solution.py:557
  89.7 3.0 %output.1 = (bf16[128,1024]{1,0:T(8,128)(2,1)}, bf16[1152,128]{1,0:T(8,128)(2,1)}) custom-call(s32[3]{0:T(128)S(1)} %pad_add_fusion.where, bf16[640,128]{1,0:T(8,128)(2,1)S(1)} %get-tuple-element.35.att_own, bf16[512,128]{1,0:T(8,128)(2,1)S(1)} %collective-permute-done.4.att_rest, bf16[1024,1152]{1,0:T(8,128)(2,1)S(1)} %copy-done.1), custom_call_target="tpu_custom_call" | custom-call | flops 300000000 | bytes 3000000 | tf_op jit(solution)/shard_map/output/pallas_call | solution.py:381
  92.7 1.4 %place_keys.1 = (bf16[128,1152]{1,0:T(8,128)(2,1)}, bf16[128,1152]{1,0:T(8,128)(2,1)}) custom-call(s32[3]{0:T(128)S(1)} %pad_add_fusion.where, f32[256,640]{1,0:T(8,128)S(1)} %get-tuple-element.42.mine, bf16[256,640]{1,0:T(8,128)(2,1)S(1)} %collective-permute-done.7.received, bf16[256,512]{1,0:T(8,128)(2,1)S(1)} %collective-permute-done.9.theirs), custom_call_target="tpu_custom_call" | custom-call | bytes 2000000 | tf_op jit(solution)/shard_map/place_keys/pallas_call | solution.py:447
  (47 shorter events, 14.3 us)
Async XLA Ops:
  4.3 29.6 %copy-start.5 = (bf16[1,128,1152]{2,1,0:T(8,128)(2,1)S(1)}, bf16[1,128,1152]{2,1,0:T(8,128)(2,1)}, u32[]{:S(2)}) copy-start(bf16[1,128,1152]{2,1,0:T(8,128)(2,1)} %param.6) | copy-start | bytes 884740
  4.9 12.0 %collective-permute-start = (bf16[272,640]{1,0:T(8,128)(2,1)S(1)}, bf16[272,640]{1,0:T(8,128)(2,1)S(1)}, u32[]{:S(2)}, u32[]{:S(2)}) collective-permute-start(bf16[272,640]{1,0:T(8,128)(2,1)S(1)} %get-tuple-element.33), channel_id=1, source_target_pairs={{0,1},{1,0},{2,3},{3,2},{4,5},{5,4},{6,7},{7,6},{8,9},{9,8},{10,11... | collective-permute-start | bytes 1044488 | tf_op jit(solution)/shard_map/ppermute | solution.py:539
  7.9 13.8 %collective-permute-start.5 = (bf16[128,1024]{1,0:T(8,128)(2,1)}, bf16[128,1024]{1,0:T(8,128)(2,1)S(1)}, u32[]{:S(2)}, u32[]{:S(2)}) collective-permute-start(bf16[128,1024]{1,0:T(8,128)(2,1)} %bitcast.16), channel_id=1, source_target_pairs={{0,1},{1,0},{2,3},{3,2},{4,5},{5,4},{6,7},{7,6},{8,9},{9,8},{10,11... | collective-permute-start | bytes 786440 | tf_op jit(solution)/shard_map/ppermute | solution.py:539
  8.0 25.9 %collective-permute-start.1 = (bf16[272,640]{1,0:T(8,128)(2,1)S(1)}, bf16[272,640]{1,0:T(8,128)(2,1)S(1)}, u32[]{:S(2)}, u32[]{:S(2)}) collective-permute-start(bf16[272,640]{1,0:T(8,128)(2,1)S(1)} %get-tuple-element.32.own), channel_id=1, source_target_pairs={{0,2},{1,3},{2,4},{3,5},{4,6},{5,7},{8,10},{9,11},{10,12},{11,13},... | collective-permute-start | bytes 1044488 | tf_op jit(solution)/shard_map/ppermute | solution.py:545
  16.9 17.0 %collective-permute-start.2 = (bf16[272,640]{1,0:T(8,128)(2,1)S(1)}, bf16[272,640]{1,0:T(8,128)(2,1)S(1)}, u32[]{:S(2)}, u32[]{:S(2)}) collective-permute-start(bf16[272,640]{1,0:T(8,128)(2,1)S(1)} %collective-permute-done.partner), channel_id=1, source_target_pairs={{0,2},{1,3},{2,4},{3,5},{4,6},{5,7},{8,10},{9,11},{10,12},{11,13},... | collective-permute-start | bytes 1044488 | tf_op jit(solution)/shard_map/ppermute | solution.py:545
  21.7 1.7 %copy-start = (bf16[1024,1152]{1,0:T(8,128)(2,1)S(1)}, bf16[1024,1152]{1,0:T(8,128)(2,1)}, u32[]{:S(2)}) copy-start(bf16[1024,1152]{1,0:T(8,128)(2,1)} %weight.3) | copy-start | bytes 7077892
  26.7 14.8 %collective-permute-start.14 = (bf16[256,1024]{1,0:T(8,128)(2,1)S(1)}, bf16[256,1024]{1,0:T(8,128)(2,1)S(1)}, u32[]{:S(2)}, u32[]{:S(2)}) collective-permute-start(bf16[256,1024]{1,0:T(8,128)(2,1)S(1)} %get-tuple-element.52.cot0), channel_id=1, source_target_pairs={{0,16},{8,24},{16,0},{24,8},{1,17},{9,25},{17,1},{25,9},{2,18},{10... | collective-permute-start | bytes 1572872 | tf_op jit(solution)/shard_map/ppermute | solution.py:539
  28.5 5.3 %collective-permute-start.3 = (bf16[128,640]{1,0:T(8,128)(2,1)S(1)}, bf16[128,640]{1,0:T(8,128)(2,1)S(1)}, u32[]{:S(2)}, u32[]{:S(2)}) collective-permute-start(bf16[128,640]{1,0:T(8,128)(2,1)S(1)} %get-tuple-element.34), channel_id=1, source_target_pairs={{0,1},{1,0},{2,3},{3,2},{4,5},{5,4},{6,7},{7,6},{8,9},{9,8},{10,11... | collective-permute-start | bytes 491528 | tf_op jit(solution)/shard_map/ppermute | solution.py:539
  30.0 35.3 %collective-permute-start.13 = (bf16[256,1024]{1,0:T(8,128)(2,1)S(1)}, bf16[256,1024]{1,0:T(8,128)(2,1)S(1)}, u32[]{:S(2)}, u32[]{:S(2)}) collective-permute-start(bf16[256,1024]{1,0:T(8,128)(2,1)S(1)} %get-tuple-element.52.cot0), channel_id=1, source_target_pairs={{0,8},{8,0},{16,24},{24,16},{1,9},{9,1},{17,25},{25,17},{2,10},{10... | collective-permute-start | bytes 1572872 | tf_op jit(solution)/shard_map/ppermute | solution.py:539
  41.5 23.8 %collective-permute-start.15 = (bf16[256,1024]{1,0:T(8,128)(2,1)S(1)}, bf16[256,1024]{1,0:T(8,128)(2,1)S(1)}, u32[]{:S(2)}, u32[]{:S(2)}) collective-permute-start(bf16[256,1024]{1,0:T(8,128)(2,1)S(1)} %collective-permute-done.14.cot2), channel_id=1, source_target_pairs={{0,8},{8,0},{16,24},{24,16},{1,9},{9,1},{17,25},{25,17},{2,10},{10... | collective-permute-start | bytes 1572872 | tf_op jit(solution)/shard_map/ppermute | solution.py:539
  49.6 40.0 %copy-start.1 = (bf16[1024,1152]{1,0:T(8,128)(2,1)S(1)}, bf16[1024,1152]{1,0:T(8,128)(2,1)}, u32[]{:S(2)}) copy-start(bf16[1024,1152]{1,0:T(8,128)(2,1)} %weight.3) | copy-start | bytes 7077892
  49.7 12.2 %collective-permute-start.8 = (bf16[256,640]{1,0:T(8,128)(2,1)S(1)}, bf16[256,640]{1,0:T(8,128)(2,1)S(1)}, u32[]{:S(2)}, u32[]{:S(2)}) collective-permute-start(bf16[256,640]{1,0:T(8,128)(2,1)S(1)} %get-tuple-element.45), channel_id=1, source_target_pairs={{2,0},{3,1},{4,2},{5,3},{6,4},{7,5},{10,8},{11,9},{12,10},{13,11},... | collective-permute-start | bytes 983048 | tf_op jit(solution)/shard_map/ppermute | solution.py:545
  51.1 1.5 %collective-permute-start.10 = (bf16[144,256]{1,0:T(8,128)(2,1)S(1)}, bf16[144,256]{1,0:T(8,128)(2,1)S(1)}, u32[]{:S(2)}, u32[]{:S(2)}) collective-permute-start(bf16[144,256]{1,0:T(8,128)(2,1)S(1)} %get-tuple-element.49), channel_id=1, source_target_pairs={{0,8},{8,0},{16,24},{24,16},{1,9},{9,1},{17,25},{25,17},{2,10},{10... | collective-permute-start | bytes 221192 | tf_op jit(solution)/shard_map/ppermute | solution.py:539
  51.7 12.0 %collective-permute-start.11 = (bf16[144,256]{1,0:T(8,128)(2,1)S(1)}, bf16[144,256]{1,0:T(8,128)(2,1)S(1)}, u32[]{:S(2)}, u32[]{:S(2)}) collective-permute-start(bf16[144,256]{1,0:T(8,128)(2,1)S(1)} %get-tuple-element.50), channel_id=1, source_target_pairs={{0,16},{8,24},{16,0},{24,8},{1,17},{9,25},{17,1},{25,9},{2,18},{10... | collective-permute-start | bytes 221192 | tf_op jit(solution)/shard_map/ppermute | solution.py:539
  52.6 12.7 %collective-permute-start.12 = (bf16[144,256]{1,0:T(8,128)(2,1)S(1)}, bf16[144,256]{1,0:T(8,128)(2,1)S(1)}, u32[]{:S(2)}, u32[]{:S(2)}) collective-permute-start(bf16[144,256]{1,0:T(8,128)(2,1)S(1)} %get-tuple-element.51), channel_id=1, source_target_pairs={{0,24},{8,16},{16,8},{24,0},{1,25},{9,17},{17,9},{25,1},{2,26},{10... | collective-permute-start | bytes 221192 | tf_op jit(solution)/shard_map/ppermute | solution.py:539
  61.8 30.9 %collective-permute-start.7 = (bf16[256,640]{1,0:T(8,128)(2,1)S(1)}, bf16[256,640]{1,0:T(8,128)(2,1)S(1)}, u32[]{:S(2)}, u32[]{:S(2)}) collective-permute-start(bf16[256,640]{1,0:T(8,128)(2,1)S(1)} %get-tuple-element.43), channel_id=1, source_target_pairs={{2,0},{3,1},{4,2},{5,3},{6,4},{7,5},{10,8},{11,9},{12,10},{13,11},... | collective-permute-start | bytes 983048 | tf_op jit(solution)/shard_map/ppermute | solution.py:545
  63.7 29.0 %collective-permute-start.9 = (bf16[256,512]{1,0:T(8,128)(2,1)S(1)}, bf16[256,512]{1,0:T(8,128)(2,1)S(1)}, u32[]{:S(2)}, u32[]{:S(2)}) collective-permute-start(bf16[256,512]{1,0:T(8,128)(2,1)S(1)} %add_partner.1), channel_id=1, source_target_pairs={{0,1},{1,0},{2,3},{3,2},{4,5},{5,4},{6,7},{7,6},{8,9},{9,8},{10,11... | collective-permute-start | bytes 786440 | tf_op jit(solution)/shard_map/ppermute | solution.py:539
  66.4 9.8 %collective-permute-start.16 = (bf16[144,256]{1,0:T(8,128)(2,1)S(1)}, bf16[144,256]{1,0:T(8,128)(2,1)S(1)}, u32[]{:S(2)}, u32[]{:S(2)}) collective-permute-start(bf16[144,256]{1,0:T(8,128)(2,1)S(1)} %get-tuple-element.54), channel_id=1, source_target_pairs={{0,2},{1,3},{2,0},{3,1},{4,6},{5,7},{6,4},{7,5},{8,10},{9,11},{10,... | collective-permute-start | bytes 221192 | tf_op jit(solution)/shard_map/ppermute | solution.py:539
  69.1 8.6 %collective-permute-start.17 = (bf16[144,256]{1,0:T(8,128)(2,1)S(1)}, bf16[144,256]{1,0:T(8,128)(2,1)S(1)}, u32[]{:S(2)}, u32[]{:S(2)}) collective-permute-start(bf16[144,256]{1,0:T(8,128)(2,1)S(1)} %get-tuple-element.55), channel_id=1, source_target_pairs={{0,4},{1,5},{2,6},{3,7},{4,0},{5,1},{6,2},{7,3},{8,12},{9,13},{10,... | collective-permute-start | bytes 221192 | tf_op jit(solution)/shard_map/ppermute | solution.py:539
  71.7 13.5 %collective-permute-start.6 = (bf16[128,512]{1,0:T(8,128)(2,1)S(1)}, bf16[128,512]{1,0:T(8,128)(2,1)S(1)}, u32[]{:S(2)}, u32[]{:S(2)}) collective-permute-start(bf16[128,512]{1,0:T(8,128)(2,1)S(1)} %get-tuple-element.41), channel_id=1, source_target_pairs={{0,1},{1,0},{2,3},{3,2},{4,5},{5,4},{6,7},{7,6},{8,9},{9,8},{10,11... | collective-permute-start | bytes 393224 | tf_op jit(solution)/shard_map/ppermute | solution.py:539
  76.2 13.5 %collective-permute-start.4 = (bf16[512,128]{1,0:T(8,128)(2,1)S(1)}, bf16[512,128]{1,0:T(8,128)(2,1)S(1)}, u32[]{:S(2)}, u32[]{:S(2)}) collective-permute-start(bf16[512,128]{1,0:T(8,128)(2,1)S(1)} %get-tuple-element.36), channel_id=1, source_target_pairs={{0,1},{1,0},{2,3},{3,2},{4,5},{5,4},{6,7},{7,6},{8,9},{9,8},{10,11... | collective-permute-start | bytes 393224 | tf_op jit(solution)/shard_map/ppermute | solution.py:539
  77.7 6.2 %collective-permute-start.18 = (bf16[144,256]{1,0:T(8,128)(2,1)S(1)}, bf16[144,256]{1,0:T(8,128)(2,1)S(1)}, u32[]{:S(2)}, u32[]{:S(2)}) collective-permute-start(bf16[144,256]{1,0:T(8,128)(2,1)S(1)} %get-tuple-element.56), channel_id=1, source_target_pairs={{0,6},{1,7},{2,4},{3,5},{4,2},{5,3},{6,0},{7,1},{8,14},{9,15},{10,... | collective-permute-start | bytes 221192 | tf_op jit(solution)/shard_map/ppermute | solution.py:539
  84.5 9.7 %collective-permute-start.19 = (f32[144,128]{1,0:T(8,128)S(1)}, f32[144,128]{1,0:T(8,128)S(1)}, u32[]{:S(2)}, u32[]{:S(2)}) collective-permute-start(f32[144,128]{1,0:T(8,128)S(1)} %get-tuple-element.57), channel_id=1, source_target_pairs={{0,0},{1,16},{2,2},{3,18},{4,4},{5,20},{6,6},{7,22},{8,1},{9,17},{... | collective-permute-start | bytes 221192 | tf_op jit(solution)/shard_map/ppermute | solution.py:557
  85.2 9.0 %collective-permute-start.20 = (f32[144,128]{1,0:T(8,128)S(1)}, f32[144,128]{1,0:T(8,128)S(1)}, u32[]{:S(2)}, u32[]{:S(2)}) collective-permute-start(f32[144,128]{1,0:T(8,128)S(1)} %get-tuple-element.58), channel_id=1, source_target_pairs={{0,1},{1,17},{2,3},{3,19},{4,5},{5,21},{6,7},{7,23},{8,0},{9,16},{... | collective-permute-start | bytes 221192 | tf_op jit(solution)/shard_map/ppermute | solution.py:557
  (5 other events, 5.1 us)

commit v2 on v1

v2 whole, which is shorter than its diff:
```python
import functools
import math

import jax
import jax.numpy as jnp
from jax import lax
from jax.experimental import pallas as pl
from jax.experimental.pallas import tpu as pltpu
from jax.sharding import PartitionSpec as P

HEADS = 18
HDIM = 64
BLOCK = 128
WIN = 256
PAIR = 2 * HDIM
WIDTH = HEADS * HDIM
PAIRS = (HEADS + 2) // 4
PART = PAIRS * PAIR
START = WIDTH - PART
REST = WIDTH - PART
CLIP_ROWS = 16
CHUNKS = 4
DELTA_ROWS = (2 * PAIRS + 7) // 8 * 8
PAYLOAD = 2 * BLOCK + CLIP_ROWS
SCALING = 1.0 / math.sqrt(HDIM)
VMEM_LIMIT = 24 * 1024 * 1024

big_negative = -1e30
bf16 = jnp.bfloat16
f32 = jnp.float32

SMEM = pl.BlockSpec(memory_space=pltpu.SMEM)
VMEM = pl.BlockSpec(memory_space=pltpu.VMEM)
HBM = pl.BlockSpec(memory_space=pltpu.HBM)


def shaped(shape, dtype):
    return jax.ShapeDtypeStruct(shape, dtype)


def estimate(flops, moved):
    return pl.CostEstimate(flops=flops, bytes_accessed=moved, transcendentals=0)


def params():
    return pltpu.CompilerParams(vmem_limit_bytes=VMEM_LIMIT)


def in_hbm(value):
    return pltpu.with_memory_space_constraint(value, pltpu.HBM)


def my_half():
    return jnp.bitwise_and(lax.axis_index("ctx"), 1)


def my_group():
    return jnp.right_shift(lax.axis_index("ctx"), 1)


def at(index, size):
    return pl.ds(pl.multiple_of(index * size, size), size)


def span(start, size, unit):
    return pl.ds(pl.multiple_of(start, unit), size)


def times(a, b, dims):
    return lax.dot_general(a, b, (dims, ((), ())), preferred_element_type=f32)


def pack_kernel(clip, query, key, value, swap_kv, own_kv, swap_query, query_kept, sems):
    half = my_half()
    mine = span(half * START, PART, 128)
    other = span((1 - half) * START, PART, 128)
    first, second = pl.ds(0, BLOCK), pl.ds(BLOCK, BLOCK)
    copies = [
        pltpu.make_async_copy(source.at[:, columns], target, sems.at[number])
        for number, (source, columns, target) in enumerate(
            (
                (key, other, swap_kv.at[first]),
                (value, other, swap_kv.at[second]),
                (key, mine, own_kv.at[first]),
                (value, mine, own_kv.at[second]),
                (query, other, swap_query),
                (query, mine, query_kept),
            )
        )
    ]
    for copy in copies:
        copy.start()
    clip_rows = jnp.full((CLIP_ROWS, PART), clip[0, 0].astype(f32), f32).astype(bf16)
    swap_kv[2 * BLOCK :] = clip_rows
    own_kv[2 * BLOCK :] = clip_rows
    for copy in copies:
        copy.wait()


def pack(clip, query, key, value):
    return pl.pallas_call(
        pack_kernel,
        out_shape=(
            shaped((PAYLOAD, PART), bf16),
            shaped((PAYLOAD, PART), bf16),
            shaped((BLOCK, PART), bf16),
            shaped((BLOCK, PART), bf16),
        ),
        in_specs=[SMEM, HBM, HBM, HBM],
        out_specs=(VMEM,) * 4,
        scratch_shapes=[pltpu.SemaphoreType.DMA((6,))],
        compiler_params=params(),
        cost_estimate=estimate(1_000_000, 10_000),
        name="pack",
    )(clip, in_hbm(query), in_hbm(key), in_hbm(value))


def gather_rows(target, half, offset, own, partner, start=0):
    target[at(offset + half, BLOCK)] = own[start : start + BLOCK]
    target[at(offset + 1 - half, BLOCK)] = partner[start : start + BLOCK]


def doubled(rows, factor=1.0):
    lane = lax.broadcasted_iota(jnp.int32, (1, PAIR), 1)
    first = jnp.where(lane < HDIM, factor, 0.0).astype(bf16)
    second = jnp.where(lane < HDIM, 0.0, factor).astype(bf16)
    return jnp.concatenate([rows * first, rows * second], axis=0)


def diagonal(pair):
    return jnp.concatenate([pair[:HDIM, :BLOCK], pair[HDIM:, BLOCK:]], axis=0)


def fill_mask(clips, mask):
    row = lax.broadcasted_iota(jnp.int32, (BLOCK, BLOCK), 0)
    lane = lax.broadcasted_iota(jnp.int32, (BLOCK, BLOCK), 1)
    older = jnp.where(row > lane, 1.0, 0.0)
    every = jnp.ones((BLOCK, BLOCK), f32)
    causal = jnp.where(row <= lane, 1.0, 0.0)
    for query_block in range(2):
        at_query = (2 + query_block) * CLIP_ROWS
        query_clip = clips[at_query : at_query + CLIP_ROWS].astype(f32)[0:1]
        for step, shape in enumerate((older, every, causal)):
            block = query_block + step
            key_clip = clips[block * CLIP_ROWS : (block + 1) * CLIP_ROWS].astype(f32)[0:1]
            same = jnp.where(key_clip == query_clip, 1.0, 0.0)
            present = jnp.where(2 * my_group() - 2 + block >= 0, 1.0, 0.0)
            mask[query_block, step * BLOCK : (step + 1) * BLOCK] = shape * same * present


def forward_kernel(
    pieces_wanted,
    own,
    partner,
    halo,
    halo_other,
    query_own,
    query_partner,
    d_turned_own,
    d_turned_partner,
    weights_out,
    delta_out,
    att_own,
    att_swap,
    *rest,
):
    pieces = rest[:pieces_wanted]
    att, mask, key_all, value_all, query_all, clips, d_turned = rest[pieces_wanted:]
    half = my_half()
    for target, start in ((key_all, 0), (value_all, BLOCK)):
        gather_rows(target, half, 0, halo, halo_other, start)
        gather_rows(target, half, 2, own, partner, start)
    gather_rows(query_all, half, 0, query_own, query_partner)
    d_turned[:, at(half, BLOCK)] = d_turned_own[...]
    d_turned[:, at(1 - half, BLOCK)] = d_turned_partner[...]
    for offset, mine, theirs in ((0, halo, halo_other), (2, own, partner)):
        clips[at(offset + half, CLIP_ROWS)] = mine[2 * BLOCK :, :PAIR]
        clips[at(offset + 1 - half, CLIP_ROWS)] = theirs[2 * BLOCK :, :PAIR]
    fill_mask(clips, mask)

    for pair in range(PAIRS):
        columns = slice(pair * PAIR, (pair + 1) * PAIR)
        for query_block in range(2):
            keys = slice(query_block * BLOCK, query_block * BLOCK + WIN + BLOCK)
            steps = slice(query_block * BLOCK, (query_block + 1) * BLOCK)
            query_rows = doubled(query_all[steps, columns], SCALING)
            scores = times(key_all[keys, columns], query_rows, ((1,), (1,)))
            visible = mask[query_block]
            visible = jnp.concatenate([visible, visible], axis=1)
            scores = jnp.where(visible > 0.5, scores, big_negative)
            maximum = jnp.max(scores, axis=0, keepdims=True)
            powers = jnp.exp(scores - maximum)
            total = jnp.sum(powers, axis=0, keepdims=True)
            weights = (powers * (1.0 / total)).astype(bf16)
            weights_out[pair, query_block] = weights
            mixed = times(value_all[keys, columns], weights, ((0,), (0,)))
            attended = diagonal(mixed).astype(bf16)
            att[columns, steps] = attended
            dots = d_turned[columns, steps].astype(f32) * attended.astype(f32)
            number = 2 * pair + query_block
            delta_out[number : number + 1, :BLOCK] = jnp.sum(dots[:HDIM], axis=0, keepdims=True)
            delta_out[number : number + 1, BLOCK:] = jnp.sum(dots[HDIM:], axis=0, keepdims=True)

    att_own[...] = att[:, at(half, BLOCK)]
    att_swap[...] = att[span(half * PAIR, REST, PAIR), at(1 - half, BLOCK)]
    if pieces_wanted:
        rows = pieces[0].shape[0]
        for number, piece in enumerate(pieces):
            begin = half * HDIM + rows * jnp.bitwise_xor(lax.axis_index("dp"), number)
            piece[...] = att[span(begin, rows, 16), :]


def forward(pieces_wanted, *sources):
    piece = (WIDTH // 2 // max(pieces_wanted, 1), 2 * BLOCK)
    return pl.pallas_call(
        functools.partial(forward_kernel, pieces_wanted),
        out_shape=(
            shaped((PAIRS, 2, WIN + BLOCK, 2 * BLOCK), bf16),
            shaped((DELTA_ROWS, 2 * BLOCK), f32),
            shaped((PART, BLOCK), bf16),
            shaped((REST, BLOCK), bf16),
        )
        + (shaped(piece, bf16),) * pieces_wanted,
        in_specs=[VMEM] * 8,
        out_specs=(VMEM,) * (4 + pieces_wanted),
        scratch_shapes=[
            pltpu.VMEM((PART, 2 * BLOCK), bf16),
            pltpu.VMEM((2, WIN + BLOCK, BLOCK), f32),
            pltpu.VMEM((4 * BLOCK, PART), bf16),
            pltpu.VMEM((4 * BLOCK, PART), bf16),
            pltpu.VMEM((2 * BLOCK, PART), bf16),
            pltpu.VMEM((4 * CLIP_ROWS, PAIR), bf16),
            pltpu.VMEM((PART, 2 * BLOCK), bf16),
        ],
        compiler_params=params(),
        cost_estimate=estimate(1_000_000, 10_000),
        name="forward",
    )(*sources)


def own_cotangent_kernel(cotangent, weight, d_attended, d_turned, kept, rows, sems):
    chunk = rows.shape[1] // CHUNKS
    copies = [pltpu.make_async_copy(cotangent, rows, sems.at[CHUNKS])]
    for number in range(CHUNKS):
        part = pl.ds(number * chunk, chunk)
        copies.append(pltpu.make_async_copy(weight.at[part], kept.at[part], sems.at[number]))
    for copy in copies:
        copy.start()
    copies[0].wait()
    mine = span(my_half() * START, PART, 128)
    value = None
    for number in range(CHUNKS):
        copies[number + 1].wait()
        part = slice(number * chunk, (number + 1) * chunk)
        product = times(rows[:, part], kept[part, mine], ((1,), (0,)))
        value = product if value is None else value + product
    value = value.astype(bf16)
    d_attended[...] = value
    d_turned[...] = value.T


def own_cotangents(cotangent, weight):
    return pl.pallas_call(
        own_cotangent_kernel,
        out_shape=(
            shaped((BLOCK, PART), bf16),
            shaped((PART, BLOCK), bf16),
            shaped(weight.shape, bf16),
        ),
        in_specs=[HBM, HBM],
        out_specs=(VMEM,) * 3,
        scratch_shapes=[
            pltpu.VMEM(cotangent.shape, bf16),
            pltpu.SemaphoreType.DMA((CHUNKS + 1,)),
        ],
        compiler_params=params(),
        cost_estimate=estimate(1_000_000, 10_000),
        name="own_cotangents",
    )(in_hbm(cotangent), in_hbm(weight))


def cotangent_kernel(cotangent, weight, d_attended, d_turned):
    mine = span(my_half() * START, PART, 128)
    value = times(cotangent[...], weight[:, mine], ((1,), (0,))).astype(bf16)
    d_attended[...] = value
    d_turned[...] = value.T


def cotangents(cotangent, weight):
    return pl.pallas_call(
        cotangent_kernel,
        out_shape=(shaped((BLOCK, PART), bf16), shaped((PART, BLOCK), bf16)),
        in_specs=[VMEM, VMEM],
        out_specs=(VMEM,) * 2,
        compiler_params=params(),
        cost_estimate=estimate(1_000_000, 10_000),
        name="cotangents",
    )(cotangent, weight)


def halo_kernel(
    halo,
    halo_other,
    query_own,
    query_partner,
    d_own,
    d_partner,
    weights_in,
    delta_in,
    halo_grads,
    halo_other_grads,
    dq_part,
    key_all,
    value_all,
    query_all,
    d_all,
    dk_all,
    dv_all,
):
    half = my_half()
    gather_rows(key_all, half, 0, halo, halo_other)
    gather_rows(value_all, half, 0, halo, halo_other, BLOCK)
    gather_rows(query_all, half, 0, query_own, query_partner)
    gather_rows(d_all, half, 0, d_own, d_partner)
    for pair in range(PAIRS):
        columns = slice(pair * PAIR, (pair + 1) * PAIR)
        for query_block in range(2):
            keys = slice(query_block * BLOCK, WIN)
            steps = slice(query_block * BLOCK, (query_block + 1) * BLOCK)
            weights = weights_in[pair, query_block, : WIN - query_block * BLOCK]
            delta = delta_in[2 * pair + query_block : 2 * pair + query_block + 1]
            dq, dk, dv = gradients(
                key_all[keys, columns],
                value_all[keys, columns],
                query_all[steps, columns],
                d_all[steps, columns],
                weights,
                delta,
            )
            dq_part[columns, steps] = dq
            if query_block == 0:
                dk_all[:, columns] = dk
                dv_all[:, columns] = dv
            else:
                dk_all[BLOCK:, columns] += dk
                dv_all[BLOCK:, columns] += dv
    for start, grads in ((0, dk_all), (BLOCK, dv_all)):
        rows = slice(start, start + BLOCK)
        halo_grads[rows] = grads[at(half, BLOCK)].astype(bf16)
        halo_other_grads[rows] = grads[at(1 - half, BLOCK)].astype(bf16)


def gradients(keys, values, query_rows, d_rows, weights, delta):
    d_rows = doubled(d_rows)
    d_weights = times(values, d_rows, ((1,), (1,)))
    d_scores = (weights.astype(f32) * (d_weights - delta)).astype(bf16)
    dv = times(weights, d_rows, ((1,), (0,)))
    dk = times(d_scores, doubled(query_rows, SCALING), ((1,), (0,)))
    dq = diagonal(times(keys, d_scores, ((0,), (0,))))
    return dq, dk, dv


def halo_gradients(*sources):
    return pl.pallas_call(
        halo_kernel,
        out_shape=(
            shaped((2 * BLOCK, PART), bf16),
            shaped((2 * BLOCK, PART), bf16),
            shaped((PART, 2 * BLOCK), f32),
        ),
        in_specs=[VMEM] * 8,
        out_specs=(VMEM,) * 3,
        scratch_shapes=[pltpu.VMEM((2 * BLOCK, PART), bf16)] * 4
        + [pltpu.VMEM((2 * BLOCK, PART), f32)] * 2,
        compiler_params=params(),
        cost_estimate=estimate(1_000_000, 10_000),
        name="halo_gradients",
    )(*sources)


def own_kernel(
    own,
    partner,
    query_own,
    query_partner,
    d_own,
    d_partner,
    weights_in,
    delta_in,
    dq_part,
    att_swap,
    dq_own,
    swap,
    own_grads,
    partner_grads,
    key_all,
    value_all,
    query_all,
    d_all,
    dq_all,
    dk_all,
    dv_all,
):
    half = my_half()
    gather_rows(key_all, half, 0, own, partner)
    gather_rows(value_all, half, 0, own, partner, BLOCK)
    gather_rows(query_all, half, 0, query_own, query_partner)
    gather_rows(d_all, half, 0, d_own, d_partner)
    for pair in range(PAIRS):
        columns = slice(pair * PAIR, (pair + 1) * PAIR)
        for query_block in (1, 0):
            keys = slice(0, (query_block + 1) * BLOCK)
            steps = slice(query_block * BLOCK, (query_block + 1) * BLOCK)
            weights = weights_in[pair, query_block, WIN - query_block * BLOCK :]
            delta = delta_in[2 * pair + query_block : 2 * pair + query_block + 1]
            dq, dk, dv = gradients(
                key_all[keys, columns],
                value_all[keys, columns],
                query_all[steps, columns],
                d_all[steps, columns],
                weights,
                delta,
            )
            dq = dq + dq_part[columns, steps]
            dq_all[columns, steps] = (dq * SCALING).astype(bf16)
            if query_block == 1:
                dk_all[:, columns] = dk
                dv_all[:, columns] = dv
            else:
                dk_all[:BLOCK, columns] += dk
                dv_all[:BLOCK, columns] += dv
    dq_own[...] = dq_all[:, at(half, BLOCK)].T
    swap[:, :BLOCK] = att_swap[...]
    swap[:, BLOCK:] = dq_all[span(half * PAIR, REST, PAIR), at(1 - half, BLOCK)]
    for start, grads in ((0, dk_all), (BLOCK, dv_all)):
        rows = slice(start, start + BLOCK)
        own_grads[rows] = grads[at(half, BLOCK)]
        partner_grads[rows] = grads[at(1 - half, BLOCK)]


def own_gradients(*sources):
    return pl.pallas_call(
        own_kernel,
        out_shape=(
            shaped((BLOCK, PART), bf16),
            shaped((REST, 2 * BLOCK), bf16),
            shaped((2 * BLOCK, PART), f32),
            shaped((2 * BLOCK, PART), f32),
        ),
        in_specs=[VMEM] * 10,
        out_specs=(VMEM,) * 4,
        scratch_shapes=[pltpu.VMEM((2 * BLOCK, PART), bf16)] * 4
        + [pltpu.VMEM((PART, 2 * BLOCK), bf16)]
        + [pltpu.VMEM((2 * BLOCK, PART), f32)] * 2,
        compiler_params=params(),
        cost_estimate=estimate(1_000_000, 10_000),
        name="own_gradients",
    )(*sources)


def output_kernel(att_own, received, weight, out, full, dq_rest):
    half = my_half()
    full[span(half * START, PART, 128)] = att_own[...]
    full[span((1 - half) * PART, REST, 128)] = received[:, :BLOCK]
    out[...] = times(weight[...], full[...], ((1,), (0,))).T.astype(bf16)
    dq_rest[...] = received[:, BLOCK:].T


def output_rows(att_own, received, weight):
    outs = weight.shape[0]
    return pl.pallas_call(
        output_kernel,
        out_shape=(
            shaped((BLOCK, outs), bf16),
            shaped((WIDTH, BLOCK), bf16),
            shaped((BLOCK, REST), bf16),
        ),
        in_specs=[VMEM] * 3,
        out_specs=(VMEM,) * 3,
        compiler_params=params(),
        cost_estimate=estimate(1_000_000, 10_000),
        name="output",
    )(att_own, received, weight)


def add_partner_kernel(partner_grads, received, out):
    columns = span(my_half() * PAIR, REST, PAIR)
    out[...] = (partner_grads[:, columns] + received[:, columns].astype(f32)).astype(bf16)


def add_partner(partner_grads, received):
    return pl.pallas_call(
        add_partner_kernel,
        out_shape=shaped((2 * BLOCK, REST), bf16),
        in_specs=[VMEM, VMEM],
        out_specs=VMEM,
        compiler_params=params(),
        cost_estimate=estimate(1_000_000, 10_000),
        name="add_partner",
    )(partner_grads, received)


def weight_kernel(count, *refs):
    pieces, cots = refs[:count], refs[count : 3 * count]
    kept, *sent = refs[3 * count :]
    total = sent.pop()
    half = my_half()
    products = None
    for piece, first, second in zip(pieces, cots[:count], cots[count:]):
        att = jnp.concatenate([piece[:, at(half, BLOCK)], piece[:, at(1 - half, BLOCK)]], axis=1)
        product = times(att, jnp.concatenate([first[...], second[...]], axis=0), ((1,), (0,)))
        products = product if products is None else products + product
    total[...] = products
    group = my_group()
    lanes = kept.shape[1]
    kept[...] = total[:, at(group, lanes)]
    for number, out in enumerate(sent):
        target = jnp.bitwise_xor(group, number + 1)
        out[...] = total[:, at(target, lanes)].astype(bf16)


def weight_products(pieces, cots, groups):
    rows = pieces[0].shape[0]
    outs = cots[0].shape[1]
    part = (rows, outs // groups)
    return pl.pallas_call(
        functools.partial(weight_kernel, len(pieces)),
        out_shape=(shaped(part, f32),) + (shaped(part, bf16),) * (groups - 1),
        in_specs=[VMEM] * (3 * len(pieces)),
        out_specs=(VMEM,) * groups,
        scratch_shapes=[pltpu.VMEM((rows, outs), f32)],
        compiler_params=params(),
        cost_estimate=estimate(1_000_000, 10_000),
        name="weight_products",
    )(*pieces, *cots)


def weight_sum_kernel(kept, *rest):
    received, (first, second, total) = rest[:-3], rest[-3:]
    value = kept[...]
    for part in received:
        value = value + part[...].astype(f32)
    total[...] = value
    lanes = first.shape[1]
    odd = jnp.bitwise_and(lax.axis_index("dp"), 1)
    first[...] = total[:, at(odd, lanes)]
    second[...] = total[:, at(1 - odd, lanes)]


def weight_sum(kept, received):
    rows, lanes = kept.shape
    return pl.pallas_call(
        weight_sum_kernel,
        out_shape=(shaped((rows, lanes // 2), f32),) * 2,
        in_specs=[VMEM] + [VMEM] * len(received),
        out_specs=(VMEM, VMEM),
        scratch_shapes=[pltpu.VMEM((rows, lanes), f32)],
        compiler_params=params(),
        cost_estimate=estimate(1_000_000, 10_000),
        name="weight_sum",
    )(kept, *received)


def place_kernel(
    dq_mine,
    dq_theirs,
    mine,
    received,
    theirs,
    first,
    second,
    query_out,
    key_out,
    value_out,
    weight_out,
    total,
    sems,
):
    half = my_half()
    rows = first.shape[0]
    left, right = span(half * START, PART, 128), span((1 - half) * PART, REST, 128)
    upper, lower = pl.ds(0, BLOCK), pl.ds(BLOCK, BLOCK)
    moves = [
        (first, weight_out.at[span(half * rows, rows, 16)]),
        (second, weight_out.at[span((1 - half) * rows, rows, 16)]),
        (dq_mine, query_out.at[:, left]),
        (dq_theirs, query_out.at[:, right]),
        (theirs.at[upper], key_out.at[:, right]),
        (theirs.at[lower], value_out.at[:, right]),
        (total.at[upper], key_out.at[:, left]),
        (total.at[lower], value_out.at[:, left]),
    ]
    copies = [
        pltpu.make_async_copy(source, target, sems.at[number])
        for number, (source, target) in enumerate(moves)
    ]
    for copy in copies[:6]:
        copy.start()
    total[...] = (mine[...] + received[...].astype(f32)).astype(bf16)
    for copy in copies[6:]:
        copy.start()
    for copy in copies:
        copy.wait()


def place(*sources):
    rows, lanes = sources[-1].shape
    *grads, weight = pl.pallas_call(
        place_kernel,
        out_shape=(shaped((BLOCK, WIDTH), bf16),) * 3 + (shaped((2 * rows, lanes), f32),),
        in_specs=[VMEM] * 7,
        out_specs=(HBM,) * 4,
        scratch_shapes=[
            pltpu.VMEM((2 * BLOCK, PART), bf16),
            pltpu.SemaphoreType.DMA((8,)),
        ],
        compiler_params=params(),
        cost_estimate=estimate(1_000_000, 10_000),
        name="place",
    )(*sources)
    return *grads, weight.T


def swapped(value, axis, bits):
    count = lax.axis_size(axis)
    return lax.ppermute(value, axis, [(source, source ^ bits) for source in range(count)])


def moved(value, axis, steps):
    count = lax.axis_size(axis)
    first, last = (max(0, -steps), min(count, count - steps))
    return lax.ppermute(value, axis, [(source, source + steps) for source in range(first, last)])


def placed(value, flip):
    lanes = lax.axis_size("ctx")
    moves = []
    for source in range(lax.axis_size("dp")):
        for index in range(lanes):
            group, half = index // 2, index % 2
            target_half = (source % 2) ^ flip
            target = 2 * half + source // 2
            moves.append((source * lanes + index, target * lanes + 2 * group + target_half))
    return lax.ppermute(value, ("dp", "ctx"), moves)


def after(*values):
    return lax.optimization_barrier(values)


def per_device(queries, key_states, value_states, out_cotangent, out_weight, block_clip):
    sequences = lax.axis_size("dp")
    groups = lax.axis_size("ctx") // 2
    short = sequences == 4 and groups in (2, 4)
    query, cotangent = queries[0], out_cotangent[0]

    swap_kv, own, swap_query, query = pack(block_clip, query, key_states[0], value_states[0])
    partner = swapped(swap_kv, "ctx", 1)
    halo = moved(own, "ctx", 2)
    d_own, d_turned_own, weight = own_cotangents(cotangent, out_weight)
    cots, later = [cotangent], []
    if short:
        cots += [swapped(cotangent, "dp", n) for n in (1, 2)]
    partner, halo, d_own, swap_query, cot_late = after(
        partner, halo, d_own, swap_query, cotangent
    )

    halo_other = moved(partner, "ctx", 2)
    cot_partner = swapped(cot_late, "ctx", 1)
    query_partner = swapped(swap_query, "ctx", 1)
    if short:
        cots.append(swapped(cots[2], "dp", 1))
    d_partner, d_turned_partner = cotangents(cot_partner, weight)
    halo_other, query_partner, d_partner, cot_partner, *cots = after(
        halo_other, query_partner, d_partner, cot_partner, *cots
    )

    if short:
        later = [cot_partner, swapped(cot_partner, "dp", 2)]
    queries_pair, d_pair = (query, query_partner), (d_own, d_partner)
    weights, delta, att_own, att_swap, *pieces = forward(
        4 if short else 0,
        own,
        partner,
        halo,
        halo_other,
        *queries_pair,
        d_turned_own,
        d_turned_partner,
    )
    delta, *rest = after(delta, *pieces, *later)
    pieces, later = rest[: len(pieces)], rest[len(pieces) :]

    if short:
        pieces[1:] = [swapped(pieces[n], "dp", n) for n in (1, 2, 3)]
        later.insert(1, swapped(later[0], "dp", 1))
        later.append(swapped(later[2], "dp", 1))
    halo_grads, halo_other_grads, dq_part = halo_gradients(
        halo, halo_other, *queries_pair, *d_pair, weights, delta
    )
    halo_grads, halo_other_grads, dq_part, *pieces = after(
        halo_grads, halo_other_grads, dq_part, *pieces
    )

    partner_late = moved(halo_other_grads, "ctx", -2)
    own_late = moved(halo_grads, "ctx", -2)
    if short:
        kept, *sent = weight_products(pieces, [*cots, *later], groups)
        arrived = [swapped(part, "ctx", 2 * (n + 1)) for n, part in enumerate(sent)]
        kept, dq_part = after(kept, dq_part)
    dq_own, swap, own_grads, partner_grads = own_gradients(
        own, partner, *queries_pair, *d_pair, weights, delta, dq_part, att_swap
    )
    received = swapped(swap, "ctx", 1)
    if short:
        partner_late, dq_own, kept, *arrived = after(partner_late, dq_own, kept, *arrived)
        first, second = weight_sum(kept, arrived)
        first, second = placed(first, 0), placed(second, 1)
    kv_rest = swapped(add_partner(partner_grads, partner_late), "ctx", 1)
    sublayer_out, att_full, dq_rest = output_rows(att_own, received, weight)
    if not short:
        product = lax.dot_general(
            cotangent, att_full, (((0,), (1,)), ((), ())), preferred_element_type=f32
        ).astype(bf16)
        sequence_grad = lax.psum_scatter(product, "ctx", scatter_dimension=0, tiled=True)
        weight_grad = lax.psum_scatter(
            sequence_grad.astype(f32), "dp", scatter_dimension=1, tiled=True
        )
        first = second = jnp.zeros((16, 128), f32)
    query_grad, key_grad, value_grad, placed_weight = place(
        dq_own, dq_rest, own_grads, own_late, kv_rest, first, second
    )
    if short:
        weight_grad = placed_weight
    return (
        sublayer_out[None],
        query_grad[None],
        key_grad[None],
        value_grad[None],
        weight_grad,
    )


def solution(mesh):
    return jax.shard_map(
        per_device,
        mesh=mesh,
        in_specs=(
            P("dp", "ctx", None),
            P("dp", "ctx", None),
            P("dp", "ctx", None),
            P("dp", "ctx", None),
            P(),
            P("dp", "ctx"),
        ),
        out_specs=(
            P("dp", "ctx", None),
            P("dp", "ctx", None),
            P("dp", "ctx", None),
            P("dp", "ctx", None),
            P("ctx", "dp"),
        ),
        check_vma=False,
    )
```

time: 96 us -> 72.8 us (0.76)
  the two profiles are of different devices: /device:TPU:0 before, /device:TPU:3 now
where the time goes in v2:
time: 72.8 us; the launch traced here: 72.5 us
  starting transfers between devices  34.7 us (48%)
  waiting for transfers between devices  19.7 us (27%)
  Pallas kernels  16.6 us (23%)
  between operations  1.49 us (2%)
    ppermute x17, starting transfers between devices, swapped(): lax.ppermute(value, axis, [(source, source ^ bits) for source in range(co...  17.9 us
    ppermute x17, waiting for transfers between devices, swapped(): lax.ppermute(value, axis, [(source, source ^ bits) for source in range(co...  12.1 us
    ppermute x4, starting transfers between devices, moved(): lax.ppermute(value, axis, [(source, source + steps) for source in range(f...  8.98 us
    ppermute x2, starting transfers between devices, placed(): return lax.ppermute(value, ('dp', 'ctx'), moves)  7.76 us
    pallas_call x1, Pallas kernels, forward(): pl.pallas_call(functools.partial(forward_kernel, pieces_wanted), out_shap...  4.59 us
    ppermute x2, waiting for transfers between devices, placed(): return lax.ppermute(value, ('dp', 'ctx'), moves)  4.57 us
    ppermute x4, waiting for transfers between devices, moved(): lax.ppermute(value, axis, [(source, source + steps) for source in range(f...  3.07 us
    pallas_call x1, Pallas kernels, own_gradients(): pl.pallas_call(own_kernel, out_shape=(shaped((BLOCK, PART), bf16), shaped...  2.5 us
  transfers between devices with their start and end apart: 23, of which 10 were waited for; matrix products, arithmetic and copies ran while one was open for 0% of the time, Pallas kernels for 20%

profile of v2, /device:TPU:3, one launch (start us, length us, event | category | flops | bytes accessed | tf_op | source)
XLA Modules:
  0.0 72.5 jit_solution(3977381459274855442)
XLA Ops:
  1.3 1.3 %pack.1 = (bf16[272,640]{1,0:T(8,128)(2,1)S(1)}, bf16[272,640]{1,0:T(8,128)(2,1)S(1)}, bf16[128,640]{1,0:T(8,128)(2,1)S(1)}, bf16[128,640]{1,0:T(8,128)(2,1)S(1)}) custom-call(s32[1,1]{1,0:T(1,128)S(6)} %copy.11.clip, bf16[128,1152]{1,0:T(8,128)(2,1)} %bitcast.14, bf16[128,1152]{1,0:T(8,128)(2,1)} %bitcast.15, bf16[128,1152]{1,0:T(8,128)(2,1)} %bitcast.16), custom_call_target="tpu_custom_call" | custom-call | flops 1000000 | bytes 10000 | tf_op jit(solution)/shard_map/pack/pallas_call | solution.py:101
  2.7 3.2 %collective-permute-start.1 = (bf16[272,640]{1,0:T(8,128)(2,1)S(1)}, bf16[272,640]{1,0:T(8,128)(2,1)S(1)}, u32[]{:S(2)}, u32[]{:S(2)}) collective-permute-start(bf16[272,640]{1,0:T(8,128)(2,1)S(1)} %get-tuple-element.76.own), channel_id=1, source_target_pairs={{0,2},{1,3},{2,4},{3,5},{4,6},{5,7},{8,10},{9,11},{10,12},{11,13},... | collective-permute-start | bytes 1044488 | tf_op jit(solution)/shard_map/ppermute | solution.py:632
  6.2 1.2 %collective-permute-start.6 = (bf16[128,1024]{1,0:T(8,128)(2,1)}, bf16[128,1024]{1,0:T(8,128)(2,1)S(1)}, u32[]{:S(2)}, u32[]{:S(2)}) collective-permute-start(bf16[128,1024]{1,0:T(8,128)(2,1)} %bitcast.9), channel_id=1, source_target_pairs={{0,16},{8,24},{16,0},{24,8},{1,17},{9,25},{17,1},{25,9},{2,18},{10... | collective-permute-start | bytes 786440 | tf_op jit(solution)/shard_map/ppermute | solution.py:626
  7.5 2.1 %own_cotangents.1 = (bf16[128,640]{1,0:T(8,128)(2,1)S(1)}, bf16[640,128]{1,0:T(8,128)(2,1)S(1)}, bf16[1024,1152]{1,0:T(8,128)(2,1)S(1)}) custom-call(bf16[128,1024]{1,0:T(8,128)(2,1)} %bitcast.10, bf16[1024,1152]{1,0:T(8,128)(2,1)} %weight.1), custom_call_target="tpu_custom_call" | custom-call | flops 1000000 | bytes 10000 | tf_op jit(solution)/shard_map/own_cotangents/pallas_call | solution.py:263
  9.6 3.1 %collective-permute-done.1.halo = bf16[272,640]{1,0:T(8,128)(2,1)S(1)} collective-permute-done((bf16[272,640]{1,0:T(8,128)(2,1)S(1)}, bf16[272,640]{1,0:T(8,128)(2,1)S(1)}, u32[]{:S(2)}, u32[]{:S(2)}) %collective-permute-start.1) | collective-permute-done | bytes 348192 | tf_op jit(solution)/shard_map/ppermute | solution.py:632
  12.7 2.0 %collective-permute-done.partner = bf16[272,640]{1,0:T(8,128)(2,1)S(1)} collective-permute-done((bf16[272,640]{1,0:T(8,128)(2,1)S(1)}, bf16[272,640]{1,0:T(8,128)(2,1)S(1)}, u32[]{:S(2)}, u32[]{:S(2)}) %collective-permute-start) | collective-permute-done | bytes 348192 | tf_op jit(solution)/shard_map/ppermute | solution.py:626
  14.7 3.2 %collective-permute-start.2 = (bf16[272,640]{1,0:T(8,128)(2,1)S(1)}, bf16[272,640]{1,0:T(8,128)(2,1)S(1)}, u32[]{:S(2)}, u32[]{:S(2)}) collective-permute-start(bf16[272,640]{1,0:T(8,128)(2,1)S(1)} %collective-permute-done.partner), channel_id=1, source_target_pairs={{0,2},{1,3},{2,4},{3,5},{4,6},{5,7},{8,10},{9,11},{10,12},{11,13},... | collective-permute-start | bytes 1044488 | tf_op jit(solution)/shard_map/ppermute | solution.py:632
  18.2 2.4 %collective-permute-start.5 = (bf16[128,1024]{1,0:T(8,128)(2,1)S(1)}, bf16[128,1024]{1,0:T(8,128)(2,1)S(1)}, u32[]{:S(2)}, u32[]{:S(2)}) collective-permute-start(bf16[128,1024]{1,0:T(8,128)(2,1)S(1)} %bitcast.12), channel_id=1, source_target_pairs={{0,8},{8,0},{16,24},{24,16},{1,9},{9,1},{17,25},{25,17},{2,10},{10... | collective-permute-start | bytes 786440 | tf_op jit(solution)/shard_map/ppermute | solution.py:626
  21.9 1.8 %collective-permute-done.4.cotangent.refs_8_ = bf16[128,1024]{1,0:T(8,128)(2,1)S(1)} collective-permute-done((bf16[128,1024]{1,0:T(8,128)(2,1)S(1)}, bf16[128,1024]{1,0:T(8,128)(2,1)S(1)}, u32[]{:S(2)}, u32[]{:S(2)}) %collective-permute-start.4) | collective-permute-done | bytes 262176 | tf_op jit(solution)/shard_map/ppermute | solution.py:626
  24.1 3.1 %collective-permute-done.3.query_partner = bf16[128,640]{1,0:T(8,128)(2,1)S(1)} collective-permute-done((bf16[128,640]{1,0:T(8,128)(2,1)S(1)}, bf16[128,640]{1,0:T(8,128)(2,1)S(1)}, u32[]{:S(2)}, u32[]{:S(2)}) %collective-permute-start.3) | collective-permute-done | bytes 163872 | tf_op jit(solution)/shard_map/ppermute | solution.py:626
  27.1 1.2 %collective-permute-start.8 = (bf16[128,1024]{1,0:T(8,128)(2,1)S(1)}, bf16[128,1024]{1,0:T(8,128)(2,1)S(1)}, u32[]{:S(2)}, u32[]{:S(2)}) collective-permute-start(bf16[128,1024]{1,0:T(8,128)(2,1)S(1)} %collective-permute-done.4.cotangent.refs_8_), channel_id=1, source_target_pairs={{0,16},{8,24},{16,0},{24,8},{1,17},{9,25},{17,1},{25,9},{2,18},{10... | collective-permute-start | bytes 786440 | tf_op jit(solution)/shard_map/ppermute | solution.py:626
  28.4 4.6 %forward.1 = (bf16[5,2,384,256]{3,2,1,0:T(8,128)(2,1)S(1)}, f32[16,256]{1,0:T(8,128)S(1)}, bf16[640,128]{1,0:T(8,128)(2,1)S(1)}, bf16[512,128]{1,0:T(8,128)(2,1)...) custom-call(bf16[272,640]{1,0:T(8,128)(2,1)S(1)} %get-tuple-element., ...), custom_call_target="tpu_custom_call" | custom-call | flops 1000000 | bytes 10000 | tf_op jit(solution)/shard_map/forward/pallas_call | solution.py:215
  33.6 5.0 %collective-permute-start.11 = (bf16[144,256]{1,0:T(8,128)(2,1)S(1)}, bf16[144,256]{1,0:T(8,128)(2,1)S(1)}, u32[]{:S(2)}, u32[]{:S(2)}) collective-permute-start(bf16[144,256]{1,0:T(8,128)(2,1)S(1)} %get-tuple-element.108), channel_id=1, source_target_pairs={{0,24},{8,16},{16,8},{24,0},{1,25},{9,17},{17,9},{25,1},{2,26},{10... | collective-permute-start | bytes 221192 | tf_op jit(solution)/shard_map/ppermute | solution.py:626
  39.4 2.3 %halo_gradients.1 = (bf16[256,640]{1,0:T(8,128)(2,1)S(1)}, bf16[256,640]{1,0:T(8,128)(2,1)S(1)}, f32[640,256]{1,0:T(8,128)S(1)}) custom-call(bf16[272,640]{1,0:T(8,128)(2,1)S(1)} %collective-permute-done.1.halo, bf16[272,640]{1,0:T(8,128)(2,1)S(1)} %collective-permute-done.2.halo_other, bf16[128,640]{1,0:T(8,128)(2,1)S(1)} %get-tuple-element.87.query_own, ...), custom_call_target="tpu_custom_call" | custom-call | flops 1000000 | bytes 10000 | tf_op jit(solution)/shard_map/halo_gradients/pallas_call | solution.py:364
  41.8 1.3 %collective-permute-start.15 = (bf16[256,640]{1,0:T(8,128)(2,1)S(1)}, bf16[256,640]{1,0:T(8,128)(2,1)S(1)}, u32[]{:S(2)}, u32[]{:S(2)}) collective-permute-start(bf16[256,640]{1,0:T(8,128)(2,1)S(1)} %get-tuple-element.125), channel_id=1, source_target_pairs={{2,0},{3,1},{4,2},{5,3},{6,4},{7,5},{10,8},{11,9},{12,10},{13,11},... | collective-permute-start | bytes 983048 | tf_op jit(solution)/shard_map/ppermute | solution.py:632
  43.7 2.1 %collective-permute-start.16 = (bf16[144,256]{1,0:T(8,128)(2,1)S(1)}, bf16[144,256]{1,0:T(8,128)(2,1)S(1)}, u32[]{:S(2)}, u32[]{:S(2)}) collective-permute-start(bf16[144,256]{1,0:T(8,128)(2,1)S(1)} %get-tuple-element.128), channel_id=1, source_target_pairs={{0,2},{1,3},{2,0},{3,1},{4,6},{5,7},{6,4},{7,5},{8,10},{9,11},{10,... | collective-permute-start | bytes 221192 | tf_op jit(solution)/shard_map/ppermute | solution.py:626
  48.1 1.3 %collective-permute-start.19 = (bf16[256,640]{1,0:T(8,128)(2,1)S(1)}, bf16[256,640]{1,0:T(8,128)(2,1)S(1)}, u32[]{:S(2)}, u32[]{:S(2)}) collective-permute-start(bf16[256,640]{1,0:T(8,128)(2,1)S(1)} %get-tuple-element.134), channel_id=1, source_target_pairs={{2,0},{3,1},{4,2},{5,3},{6,4},{7,5},{10,8},{11,9},{12,10},{13,11},... | collective-permute-start | bytes 983048 | tf_op jit(solution)/shard_map/ppermute | solution.py:632
  49.3 2.5 %own_gradients.1 = (bf16[128,640]{1,0:T(8,128)(2,1)S(1)}, bf16[512,256]{1,0:T(8,128)(2,1)S(1)}, f32[256,640]{1,0:T(8,128)S(1)}, f32[256,640]{1,0:T(8,128)S(1)}) custom-call(bf16[272,640]{1,0:T(8,128)(2,1)S(1)} %get-tuple-element.76.own, bf16[272,640]{1,0:T(8,128)(2,1)S(1)} %collective-permute-done.partner, bf16[128,640]{1,0:T(8,128)(2,1)S(1)} %get-tuple-element.87.query_own, ...), custom_call_target="tpu_custom_call" | custom-call | flops 1000000 | bytes 10000 | tf_op jit(solution)/shard_map/own_gradients/pallas_call | solution.py:442
  51.8 2.2 %collective-permute-done.16.rest_0_ = bf16[144,256]{1,0:T(8,128)(2,1)S(1)} collective-permute-done((bf16[144,256]{1,0:T(8,128)(2,1)S(1)}, bf16[144,256]{1,0:T(8,128)(2,1)S(1)}, u32[]{:S(2)}, u32[]{:S(2)}) %collective-permute-start.16) | collective-permute-done | bytes 73760 | tf_op jit(solution)/shard_map/ppermute | solution.py:626
  54.4 2.6 %collective-permute-done.18.rest_2_ = bf16[144,256]{1,0:T(8,128)(2,1)S(1)} collective-permute-done((bf16[144,256]{1,0:T(8,128)(2,1)S(1)}, bf16[144,256]{1,0:T(8,128)(2,1)S(1)}, u32[]{:S(2)}, u32[]{:S(2)}) %collective-permute-start.18) | collective-permute-done | bytes 73760 | tf_op jit(solution)/shard_map/ppermute | solution.py:626
  57.5 6.6 %collective-permute-start.21 = (f32[144,128]{1,0:T(8,128)S(1)}, f32[144,128]{1,0:T(8,128)S(1)}, u32[]{:S(2)}, u32[]{:S(2)}) collective-permute-start(f32[144,128]{1,0:T(8,128)S(1)} %get-tuple-element.141), channel_id=1, source_target_pairs={{0,0},{1,16},{2,2},{3,18},{4,4},{5,20},{6,6},{7,22},{8,1},{9,17},{... | collective-permute-start | bytes 221192 | tf_op jit(solution)/shard_map/ppermute | solution.py:644
  65.3 1.6 %output.1 = (bf16[128,1024]{1,0:T(8,128)(2,1)}, bf16[1152,128]{1,0:T(8,128)(2,1)}, bf16[128,512]{1,0:T(8,128)(2,1)S(1)}) custom-call(bf16[640,128]{1,0:T(8,128)(2,1)S(1)} %get-tuple-element.91.att_own, bf16[512,256]{1,0:T(8,128)(2,1)S(1)} %collective-permute-done.14.received, bf16[1024,1152]{1,0:T(8,128)(2,1)S(1)} %get-tuple-element.84.weight), custom_call_target="tpu_custom_call" | custom-call | flops 1000000 | bytes 10000 | tf_op jit(solution)/shard_map/output/pallas_call | solution.py:471
  66.9 2.4 %collective-permute-done.21.first = f32[144,128]{1,0:T(8,128)S(1)} collective-permute-done((f32[144,128]{1,0:T(8,128)S(1)}, f32[144,128]{1,0:T(8,128)S(1)}, u32[]{:S(2)}, u32[]{:S(2)}) %collective-permute-start.21) | collective-permute-done | bytes 73760 | tf_op jit(solution)/shard_map/ppermute | solution.py:644
  69.3 2.2 %collective-permute-done.22.second = f32[144,128]{1,0:T(8,128)S(1)} collective-permute-done((f32[144,128]{1,0:T(8,128)S(1)}, f32[144,128]{1,0:T(8,128)S(1)}, u32[]{:S(2)}, u32[]{:S(2)}) %collective-permute-start.22) | collective-permute-done | bytes 73760 | tf_op jit(solution)/shard_map/ppermute | solution.py:644
  (35 shorter events, 9.6 us)
Async XLA Ops:
  0.6 17.3 %copy-start = (bf16[1,128,1024]{2,1,0:T(8,128)(2,1)S(1)}, bf16[1,128,1024]{2,1,0:T(8,128)(2,1)}, u32[]{:S(2)}) copy-start(bf16[1,128,1024]{2,1,0:T(8,128)(2,1)} %param.9) | copy-start | bytes 786436
  2.7 10.0 %collective-permute-start.1 = (bf16[272,640]{1,0:T(8,128)(2,1)S(1)}, bf16[272,640]{1,0:T(8,128)(2,1)S(1)}, u32[]{:S(2)}, u32[]{:S(2)}) collective-permute-start(bf16[272,640]{1,0:T(8,128)(2,1)S(1)} %get-tuple-element.76.own), channel_id=1, source_target_pairs={{0,2},{1,3},{2,4},{3,5},{4,6},{5,7},{8,10},{9,11},{10,12},{11,13},... | collective-permute-start | bytes 1044488 | tf_op jit(solution)/shard_map/ppermute | solution.py:632
  5.9 8.8 %collective-permute-start = (bf16[272,640]{1,0:T(8,128)(2,1)S(1)}, bf16[272,640]{1,0:T(8,128)(2,1)S(1)}, u32[]{:S(2)}, u32[]{:S(2)}) collective-permute-start(bf16[272,640]{1,0:T(8,128)(2,1)S(1)} %get-tuple-element.77), channel_id=1, source_target_pairs={{0,1},{1,0},{2,3},{3,2},{4,5},{5,4},{6,7},{7,6},{8,9},{9,8},{10,11... | collective-permute-start | bytes 1044488 | tf_op jit(solution)/shard_map/ppermute | solution.py:626
  6.2 14.4 %collective-permute-start.6 = (bf16[128,1024]{1,0:T(8,128)(2,1)}, bf16[128,1024]{1,0:T(8,128)(2,1)S(1)}, u32[]{:S(2)}, u32[]{:S(2)}) collective-permute-start(bf16[128,1024]{1,0:T(8,128)(2,1)} %bitcast.9), channel_id=1, source_target_pairs={{0,16},{8,24},{16,0},{24,8},{1,17},{9,25},{17,1},{25,9},{2,18},{10... | collective-permute-start | bytes 786440 | tf_op jit(solution)/shard_map/ppermute | solution.py:626
  14.7 12.4 %collective-permute-start.2 = (bf16[272,640]{1,0:T(8,128)(2,1)S(1)}, bf16[272,640]{1,0:T(8,128)(2,1)S(1)}, u32[]{:S(2)}, u32[]{:S(2)}) collective-permute-start(bf16[272,640]{1,0:T(8,128)(2,1)S(1)} %collective-permute-done.partner), channel_id=1, source_target_pairs={{0,2},{1,3},{2,4},{3,5},{4,6},{5,7},{8,10},{9,11},{10,12},{11,13},... | collective-permute-start | bytes 1044488 | tf_op jit(solution)/shard_map/ppermute | solution.py:632
  17.9 5.7 %collective-permute-start.4 = (bf16[128,1024]{1,0:T(8,128)(2,1)S(1)}, bf16[128,1024]{1,0:T(8,128)(2,1)S(1)}, u32[]{:S(2)}, u32[]{:S(2)}) collective-permute-start(bf16[128,1024]{1,0:T(8,128)(2,1)S(1)} %bitcast.11), channel_id=1, source_target_pairs={{0,1},{1,0},{2,3},{3,2},{4,5},{5,4},{6,7},{7,6},{8,9},{9,8},{10,11... | collective-permute-start | bytes 786440 | tf_op jit(solution)/shard_map/ppermute | solution.py:626
  18.2 5.8 %collective-permute-start.5 = (bf16[128,1024]{1,0:T(8,128)(2,1)S(1)}, bf16[128,1024]{1,0:T(8,128)(2,1)S(1)}, u32[]{:S(2)}, u32[]{:S(2)}) collective-permute-start(bf16[128,1024]{1,0:T(8,128)(2,1)S(1)} %bitcast.12), channel_id=1, source_target_pairs={{0,8},{8,0},{16,24},{24,16},{1,9},{9,1},{17,25},{25,17},{2,10},{10... | collective-permute-start | bytes 786440 | tf_op jit(solution)/shard_map/ppermute | solution.py:626
  20.6 6.5 %collective-permute-start.7 = (bf16[128,1024]{1,0:T(8,128)(2,1)S(1)}, bf16[128,1024]{1,0:T(8,128)(2,1)S(1)}, u32[]{:S(2)}, u32[]{:S(2)}) collective-permute-start(bf16[128,1024]{1,0:T(8,128)(2,1)S(1)} %collective-permute-done.6.refs_6_), channel_id=1, source_target_pairs={{0,8},{8,0},{16,24},{24,16},{1,9},{9,1},{17,25},{25,17},{2,10},{10... | collective-permute-start | bytes 786440 | tf_op jit(solution)/shard_map/ppermute | solution.py:626
  20.6 6.5 %collective-permute-start.3 = (bf16[128,640]{1,0:T(8,128)(2,1)S(1)}, bf16[128,640]{1,0:T(8,128)(2,1)S(1)}, u32[]{:S(2)}, u32[]{:S(2)}) collective-permute-start(bf16[128,640]{1,0:T(8,128)(2,1)S(1)} %get-tuple-element.82), channel_id=1, source_target_pairs={{0,1},{1,0},{2,3},{3,2},{4,5},{5,4},{6,7},{7,6},{8,9},{9,8},{10,11... | collective-permute-start | bytes 491528 | tf_op jit(solution)/shard_map/ppermute | solution.py:626
  27.1 5.8 %collective-permute-start.8 = (bf16[128,1024]{1,0:T(8,128)(2,1)S(1)}, bf16[128,1024]{1,0:T(8,128)(2,1)S(1)}, u32[]{:S(2)}, u32[]{:S(2)}) collective-permute-start(bf16[128,1024]{1,0:T(8,128)(2,1)S(1)} %collective-permute-done.4.cotangent.refs_8_), channel_id=1, source_target_pairs={{0,16},{8,24},{16,0},{24,8},{1,17},{9,25},{17,1},{25,9},{2,18},{10... | collective-permute-start | bytes 786440 | tf_op jit(solution)/shard_map/ppermute | solution.py:626
  33.0 8.7 %collective-permute-start.10 = (bf16[144,256]{1,0:T(8,128)(2,1)S(1)}, bf16[144,256]{1,0:T(8,128)(2,1)S(1)}, u32[]{:S(2)}, u32[]{:S(2)}) collective-permute-start(bf16[144,256]{1,0:T(8,128)(2,1)S(1)} %get-tuple-element.107), channel_id=1, source_target_pairs={{0,16},{8,24},{16,0},{24,8},{1,17},{9,25},{17,1},{25,9},{2,18},{10... | collective-permute-start | bytes 221192 | tf_op jit(solution)/shard_map/ppermute | solution.py:626
  33.6 8.2 %collective-permute-start.11 = (bf16[144,256]{1,0:T(8,128)(2,1)S(1)}, bf16[144,256]{1,0:T(8,128)(2,1)S(1)}, u32[]{:S(2)}, u32[]{:S(2)}) collective-permute-start(bf16[144,256]{1,0:T(8,128)(2,1)S(1)} %get-tuple-element.108), channel_id=1, source_target_pairs={{0,24},{8,16},{16,8},{24,0},{1,25},{9,17},{17,9},{25,1},{2,26},{10... | collective-permute-start | bytes 221192 | tf_op jit(solution)/shard_map/ppermute | solution.py:626
  38.6 3.3 %collective-permute-start.9 = (bf16[144,256]{1,0:T(8,128)(2,1)S(1)}, bf16[144,256]{1,0:T(8,128)(2,1)S(1)}, u32[]{:S(2)}, u32[]{:S(2)}) collective-permute-start(bf16[144,256]{1,0:T(8,128)(2,1)S(1)} %get-tuple-element.106), channel_id=1, source_target_pairs={{0,8},{8,0},{16,24},{24,16},{1,9},{9,1},{17,25},{25,17},{2,10},{10... | collective-permute-start | bytes 221192 | tf_op jit(solution)/shard_map/ppermute | solution.py:626
  38.9 4.2 %collective-permute-start.12 = (bf16[128,1024]{1,0:T(8,128)(2,1)S(1)}, bf16[128,1024]{1,0:T(8,128)(2,1)S(1)}, u32[]{:S(2)}, u32[]{:S(2)}) collective-permute-start(bf16[128,1024]{1,0:T(8,128)(2,1)S(1)} %collective-permute-done.4.cotangent.refs_8_), channel_id=1, source_target_pairs={{0,8},{8,0},{16,24},{24,16},{1,9},{9,1},{17,25},{25,17},{2,10},{10... | collective-permute-start | bytes 786440 | tf_op jit(solution)/shard_map/ppermute | solution.py:626
  39.1 4.1 %collective-permute-start.13 = (bf16[128,1024]{1,0:T(8,128)(2,1)S(1)}, bf16[128,1024]{1,0:T(8,128)(2,1)S(1)}, u32[]{:S(2)}, u32[]{:S(2)}) collective-permute-start(bf16[128,1024]{1,0:T(8,128)(2,1)S(1)} %collective-permute-done.8.refs_10_), channel_id=1, source_target_pairs={{0,8},{8,0},{16,24},{24,16},{1,9},{9,1},{17,25},{25,17},{2,10},{10... | collective-permute-start | bytes 786440 | tf_op jit(solution)/shard_map/ppermute | solution.py:626
  41.8 15.2 %collective-permute-start.15 = (bf16[256,640]{1,0:T(8,128)(2,1)S(1)}, bf16[256,640]{1,0:T(8,128)(2,1)S(1)}, u32[]{:S(2)}, u32[]{:S(2)}) collective-permute-start(bf16[256,640]{1,0:T(8,128)(2,1)S(1)} %get-tuple-element.125), channel_id=1, source_target_pairs={{2,0},{3,1},{4,2},{5,3},{6,4},{7,5},{10,8},{11,9},{12,10},{13,11},... | collective-permute-start | bytes 983048 | tf_op jit(solution)/shard_map/ppermute | solution.py:632
  43.7 10.3 %collective-permute-start.16 = (bf16[144,256]{1,0:T(8,128)(2,1)S(1)}, bf16[144,256]{1,0:T(8,128)(2,1)S(1)}, u32[]{:S(2)}, u32[]{:S(2)}) collective-permute-start(bf16[144,256]{1,0:T(8,128)(2,1)S(1)} %get-tuple-element.128), channel_id=1, source_target_pairs={{0,2},{1,3},{2,0},{3,1},{4,6},{5,7},{6,4},{7,5},{8,10},{9,11},{10,... | collective-permute-start | bytes 221192 | tf_op jit(solution)/shard_map/ppermute | solution.py:626
  45.9 8.6 %collective-permute-start.17 = (bf16[144,256]{1,0:T(8,128)(2,1)S(1)}, bf16[144,256]{1,0:T(8,128)(2,1)S(1)}, u32[]{:S(2)}, u32[]{:S(2)}) collective-permute-start(bf16[144,256]{1,0:T(8,128)(2,1)S(1)} %get-tuple-element.129), channel_id=1, source_target_pairs={{0,4},{1,5},{2,6},{3,7},{4,0},{5,1},{6,2},{7,3},{8,12},{9,13},{10,... | collective-permute-start | bytes 221192 | tf_op jit(solution)/shard_map/ppermute | solution.py:626
  47.0 10.1 %collective-permute-start.18 = (bf16[144,256]{1,0:T(8,128)(2,1)S(1)}, bf16[144,256]{1,0:T(8,128)(2,1)S(1)}, u32[]{:S(2)}, u32[]{:S(2)}) collective-permute-start(bf16[144,256]{1,0:T(8,128)(2,1)S(1)} %get-tuple-element.130), channel_id=1, source_target_pairs={{0,6},{1,7},{2,4},{3,5},{4,2},{5,3},{6,0},{7,1},{8,14},{9,15},{10,... | collective-permute-start | bytes 221192 | tf_op jit(solution)/shard_map/ppermute | solution.py:626
  48.1 18.8 %collective-permute-start.19 = (bf16[256,640]{1,0:T(8,128)(2,1)S(1)}, bf16[256,640]{1,0:T(8,128)(2,1)S(1)}, u32[]{:S(2)}, u32[]{:S(2)}) collective-permute-start(bf16[256,640]{1,0:T(8,128)(2,1)S(1)} %get-tuple-element.134), channel_id=1, source_target_pairs={{2,0},{3,1},{4,2},{5,3},{6,4},{7,5},{10,8},{11,9},{12,10},{13,11},... | collective-permute-start | bytes 983048 | tf_op jit(solution)/shard_map/ppermute | solution.py:632
  54.0 11.2 %collective-permute-start.14 = (bf16[512,256]{1,0:T(8,128)(2,1)S(1)}, bf16[512,256]{1,0:T(8,128)(2,1)S(1)}, u32[]{:S(2)}, u32[]{:S(2)}) collective-permute-start(bf16[512,256]{1,0:T(8,128)(2,1)S(1)} %get-tuple-element.123), channel_id=1, source_target_pairs={{0,1},{1,0},{2,3},{3,2},{4,5},{5,4},{6,7},{7,6},{8,9},{9,8},{10,11... | collective-permute-start | bytes 786440 | tf_op jit(solution)/shard_map/ppermute | solution.py:626
  57.1 14.3 %collective-permute-start.20 = (bf16[256,512]{1,0:T(8,128)(2,1)S(1)}, bf16[256,512]{1,0:T(8,128)(2,1)S(1)}, u32[]{:S(2)}, u32[]{:S(2)}) collective-permute-start(bf16[256,512]{1,0:T(8,128)(2,1)S(1)} %add_partner.1), channel_id=1, source_target_pairs={{0,1},{1,0},{2,3},{3,2},{4,5},{5,4},{6,7},{7,6},{8,9},{9,8},{10,11... | collective-permute-start | bytes 786440 | tf_op jit(solution)/shard_map/ppermute | solution.py:626
  57.5 11.8 %collective-permute-start.21 = (f32[144,128]{1,0:T(8,128)S(1)}, f32[144,128]{1,0:T(8,128)S(1)}, u32[]{:S(2)}, u32[]{:S(2)}) collective-permute-start(f32[144,128]{1,0:T(8,128)S(1)} %get-tuple-element.141), channel_id=1, source_target_pairs={{0,0},{1,16},{2,2},{3,18},{4,4},{5,20},{6,6},{7,22},{8,1},{9,17},{... | collective-permute-start | bytes 221192 | tf_op jit(solution)/shard_map/ppermute | solution.py:644
  64.1 7.3 %collective-permute-start.22 = (f32[144,128]{1,0:T(8,128)S(1)}, f32[144,128]{1,0:T(8,128)S(1)}, u32[]{:S(2)}, u32[]{:S(2)}) collective-permute-start(f32[144,128]{1,0:T(8,128)S(1)} %get-tuple-element.142), channel_id=1, source_target_pairs={{0,1},{1,17},{2,3},{3,19},{4,5},{5,21},{6,7},{7,23},{8,0},{9,16},{... | collective-permute-start | bytes 221192 | tf_op jit(solution)/shard_map/ppermute | solution.py:644

commit v3 on v0

v3 whole, which is shorter than its diff:
```python
import functools
import math

import jax
import jax.numpy as jnp
from jax import lax
from jax.experimental import pallas as pl
from jax.experimental.pallas import tpu as pltpu
from jax.sharding import PartitionSpec as P

HEADS = 18
HDIM = 64
BLOCK = 128
WIN = 256
PAIR = 2 * HDIM
WIDTH = HEADS * HDIM
HALF = WIDTH // 2
PAIRS = HEADS // 4
SHARED = PAIRS * PAIR
MIXED = 2 * PAIRS
ROWS = (MIXED + 1) * BLOCK
CLIP_ROWS = 16
CLIP_STAT = 2 * PAIRS + 2
DELTA_STAT = CLIP_STAT + 2
STAT_ROWS = 24
SENT_ROWS = ROWS + 6 * STAT_ROWS
CHUNKS = 4
SCALING = 1.0 / math.sqrt(HDIM)
COST_GATHER = 2_000_000_000
COST_KEYS = 1_000_000
COST_FIRST = 2_000_000_000
COST_SUM = 2_000_000_000
VMEM_LIMIT = 24 * 1024 * 1024

big_negative = -1e30
bf16 = jnp.bfloat16
f32 = jnp.float32

SMEM = pl.BlockSpec(memory_space=pltpu.SMEM)
VMEM = pl.BlockSpec(memory_space=pltpu.VMEM)
HBM = pl.BlockSpec(memory_space=pltpu.HBM)


def shaped(shape, dtype):
    return jax.ShapeDtypeStruct(shape, dtype)


def kernel(body, name, ins, outs, scratch=(), out_space=VMEM, flops=1_000_000):
    return pl.pallas_call(
        body,
        out_shape=tuple(outs),
        in_specs=list(ins),
        out_specs=(out_space,) * len(outs),
        scratch_shapes=list(scratch),
        compiler_params=pltpu.CompilerParams(vmem_limit_bytes=VMEM_LIMIT),
        cost_estimate=pl.CostEstimate(flops=flops, bytes_accessed=10_000, transcendentals=0),
        name=name,
    )


def in_hbm(value):
    return pltpu.with_memory_space_constraint(value, pltpu.HBM)


def my_half():
    return jnp.bitwise_and(lax.axis_index("ctx"), 1)


def my_group():
    return jnp.right_shift(lax.axis_index("ctx"), 1)


def at(index, size):
    return pl.ds(pl.multiple_of(index * size, size), size)


def span(start, size, unit):
    return pl.ds(pl.multiple_of(start, unit), size)


def rows_of(block):
    return slice(block * BLOCK, (block + 1) * BLOCK)


def columns_of(half, pair):
    return span(half * (SHARED + PAIR) + pair * PAIR, PAIR, PAIR)


def head_rows(half, pair):
    return span(half * HDIM + pair * PAIR, PAIR, HDIM)


def single_rows(half):
    return span((1 - half) * SHARED, HDIM, HDIM)


def times(a, b, dims):
    return lax.dot_general(a, b, (dims, ((), ())), preferred_element_type=f32)


def is_low():
    return lax.broadcasted_iota(jnp.int32, (1, PAIR), 1) < HDIM


def low_or_high(low_value, high_value):
    return jnp.where(is_low(), low_value, high_value)


def turned(value):
    return pltpu.roll(value, HDIM, 1)


def pack_kernel(clip, query, key, value, swap_kv, own_kv, swap_query, own_query, *scratch):
    query_all, key_all, value_all, mixed, single, sems = scratch
    half = my_half()
    pairs = ((key, key_all), (value, value_all), (query, query_all))
    copies = [pltpu.make_async_copy(a, b, sems.at[n]) for n, (a, b) in enumerate(pairs)]
    for copy in copies:
        copy.start()
    clip_rows = jnp.full((CLIP_ROWS, PAIR), clip[0, 0].astype(f32), f32).astype(bf16)
    shared = slice(SHARED, SHARED + PAIR)
    for copy in copies:
        copy.wait()
    for side, target in ((1 - half, swap_kv), (half, own_kv)):
        for pair in range(PAIRS):
            target[rows_of(pair)] = key_all[:, columns_of(side, pair)]
            target[rows_of(PAIRS + pair)] = value_all[:, columns_of(side, pair)]
        target[ROWS:] = clip_rows
    key_shared = key_all[:, shared].astype(f32)
    value_shared = value_all[:, shared].astype(f32)
    mixed[0] = low_or_high(key_shared, turned(value_shared)).astype(bf16)
    mixed[1] = low_or_high(turned(key_shared), value_shared).astype(bf16)
    swap_kv[rows_of(MIXED)] = mixed[1 - half]
    own_kv[rows_of(MIXED)] = mixed[half]
    for pair in range(PAIRS):
        swap_query[rows_of(pair)] = query_all[:, columns_of(1 - half, pair)]
        own_query[rows_of(pair)] = query_all[:, columns_of(half, pair)]
    query_shared = query_all[:, shared].astype(f32)
    single[0] = low_or_high(query_shared, 0.0)
    single[1] = low_or_high(turned(query_shared), 0.0)
    own_query[rows_of(PAIRS)] = single[half].astype(bf16)
    theirs = single[1 - half]
    swap_query[SHARED:] = low_or_high(theirs[:HDIM], turned(theirs[HDIM:])).astype(bf16)


def pack(clip, query, key, value):
    wide = pltpu.VMEM((BLOCK, WIDTH), bf16)
    return kernel(
        pack_kernel,
        "pack",
        [SMEM, HBM, HBM, HBM],
        [shaped((ROWS + CLIP_ROWS, PAIR), bf16)] * 2
        + [shaped((HALF, PAIR), bf16), shaped((SHARED + PAIR, PAIR), bf16)],
        [
            wide,
            wide,
            wide,
            pltpu.VMEM((2, BLOCK, PAIR), bf16),
            pltpu.VMEM((2, BLOCK, PAIR), f32),
            pltpu.SemaphoreType.DMA((3,)),
        ],
    )(clip, in_hbm(query), in_hbm(key), in_hbm(value))


def unpacked_single(packed):
    packed = packed.astype(f32)
    top, bottom = low_or_high(packed, 0.0), low_or_high(turned(packed), 0.0)
    return jnp.concatenate([top, bottom], axis=0).astype(bf16)


def join_query(target, d_turned, single, query, query_single, d_pairs, d_shared):
    half = my_half()
    for pair in range(PAIRS):
        d_pair = d_pairs[:, pair * PAIR : (pair + 1) * PAIR].astype(bf16)
        target[rows_of(pair)] = query[rows_of(pair)]
        target[rows_of(PAIRS + pair)] = d_pair
        d_turned[head_rows(half, pair)] = d_pair.T
    single[0] = low_or_high(0.0, turned(d_shared)).astype(bf16)
    single[1] = low_or_high(0.0, d_shared).astype(bf16)
    d_single = single[half]
    target[rows_of(MIXED)] = query_single + d_single
    d_turned[single_rows(half)] = d_single.T[HDIM:]


def own_cotangent_kernel(cotangent, weight, query, both, d_turned, kept, rows, single, sems):
    half = my_half()
    chunk = rows.shape[1] // CHUNKS
    copies = [pltpu.make_async_copy(cotangent, rows, sems.at[CHUNKS])]
    for number in range(CHUNKS):
        part = pl.ds(number * chunk, chunk)
        copies.append(pltpu.make_async_copy(weight.at[part], kept.at[part], sems.at[number]))
    for copy in copies:
        copy.start()
    copies[0].wait()
    pairs = shared = None
    for number in range(CHUNKS):
        copies[number + 1].wait()
        part = slice(number * chunk, (number + 1) * chunk)
        wide = times(rows[:, part], kept[part, span(half * (SHARED + PAIR), SHARED, PAIR)], ((1,), (0,)))
        narrow = times(rows[:, part], kept[part, SHARED : SHARED + PAIR], ((1,), (0,)))
        pairs = wide if pairs is None else pairs + wide
        shared = narrow if shared is None else shared + narrow
    join_query(both, d_turned, single, query, query[rows_of(PAIRS)], pairs, shared)


def own_cotangents(cotangent, weight, query):
    return kernel(
        own_cotangent_kernel,
        "own_cotangents",
        [HBM, HBM, VMEM],
        [shaped((ROWS, PAIR), bf16), shaped((HALF, BLOCK), bf16), shaped(weight.shape, bf16)],
        [
            pltpu.VMEM(cotangent.shape, bf16),
            pltpu.VMEM((2, BLOCK, PAIR), bf16),
            pltpu.SemaphoreType.DMA((CHUNKS + 1,)),
        ],
    )(in_hbm(cotangent), in_hbm(weight), query)


def cotangent_kernel(
    cotangent, weight, query, att, d_turned_own, totals, both, stats, d_turned, d_all, single
):
    half = my_half()
    rows = cotangent[...]
    pairs = times(rows, weight[:, span(half * (SHARED + PAIR), SHARED, PAIR)], ((1,), (0,)))
    shared = times(rows, weight[:, SHARED : SHARED + PAIR], ((1,), (0,)))
    query_single = unpacked_single(query[SHARED:])
    join_query(both, d_turned, single, query, query_single, pairs, shared)
    d_all[:, at(half, BLOCK)] = d_turned_own[...]
    d_all[:, at(1 - half, BLOCK)] = d_turned[...]
    stats[...] = totals[...]
    for query_block in range(2):
        steps = rows_of(query_block)
        for pair in range(PAIRS):
            which = head_rows(half, pair)
            dots = d_all[which, steps].astype(f32) * att[which, steps].astype(f32)
            row = DELTA_STAT + 2 * pair + query_block
            stats[row : row + 1, :BLOCK] = jnp.sum(dots[:HDIM], axis=0, keepdims=True)
            stats[row : row + 1, BLOCK:] = jnp.sum(dots[HDIM:], axis=0, keepdims=True)
        which = single_rows(half)
        dots = d_all[which, steps].astype(f32) * att[which, steps].astype(f32)
        row = DELTA_STAT + 2 * PAIRS + query_block
        stats[row : row + 1, :BLOCK] = jnp.sum(dots, axis=0, keepdims=True)
    rest = jnp.concatenate([stats[:, :BLOCK], stats[:, BLOCK:]], axis=0)
    for number in range(3):
        begin = ROWS + 2 * STAT_ROWS * number
        part = rest.astype(bf16)
        both[begin : begin + 2 * STAT_ROWS] = part
        rest = rest - part.astype(f32)


def stats_of(both):
    parts = []
    for number in range(3):
        begin = ROWS + 2 * STAT_ROWS * number
        parts.append(both[begin : begin + 2 * STAT_ROWS].astype(f32))
    total = (parts[0] + parts[1]) + parts[2]
    return jnp.concatenate([total[:STAT_ROWS], total[STAT_ROWS:]], axis=1)


def cotangents(cotangent, weight, query, att, d_turned_own, totals):
    return kernel(
        cotangent_kernel,
        "cotangents",
        [VMEM] * 6,
        [shaped((SENT_ROWS, PAIR), bf16), shaped((STAT_ROWS, 2 * BLOCK), f32)],
        [
            pltpu.VMEM((HALF, BLOCK), bf16),
            pltpu.VMEM((HALF, 2 * BLOCK), bf16),
            pltpu.VMEM((2, BLOCK, PAIR), bf16),
        ],
    )(cotangent, weight, query, att, d_turned_own, totals)


def gather_blocks(target, offset, own, partner):
    half = my_half()
    for block in range(target.shape[0]):
        target[block, at(offset + half, BLOCK)] = own[rows_of(block)]
        target[block, at(offset + 1 - half, BLOCK)] = partner[rows_of(block)]


def doubled(rows, factor=1.0):
    first = low_or_high(factor, 0.0).astype(bf16)
    second = low_or_high(0.0, factor).astype(bf16)
    return jnp.concatenate([rows * first, rows * second], axis=0)


def diagonal(pair):
    return jnp.concatenate([pair[:HDIM, :BLOCK], pair[HDIM:, BLOCK:]], axis=0)


def triangles():
    row = lax.broadcasted_iota(jnp.int32, (BLOCK, BLOCK), 0)
    lane = lax.broadcasted_iota(jnp.int32, (BLOCK, BLOCK), 1)
    older = jnp.where(row > lane, 1.0, 0.0)
    return older, jnp.ones((BLOCK, BLOCK), f32), 1.0 - older


def hidden(scores, visible):
    if scores.shape[1] > visible.shape[1]:
        visible = jnp.concatenate([visible, visible], axis=1)
    return jnp.where(visible > 0.5, scores, big_negative)


def gather_kernel(
    own, partner, halo, halo_other, query_own, query_partner, keys_all, query_all, mask, clip_row, clips
):
    half = my_half()
    gather_blocks(keys_all, 0, halo, halo_other)
    gather_blocks(keys_all, 2, own, partner)
    for pair in range(PAIRS):
        query_all[pair, at(half, BLOCK)] = query_own[rows_of(pair)]
        query_all[pair, at(1 - half, BLOCK)] = query_partner[rows_of(pair)]
    query_all[PAIRS, at(half, BLOCK)] = query_own[rows_of(PAIRS)]
    query_all[PAIRS, at(1 - half, BLOCK)] = unpacked_single(query_partner[SHARED:])
    for offset, mine, theirs in ((0, halo, halo_other), (2, own, partner)):
        clips[at(offset + half, CLIP_ROWS)] = mine[ROWS:]
        clips[at(offset + 1 - half, CLIP_ROWS)] = theirs[ROWS:]

    def clip_of(block):
        return clips[block * CLIP_ROWS : (block + 1) * CLIP_ROWS].astype(f32)[0:1]

    for query_block in range(2):
        query_clip = clip_of(2 + query_block)
        for step, shape in enumerate(triangles()):
            block = query_block + step
            same = jnp.where(clip_of(block) == query_clip, 1.0, 0.0)
            present = jnp.where(2 * my_group() - 2 + block >= 0, 1.0, 0.0)
            mask[query_block, rows_of(step)] = shape * same * present
        clip_row[:, rows_of(query_block)] = query_clip


def gathered(*sources):
    return kernel(
        gather_kernel,
        "gathered",
        [VMEM] * 6,
        [
            shaped((MIXED + 1, 4 * BLOCK, PAIR), bf16),
            shaped((PAIRS + 1, 2 * BLOCK, PAIR), bf16),
            shaped((2, WIN + BLOCK, BLOCK), f32),
            shaped((1, 2 * BLOCK), f32),
        ],
        [pltpu.VMEM((4 * CLIP_ROWS, PAIR), bf16)],
        flops=COST_GATHER,
    )(*sources)


def forward_kernel(
    pieces_wanted,
    keys_all,
    query_all,
    mask,
    clip_row,
    weights_out,
    single_out,
    totals,
    att,
    att_own,
    att_swap,
    *pieces,
):
    half = my_half()
    totals[CLIP_STAT : CLIP_STAT + 1] = clip_row[...]

    def softmax(scores, row):
        lanes = slice(0, scores.shape[1])
        maximum = jnp.max(scores, axis=0, keepdims=True)
        powers = jnp.exp(scores - maximum)
        total = jnp.sum(powers, axis=0, keepdims=True)
        totals[row : row + 1, lanes] = maximum + jnp.log(total)
        return (powers * (1.0 / total)).astype(bf16)

    for pair in range(PAIRS):
        for query_block in range(2):
            keys = slice(query_block * BLOCK, query_block * BLOCK + WIN + BLOCK)
            steps = rows_of(query_block)
            query_rows = doubled(query_all[pair, steps], SCALING)
            scores = times(keys_all[pair, keys], query_rows, ((1,), (1,)))
            weights = softmax(hidden(scores, mask[query_block]), 2 * pair + query_block)
            weights_out[pair, query_block] = weights
            mixed = times(keys_all[PAIRS + pair, keys], weights, ((0,), (0,)))
            att[head_rows(half, pair), steps] = diagonal(mixed).astype(bf16)
    for query_block in range(2):
        keys = slice(query_block * BLOCK, query_block * BLOCK + WIN + BLOCK)
        steps = rows_of(query_block)
        query_rows = query_all[PAIRS, steps] * low_or_high(SCALING, 0.0).astype(bf16)
        scores = times(keys_all[MIXED, keys], query_rows, ((1,), (1,)))
        weights = softmax(hidden(scores, mask[query_block]), 2 * PAIRS + query_block)
        single_out[query_block] = weights
        mixed = times(keys_all[MIXED, keys], weights, ((0,), (0,)))
        att[single_rows(half), steps] = mixed[HDIM:].astype(bf16)

    att_own[...] = att[:, at(half, BLOCK)]
    att_swap[...] = att[:, at(1 - half, BLOCK)]
    if pieces_wanted:
        rows = pieces[0].shape[0]
        for number, piece in enumerate(pieces):
            begin = rows * jnp.bitwise_xor(lax.axis_index("dp"), number)
            piece[...] = att[span(begin, rows, 16), :]


def forward(pieces_wanted, *sources):
    piece = (HALF // max(pieces_wanted, 1), 2 * BLOCK)
    return kernel(
        functools.partial(forward_kernel, pieces_wanted),
        "forward",
        [VMEM] * 4,
        [
            shaped((PAIRS, 2, WIN + BLOCK, 2 * BLOCK), bf16),
            shaped((2, WIN + BLOCK, BLOCK), bf16),
            shaped((STAT_ROWS, 2 * BLOCK), f32),
            shaped((HALF, 2 * BLOCK), bf16),
            shaped((HALF, BLOCK), bf16),
            shaped((HALF, BLOCK), bf16),
        ]
        + [shaped(piece, bf16)] * pieces_wanted,
    )(*sources)


def score_gradients(weights, values, d_rows, delta):
    d_weights = times(values, d_rows, ((1,), (1,)))
    return (weights.astype(f32) * (d_weights - delta)).astype(bf16)


def own_kernel(
    keys_all,
    both_own,
    both_partner,
    weights_in,
    single_in,
    stats,
    att_swap,
    dq_own,
    swap,
    own_grads,
    partner_grads,
    query_all,
    dq_all,
    grads,
):
    half = my_half()
    gather_blocks(query_all, 0, both_own, both_partner)

    def delta_of(row, lanes):
        return stats[DELTA_STAT + row : DELTA_STAT + row + 1, :lanes]

    def accumulate(block, query_block, value):
        if query_block == 1:
            grads[block] = value
        else:
            grads[block, :BLOCK] += value

    for query_block in (1, 0):
        keys = slice(query_block * BLOCK, query_block * BLOCK + WIN + BLOCK)
        mine = slice(WIN - query_block * BLOCK, WIN + BLOCK)
        steps = rows_of(query_block)
        for pair in range(PAIRS):
            query_rows = doubled(query_all[pair, steps], SCALING)
            d_rows = doubled(query_all[PAIRS + pair, steps])
            weights = weights_in[pair, query_block]
            d_scores = score_gradients(
                weights,
                keys_all[PAIRS + pair, keys],
                d_rows,
                delta_of(2 * pair + query_block, 2 * BLOCK),
            )
            dq = diagonal(times(keys_all[pair, keys], d_scores, ((0,), (0,))))
            dq_all[head_rows(half, pair), steps] = (dq * SCALING).astype(bf16)
            accumulate(pair, query_block, times(d_scores[mine], query_rows, ((1,), (0,))))
            accumulate(PAIRS + pair, query_block, times(weights[mine], d_rows, ((1,), (0,))))
        rows = query_all[MIXED, steps]
        query_rows = rows * low_or_high(SCALING, 0.0).astype(bf16)
        d_rows = rows * low_or_high(0.0, 1.0).astype(bf16)
        weights = single_in[query_block]
        mixed = keys_all[MIXED, keys]
        d_scores = score_gradients(
            weights, mixed, d_rows, delta_of(2 * PAIRS + query_block, BLOCK)
        )
        dq = times(mixed, d_scores, ((0,), (0,)))[:HDIM]
        dq_all[single_rows(half), steps] = (dq * SCALING).astype(bf16)
        value = times(d_scores[mine], query_rows, ((1,), (0,)))
        accumulate(MIXED, query_block, value + times(weights[mine], d_rows, ((1,), (0,))))
    dq_own[...] = dq_all[:, at(half, BLOCK)]
    swap[:, :BLOCK] = att_swap[...]
    swap[:, BLOCK:] = dq_all[:, at(1 - half, BLOCK)]
    for block in range(MIXED + 1):
        own_grads[rows_of(block)] = grads[block, at(half, BLOCK)]
        partner_grads[rows_of(block)] = grads[block, at(1 - half, BLOCK)]


def own_gradients(*sources):
    return kernel(
        own_kernel,
        "own_gradients",
        [VMEM] * 7,
        [shaped((HALF, BLOCK), bf16), shaped((HALF, 2 * BLOCK), bf16)]
        + [shaped((ROWS, PAIR), f32)] * 2,
        [
            pltpu.VMEM((MIXED + 1, 2 * BLOCK, PAIR), bf16),
            pltpu.VMEM((HALF, 2 * BLOCK), bf16),
            pltpu.VMEM((MIXED + 1, 2 * BLOCK, PAIR), f32),
        ],
    )(*sources)


def next_kernel(
    groups,
    own,
    partner,
    both_own,
    both_partner,
    own_grads,
    partner_grads,
    mine,
    swap,
    keys_all,
    query_all,
    mask,
    grads,
    clips,
    stats,
):
    half = my_half()
    stats[...] = stats_of(both_partner)
    gather_blocks(keys_all, 0, own, partner)
    gather_blocks(query_all, 0, both_own, both_partner)
    for block in range(MIXED + 1):
        grads[block, at(half, BLOCK)] = own_grads[rows_of(block)]
        grads[block, at(1 - half, BLOCK)] = partner_grads[rows_of(block)]
    clips[at(half, CLIP_ROWS)] = own[ROWS:]
    clips[at(1 - half, CLIP_ROWS)] = partner[ROWS:]
    present = jnp.where(my_group() < groups - 1, 1.0, 0.0)
    older, every, _ = triangles()
    for query_block, block, shape in ((0, 0, older), (0, 1, every), (1, 1, older)):
        query_clip = stats[CLIP_STAT : CLIP_STAT + 1, rows_of(query_block)]
        key_clip = clips[block * CLIP_ROWS : (block + 1) * CLIP_ROWS].astype(f32)[0:1]
        same = jnp.where(key_clip == query_clip, 1.0, 0.0)
        mask[query_block, rows_of(block)] = shape * same * present

    for query_block in range(2):
        keys = slice(query_block * BLOCK, WIN)
        steps = rows_of(query_block)
        visible = mask[query_block, keys]
        for pair in range(PAIRS + 1):
            row = 2 * pair + query_block
            lanes = slice(0, 2 * BLOCK if pair < PAIRS else BLOCK)
            if pair < PAIRS:
                key_rows, value_rows = keys_all[pair, keys], keys_all[PAIRS + pair, keys]
                query_rows = doubled(query_all[pair, steps], SCALING)
                d_rows = doubled(query_all[PAIRS + pair, steps])
            else:
                key_rows = value_rows = keys_all[MIXED, keys]
                query_rows = query_all[MIXED, steps] * low_or_high(SCALING, 0.0).astype(bf16)
                d_rows = query_all[MIXED, steps] * low_or_high(0.0, 1.0).astype(bf16)
            scores = hidden(times(key_rows, query_rows, ((1,), (1,))), visible)
            weights = jnp.exp(scores - stats[row : row + 1, lanes]).astype(bf16)
            delta = stats[DELTA_STAT + row : DELTA_STAT + row + 1, lanes]
            d_scores = score_gradients(weights, value_rows, d_rows, delta)
            dk = times(d_scores, query_rows, ((1,), (0,)))
            dv = times(weights, d_rows, ((1,), (0,)))
            if pair < PAIRS:
                grads[pair, keys] += dk
                grads[PAIRS + pair, keys] += dv
            else:
                grads[MIXED, keys] += dk + dv
    for block in range(MIXED + 1):
        mine[rows_of(block)] = grads[block, at(half, BLOCK)].astype(bf16)
        swap[rows_of(block)] = grads[block, at(1 - half, BLOCK)].astype(bf16)


def next_gradients(groups, *sources):
    return kernel(
        functools.partial(next_kernel, groups),
        "next_gradients",
        [VMEM] * 6,
        [shaped((ROWS, PAIR), bf16)] * 2,
        [
            pltpu.VMEM((MIXED + 1, 2 * BLOCK, PAIR), bf16),
            pltpu.VMEM((MIXED + 1, 2 * BLOCK, PAIR), bf16),
            pltpu.VMEM((2, 2 * BLOCK, BLOCK), f32),
            pltpu.VMEM((MIXED + 1, 2 * BLOCK, PAIR), f32),
            pltpu.VMEM((2 * CLIP_ROWS, PAIR), bf16),
            pltpu.VMEM((STAT_ROWS, 2 * BLOCK), f32),
        ],
    )(*sources)


def output_kernel(att_own, received, weight, out, full):
    half = my_half()
    full[at(half, HALF)] = att_own[...]
    full[at(1 - half, HALF)] = received[:, :BLOCK]
    out[...] = times(weight[...], full[...], ((1,), (0,))).T.astype(bf16)


def output_rows(att_own, received, weight):
    return kernel(
        output_kernel,
        "output",
        [VMEM] * 3,
        [shaped((BLOCK, weight.shape[0]), bf16), shaped((WIDTH, BLOCK), bf16)],
    )(att_own, received, weight)


def place_keys_kernel(mine, theirs, key_out, value_out, key, value, mixed, sems):
    half = my_half()
    for side, source in ((half, mine), (1 - half, theirs)):
        for pair in range(PAIRS):
            key[:, columns_of(side, pair)] = source[rows_of(pair)]
            value[:, columns_of(side, pair)] = source[rows_of(PAIRS + pair)]
        mixed[side] = source[rows_of(MIXED)].astype(f32)
    shared = slice(SHARED, SHARED + PAIR)
    key[:, shared] = low_or_high(mixed[0], turned(mixed[1])).astype(bf16)
    value[:, shared] = low_or_high(turned(mixed[0]), mixed[1]).astype(bf16)
    pairs = ((key, key_out), (value, value_out))
    copies = [pltpu.make_async_copy(a, b, sems.at[n]) for n, (a, b) in enumerate(pairs)]
    for copy in copies:
        copy.start()
    for copy in copies:
        copy.wait()


def place_keys(*sources):
    wide = pltpu.VMEM((BLOCK, WIDTH), bf16)
    mixed = pltpu.VMEM((2, BLOCK, PAIR), f32)
    return kernel(
        place_keys_kernel,
        "place_keys",
        [VMEM] * 2,
        [shaped((BLOCK, WIDTH), bf16)] * 2,
        [wide, wide, mixed, pltpu.SemaphoreType.DMA((2,))],
        HBM,
        COST_KEYS,
    )(*sources)


def place_kernel(dq_mine, received, first, second, query_out, weight_out, dq_all, query, both, sems):
    half = my_half()
    rows = first.shape[0]
    moves = [(both, weight_out), (query, query_out)]
    copies = [pltpu.make_async_copy(a, b, sems.at[n]) for n, (a, b) in enumerate(moves)]
    both[span(half * rows, rows, 16)] = first[...].astype(f32)
    both[span((1 - half) * rows, rows, 16)] = second[...].astype(f32)
    copies[0].start()
    dq_all[at(half, HALF)] = dq_mine[...]
    dq_all[at(1 - half, HALF)] = received[:, BLOCK:]
    for block in range(WIDTH // PAIR):
        query[:, block * PAIR : (block + 1) * PAIR] = dq_all[rows_of(block)].T
    copies[1].start()
    for copy in copies:
        copy.wait()


def place(*sources):
    rows, lanes = sources[-1].shape
    query, weight = kernel(
        place_kernel,
        "place",
        [VMEM] * 4,
        [shaped((BLOCK, WIDTH), bf16), shaped((2 * rows, lanes), f32)],
        [
            pltpu.VMEM((WIDTH, BLOCK), bf16),
            pltpu.VMEM((BLOCK, WIDTH), bf16),
            pltpu.VMEM((2 * rows, lanes), f32),
            pltpu.SemaphoreType.DMA((2,)),
        ],
        HBM,
    )(*sources)
    return query, weight.T


def weight_kernel(count, *refs):
    pieces, cots, products = refs[:count], refs[count : 2 * count], refs[-1]
    half = my_half()
    att = jnp.concatenate([piece[:, at(half, BLOCK)] for piece in pieces], axis=1)
    products[...] = times(att, jnp.concatenate([cot[...] for cot in cots], axis=0), ((1,), (0,)))


def weight_products(pieces, cots):
    return kernel(
        functools.partial(weight_kernel, len(pieces)),
        "weight_products",
        [VMEM] * (2 * len(pieces)),
        [shaped((pieces[0].shape[0], cots[0].shape[1]), f32)],
        flops=COST_FIRST,
    )(*pieces, *cots)[0]


def weight_rest_kernel(count, products, *refs):
    pieces, cots = refs[:count], refs[count : 2 * count]
    kept, *sent = refs[2 * count :]
    total = sent.pop()
    half = my_half()
    att = jnp.concatenate([piece[:, at(1 - half, BLOCK)] for piece in pieces], axis=1)
    cot = jnp.concatenate([cot[...] for cot in cots], axis=0)
    total[...] = products[...] + times(att, cot, ((1,), (0,)))
    group = my_group()
    lanes = kept.shape[1]
    kept[...] = total[:, at(group, lanes)]
    for number, out in enumerate(sent):
        target = jnp.bitwise_xor(group, number + 1)
        out[...] = total[:, at(target, lanes)].astype(bf16)


def weight_rest(products, pieces, cots, groups):
    rows, outs = products.shape
    part = (rows, outs // groups)
    return kernel(
        functools.partial(weight_rest_kernel, len(pieces)),
        "weight_rest",
        [VMEM] * (1 + 2 * len(pieces)),
        [shaped(part, f32)] + [shaped(part, bf16)] * (groups - 1),
        [pltpu.VMEM((rows, outs), f32)],
    )(products, *pieces, *cots)


def weight_sum_kernel(kept, *rest):
    received, (first, second, total) = rest[:-3], rest[-3:]
    value = kept[...]
    for part in received:
        value = value + part[...].astype(f32)
    total[...] = value
    lanes = first.shape[1]
    odd = jnp.bitwise_and(lax.axis_index("dp"), 1)
    first[...] = total[:, at(odd, lanes)].astype(bf16)
    second[...] = total[:, at(1 - odd, lanes)].astype(bf16)


def weight_sum(kept, received):
    rows, lanes = kept.shape
    return kernel(
        weight_sum_kernel,
        "weight_sum",
        [VMEM] * (1 + len(received)),
        [shaped((rows, lanes // 2), bf16)] * 2,
        [pltpu.VMEM((rows, lanes), f32)],
        flops=COST_SUM,
    )(kept, *received)


def swapped(value, axis, bits):
    count = lax.axis_size(axis)
    return lax.ppermute(value, axis, [(source, source ^ bits) for source in range(count)])


def rotated(value, axis, steps):
    count = lax.axis_size(axis)
    return lax.ppermute(
        value, axis, [(source, (source + steps) % count) for source in range(count)]
    )


def moved(value, axis, steps):
    count = lax.axis_size(axis)
    first, last = (max(0, -steps), min(count, count - steps))
    return lax.ppermute(value, axis, [(source, source + steps) for source in range(first, last)])


def placed(value, flip):
    lanes = lax.axis_size("ctx")
    moves = []
    for source in range(lax.axis_size("dp")):
        for index in range(lanes):
            group, half = index // 2, index % 2
            target_half = (source % 2) ^ flip
            target = 2 * half + source // 2
            moves.append((source * lanes + index, target * lanes + 2 * group + target_half))
    return lax.ppermute(value, ("dp", "ctx"), moves)


def after(*values):
    return lax.optimization_barrier(values)


def per_device(queries, key_states, value_states, out_cotangent, out_weight, block_clip):
    sequences = lax.axis_size("dp")
    groups = lax.axis_size("ctx") // 2
    short = sequences == 4 and groups in (2, 4)
    cotangent = out_cotangent[0]

    swap_kv, own, swap_query, query = pack(
        block_clip, queries[0], key_states[0], value_states[0]
    )
    swap_kv, cot_early = after(swap_kv, cotangent)
    partner = swapped(swap_kv, "ctx", 1)
    halo = rotated(own, "ctx", 2)
    both_own, d_turned_own, weight = own_cotangents(cotangent, out_weight, query)
    cots = [cotangent]
    if short:
        cots += [swapped(cot_early, "dp", n) for n in (1, 2)]

    partner, both_own, swap_query = after(partner, both_own, swap_query)
    halo_other = rotated(partner, "ctx", 2)
    query_partner = swapped(swap_query, "ctx", 1)
    halo, both_own, cot_late, *cots = after(halo, both_own, cotangent, *cots)
    cot_partner = swapped(cot_late, "ctx", 1)
    next_own = moved(both_own, "ctx", -2)
    if short:
        cots.append(swapped(cots[2], "dp", 1))
    keys_all, query_all, mask, clip_row = gathered(
        own, partner, halo, halo_other, query, query_partner
    )
    keys_all, cot_partner = after(keys_all, cot_partner)

    later = [cot_partner]
    if short:
        later += [swapped(cot_partner, "dp", n) for n in (1, 2)]
    weights, single, totals, att, att_own, att_swap, *pieces = forward(
        4 if short else 0, keys_all, query_all, mask, clip_row
    )
    weights, next_own, *rest = after(weights, next_own, *pieces, *cots)
    pieces, cots = rest[: len(pieces)], rest[len(pieces) :]

    if short:
        pieces[1:] = [swapped(pieces[n], "dp", n) for n in (1, 2, 3)]
        weights, *later = after(weights, *later)
        later.append(swapped(later[2], "dp", 1))
    both_partner, stats = cotangents(
        cot_partner, weight, query_partner, att, d_turned_own, totals
    )
    next_partner = rotated(both_partner, "ctx", -2)
    dq_own, swap, own_grads, partner_grads = own_gradients(
        keys_all, both_own, both_partner, weights, single, stats, att_swap
    )
    own_grads, swap, *pieces = after(own_grads, swap, *pieces)

    if short:
        products = weight_products(pieces, cots)
        products, *later = after(products, *later)
        kept, *sent = weight_rest(products, pieces, later, groups)
        sent[-1], next_partner = after(sent[-1], next_partner)
        arrived = [swapped(part, "ctx", 2 * (n + 1)) for n, part in enumerate(sent)]
        kept, own_grads = after(kept, own_grads)
    received = swapped(swap, "ctx", 1)
    kv_own, kv_swap = next_gradients(
        groups, own, partner, next_own, next_partner, own_grads, partner_grads
    )
    kv_rest = swapped(kv_swap, "ctx", 1)
    if short:
        kept, kv_own, received, *arrived = after(kept, kv_own, received, *arrived)
        first, second = weight_sum(kept, arrived)
        first, second = placed(first, 0), placed(second, 1)
    sublayer_out, att_full = output_rows(att_own, received, weight)
    if not short:
        product = lax.dot_general(
            cotangent, att_full, (((0,), (1,)), ((), ())), preferred_element_type=f32
        ).astype(bf16)
        sequence_grad = lax.psum_scatter(product, "ctx", scatter_dimension=0, tiled=True)
        weight_grad = lax.psum_scatter(
            sequence_grad.astype(f32), "dp", scatter_dimension=1, tiled=True
        )
        first = second = jnp.zeros((16, 128), bf16)
    kv_own, sublayer_out = after(kv_own, sublayer_out)
    key_grad, value_grad = place_keys(kv_own, kv_rest)
    dq_own, key_grad = after(dq_own, key_grad)
    query_grad, placed_weight = place(dq_own, received, first, second)
    if short:
        weight_grad = placed_weight
    return (
        sublayer_out[None],
        query_grad[None],
        key_grad[None],
        value_grad[None],
        weight_grad,
    )


def solution(mesh):
    return jax.shard_map(
        per_device,
        mesh=mesh,
        in_specs=(
            P("dp", "ctx", None),
            P("dp", "ctx", None),
            P("dp", "ctx", None),
            P("dp", "ctx", None),
            P(),
            P("dp", "ctx"),
        ),
        out_specs=(
            P("dp", "ctx", None),
            P("dp", "ctx", None),
            P("dp", "ctx", None),
            P("dp", "ctx", None),
            P("ctx", "dp"),
        ),
        check_vma=False,
    )
```

time: 212 us -> 59 us (0.28); the launches traced: 208 us -> 58.8 us
  matrix products: 82.3 us -> 0 us
  local copies, waits for them, and re-layouts: 30.2 us -> 0.01 us
  other arithmetic: 18.4 us -> 0 us
  Pallas kernels: 0 us -> 18.2 us
  waiting for transfers between devices: 25.8 us -> 10.1 us
  between operations: 14.9 us -> 1.49 us
  starting transfers between devices: 36.2 us -> 29 us
    dot_general x66 -> x0, matrix products: 82.3 us -> none  [the longest x9 14.2 us: backward_one_group(): jnp.einsum('hqk,hqd->hkd', d_scores, query_head, preferred_element_type=j...]
    pallas_call x0 -> x13, Pallas kernels: none -> 18.2 us  [the longest x1 3.97 us: forward(): kernel(functools.partial(forward_kernel, pieces_wanted), 'forward', [VMEM...]
    unnamed x24 -> x2, local copies, waits for them, and re-layouts: 14.7 us -> 0.01 us
    reduce_scatter x1 -> x0, waiting for transfers between devices: 8.83 us -> none  [per_device(): lax.psum_scatter(sequence_grad, 'dp', scatter_dimension=1, tiled=True)]
    ppermute x10 -> x23, starting transfers between devices: 36.1 us -> 29 us  [the longest x17 17.7 us: swapped(): lax.ppermute(value, axis, [(source, source ^ bits) for source in range(co...]
    ppermute x10 -> x23, waiting for transfers between devices: 16.9 us -> 10.1 us  [the longest x17 8.49 us: swapped(): lax.ppermute(value, axis, [(source, source ^ bits) for source in range(co...]
    sub x9 -> x0, local copies, waits for them, and re-layouts: 6.21 us -> none  [backward_one_group(): probs = jnp.exp(scores - total_head[:, :, None])]
    dynamic_update_slice x9 -> x0, other arithmetic: 5.2 us -> none  [forward_block(): mixed, log_total = lax.map(forward_one_group, stacked)]
  transfers between devices with their start and end apart: 12 -> 23, of which waited for: 4 -> 6; matrix products, arithmetic and copies ran while one was open for 39% -> 0% of each run, Pallas kernels for 0% -> 27%
where the time goes in v3:
time: 59 us; the launch traced here: 58.8 us
  starting transfers between devices  29 us (49%)
  Pallas kernels  18.2 us (31%)
  waiting for transfers between devices  10.1 us (17%)
  between operations  1.49 us (3%)
    ppermute x17, starting transfers between devices, swapped(): lax.ppermute(value, axis, [(source, source ^ bits) for source in range(co...  17.7 us
    ppermute x17, waiting for transfers between devices, swapped(): lax.ppermute(value, axis, [(source, source ^ bits) for source in range(co...  8.49 us
    ppermute x3, starting transfers between devices, rotated(): lax.ppermute(value, axis, [(source, (source + steps) % count) for source...  5.76 us
    ppermute x2, starting transfers between devices, placed(): return lax.ppermute(value, ('dp', 'ctx'), moves)  4.28 us
    pallas_call x1, Pallas kernels, forward(): kernel(functools.partial(forward_kernel, pieces_wanted), 'forward', [VMEM...  3.97 us
    pallas_call x1, Pallas kernels, own_gradients(): kernel(own_kernel, 'own_gradients', [VMEM] * 7, [shaped((HALF, BLOCK), bf...  3.19 us
    pallas_call x1, Pallas kernels, next_gradients(): kernel(functools.partial(next_kernel, groups), 'next_gradients', [VMEM] *...  2.25 us
    pallas_call x1, Pallas kernels, own_cotangents(): kernel(own_cotangent_kernel, 'own_cotangents', [HBM, HBM, VMEM], [shaped(...  2.24 us
  transfers between devices with their start and end apart: 23, of which 6 were waited for; matrix products, arithmetic and copies ran while one was open for 0% of the time, Pallas kernels for 27%

profile of v3, /device:TPU:0, one launch (start us, length us, event | category | flops | bytes accessed | tf_op | source)
XLA Modules:
  0.0 58.8 jit_solution(4159169959084501031)
XLA Ops:
  1.3 1.4 %pack.1 = (bf16[1168,128]{1,0:T(8,128)(2,1)S(1)}, bf16[1168,128]{1,0:T(8,128)(2,1)S(1)}, bf16[576,128]{1,0:T(8,128)(2,1)S(1)}, bf16[640,128]{1,0:T(8,128)(2,1)S(1)}) custom-call(s32[1,1]{1,0:T(1,128)S(6)} %copy.11.clip, bf16[128,1152]{1,0:T(8,128)(2,1)} %bitcast.14, bf16[128,1152]{1,0:T(8,128)(2,1)} %bitcast.15, bf16[128,1152]{1,0:T(8,128)(2,1)} %bitcast.16), custom_call_target="tpu_custom_call" | custom-call | flops 1000000 | bytes 10000 | tf_op jit(solution)/shard_map/pack/pallas_call | solution.py:148
  2.7 3.0 %collective-permute-start = (bf16[1168,128]{1,0:T(8,128)(2,1)S(1)}, bf16[1168,128]{1,0:T(8,128)(2,1)S(1)}, u32[]{:S(2)}, u32[]{:S(2)}) collective-permute-start(bf16[1168,128]{1,0:T(8,128)(2,1)S(1)} %get-tuple-element.99), channel_id=1, source_target_pairs={{0,1},{1,0},{2,3},{3,2},{4,5},{5,4},{6,7},{7,6},{8,9},{9,8},{10,11... | collective-permute-start | bytes 897032 | tf_op jit(solution)/shard_map/ppermute | solution.py:743
  5.7 1.6 %collective-permute-start.1 = (bf16[1168,128]{1,0:T(8,128)(2,1)S(1)}, bf16[1168,128]{1,0:T(8,128)(2,1)S(1)}, u32[]{:S(2)}, u32[]{:S(2)}) collective-permute-start(bf16[1168,128]{1,0:T(8,128)(2,1)S(1)} %get-tuple-element.97.own), channel_id=1, source_target_pairs={{0,2},{1,3},{2,4},{3,5},{4,6},{5,7},{6,0},{7,1},{8,10},{9,11},{10,... | collective-permute-start | bytes 897032 | tf_op jit(solution)/shard_map/ppermute | solution.py:748
  7.3 1.5 %collective-permute-start.3 = (bf16[128,1024]{1,0:T(8,128)(2,1)}, bf16[128,1024]{1,0:T(8,128)(2,1)S(1)}, u32[]{:S(2)}, u32[]{:S(2)}) collective-permute-start(bf16[128,1024]{1,0:T(8,128)(2,1)} %bitcast.9), channel_id=1, source_target_pairs={{0,16},{8,24},{16,0},{24,8},{1,17},{9,25},{17,1},{25,9},{2,18},{10... | collective-permute-start | bytes 786440 | tf_op jit(solution)/shard_map/ppermute | solution.py:743
  8.8 2.2 %own_cotangents.1 = (bf16[1152,128]{1,0:T(8,128)(2,1)S(1)}, bf16[576,128]{1,0:T(8,128)(2,1)S(1)}, bf16[1024,1152]{1,0:T(8,128)(2,1)S(1)}) custom-call(bf16[128,1024]{1,0:T(8,128)(2,1)} %bitcast.11, bf16[1024,1152]{1,0:T(8,128)(2,1)} %weight.1, bf16[640,128]{1,0:T(8,128)(2,1)S(1)} %get-tuple-element.100.query.query_own), custom_call_target="tpu_custom_call" | custom-call | flops 1000000 | bytes 10000 | tf_op jit(solution)/shard_map/own_cotangents/pallas_call | solution.py:207
  11.1 1.7 %collective-permute-done.partner = bf16[1168,128]{1,0:T(8,128)(2,1)S(1)} collective-permute-done((bf16[1168,128]{1,0:T(8,128)(2,1)S(1)}, bf16[1168,128]{1,0:T(8,128)(2,1)S(1)}, u32[]{:S(2)}, u32[]{:S(2)}) %collective-permute-start) | collective-permute-done | bytes 299040 | tf_op jit(solution)/shard_map/ppermute | solution.py:743
  12.8 1.8 %collective-permute-start.4 = (bf16[1168,128]{1,0:T(8,128)(2,1)S(1)}, bf16[1168,128]{1,0:T(8,128)(2,1)S(1)}, u32[]{:S(2)}, u32[]{:S(2)}) collective-permute-start(bf16[1168,128]{1,0:T(8,128)(2,1)S(1)} %collective-permute-done.partner), channel_id=1, source_target_pairs={{0,2},{1,3},{2,4},{3,5},{4,6},{5,7},{6,0},{7,1},{8,10},{9,11},{10,... | collective-permute-start | bytes 897032 | tf_op jit(solution)/shard_map/ppermute | solution.py:748
  14.7 1.5 %collective-permute-start.5 = (bf16[576,128]{1,0:T(8,128)(2,1)S(1)}, bf16[576,128]{1,0:T(8,128)(2,1)S(1)}, u32[]{:S(2)}, u32[]{:S(2)}) collective-permute-start(bf16[576,128]{1,0:T(8,128)(2,1)S(1)} %get-tuple-element.107), channel_id=1, source_target_pairs={{0,1},{1,0},{2,3},{3,2},{4,5},{5,4},{6,7},{7,6},{8,9},{9,8},{10,11... | collective-permute-start | bytes 442376 | tf_op jit(solution)/shard_map/ppermute | solution.py:743
  16.8 1.3 %collective-permute-start.7 = (bf16[1152,128]{1,0:T(8,128)(2,1)S(1)}, bf16[1152,128]{1,0:T(8,128)(2,1)S(1)}, u32[]{:S(2)}, u32[]{:S(2)}) collective-permute-start(bf16[1152,128]{1,0:T(8,128)(2,1)S(1)} %get-tuple-element.111.both_own), channel_id=1, source_target_pairs={{2,0},{3,1},{4,2},{5,3},{6,4},{7,5},{10,8},{11,9},{12,10},{13,11},... | collective-permute-start | bytes 884744 | tf_op jit(solution)/shard_map/ppermute | solution.py:756
  18.1 3.4 %collective-permute-done.5.query_partner.query = bf16[576,128]{1,0:T(8,128)(2,1)S(1)} collective-permute-done((bf16[576,128]{1,0:T(8,128)(2,1)S(1)}, bf16[576,128]{1,0:T(8,128)(2,1)S(1)}, u32[]{:S(2)}, u32[]{:S(2)}) %collective-permute-start.5) | collective-permute-done | bytes 147488 | tf_op jit(solution)/shard_map/ppermute | solution.py:743
  21.4 1.6 %collective-permute-done.4.halo_other = bf16[1168,128]{1,0:T(8,128)(2,1)S(1)} collective-permute-done((bf16[1168,128]{1,0:T(8,128)(2,1)S(1)}, bf16[1168,128]{1,0:T(8,128)(2,1)S(1)}, u32[]{:S(2)}, u32[]{:S(2)}) %collective-permute-start.4) | collective-permute-done | bytes 299040 | tf_op jit(solution)/shard_map/ppermute | solution.py:748
  23.2 1.5 %collective-permute-done.6.cotangent.refs_4_ = bf16[128,1024]{1,0:T(8,128)(2,1)S(1)} collective-permute-done((bf16[128,1024]{1,0:T(8,128)(2,1)S(1)}, bf16[128,1024]{1,0:T(8,128)(2,1)S(1)}, u32[]{:S(2)}, u32[]{:S(2)}) %collective-permute-start.6) | collective-permute-done | bytes 262176 | tf_op jit(solution)/shard_map/ppermute | solution.py:743
  24.7 1.5 %collective-permute-start.10 = (bf16[128,1024]{1,0:T(8,128)(2,1)S(1)}, bf16[128,1024]{1,0:T(8,128)(2,1)S(1)}, u32[]{:S(2)}, u32[]{:S(2)}) collective-permute-start(bf16[128,1024]{1,0:T(8,128)(2,1)S(1)} %collective-permute-done.6.cotangent.refs_4_), channel_id=1, source_target_pairs={{0,16},{8,24},{16,0},{24,8},{1,17},{9,25},{17,1},{25,9},{2,18},{10... | collective-permute-start | bytes 786440 | tf_op jit(solution)/shard_map/ppermute | solution.py:743
  26.2 4.0 %forward.1 = (bf16[4,2,384,256]{3,2,1,0:T(8,128)(2,1)S(1)}, bf16[2,384,128]{2,1,0:T(8,128)(2,1)S(1)}, f32[24,256]{1,0:T(8,128)S(1)}, bf16[576,256]{1,0:T(8,128)(...) custom-call(bf16[9,512,128]{2,1,0:T(8,128)(2,1)S(1)} %get-tuple-elem, ...), custom_call_target="tpu_custom_call" | custom-call | flops 1000000 | bytes 10000 | tf_op jit(solution)/shard_map/forward/pallas_call | solution.py:405
  30.9 2.4 %collective-permute-start.15 = (bf16[1296,128]{1,0:T(8,128)(2,1)S(1)}, bf16[1296,128]{1,0:T(8,128)(2,1)S(1)}, u32[]{:S(2)}, u32[]{:S(2)}) collective-permute-start(bf16[1296,128]{1,0:T(8,128)(2,1)S(1)} %get-tuple-element.120.both_partner), channel_id=1, source_target_pairs={{0,6},{1,7},{2,0},{3,1},{4,2},{5,3},{6,4},{7,5},{8,14},{9,15},{10,... | collective-permute-start | bytes 995336 | tf_op jit(solution)/shard_map/ppermute | solution.py:748
  35.7 3.2 %own_gradients.1 = (bf16[576,128]{1,0:T(8,128)(2,1)S(1)}, bf16[576,256]{1,0:T(8,128)(2,1)S(1)}, f32[1152,128]{1,0:T(8,128)S(1)}, f32[1152,128]{1,0:T(8,128)S(1)}) custom-call(bf16[9,512,128]{2,1,0:T(8,128)(2,1)S(1)} %get-tuple-element.110.keys_all, bf16[1152,128]{1,0:T(8,128)(2,1)S(1)} %get-tuple-element.111.both_own, ...), custom_call_target="tpu_custom_call" | custom-call | flops 1000000 | bytes 10000 | tf_op jit(solution)/shard_map/own_gradients/pallas_call | solution.py:493
  38.9 1.5 %collective-permute-start.16 = (bf16[576,256]{1,0:T(8,128)(2,1)S(1)}, bf16[576,256]{1,0:T(8,128)(2,1)S(1)}, u32[]{:S(2)}, u32[]{:S(2)}) collective-permute-start(bf16[576,256]{1,0:T(8,128)(2,1)S(1)} %get-tuple-element.165), channel_id=1, source_target_pairs={{0,1},{1,0},{2,3},{3,2},{4,5},{5,4},{6,7},{7,6},{8,9},{9,8},{10,11... | collective-permute-start | bytes 884744 | tf_op jit(solution)/shard_map/ppermute | solution.py:743
  41.2 2.3 %collective-permute-start.18 = (bf16[144,256]{1,0:T(8,128)(2,1)S(1)}, bf16[144,256]{1,0:T(8,128)(2,1)S(1)}, u32[]{:S(2)}, u32[]{:S(2)}) collective-permute-start(bf16[144,256]{1,0:T(8,128)(2,1)S(1)} %get-tuple-element.167), channel_id=1, source_target_pairs={{0,4},{1,5},{2,6},{3,7},{4,0},{5,1},{6,2},{7,3},{8,12},{9,13},{10,... | collective-permute-start | bytes 221192 | tf_op jit(solution)/shard_map/ppermute | solution.py:743
  43.5 2.1 %collective-permute-start.19 = (bf16[144,256]{1,0:T(8,128)(2,1)S(1)}, bf16[144,256]{1,0:T(8,128)(2,1)S(1)}, u32[]{:S(2)}, u32[]{:S(2)}) collective-permute-start(bf16[144,256]{1,0:T(8,128)(2,1)S(1)} %get-tuple-element.168), channel_id=1, source_target_pairs={{0,6},{1,7},{2,4},{3,5},{4,2},{5,3},{6,0},{7,1},{8,14},{9,15},{10,... | collective-permute-start | bytes 221192 | tf_op jit(solution)/shard_map/ppermute | solution.py:743
  45.6 2.2 %next_gradients.1 = (bf16[1152,128]{1,0:T(8,128)(2,1)S(1)}, bf16[1152,128]{1,0:T(8,128)(2,1)S(1)}) custom-call(bf16[1168,128]{1,0:T(8,128)(2,1)S(1)} %get-tuple-element.97.own, bf16[1168,128]{1,0:T(8,128)(2,1)S(1)} %collective-permute-done.partner, bf16[1152,128]{1,0:T(8,128)(2,1)S(1)} %collective-permute-done.7.both_own, ...), custom_call_target="tpu_custom_call" | custom-call | flops 1000000 | bytes 10000 | tf_op jit(solution)/shard_map/next_gradients/pallas_call | solution.py:573
  47.9 1.2 %collective-permute-start.20 = (bf16[1152,128]{1,0:T(8,128)(2,1)S(1)}, bf16[1152,128]{1,0:T(8,128)(2,1)S(1)}, u32[]{:S(2)}, u32[]{:S(2)}) collective-permute-start(bf16[1152,128]{1,0:T(8,128)(2,1)S(1)} %get-tuple-element.176), channel_id=1, source_target_pairs={{0,1},{1,0},{2,3},{3,2},{4,5},{5,4},{6,7},{7,6},{8,9},{9,8},{10,11... | collective-permute-start | bytes 884744 | tf_op jit(solution)/shard_map/ppermute | solution.py:743
  49.1 1.4 %collective-permute-done.18.rest_1_ = bf16[144,256]{1,0:T(8,128)(2,1)S(1)} collective-permute-done((bf16[144,256]{1,0:T(8,128)(2,1)S(1)}, bf16[144,256]{1,0:T(8,128)(2,1)S(1)}, u32[]{:S(2)}, u32[]{:S(2)}) %collective-permute-start.18) | collective-permute-done | bytes 73760 | tf_op jit(solution)/shard_map/ppermute | solution.py:743
  51.2 3.6 %collective-permute-start.22 = (bf16[144,128]{1,0:T(8,128)(2,1)S(1)}, bf16[144,128]{1,0:T(8,128)(2,1)S(1)}, u32[]{:S(2)}, u32[]{:S(2)}) collective-permute-start(bf16[144,128]{1,0:T(8,128)(2,1)S(1)} %get-tuple-element.184), channel_id=1, source_target_pairs={{0,1},{1,17},{2,3},{3,19},{4,5},{5,21},{6,7},{7,23},{8,0},{9,16},{... | collective-permute-start | bytes 110600 | tf_op jit(solution)/shard_map/ppermute | solution.py:768
  54.8 1.6 %output.1 = (bf16[128,1024]{1,0:T(8,128)(2,1)}, bf16[1152,128]{1,0:T(8,128)(2,1)}) custom-call(bf16[576,128]{1,0:T(8,128)(2,1)S(1)} %get-tuple-element.170.att_own, bf16[576,256]{1,0:T(8,128)(2,1)S(1)} %collective-permute-done.16.received, bf16[1024,1152]{1,0:T(8,128)(2,1)S(1)} %get-tuple-element.113.weight), custom_call_target="tpu_custom_call" | custom-call | flops 1000000 | bytes 10000 | tf_op jit(solution)/shard_map/output/pallas_call | solution.py:597
  (37 shorter events, 7.7 us)
Async XLA Ops:
  0.6 15.5 %copy-start = (bf16[1,128,1024]{2,1,0:T(8,128)(2,1)S(1)}, bf16[1,128,1024]{2,1,0:T(8,128)(2,1)}, u32[]{:S(2)}) copy-start(bf16[1,128,1024]{2,1,0:T(8,128)(2,1)} %param.9) | copy-start | bytes 786436
  2.7 10.1 %collective-permute-start = (bf16[1168,128]{1,0:T(8,128)(2,1)S(1)}, bf16[1168,128]{1,0:T(8,128)(2,1)S(1)}, u32[]{:S(2)}, u32[]{:S(2)}) collective-permute-start(bf16[1168,128]{1,0:T(8,128)(2,1)S(1)} %get-tuple-element.99), channel_id=1, source_target_pairs={{0,1},{1,0},{2,3},{3,2},{4,5},{5,4},{6,7},{7,6},{8,9},{9,8},{10,11... | collective-permute-start | bytes 897032 | tf_op jit(solution)/shard_map/ppermute | solution.py:743
  5.7 10.4 %collective-permute-start.1 = (bf16[1168,128]{1,0:T(8,128)(2,1)S(1)}, bf16[1168,128]{1,0:T(8,128)(2,1)S(1)}, u32[]{:S(2)}, u32[]{:S(2)}) collective-permute-start(bf16[1168,128]{1,0:T(8,128)(2,1)S(1)} %get-tuple-element.97.own), channel_id=1, source_target_pairs={{0,2},{1,3},{2,4},{3,5},{4,6},{5,7},{6,0},{7,1},{8,10},{9,11},{10,... | collective-permute-start | bytes 897032 | tf_op jit(solution)/shard_map/ppermute | solution.py:748
  7.3 8.8 %collective-permute-start.3 = (bf16[128,1024]{1,0:T(8,128)(2,1)}, bf16[128,1024]{1,0:T(8,128)(2,1)S(1)}, u32[]{:S(2)}, u32[]{:S(2)}) collective-permute-start(bf16[128,1024]{1,0:T(8,128)(2,1)} %bitcast.9), channel_id=1, source_target_pairs={{0,16},{8,24},{16,0},{24,8},{1,17},{9,25},{17,1},{25,9},{2,18},{10... | collective-permute-start | bytes 786440 | tf_op jit(solution)/shard_map/ppermute | solution.py:743
  8.8 7.3 %collective-permute-start.2 = (bf16[128,1024]{1,0:T(8,128)(2,1)}, bf16[128,1024]{1,0:T(8,128)(2,1)S(1)}, u32[]{:S(2)}, u32[]{:S(2)}) collective-permute-start(bf16[128,1024]{1,0:T(8,128)(2,1)} %bitcast.10), channel_id=1, source_target_pairs={{0,8},{8,0},{16,24},{24,16},{1,9},{9,1},{17,25},{25,17},{2,10},{10... | collective-permute-start | bytes 786440 | tf_op jit(solution)/shard_map/ppermute | solution.py:743
  12.8 10.2 %collective-permute-start.4 = (bf16[1168,128]{1,0:T(8,128)(2,1)S(1)}, bf16[1168,128]{1,0:T(8,128)(2,1)S(1)}, u32[]{:S(2)}, u32[]{:S(2)}) collective-permute-start(bf16[1168,128]{1,0:T(8,128)(2,1)S(1)} %collective-permute-done.partner), channel_id=1, source_target_pairs={{0,2},{1,3},{2,4},{3,5},{4,6},{5,7},{6,0},{7,1},{8,10},{9,11},{10,... | collective-permute-start | bytes 897032 | tf_op jit(solution)/shard_map/ppermute | solution.py:748
  14.7 6.8 %collective-permute-start.5 = (bf16[576,128]{1,0:T(8,128)(2,1)S(1)}, bf16[576,128]{1,0:T(8,128)(2,1)S(1)}, u32[]{:S(2)}, u32[]{:S(2)}) collective-permute-start(bf16[576,128]{1,0:T(8,128)(2,1)S(1)} %get-tuple-element.107), channel_id=1, source_target_pairs={{0,1},{1,0},{2,3},{3,2},{4,5},{5,4},{6,7},{7,6},{8,9},{9,8},{10,11... | collective-permute-start | bytes 442376 | tf_op jit(solution)/shard_map/ppermute | solution.py:743
  16.2 8.5 %collective-permute-start.6 = (bf16[128,1024]{1,0:T(8,128)(2,1)S(1)}, bf16[128,1024]{1,0:T(8,128)(2,1)S(1)}, u32[]{:S(2)}, u32[]{:S(2)}) collective-permute-start(bf16[128,1024]{1,0:T(8,128)(2,1)S(1)} %bitcast.12), channel_id=1, source_target_pairs={{0,1},{1,0},{2,3},{3,2},{4,5},{5,4},{6,7},{7,6},{8,9},{9,8},{10,11... | collective-permute-start | bytes 786440 | tf_op jit(solution)/shard_map/ppermute | solution.py:743
  16.8 16.5 %collective-permute-start.8 = (bf16[128,1024]{1,0:T(8,128)(2,1)S(1)}, bf16[128,1024]{1,0:T(8,128)(2,1)S(1)}, u32[]{:S(2)}, u32[]{:S(2)}) collective-permute-start(bf16[128,1024]{1,0:T(8,128)(2,1)S(1)} %collective-permute-done.3.refs_6_), channel_id=1, source_target_pairs={{0,8},{8,0},{16,24},{24,16},{1,9},{9,1},{17,25},{25,17},{2,10},{10... | collective-permute-start | bytes 786440 | tf_op jit(solution)/shard_map/ppermute | solution.py:743
  16.8 16.5 %collective-permute-start.7 = (bf16[1152,128]{1,0:T(8,128)(2,1)S(1)}, bf16[1152,128]{1,0:T(8,128)(2,1)S(1)}, u32[]{:S(2)}, u32[]{:S(2)}) collective-permute-start(bf16[1152,128]{1,0:T(8,128)(2,1)S(1)} %get-tuple-element.111.both_own), channel_id=1, source_target_pairs={{2,0},{3,1},{4,2},{5,3},{6,4},{7,5},{10,8},{11,9},{12,10},{13,11},... | collective-permute-start | bytes 884744 | tf_op jit(solution)/shard_map/ppermute | solution.py:756
  24.7 9.3 %collective-permute-start.10 = (bf16[128,1024]{1,0:T(8,128)(2,1)S(1)}, bf16[128,1024]{1,0:T(8,128)(2,1)S(1)}, u32[]{:S(2)}, u32[]{:S(2)}) collective-permute-start(bf16[128,1024]{1,0:T(8,128)(2,1)S(1)} %collective-permute-done.6.cotangent.refs_4_), channel_id=1, source_target_pairs={{0,16},{8,24},{16,0},{24,8},{1,17},{9,25},{17,1},{25,9},{2,18},{10... | collective-permute-start | bytes 786440 | tf_op jit(solution)/shard_map/ppermute | solution.py:743
  26.2 8.9 %collective-permute-start.9 = (bf16[128,1024]{1,0:T(8,128)(2,1)S(1)}, bf16[128,1024]{1,0:T(8,128)(2,1)S(1)}, u32[]{:S(2)}, u32[]{:S(2)}) collective-permute-start(bf16[128,1024]{1,0:T(8,128)(2,1)S(1)} %collective-permute-done.6.cotangent.refs_4_), channel_id=1, source_target_pairs={{0,8},{8,0},{16,24},{24,16},{1,9},{9,1},{17,25},{25,17},{2,10},{10... | collective-permute-start | bytes 786440 | tf_op jit(solution)/shard_map/ppermute | solution.py:743
  30.9 12.6 %collective-permute-start.15 = (bf16[1296,128]{1,0:T(8,128)(2,1)S(1)}, bf16[1296,128]{1,0:T(8,128)(2,1)S(1)}, u32[]{:S(2)}, u32[]{:S(2)}) collective-permute-start(bf16[1296,128]{1,0:T(8,128)(2,1)S(1)} %get-tuple-element.120.both_partner), channel_id=1, source_target_pairs={{0,6},{1,7},{2,0},{3,1},{4,2},{5,3},{6,4},{7,5},{8,14},{9,15},{10,... | collective-permute-start | bytes 995336 | tf_op jit(solution)/shard_map/ppermute | solution.py:748
  33.3 5.6 %collective-permute-start.11 = (bf16[144,256]{1,0:T(8,128)(2,1)S(1)}, bf16[144,256]{1,0:T(8,128)(2,1)S(1)}, u32[]{:S(2)}, u32[]{:S(2)}) collective-permute-start(bf16[144,256]{1,0:T(8,128)(2,1)S(1)} %get-tuple-element.137), channel_id=1, source_target_pairs={{0,8},{8,0},{16,24},{24,16},{1,9},{9,1},{17,25},{25,17},{2,10},{10... | collective-permute-start | bytes 221192 | tf_op jit(solution)/shard_map/ppermute | solution.py:743
  33.5 5.4 %collective-permute-start.12 = (bf16[144,256]{1,0:T(8,128)(2,1)S(1)}, bf16[144,256]{1,0:T(8,128)(2,1)S(1)}, u32[]{:S(2)}, u32[]{:S(2)}) collective-permute-start(bf16[144,256]{1,0:T(8,128)(2,1)S(1)} %get-tuple-element.138), channel_id=1, source_target_pairs={{0,16},{8,24},{16,0},{24,8},{1,17},{9,25},{17,1},{25,9},{2,18},{10... | collective-permute-start | bytes 221192 | tf_op jit(solution)/shard_map/ppermute | solution.py:743
  34.0 4.9 %collective-permute-start.13 = (bf16[144,256]{1,0:T(8,128)(2,1)S(1)}, bf16[144,256]{1,0:T(8,128)(2,1)S(1)}, u32[]{:S(2)}, u32[]{:S(2)}) collective-permute-start(bf16[144,256]{1,0:T(8,128)(2,1)S(1)} %get-tuple-element.139), channel_id=1, source_target_pairs={{0,24},{8,16},{16,8},{24,0},{1,25},{9,17},{17,9},{25,1},{2,26},{10... | collective-permute-start | bytes 221192 | tf_op jit(solution)/shard_map/ppermute | solution.py:743
  35.1 5.6 %collective-permute-start.14 = (bf16[128,1024]{1,0:T(8,128)(2,1)S(1)}, bf16[128,1024]{1,0:T(8,128)(2,1)S(1)}, u32[]{:S(2)}, u32[]{:S(2)}) collective-permute-start(bf16[128,1024]{1,0:T(8,128)(2,1)S(1)} %collective-permute-done.10.refs_6_), channel_id=1, source_target_pairs={{0,8},{8,0},{16,24},{24,16},{1,9},{9,1},{17,25},{25,17},{2,10},{10... | collective-permute-start | bytes 786440 | tf_op jit(solution)/shard_map/ppermute | solution.py:743
  38.9 10.2 %collective-permute-start.16 = (bf16[576,256]{1,0:T(8,128)(2,1)S(1)}, bf16[576,256]{1,0:T(8,128)(2,1)S(1)}, u32[]{:S(2)}, u32[]{:S(2)}) collective-permute-start(bf16[576,256]{1,0:T(8,128)(2,1)S(1)} %get-tuple-element.165), channel_id=1, source_target_pairs={{0,1},{1,0},{2,3},{3,2},{4,5},{5,4},{6,7},{7,6},{8,9},{9,8},{10,11... | collective-permute-start | bytes 884744 | tf_op jit(solution)/shard_map/ppermute | solution.py:743
  41.1 8.0 %collective-permute-start.17 = (bf16[144,256]{1,0:T(8,128)(2,1)S(1)}, bf16[144,256]{1,0:T(8,128)(2,1)S(1)}, u32[]{:S(2)}, u32[]{:S(2)}) collective-permute-start(bf16[144,256]{1,0:T(8,128)(2,1)S(1)} %get-tuple-element.166), channel_id=1, source_target_pairs={{0,2},{1,3},{2,0},{3,1},{4,6},{5,7},{6,4},{7,5},{8,10},{9,11},{10,... | collective-permute-start | bytes 221192 | tf_op jit(solution)/shard_map/ppermute | solution.py:743
  41.2 9.2 %collective-permute-start.18 = (bf16[144,256]{1,0:T(8,128)(2,1)S(1)}, bf16[144,256]{1,0:T(8,128)(2,1)S(1)}, u32[]{:S(2)}, u32[]{:S(2)}) collective-permute-start(bf16[144,256]{1,0:T(8,128)(2,1)S(1)} %get-tuple-element.167), channel_id=1, source_target_pairs={{0,4},{1,5},{2,6},{3,7},{4,0},{5,1},{6,2},{7,3},{8,12},{9,13},{10,... | collective-permute-start | bytes 221192 | tf_op jit(solution)/shard_map/ppermute | solution.py:743
  43.5 6.9 %collective-permute-start.19 = (bf16[144,256]{1,0:T(8,128)(2,1)S(1)}, bf16[144,256]{1,0:T(8,128)(2,1)S(1)}, u32[]{:S(2)}, u32[]{:S(2)}) collective-permute-start(bf16[144,256]{1,0:T(8,128)(2,1)S(1)} %get-tuple-element.168), channel_id=1, source_target_pairs={{0,6},{1,7},{2,4},{3,5},{4,2},{5,3},{6,0},{7,1},{8,14},{9,15},{10,... | collective-permute-start | bytes 221192 | tf_op jit(solution)/shard_map/ppermute | solution.py:743
  47.9 9.0 %collective-permute-start.20 = (bf16[1152,128]{1,0:T(8,128)(2,1)S(1)}, bf16[1152,128]{1,0:T(8,128)(2,1)S(1)}, u32[]{:S(2)}, u32[]{:S(2)}) collective-permute-start(bf16[1152,128]{1,0:T(8,128)(2,1)S(1)} %get-tuple-element.176), channel_id=1, source_target_pairs={{0,1},{1,0},{2,3},{3,2},{4,5},{5,4},{6,7},{7,6},{8,9},{9,8},{10,11... | collective-permute-start | bytes 884744 | tf_op jit(solution)/shard_map/ppermute | solution.py:743
  50.5 7.3 %collective-permute-start.21 = (bf16[144,128]{1,0:T(8,128)(2,1)S(1)}, bf16[144,128]{1,0:T(8,128)(2,1)S(1)}, u32[]{:S(2)}, u32[]{:S(2)}) collective-permute-start(bf16[144,128]{1,0:T(8,128)(2,1)S(1)} %get-tuple-element.183), channel_id=1, source_target_pairs={{0,0},{1,16},{2,2},{3,18},{4,4},{5,20},{6,6},{7,22},{8,1},{9,17},{... | collective-permute-start | bytes 110600 | tf_op jit(solution)/shard_map/ppermute | solution.py:768
  51.2 6.7 %collective-permute-start.22 = (bf16[144,128]{1,0:T(8,128)(2,1)S(1)}, bf16[144,128]{1,0:T(8,128)(2,1)S(1)}, u32[]{:S(2)}, u32[]{:S(2)}) collective-permute-start(bf16[144,128]{1,0:T(8,128)(2,1)S(1)} %get-tuple-element.184), channel_id=1, source_target_pairs={{0,1},{1,17},{2,3},{3,19},{4,5},{5,21},{6,7},{7,23},{8,0},{9,16},{... | collective-permute-start | bytes 110600 | tf_op jit(solution)/shard_map/ppermute | solution.py:768

commit v4 on v3

--- a/solution.py
+++ b/solution.py
@@ -29,6 +29,7 @@
 COST_GATHER = 2_000_000_000
 COST_KEYS = 1_000_000
 COST_FIRST = 2_000_000_000
+COST_NEXT = 4_000_000_000
 COST_SUM = 2_000_000_000
 VMEM_LIMIT = 24 * 1024 * 1024
 
@@ -36,7 +37,6 @@
 bf16 = jnp.bfloat16
 f32 = jnp.float32
 
-SMEM = pl.BlockSpec(memory_space=pltpu.SMEM)
 VMEM = pl.BlockSpec(memory_space=pltpu.VMEM)
 HBM = pl.BlockSpec(memory_space=pltpu.HBM)
 
@@ -117,10 +117,10 @@
     copies = [pltpu.make_async_copy(a, b, sems.at[n]) for n, (a, b) in enumerate(pairs)]
     for copy in copies:
         copy.start()
-    clip_rows = jnp.full((CLIP_ROWS, PAIR), clip[0, 0].astype(f32), f32).astype(bf16)
     shared = slice(SHARED, SHARED + PAIR)
     for copy in copies:
         copy.wait()
+    clip_rows = jnp.broadcast_to(clip[...].astype(f32), (CLIP_ROWS, PAIR)).astype(bf16)
     for side, target in ((1 - half, swap_kv), (half, own_kv)):
         for pair in range(PAIRS):
             target[rows_of(pair)] = key_all[:, columns_of(side, pair)]
@@ -148,7 +148,7 @@
     return kernel(
         pack_kernel,
         "pack",
-        [SMEM, HBM, HBM, HBM],
+        [VMEM, HBM, HBM, HBM],
         [shaped((ROWS + CLIP_ROWS, PAIR), bf16)] * 2
         + [shaped((HALF, PAIR), bf16), shaped((SHARED + PAIR, PAIR), bf16)],
         [
@@ -346,6 +346,15 @@
     )(*sources)
 
 
+def staggered(items, *stages):
+    values = [None] * len(items)
+    for step in range(len(items) + len(stages) - 1):
+        for number, stage in enumerate(stages):
+            index = step - number
+            if 0 <= index < len(items):
+                values[index] = stage(*items[index], values[index])
+
+
 def forward_kernel(
     pieces_wanted,
     keys_all,
@@ -371,25 +380,34 @@
         totals[row : row + 1, lanes] = maximum + jnp.log(total)
         return (powers * (1.0 / total)).astype(bf16)
 
-    for pair in range(PAIRS):
-        for query_block in range(2):
-            keys = slice(query_block * BLOCK, query_block * BLOCK + WIN + BLOCK)
-            steps = rows_of(query_block)
-            query_rows = doubled(query_all[pair, steps], SCALING)
-            scores = times(keys_all[pair, keys], query_rows, ((1,), (1,)))
-            weights = softmax(hidden(scores, mask[query_block]), 2 * pair + query_block)
+    def keys_of(query_block):
+        return slice(query_block * BLOCK, query_block * BLOCK + WIN + BLOCK)
+
+    def score(pair, query_block, _):
+        rows = query_all[pair, rows_of(query_block)]
+        if pair < PAIRS:
+            key_rows, rows = keys_all[pair, keys_of(query_block)], doubled(rows, SCALING)
+        else:
+            key_rows = keys_all[MIXED, keys_of(query_block)]
+            rows = rows * low_or_high(SCALING, 0.0).astype(bf16)
+        return times(key_rows, rows, ((1,), (1,)))
+
+    def weigh(pair, query_block, scores):
+        return softmax(hidden(scores, mask[query_block]), 2 * pair + query_block)
+
+    def mix(pair, query_block, weights):
+        steps = rows_of(query_block)
+        if pair < PAIRS:
             weights_out[pair, query_block] = weights
-            mixed = times(keys_all[PAIRS + pair, keys], weights, ((0,), (0,)))
+            mixed = times(keys_all[PAIRS + pair, keys_of(query_block)], weights, ((0,), (0,)))
             att[head_rows(half, pair), steps] = diagonal(mixed).astype(bf16)
-    for query_block in range(2):
-        keys = slice(query_block * BLOCK, query_block * BLOCK + WIN + BLOCK)
-        steps = rows_of(query_block)
-        query_rows = query_all[PAIRS, steps] * low_or_high(SCALING, 0.0).astype(bf16)
-        scores = times(keys_all[MIXED, keys], query_rows, ((1,), (1,)))
-        weights = softmax(hidden(scores, mask[query_block]), 2 * PAIRS + query_block)
-        single_out[query_block] = weights
-        mixed = times(keys_all[MIXED, keys], weights, ((0,), (0,)))
-        att[single_rows(half), steps] = mixed[HDIM:].astype(bf16)
+        else:
+            single_out[query_block] = weights
+            mixed = times(keys_all[MIXED, keys_of(query_block)], weights, ((0,), (0,)))
+            att[single_rows(half), steps] = mixed[HDIM:].astype(bf16)
+
+    items = [(pair, query_block) for pair in range(PAIRS + 1) for query_block in range(2)]
+    staggered(items, score, weigh, mix)
 
     att_own[...] = att[:, at(half, BLOCK)]
     att_swap[...] = att[:, at(1 - half, BLOCK)]
@@ -416,11 +434,6 @@
         ]
         + [shaped(piece, bf16)] * pieces_wanted,
     )(*sources)
-
-
-def score_gradients(weights, values, d_rows, delta):
-    d_weights = times(values, d_rows, ((1,), (1,)))
-    return (weights.astype(f32) * (d_weights - delta)).astype(bf16)
 
 
 def own_kernel(
@@ -451,36 +464,47 @@
         else:
             grads[block, :BLOCK] += value
 
-    for query_block in (1, 0):
-        keys = slice(query_block * BLOCK, query_block * BLOCK + WIN + BLOCK)
-        mine = slice(WIN - query_block * BLOCK, WIN + BLOCK)
+    def keys_of(query_block):
+        return slice(query_block * BLOCK, query_block * BLOCK + WIN + BLOCK)
+
+    def operands(pair, query_block):
         steps = rows_of(query_block)
-        for pair in range(PAIRS):
+        if pair < PAIRS:
             query_rows = doubled(query_all[pair, steps], SCALING)
-            d_rows = doubled(query_all[PAIRS + pair, steps])
-            weights = weights_in[pair, query_block]
-            d_scores = score_gradients(
-                weights,
-                keys_all[PAIRS + pair, keys],
-                d_rows,
-                delta_of(2 * pair + query_block, 2 * BLOCK),
-            )
-            dq = diagonal(times(keys_all[pair, keys], d_scores, ((0,), (0,))))
-            dq_all[head_rows(half, pair), steps] = (dq * SCALING).astype(bf16)
-            accumulate(pair, query_block, times(d_scores[mine], query_rows, ((1,), (0,))))
-            accumulate(PAIRS + pair, query_block, times(weights[mine], d_rows, ((1,), (0,))))
+            return query_rows, doubled(query_all[PAIRS + pair, steps]), weights_in[pair, query_block]
         rows = query_all[MIXED, steps]
         query_rows = rows * low_or_high(SCALING, 0.0).astype(bf16)
         d_rows = rows * low_or_high(0.0, 1.0).astype(bf16)
-        weights = single_in[query_block]
-        mixed = keys_all[MIXED, keys]
-        d_scores = score_gradients(
-            weights, mixed, d_rows, delta_of(2 * PAIRS + query_block, BLOCK)
-        )
-        dq = times(mixed, d_scores, ((0,), (0,)))[:HDIM]
-        dq_all[single_rows(half), steps] = (dq * SCALING).astype(bf16)
-        value = times(d_scores[mine], query_rows, ((1,), (0,)))
-        accumulate(MIXED, query_block, value + times(weights[mine], d_rows, ((1,), (0,))))
+        return query_rows, d_rows, single_in[query_block]
+
+    def d_weights_of(pair, query_block, _):
+        block = PAIRS + pair if pair < PAIRS else MIXED
+        _, d_rows, _ = operands(pair, query_block)
+        return times(keys_all[block, keys_of(query_block)], d_rows, ((1,), (1,)))
+
+    def d_scores_of(pair, query_block, d_weights):
+        _, _, weights = operands(pair, query_block)
+        delta = delta_of(2 * pair + query_block, d_weights.shape[1])
+        return (weights.astype(f32) * (d_weights - delta)).astype(bf16)
+
+    def products(pair, query_block, d_scores):
+        query_rows, d_rows, weights = operands(pair, query_block)
+        mine = slice(WIN - query_block * BLOCK, WIN + BLOCK)
+        steps = rows_of(query_block)
+        block = pair if pair < PAIRS else MIXED
+        dq = times(keys_all[block, keys_of(query_block)], d_scores, ((0,), (0,)))
+        dk = times(d_scores[mine], query_rows, ((1,), (0,)))
+        dv = times(weights[mine], d_rows, ((1,), (0,)))
+        if pair < PAIRS:
+            dq_all[head_rows(half, pair), steps] = (diagonal(dq) * SCALING).astype(bf16)
+            accumulate(pair, query_block, dk)
+            accumulate(PAIRS + pair, query_block, dv)
+        else:
+            dq_all[single_rows(half), steps] = (dq[:HDIM] * SCALING).astype(bf16)
+            accumulate(MIXED, query_block, dk + dv)
+
+    items = [(pair, query_block) for pair in range(PAIRS + 1) for query_block in (1, 0)]
+    staggered(items, d_weights_of, d_scores_of, products)
     dq_own[...] = dq_all[:, at(half, BLOCK)]
     swap[:, :BLOCK] = att_swap[...]
     swap[:, BLOCK:] = dq_all[:, at(1 - half, BLOCK)]
@@ -538,32 +562,45 @@
         same = jnp.where(key_clip == query_clip, 1.0, 0.0)
         mask[query_block, rows_of(block)] = shape * same * present
 
-    for query_block in range(2):
+    def operands(pair, query_block):
+        steps = rows_of(query_block)
+        if pair < PAIRS:
+            query_rows = doubled(query_all[pair, steps], SCALING)
+            return query_rows, doubled(query_all[PAIRS + pair, steps])
+        rows = query_all[MIXED, steps]
+        query_rows = rows * low_or_high(SCALING, 0.0).astype(bf16)
+        return query_rows, rows * low_or_high(0.0, 1.0).astype(bf16)
+
+    def score(pair, query_block, _):
         keys = slice(query_block * BLOCK, WIN)
-        steps = rows_of(query_block)
-        visible = mask[query_block, keys]
-        for pair in range(PAIRS + 1):
-            row = 2 * pair + query_block
-            lanes = slice(0, 2 * BLOCK if pair < PAIRS else BLOCK)
-            if pair < PAIRS:
-                key_rows, value_rows = keys_all[pair, keys], keys_all[PAIRS + pair, keys]
-                query_rows = doubled(query_all[pair, steps], SCALING)
-                d_rows = doubled(query_all[PAIRS + pair, steps])
-            else:
-                key_rows = value_rows = keys_all[MIXED, keys]
-                query_rows = query_all[MIXED, steps] * low_or_high(SCALING, 0.0).astype(bf16)
-                d_rows = query_all[MIXED, steps] * low_or_high(0.0, 1.0).astype(bf16)
-            scores = hidden(times(key_rows, query_rows, ((1,), (1,))), visible)
-            weights = jnp.exp(scores - stats[row : row + 1, lanes]).astype(bf16)
-            delta = stats[DELTA_STAT + row : DELTA_STAT + row + 1, lanes]
-            d_scores = score_gradients(weights, value_rows, d_rows, delta)
-            dk = times(d_scores, query_rows, ((1,), (0,)))
-            dv = times(weights, d_rows, ((1,), (0,)))
-            if pair < PAIRS:
-                grads[pair, keys] += dk
-                grads[PAIRS + pair, keys] += dv
-            else:
-                grads[MIXED, keys] += dk + dv
+        query_rows, d_rows = operands(pair, query_block)
+        key_block, value_block = (pair, PAIRS + pair) if pair < PAIRS else (MIXED, MIXED)
+        scores = times(keys_all[key_block, keys], query_rows, ((1,), (1,)))
+        return scores, times(keys_all[value_block, keys], d_rows, ((1,), (1,)))
+
+    def weigh(pair, query_block, values):
+        scores, d_weights = values
+        row = 2 * pair + query_block
+        lanes = slice(0, scores.shape[1])
+        scores = hidden(scores, mask[query_block, query_block * BLOCK : WIN])
+        weights = jnp.exp(scores - stats[row : row + 1, lanes]).astype(bf16)
+        delta = stats[DELTA_STAT + row : DELTA_STAT + row + 1, lanes]
+        return weights, (weights.astype(f32) * (d_weights - delta)).astype(bf16)
+
+    def products(pair, query_block, values):
+        weights, d_scores = values
+        keys = slice(query_block * BLOCK, WIN)
+        query_rows, d_rows = operands(pair, query_block)
+        dk = times(d_scores, query_rows, ((1,), (0,)))
+        dv = times(weights, d_rows, ((1,), (0,)))
+        if pair < PAIRS:
+            grads[pair, keys] += dk
+            grads[PAIRS + pair, keys] += dv
+        else:
+            grads[MIXED, keys] += dk + dv
+
+    items = [(pair, query_block) for pair in range(PAIRS + 1) for query_block in range(2)]
+    staggered(items, score, weigh, products)
     for block in range(MIXED + 1):
         mine[rows_of(block)] = grads[block, at(half, BLOCK)].astype(bf16)
         swap[rows_of(block)] = grads[block, at(1 - half, BLOCK)].astype(bf16)
@@ -583,6 +620,7 @@
             pltpu.VMEM((2 * CLIP_ROWS, PAIR), bf16),
             pltpu.VMEM((STAT_ROWS, 2 * BLOCK), f32),
         ],
+        flops=COST_NEXT,
     )(*sources)
 
 
@@ -634,12 +672,17 @@
     )(*sources)
 
 
-def place_kernel(dq_mine, received, first, second, query_out, weight_out, dq_all, query, both, sems):
+def place_kernel(dq_mine, received, stays, first, second, query_out, weight_out, dq_all, query, both, sems):
     half = my_half()
     rows = first.shape[0]
     moves = [(both, weight_out), (query, query_out)]
     copies = [pltpu.make_async_copy(a, b, sems.at[n]) for n, (a, b) in enumerate(moves)]
     both[span(half * rows, rows, 16)] = first[...].astype(f32)
+
+    @pl.when(lax.axis_index("dp") == 3 * half)
+    def _():
+        both[span(half * rows, rows, 16)] = stays[...].astype(f32)
+
     both[span((1 - half) * rows, rows, 16)] = second[...].astype(f32)
     copies[0].start()
     dq_all[at(half, HALF)] = dq_mine[...]
@@ -656,7 +699,7 @@
     query, weight = kernel(
         place_kernel,
         "place",
-        [VMEM] * 4,
+        [VMEM] * 5,
         [shaped((BLOCK, WIDTH), bf16), shaped((2 * rows, lanes), f32)],
         [
             pltpu.VMEM((WIDTH, BLOCK), bf16),
@@ -764,6 +807,8 @@
             group, half = index // 2, index % 2
             target_half = (source % 2) ^ flip
             target = 2 * half + source // 2
+            if (target, target_half) == (source, half):
+                target, target_half = 3 - target, 1 - target_half
             moves.append((source * lanes + index, target * lanes + 2 * group + target_half))
     return lax.ppermute(value, ("dp", "ctx"), moves)
 
@@ -789,35 +834,31 @@
     if short:
         cots += [swapped(cot_early, "dp", n) for n in (1, 2)]
 
-    partner, both_own, swap_query = after(partner, both_own, swap_query)
+    partner, both_own, swap_query, cot_late = after(partner, both_own, swap_query, cotangent)
+    cot_partner = swapped(cot_late, "ctx", 1)
     halo_other = rotated(partner, "ctx", 2)
     query_partner = swapped(swap_query, "ctx", 1)
-    halo, both_own, cot_late, *cots = after(halo, both_own, cotangent, *cots)
-    cot_partner = swapped(cot_late, "ctx", 1)
+    halo, both_own, *cots = after(halo, both_own, *cots)
     next_own = moved(both_own, "ctx", -2)
     if short:
         cots.append(swapped(cots[2], "dp", 1))
     keys_all, query_all, mask, clip_row = gathered(
         own, partner, halo, halo_other, query, query_partner
     )
-    keys_all, cot_partner = after(keys_all, cot_partner)
-
-    later = [cot_partner]
-    if short:
-        later += [swapped(cot_partner, "dp", n) for n in (1, 2)]
     weights, single, totals, att, att_own, att_swap, *pieces = forward(
         4 if short else 0, keys_all, query_all, mask, clip_row
     )
-    weights, next_own, *rest = after(weights, next_own, *pieces, *cots)
+    if short:
+        cot_across = swapped(cot_partner, "dp", 2)
+    weights, cot_partner, *rest = after(weights, cot_partner, *pieces, *cots)
     pieces, cots = rest[: len(pieces)], rest[len(pieces) :]
 
     if short:
         pieces[1:] = [swapped(pieces[n], "dp", n) for n in (1, 2, 3)]
-        weights, *later = after(weights, *later)
-        later.append(swapped(later[2], "dp", 1))
     both_partner, stats = cotangents(
         cot_partner, weight, query_partner, att, d_turned_own, totals
     )
+    both_partner, next_own = after(both_partner, next_own)
     next_partner = rotated(both_partner, "ctx", -2)
     dq_own, swap, own_grads, partner_grads = own_gradients(
         keys_all, both_own, both_partner, weights, single, stats, att_swap
@@ -825,10 +866,12 @@
     own_grads, swap, *pieces = after(own_grads, swap, *pieces)
 
     if short:
+        own_grads, cot_partner, cot_across = after(own_grads, cot_partner, cot_across)
+        later = [cot_partner, swapped(cot_partner, "dp", 1), cot_across]
+        later.append(swapped(cot_across, "dp", 1))
         products = weight_products(pieces, cots)
         products, *later = after(products, *later)
         kept, *sent = weight_rest(products, pieces, later, groups)
-        sent[-1], next_partner = after(sent[-1], next_partner)
         arrived = [swapped(part, "ctx", 2 * (n + 1)) for n, part in enumerate(sent)]
         kept, own_grads = after(kept, own_grads)
     received = swapped(swap, "ctx", 1)
@@ -836,11 +879,12 @@
         groups, own, partner, next_own, next_partner, own_grads, partner_grads
     )
     kv_rest = swapped(kv_swap, "ctx", 1)
+    kv_own, received = after(kv_own, received)
+    sublayer_out, att_full = output_rows(att_own, received, weight)
     if short:
-        kept, kv_own, received, *arrived = after(kept, kv_own, received, *arrived)
-        first, second = weight_sum(kept, arrived)
-        first, second = placed(first, 0), placed(second, 1)
-    sublayer_out, att_full = output_rows(att_own, received, weight)
+        kept, kv_own, sublayer_out, *arrived = after(kept, kv_own, sublayer_out, *arrived)
+        stays, second = weight_sum(kept, arrived)
+        first, second = placed(stays, 0), placed(second, 1)
     if not short:
         product = lax.dot_general(
             cotangent, att_full, (((0,), (1,)), ((), ())), preferred_element_type=f32
@@ -849,11 +893,10 @@
         weight_grad = lax.psum_scatter(
             sequence_grad.astype(f32), "dp", scatter_dimension=1, tiled=True
         )
-        first = second = jnp.zeros((16, 128), bf16)
-    kv_own, sublayer_out = after(kv_own, sublayer_out)
+        stays = first = second = jnp.zeros((16, 128), bf16)
     key_grad, value_grad = place_keys(kv_own, kv_rest)
     dq_own, key_grad = after(dq_own, key_grad)
-    query_grad, placed_weight = place(dq_own, received, first, second)
+    query_grad, placed_weight = place(dq_own, received, stays, first, second)
     if short:
         weight_grad = placed_weight
     return (

time: 59 us -> 53.6 us (0.908)
  Pallas kernels: 18.2 us -> 14.4 us
  starting transfers between devices: 29 us -> 27.9 us
  waiting for transfers between devices: 10.1 us -> 9.5 us
    pallas_call x1, Pallas kernels: 3.97 us -> 2 us  [forward(): kernel(functools.partial(forward_kernel, pieces_wanted), 'forward', [VMEM...]
    ppermute x2, starting transfers between devices: 4.28 us -> 3.04 us  [placed(): return lax.ppermute(value, ('dp', 'ctx'), moves)]
    pallas_call x1, Pallas kernels: 3.19 us -> 1.96 us  [own_gradients(): kernel(own_kernel, 'own_gradients', [VMEM] * 7, [shaped((HALF, BLOCK), bf...]
    ppermute x3, waiting for transfers between devices: 1.58 us -> 0.73 us  [rotated(): lax.ppermute(value, axis, [(source, (source + steps) % count) for source...]
  transfers between devices with their start and end apart: 23 -> 23, of which waited for: 6 -> 7; matrix products, arithmetic and copies ran while one was open for 0% -> 0% of each run, Pallas kernels for 27% -> 23%
where the time goes in v4:
time: 53.6 us; the launch traced here: 53.4 us
  starting transfers between devices  27.9 us (52%)
  Pallas kernels  14.4 us (27%)
  waiting for transfers between devices  9.5 us (18%)
  between operations  1.51 us (3%)
    ppermute x17, starting transfers between devices, swapped(): lax.ppermute(value, axis, [(source, source ^ bits) for source in range(co...  17.9 us
    ppermute x17, waiting for transfers between devices, swapped(): lax.ppermute(value, axis, [(source, source ^ bits) for source in range(co...  8.66 us
    ppermute x3, starting transfers between devices, rotated(): lax.ppermute(value, axis, [(source, (source + steps) % count) for source...  5.67 us
    ppermute x2, starting transfers between devices, placed(): return lax.ppermute(value, ('dp', 'ctx'), moves)  3.04 us
    pallas_call x1, Pallas kernels, own_cotangents(): kernel(own_cotangent_kernel, 'own_cotangents', [HBM, HBM, VMEM], [shaped(...  2.24 us
    pallas_call x1, Pallas kernels, forward(): kernel(functools.partial(forward_kernel, pieces_wanted), 'forward', [VMEM...  2 us
    pallas_call x1, Pallas kernels, own_gradients(): kernel(own_kernel, 'own_gradients', [VMEM] * 7, [shaped((HALF, BLOCK), bf...  1.96 us
    pallas_call x1, Pallas kernels, next_gradients(): kernel(functools.partial(next_kernel, groups), 'next_gradients', [VMEM] *...  1.67 us
  transfers between devices with their start and end apart: 23, of which 7 were waited for; matrix products, arithmetic and copies ran while one was open for 0% of the time, Pallas kernels for 23%

profile of v4, /device:TPU:0, one launch (start us, length us, event | category | flops | bytes accessed | tf_op | source)
XLA Modules:
  0.0 53.4 jit_solution(8564157485410744624)
XLA Ops:
  1.3 1.4 %pack.1 = (bf16[1168,128]{1,0:T(8,128)(2,1)S(1)}, bf16[1168,128]{1,0:T(8,128)(2,1)S(1)}, bf16[576,128]{1,0:T(8,128)(2,1)S(1)}, bf16[640,128]{1,0:T(8,128)(2,1)S(1)}) custom-call(s32[1,1]{1,0:T(1,128)S(6)} %copy.11.clip, bf16[128,1152]{1,0:T(8,128)(2,1)} %bitcast.14, bf16[128,1152]{1,0:T(8,128)(2,1)} %bitcast.15, bf16[128,1152]{1,0:T(8,128)(2,1)} %bitcast.16), custom_call_target="tpu_custom_call" | custom-call | flops 1000000 | bytes 10000 | tf_op jit(solution)/shard_map/pack/pallas_call | solution.py:148
  2.7 3.0 %collective-permute-start = (bf16[1168,128]{1,0:T(8,128)(2,1)S(1)}, bf16[1168,128]{1,0:T(8,128)(2,1)S(1)}, u32[]{:S(2)}, u32[]{:S(2)}) collective-permute-start(bf16[1168,128]{1,0:T(8,128)(2,1)S(1)} %get-tuple-element.96), channel_id=1, source_target_pairs={{0,1},{1,0},{2,3},{3,2},{4,5},{5,4},{6,7},{7,6},{8,9},{9,8},{10,11... | collective-permute-start | bytes 897032 | tf_op jit(solution)/shard_map/ppermute | solution.py:786
  5.7 1.6 %collective-permute-start.1 = (bf16[1168,128]{1,0:T(8,128)(2,1)S(1)}, bf16[1168,128]{1,0:T(8,128)(2,1)S(1)}, u32[]{:S(2)}, u32[]{:S(2)}) collective-permute-start(bf16[1168,128]{1,0:T(8,128)(2,1)S(1)} %get-tuple-element.94.own), channel_id=1, source_target_pairs={{0,2},{1,3},{2,4},{3,5},{4,6},{5,7},{6,0},{7,1},{8,10},{9,11},{10,... | collective-permute-start | bytes 897032 | tf_op jit(solution)/shard_map/ppermute | solution.py:791
  7.3 1.5 %collective-permute-start.3 = (bf16[128,1024]{1,0:T(8,128)(2,1)}, bf16[128,1024]{1,0:T(8,128)(2,1)S(1)}, u32[]{:S(2)}, u32[]{:S(2)}) collective-permute-start(bf16[128,1024]{1,0:T(8,128)(2,1)} %bitcast.10), channel_id=1, source_target_pairs={{0,16},{8,24},{16,0},{24,8},{1,17},{9,25},{17,1},{25,9},{2,18},{10... | collective-permute-start | bytes 786440 | tf_op jit(solution)/shard_map/ppermute | solution.py:786
  8.8 2.2 %own_cotangents.1 = (bf16[1152,128]{1,0:T(8,128)(2,1)S(1)}, bf16[576,128]{1,0:T(8,128)(2,1)S(1)}, bf16[1024,1152]{1,0:T(8,128)(2,1)S(1)}) custom-call(bf16[128,1024]{1,0:T(8,128)(2,1)} %bitcast.11, bf16[1024,1152]{1,0:T(8,128)(2,1)} %weight.1, bf16[640,128]{1,0:T(8,128)(2,1)S(1)} %get-tuple-element.97.query.query_own), custom_call_target="tpu_custom_call" | custom-call | flops 1000000 | bytes 10000 | tf_op jit(solution)/shard_map/own_cotangents/pallas_call | solution.py:207
  11.1 1.7 %collective-permute-done.partner = bf16[1168,128]{1,0:T(8,128)(2,1)S(1)} collective-permute-done((bf16[1168,128]{1,0:T(8,128)(2,1)S(1)}, bf16[1168,128]{1,0:T(8,128)(2,1)S(1)}, u32[]{:S(2)}, u32[]{:S(2)}) %collective-permute-start) | collective-permute-done | bytes 299040 | tf_op jit(solution)/shard_map/ppermute | solution.py:786
  12.8 1.8 %collective-permute-start.4 = (bf16[1168,128]{1,0:T(8,128)(2,1)S(1)}, bf16[1168,128]{1,0:T(8,128)(2,1)S(1)}, u32[]{:S(2)}, u32[]{:S(2)}) collective-permute-start(bf16[1168,128]{1,0:T(8,128)(2,1)S(1)} %collective-permute-done.partner), channel_id=1, source_target_pairs={{0,2},{1,3},{2,4},{3,5},{4,6},{5,7},{6,0},{7,1},{8,10},{9,11},{10,... | collective-permute-start | bytes 897032 | tf_op jit(solution)/shard_map/ppermute | solution.py:791
  14.7 1.5 %collective-permute-start.6 = (bf16[128,1024]{1,0:T(8,128)(2,1)S(1)}, bf16[128,1024]{1,0:T(8,128)(2,1)S(1)}, u32[]{:S(2)}, u32[]{:S(2)}) collective-permute-start(bf16[128,1024]{1,0:T(8,128)(2,1)S(1)} %bitcast.12), channel_id=1, source_target_pairs={{0,1},{1,0},{2,3},{3,2},{4,5},{5,4},{6,7},{7,6},{8,9},{9,8},{10,11... | collective-permute-start | bytes 786440 | tf_op jit(solution)/shard_map/ppermute | solution.py:786
  17.4 1.3 %collective-permute-start.8 = (bf16[1152,128]{1,0:T(8,128)(2,1)S(1)}, bf16[1152,128]{1,0:T(8,128)(2,1)S(1)}, u32[]{:S(2)}, u32[]{:S(2)}) collective-permute-start(bf16[1152,128]{1,0:T(8,128)(2,1)S(1)} %get-tuple-element.106.both_own), channel_id=1, source_target_pairs={{2,0},{3,1},{4,2},{5,3},{6,4},{7,5},{10,8},{11,9},{12,10},{13,11},... | collective-permute-start | bytes 884744 | tf_op jit(solution)/shard_map/ppermute | solution.py:799
  18.8 4.3 %collective-permute-done.6.cotangent.refs_4_ = bf16[128,1024]{1,0:T(8,128)(2,1)S(1)} collective-permute-done((bf16[128,1024]{1,0:T(8,128)(2,1)S(1)}, bf16[128,1024]{1,0:T(8,128)(2,1)S(1)}, u32[]{:S(2)}, u32[]{:S(2)}) %collective-permute-start.6) | collective-permute-done | bytes 262176 | tf_op jit(solution)/shard_map/ppermute | solution.py:786
  23.1 1.5 %collective-permute-start.12 = (bf16[128,1024]{1,0:T(8,128)(2,1)S(1)}, bf16[128,1024]{1,0:T(8,128)(2,1)S(1)}, u32[]{:S(2)}, u32[]{:S(2)}) collective-permute-start(bf16[128,1024]{1,0:T(8,128)(2,1)S(1)} %collective-permute-done.6.cotangent.refs_4_), channel_id=1, source_target_pairs={{0,16},{8,24},{16,0},{24,8},{1,17},{9,25},{17,1},{25,9},{2,18},{10... | collective-permute-start | bytes 786440 | tf_op jit(solution)/shard_map/ppermute | solution.py:786
  24.9 2.0 %forward.1 = (bf16[4,2,384,256]{3,2,1,0:T(8,128)(2,1)S(1)}, bf16[2,384,128]{2,1,0:T(8,128)(2,1)S(1)}, f32[24,256]{1,0:T(8,128)S(1)}, bf16[576,256]{1,0:T(8,128)(...) custom-call(bf16[9,512,128]{2,1,0:T(8,128)(2,1)S(1)} %get-tuple-elem, ...), custom_call_target="tpu_custom_call" | custom-call | flops 1000000 | bytes 10000 | tf_op jit(solution)/shard_map/forward/pallas_call | solution.py:423
  26.9 1.8 %collective-permute-start.10 = (bf16[144,256]{1,0:T(8,128)(2,1)S(1)}, bf16[144,256]{1,0:T(8,128)(2,1)S(1)}, u32[]{:S(2)}, u32[]{:S(2)}) collective-permute-start(bf16[144,256]{1,0:T(8,128)(2,1)S(1)} %get-tuple-element.134), channel_id=1, source_target_pairs={{0,16},{8,24},{16,0},{24,8},{1,17},{9,25},{17,1},{25,9},{2,18},{10... | collective-permute-start | bytes 221192 | tf_op jit(solution)/shard_map/ppermute | solution.py:786
  29.9 2.3 %collective-permute-start.15 = (bf16[1296,128]{1,0:T(8,128)(2,1)S(1)}, bf16[1296,128]{1,0:T(8,128)(2,1)S(1)}, u32[]{:S(2)}, u32[]{:S(2)}) collective-permute-start(bf16[1296,128]{1,0:T(8,128)(2,1)S(1)} %get-tuple-element.125.both_partner), channel_id=1, source_target_pairs={{0,6},{1,7},{2,0},{3,1},{4,2},{5,3},{6,4},{7,5},{8,14},{9,15},{10,... | collective-permute-start | bytes 995336 | tf_op jit(solution)/shard_map/ppermute | solution.py:791
  32.2 2.0 %own_gradients.1 = (bf16[576,128]{1,0:T(8,128)(2,1)S(1)}, bf16[576,256]{1,0:T(8,128)(2,1)S(1)}, f32[1152,128]{1,0:T(8,128)S(1)}, f32[1152,128]{1,0:T(8,128)S(1)}) custom-call(bf16[9,512,128]{2,1,0:T(8,128)(2,1)S(1)} %get-tuple-element.105.keys_all, bf16[1152,128]{1,0:T(8,128)(2,1)S(1)} %get-tuple-element.106.both_own, ...), custom_call_target="tpu_custom_call" | custom-call | flops 1000000 | bytes 10000 | tf_op jit(solution)/shard_map/own_gradients/pallas_call | solution.py:517
  34.7 1.4 %collective-permute-start.16 = (bf16[576,256]{1,0:T(8,128)(2,1)S(1)}, bf16[576,256]{1,0:T(8,128)(2,1)S(1)}, u32[]{:S(2)}, u32[]{:S(2)}) collective-permute-start(bf16[576,256]{1,0:T(8,128)(2,1)S(1)} %get-tuple-element.159), channel_id=1, source_target_pairs={{0,1},{1,0},{2,3},{3,2},{4,5},{5,4},{6,7},{7,6},{8,9},{9,8},{10,11... | collective-permute-start | bytes 884744 | tf_op jit(solution)/shard_map/ppermute | solution.py:786
  37.3 2.0 %collective-permute-start.18 = (bf16[144,256]{1,0:T(8,128)(2,1)S(1)}, bf16[144,256]{1,0:T(8,128)(2,1)S(1)}, u32[]{:S(2)}, u32[]{:S(2)}) collective-permute-start(bf16[144,256]{1,0:T(8,128)(2,1)S(1)} %get-tuple-element.165), channel_id=1, source_target_pairs={{0,4},{1,5},{2,6},{3,7},{4,0},{5,1},{6,2},{7,3},{8,12},{9,13},{10,... | collective-permute-start | bytes 221192 | tf_op jit(solution)/shard_map/ppermute | solution.py:786
  39.3 2.1 %collective-permute-start.19 = (bf16[144,256]{1,0:T(8,128)(2,1)S(1)}, bf16[144,256]{1,0:T(8,128)(2,1)S(1)}, u32[]{:S(2)}, u32[]{:S(2)}) collective-permute-start(bf16[144,256]{1,0:T(8,128)(2,1)S(1)} %get-tuple-element.166), channel_id=1, source_target_pairs={{0,6},{1,7},{2,4},{3,5},{4,2},{5,3},{6,0},{7,1},{8,14},{9,15},{10,... | collective-permute-start | bytes 221192 | tf_op jit(solution)/shard_map/ppermute | solution.py:786
  41.4 1.7 %next_gradients.1 = (bf16[1152,128]{1,0:T(8,128)(2,1)S(1)}, bf16[1152,128]{1,0:T(8,128)(2,1)S(1)}) custom-call(bf16[1168,128]{1,0:T(8,128)(2,1)S(1)} %get-tuple-element.94.own, bf16[1168,128]{1,0:T(8,128)(2,1)S(1)} %collective-permute-done.partner, bf16[1152,128]{1,0:T(8,128)(2,1)S(1)} %collective-permute-done.8.both_own, ...), custom_call_target="tpu_custom_call" | custom-call | flops 4000000000 | bytes 10000 | tf_op jit(solution)/shard_map/next_gradients/pallas_call | solution.py:610
  43.1 1.1 %collective-permute-start.20 = (bf16[1152,128]{1,0:T(8,128)(2,1)S(1)}, bf16[1152,128]{1,0:T(8,128)(2,1)S(1)}, u32[]{:S(2)}, u32[]{:S(2)}) collective-permute-start(bf16[1152,128]{1,0:T(8,128)(2,1)S(1)} %get-tuple-element.170), channel_id=1, source_target_pairs={{0,1},{1,0},{2,3},{3,2},{4,5},{5,4},{6,7},{7,6},{8,9},{9,8},{10,11... | collective-permute-start | bytes 884744 | tf_op jit(solution)/shard_map/ppermute | solution.py:786
  44.2 1.6 %output.1 = (bf16[128,1024]{1,0:T(8,128)(2,1)}, bf16[1152,128]{1,0:T(8,128)(2,1)}) custom-call(bf16[576,128]{1,0:T(8,128)(2,1)S(1)} %get-tuple-element.161.att_own, bf16[576,256]{1,0:T(8,128)(2,1)S(1)} %collective-permute-done.16.received, bf16[1024,1152]{1,0:T(8,128)(2,1)S(1)} %get-tuple-element.120.weight), custom_call_target="tpu_custom_call" | custom-call | flops 1000000 | bytes 10000 | tf_op jit(solution)/shard_map/output/pallas_call | solution.py:635
  47.4 2.1 %collective-permute-start.22 = (bf16[144,128]{1,0:T(8,128)(2,1)S(1)}, bf16[144,128]{1,0:T(8,128)(2,1)S(1)}, u32[]{:S(2)}, u32[]{:S(2)}) collective-permute-start(bf16[144,128]{1,0:T(8,128)(2,1)S(1)} %get-tuple-element.178), channel_id=1, source_target_pairs={{0,1},{1,17},{2,3},{3,19},{4,5},{5,21},{6,7},{7,23},{8,0},{9,16},{... | collective-permute-start | bytes 110600 | tf_op jit(solution)/shard_map/ppermute | solution.py:813
  49.5 1.9 %collective-permute-done.20.theirs = bf16[1152,128]{1,0:T(8,128)(2,1)S(1)} collective-permute-done((bf16[1152,128]{1,0:T(8,128)(2,1)S(1)}, bf16[1152,128]{1,0:T(8,128)(2,1)S(1)}, u32[]{:S(2)}, u32[]{:S(2)}) %collective-permute-start.20) | collective-permute-done | bytes 294944 | tf_op jit(solution)/shard_map/ppermute | solution.py:786
  51.4 1.0 %place_keys.1 = (bf16[128,1152]{1,0:T(8,128)(2,1)}, bf16[128,1152]{1,0:T(8,128)(2,1)}) custom-call(bf16[1152,128]{1,0:T(8,128)(2,1)S(1)} %get-tuple-element.169.mine, bf16[1152,128]{1,0:T(8,128)(2,1)S(1)} %collective-permute-done.20.theirs), custom_call_target="tpu_custom_call" | custom-call | flops 1000000 | bytes 10000 | tf_op jit(solution)/shard_map/place_keys/pallas_call | solution.py:664
  (37 shorter events, 7.0 us)
Async XLA Ops:
  0.6 14.0 %copy-start = (bf16[1,128,1024]{2,1,0:T(8,128)(2,1)S(1)}, bf16[1,128,1024]{2,1,0:T(8,128)(2,1)}, u32[]{:S(2)}) copy-start(bf16[1,128,1024]{2,1,0:T(8,128)(2,1)} %param.9) | copy-start | bytes 786436
  2.7 10.1 %collective-permute-start = (bf16[1168,128]{1,0:T(8,128)(2,1)S(1)}, bf16[1168,128]{1,0:T(8,128)(2,1)S(1)}, u32[]{:S(2)}, u32[]{:S(2)}) collective-permute-start(bf16[1168,128]{1,0:T(8,128)(2,1)S(1)} %get-tuple-element.96), channel_id=1, source_target_pairs={{0,1},{1,0},{2,3},{3,2},{4,5},{5,4},{6,7},{7,6},{8,9},{9,8},{10,11... | collective-permute-start | bytes 897032 | tf_op jit(solution)/shard_map/ppermute | solution.py:786
  5.7 10.4 %collective-permute-start.2 = (bf16[128,1024]{1,0:T(8,128)(2,1)}, bf16[128,1024]{1,0:T(8,128)(2,1)S(1)}, u32[]{:S(2)}, u32[]{:S(2)}) collective-permute-start(bf16[128,1024]{1,0:T(8,128)(2,1)} %bitcast.9), channel_id=1, source_target_pairs={{0,8},{8,0},{16,24},{24,16},{1,9},{9,1},{17,25},{25,17},{2,10},{10... | collective-permute-start | bytes 786440 | tf_op jit(solution)/shard_map/ppermute | solution.py:786
  5.7 11.7 %collective-permute-start.1 = (bf16[1168,128]{1,0:T(8,128)(2,1)S(1)}, bf16[1168,128]{1,0:T(8,128)(2,1)S(1)}, u32[]{:S(2)}, u32[]{:S(2)}) collective-permute-start(bf16[1168,128]{1,0:T(8,128)(2,1)S(1)} %get-tuple-element.94.own), channel_id=1, source_target_pairs={{0,2},{1,3},{2,4},{3,5},{4,6},{5,7},{6,0},{7,1},{8,10},{9,11},{10,... | collective-permute-start | bytes 897032 | tf_op jit(solution)/shard_map/ppermute | solution.py:791
  7.3 9.4 %collective-permute-start.3 = (bf16[128,1024]{1,0:T(8,128)(2,1)}, bf16[128,1024]{1,0:T(8,128)(2,1)S(1)}, u32[]{:S(2)}, u32[]{:S(2)}) collective-permute-start(bf16[128,1024]{1,0:T(8,128)(2,1)} %bitcast.10), channel_id=1, source_target_pairs={{0,16},{8,24},{16,0},{24,8},{1,17},{9,25},{17,1},{25,9},{2,18},{10... | collective-permute-start | bytes 786440 | tf_op jit(solution)/shard_map/ppermute | solution.py:786
  12.8 11.9 %collective-permute-start.4 = (bf16[1168,128]{1,0:T(8,128)(2,1)S(1)}, bf16[1168,128]{1,0:T(8,128)(2,1)S(1)}, u32[]{:S(2)}, u32[]{:S(2)}) collective-permute-start(bf16[1168,128]{1,0:T(8,128)(2,1)S(1)} %collective-permute-done.partner), channel_id=1, source_target_pairs={{0,2},{1,3},{2,4},{3,5},{4,6},{5,7},{6,0},{7,1},{8,10},{9,11},{10,... | collective-permute-start | bytes 897032 | tf_op jit(solution)/shard_map/ppermute | solution.py:791
  14.7 8.5 %collective-permute-start.6 = (bf16[128,1024]{1,0:T(8,128)(2,1)S(1)}, bf16[128,1024]{1,0:T(8,128)(2,1)S(1)}, u32[]{:S(2)}, u32[]{:S(2)}) collective-permute-start(bf16[128,1024]{1,0:T(8,128)(2,1)S(1)} %bitcast.12), channel_id=1, source_target_pairs={{0,1},{1,0},{2,3},{3,2},{4,5},{5,4},{6,7},{7,6},{8,9},{9,8},{10,11... | collective-permute-start | bytes 786440 | tf_op jit(solution)/shard_map/ppermute | solution.py:786
  16.2 8.6 %collective-permute-start.5 = (bf16[576,128]{1,0:T(8,128)(2,1)S(1)}, bf16[576,128]{1,0:T(8,128)(2,1)S(1)}, u32[]{:S(2)}, u32[]{:S(2)}) collective-permute-start(bf16[576,128]{1,0:T(8,128)(2,1)S(1)} %get-tuple-element.104), channel_id=1, source_target_pairs={{0,1},{1,0},{2,3},{3,2},{4,5},{5,4},{6,7},{7,6},{8,9},{9,8},{10,11... | collective-permute-start | bytes 442376 | tf_op jit(solution)/shard_map/ppermute | solution.py:786
  17.4 12.5 %collective-permute-start.8 = (bf16[1152,128]{1,0:T(8,128)(2,1)S(1)}, bf16[1152,128]{1,0:T(8,128)(2,1)S(1)}, u32[]{:S(2)}, u32[]{:S(2)}) collective-permute-start(bf16[1152,128]{1,0:T(8,128)(2,1)S(1)} %get-tuple-element.106.both_own), channel_id=1, source_target_pairs={{2,0},{3,1},{4,2},{5,3},{6,4},{7,5},{10,8},{11,9},{12,10},{13,11},... | collective-permute-start | bytes 884744 | tf_op jit(solution)/shard_map/ppermute | solution.py:799
  18.7 8.2 %collective-permute-start.7 = (bf16[128,1024]{1,0:T(8,128)(2,1)S(1)}, bf16[128,1024]{1,0:T(8,128)(2,1)S(1)}, u32[]{:S(2)}, u32[]{:S(2)}) collective-permute-start(bf16[128,1024]{1,0:T(8,128)(2,1)S(1)} %collective-permute-done.3.refs_6_), channel_id=1, source_target_pairs={{0,8},{8,0},{16,24},{24,16},{1,9},{9,1},{17,25},{25,17},{2,10},{10... | collective-permute-start | bytes 786440 | tf_op jit(solution)/shard_map/ppermute | solution.py:786
  23.1 11.0 %collective-permute-start.12 = (bf16[128,1024]{1,0:T(8,128)(2,1)S(1)}, bf16[128,1024]{1,0:T(8,128)(2,1)S(1)}, u32[]{:S(2)}, u32[]{:S(2)}) collective-permute-start(bf16[128,1024]{1,0:T(8,128)(2,1)S(1)} %collective-permute-done.6.cotangent.refs_4_), channel_id=1, source_target_pairs={{0,16},{8,24},{16,0},{24,8},{1,17},{9,25},{17,1},{25,9},{2,18},{10... | collective-permute-start | bytes 786440 | tf_op jit(solution)/shard_map/ppermute | solution.py:786
  26.9 7.2 %collective-permute-start.10 = (bf16[144,256]{1,0:T(8,128)(2,1)S(1)}, bf16[144,256]{1,0:T(8,128)(2,1)S(1)}, u32[]{:S(2)}, u32[]{:S(2)}) collective-permute-start(bf16[144,256]{1,0:T(8,128)(2,1)S(1)} %get-tuple-element.134), channel_id=1, source_target_pairs={{0,16},{8,24},{16,0},{24,8},{1,17},{9,25},{17,1},{25,9},{2,18},{10... | collective-permute-start | bytes 221192 | tf_op jit(solution)/shard_map/ppermute | solution.py:786
  28.7 5.5 %collective-permute-start.11 = (bf16[144,256]{1,0:T(8,128)(2,1)S(1)}, bf16[144,256]{1,0:T(8,128)(2,1)S(1)}, u32[]{:S(2)}, u32[]{:S(2)}) collective-permute-start(bf16[144,256]{1,0:T(8,128)(2,1)S(1)} %get-tuple-element.135), channel_id=1, source_target_pairs={{0,24},{8,16},{16,8},{24,0},{1,25},{9,17},{17,9},{25,1},{2,26},{10... | collective-permute-start | bytes 221192 | tf_op jit(solution)/shard_map/ppermute | solution.py:786
  28.7 5.5 %collective-permute-start.9 = (bf16[144,256]{1,0:T(8,128)(2,1)S(1)}, bf16[144,256]{1,0:T(8,128)(2,1)S(1)}, u32[]{:S(2)}, u32[]{:S(2)}) collective-permute-start(bf16[144,256]{1,0:T(8,128)(2,1)S(1)} %get-tuple-element.133), channel_id=1, source_target_pairs={{0,8},{8,0},{16,24},{24,16},{1,9},{9,1},{17,25},{25,17},{2,10},{10... | collective-permute-start | bytes 221192 | tf_op jit(solution)/shard_map/ppermute | solution.py:786
  29.9 11.5 %collective-permute-start.15 = (bf16[1296,128]{1,0:T(8,128)(2,1)S(1)}, bf16[1296,128]{1,0:T(8,128)(2,1)S(1)}, u32[]{:S(2)}, u32[]{:S(2)}) collective-permute-start(bf16[1296,128]{1,0:T(8,128)(2,1)S(1)} %get-tuple-element.125.both_partner), channel_id=1, source_target_pairs={{0,6},{1,7},{2,0},{3,1},{4,2},{5,3},{6,4},{7,5},{8,14},{9,15},{10,... | collective-permute-start | bytes 995336 | tf_op jit(solution)/shard_map/ppermute | solution.py:791
  34.2 2.3 %collective-permute-start.13 = (bf16[128,1024]{1,0:T(8,128)(2,1)S(1)}, bf16[128,1024]{1,0:T(8,128)(2,1)S(1)}, u32[]{:S(2)}, u32[]{:S(2)}) collective-permute-start(bf16[128,1024]{1,0:T(8,128)(2,1)S(1)} %collective-permute-done.6.cotangent.refs_4_), channel_id=1, source_target_pairs={{0,8},{8,0},{16,24},{24,16},{1,9},{9,1},{17,25},{25,17},{2,10},{10... | collective-permute-start | bytes 786440 | tf_op jit(solution)/shard_map/ppermute | solution.py:786
  34.2 2.3 %collective-permute-start.14 = (bf16[128,1024]{1,0:T(8,128)(2,1)S(1)}, bf16[128,1024]{1,0:T(8,128)(2,1)S(1)}, u32[]{:S(2)}, u32[]{:S(2)}) collective-permute-start(bf16[128,1024]{1,0:T(8,128)(2,1)S(1)} %collective-permute-done.12.refs_6_), channel_id=1, source_target_pairs={{0,8},{8,0},{16,24},{24,16},{1,9},{9,1},{17,25},{25,17},{2,10},{10... | collective-permute-start | bytes 786440 | tf_op jit(solution)/shard_map/ppermute | solution.py:786
  34.7 9.4 %collective-permute-start.16 = (bf16[576,256]{1,0:T(8,128)(2,1)S(1)}, bf16[576,256]{1,0:T(8,128)(2,1)S(1)}, u32[]{:S(2)}, u32[]{:S(2)}) collective-permute-start(bf16[576,256]{1,0:T(8,128)(2,1)S(1)} %get-tuple-element.159), channel_id=1, source_target_pairs={{0,1},{1,0},{2,3},{3,2},{4,5},{5,4},{6,7},{7,6},{8,9},{9,8},{10,11... | collective-permute-start | bytes 884744 | tf_op jit(solution)/shard_map/ppermute | solution.py:786
  36.9 8.9 %collective-permute-start.17 = (bf16[144,256]{1,0:T(8,128)(2,1)S(1)}, bf16[144,256]{1,0:T(8,128)(2,1)S(1)}, u32[]{:S(2)}, u32[]{:S(2)}) collective-permute-start(bf16[144,256]{1,0:T(8,128)(2,1)S(1)} %get-tuple-element.164), channel_id=1, source_target_pairs={{0,2},{1,3},{2,0},{3,1},{4,6},{5,7},{6,4},{7,5},{8,10},{9,11},{10,... | collective-permute-start | bytes 221192 | tf_op jit(solution)/shard_map/ppermute | solution.py:786
  37.3 8.5 %collective-permute-start.18 = (bf16[144,256]{1,0:T(8,128)(2,1)S(1)}, bf16[144,256]{1,0:T(8,128)(2,1)S(1)}, u32[]{:S(2)}, u32[]{:S(2)}) collective-permute-start(bf16[144,256]{1,0:T(8,128)(2,1)S(1)} %get-tuple-element.165), channel_id=1, source_target_pairs={{0,4},{1,5},{2,6},{3,7},{4,0},{5,1},{6,2},{7,3},{8,12},{9,13},{10,... | collective-permute-start | bytes 221192 | tf_op jit(solution)/shard_map/ppermute | solution.py:786
  39.3 7.1 %collective-permute-start.19 = (bf16[144,256]{1,0:T(8,128)(2,1)S(1)}, bf16[144,256]{1,0:T(8,128)(2,1)S(1)}, u32[]{:S(2)}, u32[]{:S(2)}) collective-permute-start(bf16[144,256]{1,0:T(8,128)(2,1)S(1)} %get-tuple-element.166), channel_id=1, source_target_pairs={{0,6},{1,7},{2,4},{3,5},{4,2},{5,3},{6,0},{7,1},{8,14},{9,15},{10,... | collective-permute-start | bytes 221192 | tf_op jit(solution)/shard_map/ppermute | solution.py:786
  43.1 8.3 %collective-permute-start.20 = (bf16[1152,128]{1,0:T(8,128)(2,1)S(1)}, bf16[1152,128]{1,0:T(8,128)(2,1)S(1)}, u32[]{:S(2)}, u32[]{:S(2)}) collective-permute-start(bf16[1152,128]{1,0:T(8,128)(2,1)S(1)} %get-tuple-element.170), channel_id=1, source_target_pairs={{0,1},{1,0},{2,3},{3,2},{4,5},{5,4},{6,7},{7,6},{8,9},{9,8},{10,11... | collective-permute-start | bytes 884744 | tf_op jit(solution)/shard_map/ppermute | solution.py:786
  46.5 5.9 %collective-permute-start.21 = (bf16[144,128]{1,0:T(8,128)(2,1)S(1)}, bf16[144,128]{1,0:T(8,128)(2,1)S(1)}, u32[]{:S(2)}, u32[]{:S(2)}) collective-permute-start(bf16[144,128]{1,0:T(8,128)(2,1)S(1)} %get-tuple-element.177.stays), channel_id=1, source_target_pairs={{0,25},{1,16},{2,27},{3,18},{4,29},{5,20},{6,31},{7,22},{8,1},{9,1... | collective-permute-start | bytes 110600 | tf_op jit(solution)/shard_map/ppermute | solution.py:813
  47.4 5.0 %collective-permute-start.22 = (bf16[144,128]{1,0:T(8,128)(2,1)S(1)}, bf16[144,128]{1,0:T(8,128)(2,1)S(1)}, u32[]{:S(2)}, u32[]{:S(2)}) collective-permute-start(bf16[144,128]{1,0:T(8,128)(2,1)S(1)} %get-tuple-element.178), channel_id=1, source_target_pairs={{0,1},{1,17},{2,3},{3,19},{4,5},{5,21},{6,7},{7,23},{8,0},{9,16},{... | collective-permute-start | bytes 110600 | tf_op jit(solution)/shard_map/ppermute | solution.py:813

commit v5 on v4

--- a/solution.py
+++ b/solution.py
@@ -19,6 +19,17 @@
 SHARED = PAIRS * PAIR
 MIXED = 2 * PAIRS
 ROWS = (MIXED + 1) * BLOCK
+FIRST_BLOCKS = (0, 2, 5, 7)
+HEAD_STARTS = (0, 128, 320, 448)
+SINGLE_START = 256
+PIECE_ROWS = 160
+ATT_ROWS = HEAD_STARTS[-1] + PIECE_ROWS
+SEGMENTS = (
+    ((0, 0, 128, 0), (0, 128, 32, 256), (1, 0, 128, 128)),
+    ((0, 0, 96, 0), (0, 96, 64, 224), (1, 0, 128, 96)),
+    ((0, 0, 128, 64), (1, 0, 64, 0), (1, 64, 96, 192)),
+    ((0, 0, 128, 32), (1, 0, 32, 0), (1, 32, 128, 160)),
+)
 CLIP_ROWS = 16
 CLIP_STAT = 2 * PAIRS + 2
 DELTA_STAT = CLIP_STAT + 2
@@ -45,12 +56,12 @@
     return jax.ShapeDtypeStruct(shape, dtype)
 
 
-def kernel(body, name, ins, outs, scratch=(), out_space=VMEM, flops=1_000_000):
+def kernel(body, name, ins, outs, scratch=(), spaces=None, flops=1_000_000):
     return pl.pallas_call(
         body,
         out_shape=tuple(outs),
         in_specs=list(ins),
-        out_specs=(out_space,) * len(outs),
+        out_specs=spaces or (VMEM,) * len(outs),
         scratch_shapes=list(scratch),
         compiler_params=pltpu.CompilerParams(vmem_limit_bytes=VMEM_LIMIT),
         cost_estimate=pl.CostEstimate(flops=flops, bytes_accessed=10_000, transcendentals=0),
@@ -83,15 +94,15 @@
 
 
 def columns_of(half, pair):
-    return span(half * (SHARED + PAIR) + pair * PAIR, PAIR, PAIR)
-
-
-def head_rows(half, pair):
-    return span(half * HDIM + pair * PAIR, PAIR, HDIM)
-
-
-def single_rows(half):
-    return span((1 - half) * SHARED, HDIM, HDIM)
+    return span((FIRST_BLOCKS[pair] + half) * PAIR, PAIR, PAIR)
+
+
+def head_rows(pair):
+    return slice(HEAD_STARTS[pair], HEAD_STARTS[pair] + PAIR)
+
+
+def single_rows():
+    return slice(SINGLE_START, SINGLE_START + HDIM)
 
 
 def times(a, b, dims):
@@ -174,12 +185,12 @@
         d_pair = d_pairs[:, pair * PAIR : (pair + 1) * PAIR].astype(bf16)
         target[rows_of(pair)] = query[rows_of(pair)]
         target[rows_of(PAIRS + pair)] = d_pair
-        d_turned[head_rows(half, pair)] = d_pair.T
+        d_turned[head_rows(pair)] = d_pair.T
     single[0] = low_or_high(0.0, turned(d_shared)).astype(bf16)
     single[1] = low_or_high(0.0, d_shared).astype(bf16)
     d_single = single[half]
     target[rows_of(MIXED)] = query_single + d_single
-    d_turned[single_rows(half)] = d_single.T[HDIM:]
+    d_turned[single_rows()] = d_single.T[HDIM:]
 
 
 def own_cotangent_kernel(cotangent, weight, query, both, d_turned, kept, rows, single, sems):
@@ -196,7 +207,8 @@
     for number in range(CHUNKS):
         copies[number + 1].wait()
         part = slice(number * chunk, (number + 1) * chunk)
-        wide = times(rows[:, part], kept[part, span(half * (SHARED + PAIR), SHARED, PAIR)], ((1,), (0,)))
+        columns = [kept[part, columns_of(half, pair)] for pair in range(PAIRS)]
+        wide = times(rows[:, part], jnp.concatenate(columns, axis=1), ((1,), (0,)))
         narrow = times(rows[:, part], kept[part, SHARED : SHARED + PAIR], ((1,), (0,)))
         pairs = wide if pairs is None else pairs + wide
         shared = narrow if shared is None else shared + narrow
@@ -222,7 +234,8 @@
 ):
     half = my_half()
     rows = cotangent[...]
-    pairs = times(rows, weight[:, span(half * (SHARED + PAIR), SHARED, PAIR)], ((1,), (0,)))
+    columns = [weight[:, columns_of(half, pair)] for pair in range(PAIRS)]
+    pairs = times(rows, jnp.concatenate(columns, axis=1), ((1,), (0,)))
     shared = times(rows, weight[:, SHARED : SHARED + PAIR], ((1,), (0,)))
     query_single = unpacked_single(query[SHARED:])
     join_query(both, d_turned, single, query, query_single, pairs, shared)
@@ -232,12 +245,12 @@
     for query_block in range(2):
         steps = rows_of(query_block)
         for pair in range(PAIRS):
-            which = head_rows(half, pair)
+            which = head_rows(pair)
             dots = d_all[which, steps].astype(f32) * att[which, steps].astype(f32)
             row = DELTA_STAT + 2 * pair + query_block
             stats[row : row + 1, :BLOCK] = jnp.sum(dots[:HDIM], axis=0, keepdims=True)
             stats[row : row + 1, BLOCK:] = jnp.sum(dots[HDIM:], axis=0, keepdims=True)
-        which = single_rows(half)
+        which = single_rows()
         dots = d_all[which, steps].astype(f32) * att[which, steps].astype(f32)
         row = DELTA_STAT + 2 * PAIRS + query_block
         stats[row : row + 1, :BLOCK] = jnp.sum(dots, axis=0, keepdims=True)
@@ -348,9 +361,9 @@
 
 def staggered(items, *stages):
     values = [None] * len(items)
-    for step in range(len(items) + len(stages) - 1):
+    for step in range(len(items) + 2 * len(stages) - 2):
         for number, stage in enumerate(stages):
-            index = step - number
+            index = step - 2 * number
             if 0 <= index < len(items):
                 values[index] = stage(*items[index], values[index])
 
@@ -400,26 +413,27 @@
         if pair < PAIRS:
             weights_out[pair, query_block] = weights
             mixed = times(keys_all[PAIRS + pair, keys_of(query_block)], weights, ((0,), (0,)))
-            att[head_rows(half, pair), steps] = diagonal(mixed).astype(bf16)
+            att[head_rows(pair), steps] = diagonal(mixed).astype(bf16)
         else:
             single_out[query_block] = weights
             mixed = times(keys_all[MIXED, keys_of(query_block)], weights, ((0,), (0,)))
-            att[single_rows(half), steps] = mixed[HDIM:].astype(bf16)
+            att[single_rows(), steps] = mixed[HDIM:].astype(bf16)
 
     items = [(pair, query_block) for pair in range(PAIRS + 1) for query_block in range(2)]
     staggered(items, score, weigh, mix)
 
-    att_own[...] = att[:, at(half, BLOCK)]
-    att_swap[...] = att[:, at(1 - half, BLOCK)]
-    if pieces_wanted:
-        rows = pieces[0].shape[0]
-        for number, piece in enumerate(pieces):
-            begin = rows * jnp.bitwise_xor(lax.axis_index("dp"), number)
-            piece[...] = att[span(begin, rows, 16), :]
+    att[HALF:] = jnp.zeros((ATT_ROWS - HALF, 2 * BLOCK), bf16)
+    att_own[...] = att[:HALF, at(half, BLOCK)]
+    att_swap[...] = att[:HALF, at(1 - half, BLOCK)]
+    for number, piece in enumerate(pieces):
+        target = jnp.bitwise_xor(lax.axis_index("dp"), number)
+        late = 32 * jnp.maximum(target - 2, 0)
+        begin = jnp.where(half == 0, 160 * target - late, 128 * target + late)
+        piece[...] = att[span(begin, PIECE_ROWS, 32), :]
 
 
 def forward(pieces_wanted, *sources):
-    piece = (HALF // max(pieces_wanted, 1), 2 * BLOCK)
+    piece = (PIECE_ROWS, 2 * BLOCK)
     return kernel(
         functools.partial(forward_kernel, pieces_wanted),
         "forward",
@@ -428,7 +442,7 @@
             shaped((PAIRS, 2, WIN + BLOCK, 2 * BLOCK), bf16),
             shaped((2, WIN + BLOCK, BLOCK), bf16),
             shaped((STAT_ROWS, 2 * BLOCK), f32),
-            shaped((HALF, 2 * BLOCK), bf16),
+            shaped((ATT_ROWS, 2 * BLOCK), bf16),
             shaped((HALF, BLOCK), bf16),
             shaped((HALF, BLOCK), bf16),
         ]
@@ -496,11 +510,11 @@
         dk = times(d_scores[mine], query_rows, ((1,), (0,)))
         dv = times(weights[mine], d_rows, ((1,), (0,)))
         if pair < PAIRS:
-            dq_all[head_rows(half, pair), steps] = (diagonal(dq) * SCALING).astype(bf16)
+            dq_all[head_rows(pair), steps] = (diagonal(dq) * SCALING).astype(bf16)
             accumulate(pair, query_block, dk)
             accumulate(PAIRS + pair, query_block, dv)
         else:
-            dq_all[single_rows(half), steps] = (dq[:HDIM] * SCALING).astype(bf16)
+            dq_all[single_rows(), steps] = (dq[:HDIM] * SCALING).astype(bf16)
             accumulate(MIXED, query_block, dk + dv)
 
     items = [(pair, query_block) for pair in range(PAIRS + 1) for query_block in (1, 0)]
@@ -624,24 +638,54 @@
     )(*sources)
 
 
-def output_kernel(att_own, received, weight, out, full):
-    half = my_half()
-    full[at(half, HALF)] = att_own[...]
-    full[at(1 - half, HALF)] = received[:, :BLOCK]
+def join_halves(full, halves, mine, theirs):
+    half = my_half()
+    halves[half] = mine
+    halves[1 - half] = theirs
+    for side in range(2):
+        for pair in range(PAIRS):
+            full[rows_of(FIRST_BLOCKS[pair] + side)] = halves[side, head_rows(pair)]
+        begin = SHARED + side * HDIM
+        full[begin : begin + HDIM] = halves[side, single_rows()]
+
+
+def output_kernel(att_own, received, dq_mine, weight, out, query_out, full, dq_all, halves, query, sem):
+    join_halves(dq_all, halves, dq_mine[...], received[:, BLOCK:])
+    for block in range(WIDTH // PAIR):
+        query[:, block * PAIR : (block + 1) * PAIR] = dq_all[rows_of(block)].T
+    copy = pltpu.make_async_copy(query, query_out, sem)
+    copy.start()
+    join_halves(full, halves, att_own[...], received[:, :BLOCK])
     out[...] = times(weight[...], full[...], ((1,), (0,))).T.astype(bf16)
-
-
-def output_rows(att_own, received, weight):
+    copy.wait()
+
+
+def output_rows(att_own, received, dq_mine, weight):
     return kernel(
         output_kernel,
         "output",
-        [VMEM] * 3,
-        [shaped((BLOCK, weight.shape[0]), bf16), shaped((WIDTH, BLOCK), bf16)],
-    )(att_own, received, weight)
-
-
-def place_keys_kernel(mine, theirs, key_out, value_out, key, value, mixed, sems):
-    half = my_half()
+        [VMEM] * 4,
+        [
+            shaped((BLOCK, weight.shape[0]), bf16),
+            shaped((BLOCK, WIDTH), bf16),
+            shaped((WIDTH, BLOCK), bf16),
+        ],
+        [
+            pltpu.VMEM((WIDTH, BLOCK), bf16),
+            pltpu.VMEM((2, HALF, BLOCK), bf16),
+            pltpu.VMEM((BLOCK, WIDTH), bf16),
+            pltpu.SemaphoreType.DMA,
+        ],
+        (VMEM, HBM, VMEM),
+    )(att_own, received, dq_mine, weight)
+
+
+def place_kernel(
+    mine, theirs, kept, arrived, key_out, value_out, weight_out, key, value, mixed, parts, total, sems
+):
+    half = my_half()
+    moves = [(total, weight_out), (key, key_out), (value, value_out)]
+    copies = [pltpu.make_async_copy(a, b, sems.at[n]) for n, (a, b) in enumerate(moves)]
     for side, source in ((half, mine), (1 - half, theirs)):
         for pair in range(PAIRS):
             key[:, columns_of(side, pair)] = source[rows_of(pair)]
@@ -649,67 +693,42 @@
         mixed[side] = source[rows_of(MIXED)].astype(f32)
     shared = slice(SHARED, SHARED + PAIR)
     key[:, shared] = low_or_high(mixed[0], turned(mixed[1])).astype(bf16)
+    copies[1].start()
     value[:, shared] = low_or_high(turned(mixed[0]), mixed[1]).astype(bf16)
-    pairs = ((key, key_out), (value, value_out))
-    copies = [pltpu.make_async_copy(a, b, sems.at[n]) for n, (a, b) in enumerate(pairs)]
-    for copy in copies:
-        copy.start()
+    copies[2].start()
+    parts[half] = kept[...]
+    parts[1 - half] = arrived[...].astype(f32)
+    for sequence, segments in enumerate(SEGMENTS):
+
+        @pl.when(lax.axis_index("dp") == sequence)
+        def _():
+            for side, source, size, target in segments:
+                total[target : target + size] = parts[side, source : source + size]
+
+    copies[0].start()
     for copy in copies:
         copy.wait()
 
 
-def place_keys(*sources):
+def place(*sources):
+    weight_rows = 2 * HALF // len(SEGMENTS)
     wide = pltpu.VMEM((BLOCK, WIDTH), bf16)
-    mixed = pltpu.VMEM((2, BLOCK, PAIR), f32)
-    return kernel(
-        place_keys_kernel,
-        "place_keys",
-        [VMEM] * 2,
-        [shaped((BLOCK, WIDTH), bf16)] * 2,
-        [wide, wide, mixed, pltpu.SemaphoreType.DMA((2,))],
-        HBM,
-        COST_KEYS,
-    )(*sources)
-
-
-def place_kernel(dq_mine, received, stays, first, second, query_out, weight_out, dq_all, query, both, sems):
-    half = my_half()
-    rows = first.shape[0]
-    moves = [(both, weight_out), (query, query_out)]
-    copies = [pltpu.make_async_copy(a, b, sems.at[n]) for n, (a, b) in enumerate(moves)]
-    both[span(half * rows, rows, 16)] = first[...].astype(f32)
-
-    @pl.when(lax.axis_index("dp") == 3 * half)
-    def _():
-        both[span(half * rows, rows, 16)] = stays[...].astype(f32)
-
-    both[span((1 - half) * rows, rows, 16)] = second[...].astype(f32)
-    copies[0].start()
-    dq_all[at(half, HALF)] = dq_mine[...]
-    dq_all[at(1 - half, HALF)] = received[:, BLOCK:]
-    for block in range(WIDTH // PAIR):
-        query[:, block * PAIR : (block + 1) * PAIR] = dq_all[rows_of(block)].T
-    copies[1].start()
-    for copy in copies:
-        copy.wait()
-
-
-def place(*sources):
-    rows, lanes = sources[-1].shape
-    query, weight = kernel(
+    *grads, weight = kernel(
         place_kernel,
         "place",
-        [VMEM] * 5,
-        [shaped((BLOCK, WIDTH), bf16), shaped((2 * rows, lanes), f32)],
+        [VMEM] * 4,
+        [shaped((BLOCK, WIDTH), bf16)] * 2 + [shaped((weight_rows, BLOCK), f32)],
         [
-            pltpu.VMEM((WIDTH, BLOCK), bf16),
-            pltpu.VMEM((BLOCK, WIDTH), bf16),
-            pltpu.VMEM((2 * rows, lanes), f32),
-            pltpu.SemaphoreType.DMA((2,)),
+            wide,
+            wide,
+            pltpu.VMEM((2, BLOCK, PAIR), f32),
+            pltpu.VMEM((2, PIECE_ROWS, BLOCK), f32),
+            pltpu.VMEM((weight_rows, BLOCK), f32),
+            pltpu.SemaphoreType.DMA((3,)),
         ],
-        HBM,
+        (HBM,) * 3,
     )(*sources)
-    return query, weight.T
+    return *grads, weight.T
 
 
 def weight_kernel(count, *refs):
@@ -758,15 +777,14 @@
 
 
 def weight_sum_kernel(kept, *rest):
-    received, (first, second, total) = rest[:-3], rest[-3:]
+    received, (mine, sent, total) = rest[:-3], rest[-3:]
     value = kept[...]
     for part in received:
         value = value + part[...].astype(f32)
     total[...] = value
-    lanes = first.shape[1]
-    odd = jnp.bitwise_and(lax.axis_index("dp"), 1)
-    first[...] = total[:, at(odd, lanes)].astype(bf16)
-    second[...] = total[:, at(1 - odd, lanes)].astype(bf16)
+    half = my_half()
+    mine[...] = total[:, at(half, BLOCK)]
+    sent[...] = total[:, at(1 - half, BLOCK)].astype(bf16)
 
 
 def weight_sum(kept, received):
@@ -775,7 +793,7 @@
         weight_sum_kernel,
         "weight_sum",
         [VMEM] * (1 + len(received)),
-        [shaped((rows, lanes // 2), bf16)] * 2,
+        [shaped((rows, BLOCK), f32), shaped((rows, BLOCK), bf16)],
         [pltpu.VMEM((rows, lanes), f32)],
         flops=COST_SUM,
     )(kept, *received)
@@ -797,20 +815,6 @@
     count = lax.axis_size(axis)
     first, last = (max(0, -steps), min(count, count - steps))
     return lax.ppermute(value, axis, [(source, source + steps) for source in range(first, last)])
-
-
-def placed(value, flip):
-    lanes = lax.axis_size("ctx")
-    moves = []
-    for source in range(lax.axis_size("dp")):
-        for index in range(lanes):
-            group, half = index // 2, index % 2
-            target_half = (source % 2) ^ flip
-            target = 2 * half + source // 2
-            if (target, target_half) == (source, half):
-                target, target_half = 3 - target, 1 - target_half
-            moves.append((source * lanes + index, target * lanes + 2 * group + target_half))
-    return lax.ppermute(value, ("dp", "ctx"), moves)
 
 
 def after(*values):
@@ -850,15 +854,14 @@
     )
     if short:
         cot_across = swapped(cot_partner, "dp", 2)
-    weights, cot_partner, *rest = after(weights, cot_partner, *pieces, *cots)
-    pieces, cots = rest[: len(pieces)], rest[len(pieces) :]
+    weights, cot_partner, *pieces = after(weights, cot_partner, *pieces)
 
     if short:
         pieces[1:] = [swapped(pieces[n], "dp", n) for n in (1, 2, 3)]
     both_partner, stats = cotangents(
         cot_partner, weight, query_partner, att, d_turned_own, totals
     )
-    both_partner, next_own = after(both_partner, next_own)
+    both_partner, next_own, *cots = after(both_partner, next_own, *cots)
     next_partner = rotated(both_partner, "ctx", -2)
     dq_own, swap, own_grads, partner_grads = own_gradients(
         keys_all, both_own, both_partner, weights, single, stats, att_swap
@@ -880,11 +883,11 @@
     )
     kv_rest = swapped(kv_swap, "ctx", 1)
     kv_own, received = after(kv_own, received)
-    sublayer_out, att_full = output_rows(att_own, received, weight)
+    sublayer_out, query_grad, att_full = output_rows(att_own, received, dq_own, weight)
     if short:
         kept, kv_own, sublayer_out, *arrived = after(kept, kv_own, sublayer_out, *arrived)
-        stays, second = weight_sum(kept, arrived)
-        first, second = placed(stays, 0), placed(second, 1)
+        kept, sent = weight_sum(kept, arrived)
+        arrived = swapped(sent, "ctx", 1)
     if not short:
         product = lax.dot_general(
             cotangent, att_full, (((0,), (1,)), ((), ())), preferred_element_type=f32
@@ -893,10 +896,9 @@
         weight_grad = lax.psum_scatter(
             sequence_grad.astype(f32), "dp", scatter_dimension=1, tiled=True
         )
-        stays = first = second = jnp.zeros((16, 128), bf16)
-    key_grad, value_grad = place_keys(kv_own, kv_rest)
-    dq_own, key_grad = after(dq_own, key_grad)
-    query_grad, placed_weight = place(dq_own, received, stays, first, second)
+        kept = jnp.zeros((PIECE_ROWS, BLOCK), f32)
+        arrived = kept.astype(bf16)
+    key_grad, value_grad, placed_weight = place(kv_own, kv_rest, kept, arrived)
     if short:
         weight_grad = placed_weight
     return (

time: 53.6 us -> 53 us (0.989)
  starting transfers between devices: 27.9 us -> 26.1 us
  waiting for transfers between devices: 9.5 us -> 11 us
    ppermute x2 -> x0, starting transfers between devices: 3.04 us -> none  [placed(): return lax.ppermute(value, ('dp', 'ctx'), moves)]
    ppermute x17 -> x18, waiting for transfers between devices: 8.66 us -> 10 us  [swapped(): lax.ppermute(value, axis, [(source, source ^ bits) for source in range(co...]
    ppermute x17 -> x18, starting transfers between devices: 17.9 us -> 19.3 us  [swapped(): lax.ppermute(value, axis, [(source, source ^ bits) for source in range(co...]
    pallas_call x3 -> x2, Pallas kernels: 3.56 us -> 3.52 us  [the longest x1 2.44 us: output_rows(): kernel(output_kernel, 'output', [VMEM] * 4, [shaped((BLOCK, weight.shape[...]
  transfers between devices with their start and end apart: 23 -> 22, of which waited for: 7 -> 7; matrix products, arithmetic and copies ran while one was open for 0% -> 0% of each run, Pallas kernels for 23% -> 22%
where the time goes in v5:
time: 53 us; the launch traced here: 52.8 us
  starting transfers between devices  26.1 us (49%)
  Pallas kernels  14.2 us (27%)
  waiting for transfers between devices  11 us (21%)
  between operations  1.49 us (3%)
    ppermute x18, starting transfers between devices, swapped(): lax.ppermute(value, axis, [(source, source ^ bits) for source in range(co...  19.3 us
    ppermute x18, waiting for transfers between devices, swapped(): lax.ppermute(value, axis, [(source, source ^ bits) for source in range(co...  10 us
    ppermute x3, starting transfers between devices, rotated(): lax.ppermute(value, axis, [(source, (source + steps) % count) for source...  5.55 us
    pallas_call x1, Pallas kernels, output_rows(): kernel(output_kernel, 'output', [VMEM] * 4, [shaped((BLOCK, weight.shape[...  2.44 us
    pallas_call x1, Pallas kernels, own_cotangents(): kernel(own_cotangent_kernel, 'own_cotangents', [HBM, HBM, VMEM], [shaped(...  2.24 us
    pallas_call x1, Pallas kernels, forward(): kernel(functools.partial(forward_kernel, pieces_wanted), 'forward', [VMEM...  1.91 us
    pallas_call x1, Pallas kernels, own_gradients(): kernel(own_kernel, 'own_gradients', [VMEM] * 7, [shaped((HALF, BLOCK), bf...  1.82 us
    pallas_call x1, Pallas kernels, next_gradients(): kernel(functools.partial(next_kernel, groups), 'next_gradients', [VMEM] *...  1.65 us
  transfers between devices with their start and end apart: 22, of which 7 were waited for; matrix products, arithmetic and copies ran while one was open for 0% of the time, Pallas kernels for 22%

profile of v5, /device:TPU:0, one launch (start us, length us, event | category | flops | bytes accessed | tf_op | source)
XLA Modules:
  0.0 52.8 jit_solution(11692138684511894598)
XLA Ops:
  1.3 1.4 %pack.1 = (bf16[1168,128]{1,0:T(8,128)(2,1)S(1)}, bf16[1168,128]{1,0:T(8,128)(2,1)S(1)}, bf16[576,128]{1,0:T(8,128)(2,1)S(1)}, bf16[640,128]{1,0:T(8,128)(2,1)S(1)}) custom-call(s32[1,1]{1,0:T(1,128)S(6)} %copy.11.clip, bf16[128,1152]{1,0:T(8,128)(2,1)} %bitcast.14, bf16[128,1152]{1,0:T(8,128)(2,1)} %bitcast.15, bf16[128,1152]{1,0:T(8,128)(2,1)} %bitcast.16), custom_call_target="tpu_custom_call" | custom-call | flops 1000000 | bytes 10000 | tf_op jit(solution)/shard_map/pack/pallas_call | solution.py:159
  2.7 3.0 %collective-permute-start = (bf16[1168,128]{1,0:T(8,128)(2,1)S(1)}, bf16[1168,128]{1,0:T(8,128)(2,1)S(1)}, u32[]{:S(2)}, u32[]{:S(2)}) collective-permute-start(bf16[1168,128]{1,0:T(8,128)(2,1)S(1)} %get-tuple-element.94), channel_id=1, source_target_pairs={{0,1},{1,0},{2,3},{3,2},{4,5},{5,4},{6,7},{7,6},{8,9},{9,8},{10,11... | collective-permute-start | bytes 897032 | tf_op jit(solution)/shard_map/ppermute | solution.py:804
  5.8 1.6 %collective-permute-start.1 = (bf16[1168,128]{1,0:T(8,128)(2,1)S(1)}, bf16[1168,128]{1,0:T(8,128)(2,1)S(1)}, u32[]{:S(2)}, u32[]{:S(2)}) collective-permute-start(bf16[1168,128]{1,0:T(8,128)(2,1)S(1)} %get-tuple-element.92.own), channel_id=1, source_target_pairs={{0,2},{1,3},{2,4},{3,5},{4,6},{5,7},{6,0},{7,1},{8,10},{9,11},{10,... | collective-permute-start | bytes 897032 | tf_op jit(solution)/shard_map/ppermute | solution.py:809
  7.3 1.5 %collective-permute-start.3 = (bf16[128,1024]{1,0:T(8,128)(2,1)}, bf16[128,1024]{1,0:T(8,128)(2,1)S(1)}, u32[]{:S(2)}, u32[]{:S(2)}) collective-permute-start(bf16[128,1024]{1,0:T(8,128)(2,1)} %bitcast.10), channel_id=1, source_target_pairs={{0,16},{8,24},{16,0},{24,8},{1,17},{9,25},{17,1},{25,9},{2,18},{10... | collective-permute-start | bytes 786440 | tf_op jit(solution)/shard_map/ppermute | solution.py:804
  8.8 2.2 %own_cotangents.1 = (bf16[1152,128]{1,0:T(8,128)(2,1)S(1)}, bf16[576,128]{1,0:T(8,128)(2,1)S(1)}, bf16[1024,1152]{1,0:T(8,128)(2,1)S(1)}) custom-call(bf16[128,1024]{1,0:T(8,128)(2,1)} %bitcast.11, bf16[1024,1152]{1,0:T(8,128)(2,1)} %weight.1, bf16[640,128]{1,0:T(8,128)(2,1)S(1)} %get-tuple-element.95.query.query_own), custom_call_target="tpu_custom_call" | custom-call | flops 1000000 | bytes 10000 | tf_op jit(solution)/shard_map/own_cotangents/pallas_call | solution.py:219
  11.1 1.7 %collective-permute-done.partner = bf16[1168,128]{1,0:T(8,128)(2,1)S(1)} collective-permute-done((bf16[1168,128]{1,0:T(8,128)(2,1)S(1)}, bf16[1168,128]{1,0:T(8,128)(2,1)S(1)}, u32[]{:S(2)}, u32[]{:S(2)}) %collective-permute-start) | collective-permute-done | bytes 299040 | tf_op jit(solution)/shard_map/ppermute | solution.py:804
  12.8 1.8 %collective-permute-start.4 = (bf16[1168,128]{1,0:T(8,128)(2,1)S(1)}, bf16[1168,128]{1,0:T(8,128)(2,1)S(1)}, u32[]{:S(2)}, u32[]{:S(2)}) collective-permute-start(bf16[1168,128]{1,0:T(8,128)(2,1)S(1)} %collective-permute-done.partner), channel_id=1, source_target_pairs={{0,2},{1,3},{2,4},{3,5},{4,6},{5,7},{6,0},{7,1},{8,10},{9,11},{10,... | collective-permute-start | bytes 897032 | tf_op jit(solution)/shard_map/ppermute | solution.py:809
  14.7 1.5 %collective-permute-start.6 = (bf16[128,1024]{1,0:T(8,128)(2,1)S(1)}, bf16[128,1024]{1,0:T(8,128)(2,1)S(1)}, u32[]{:S(2)}, u32[]{:S(2)}) collective-permute-start(bf16[128,1024]{1,0:T(8,128)(2,1)S(1)} %bitcast.12), channel_id=1, source_target_pairs={{0,1},{1,0},{2,3},{3,2},{4,5},{5,4},{6,7},{7,6},{8,9},{9,8},{10,11... | collective-permute-start | bytes 786440 | tf_op jit(solution)/shard_map/ppermute | solution.py:804
  17.4 1.3 %collective-permute-start.7 = (bf16[1152,128]{1,0:T(8,128)(2,1)S(1)}, bf16[1152,128]{1,0:T(8,128)(2,1)S(1)}, u32[]{:S(2)}, u32[]{:S(2)}) collective-permute-start(bf16[1152,128]{1,0:T(8,128)(2,1)S(1)} %get-tuple-element.104.both_own), channel_id=1, source_target_pairs={{2,0},{3,1},{4,2},{5,3},{6,4},{7,5},{10,8},{11,9},{12,10},{13,11},... | collective-permute-start | bytes 884744 | tf_op jit(solution)/shard_map/ppermute | solution.py:817
  18.8 4.3 %collective-permute-done.6.cotangent.refs_4_ = bf16[128,1024]{1,0:T(8,128)(2,1)S(1)} collective-permute-done((bf16[128,1024]{1,0:T(8,128)(2,1)S(1)}, bf16[128,1024]{1,0:T(8,128)(2,1)S(1)}, u32[]{:S(2)}, u32[]{:S(2)}) %collective-permute-start.6) | collective-permute-done | bytes 262176 | tf_op jit(solution)/shard_map/ppermute | solution.py:804
  23.1 1.5 %collective-permute-start.12 = (bf16[128,1024]{1,0:T(8,128)(2,1)S(1)}, bf16[128,1024]{1,0:T(8,128)(2,1)S(1)}, u32[]{:S(2)}, u32[]{:S(2)}) collective-permute-start(bf16[128,1024]{1,0:T(8,128)(2,1)S(1)} %collective-permute-done.6.cotangent.refs_4_), channel_id=1, source_target_pairs={{0,16},{8,24},{16,0},{24,8},{1,17},{9,25},{17,1},{25,9},{2,18},{10... | collective-permute-start | bytes 786440 | tf_op jit(solution)/shard_map/ppermute | solution.py:804
  24.9 1.9 %forward.1 = (bf16[4,2,384,256]{3,2,1,0:T(8,128)(2,1)S(1)}, bf16[2,384,128]{2,1,0:T(8,128)(2,1)S(1)}, f32[24,256]{1,0:T(8,128)S(1)}, bf16[608,256]{1,0:T(8,128)(...) custom-call(bf16[9,512,128]{2,1,0:T(8,128)(2,1)S(1)} %get-tuple-elem, ...), custom_call_target="tpu_custom_call" | custom-call | flops 1000000 | bytes 10000 | tf_op jit(solution)/shard_map/forward/pallas_call | solution.py:437
  26.8 1.8 %collective-permute-start.10 = (bf16[160,256]{1,0:T(8,128)(2,1)S(1)}, bf16[160,256]{1,0:T(8,128)(2,1)S(1)}, u32[]{:S(2)}, u32[]{:S(2)}) collective-permute-start(bf16[160,256]{1,0:T(8,128)(2,1)S(1)} %get-tuple-element.132), channel_id=1, source_target_pairs={{0,16},{8,24},{16,0},{24,8},{1,17},{9,25},{17,1},{25,9},{2,18},{10... | collective-permute-start | bytes 245768 | tf_op jit(solution)/shard_map/ppermute | solution.py:804
  29.9 2.2 %collective-permute-start.15 = (bf16[1296,128]{1,0:T(8,128)(2,1)S(1)}, bf16[1296,128]{1,0:T(8,128)(2,1)S(1)}, u32[]{:S(2)}, u32[]{:S(2)}) collective-permute-start(bf16[1296,128]{1,0:T(8,128)(2,1)S(1)} %get-tuple-element.123.both_partner), channel_id=1, source_target_pairs={{0,6},{1,7},{2,0},{3,1},{4,2},{5,3},{6,4},{7,5},{8,14},{9,15},{10,... | collective-permute-start | bytes 995336 | tf_op jit(solution)/shard_map/ppermute | solution.py:809
  32.1 1.8 %own_gradients.1 = (bf16[576,128]{1,0:T(8,128)(2,1)S(1)}, bf16[576,256]{1,0:T(8,128)(2,1)S(1)}, f32[1152,128]{1,0:T(8,128)S(1)}, f32[1152,128]{1,0:T(8,128)S(1)}) custom-call(bf16[9,512,128]{2,1,0:T(8,128)(2,1)S(1)} %get-tuple-element.103.keys_all, bf16[1152,128]{1,0:T(8,128)(2,1)S(1)} %get-tuple-element.104.both_own, ...), custom_call_target="tpu_custom_call" | custom-call | flops 1000000 | bytes 10000 | tf_op jit(solution)/shard_map/own_gradients/pallas_call | solution.py:531
  34.5 1.5 %collective-permute-start.16 = (bf16[576,256]{1,0:T(8,128)(2,1)S(1)}, bf16[576,256]{1,0:T(8,128)(2,1)S(1)}, u32[]{:S(2)}, u32[]{:S(2)}) collective-permute-start(bf16[576,256]{1,0:T(8,128)(2,1)S(1)} %get-tuple-element.157), channel_id=1, source_target_pairs={{0,1},{1,0},{2,3},{3,2},{4,5},{5,4},{6,7},{7,6},{8,9},{9,8},{10,11... | collective-permute-start | bytes 884744 | tf_op jit(solution)/shard_map/ppermute | solution.py:804
  37.5 1.6 %collective-permute-start.18 = (bf16[160,256]{1,0:T(8,128)(2,1)S(1)}, bf16[160,256]{1,0:T(8,128)(2,1)S(1)}, u32[]{:S(2)}, u32[]{:S(2)}) collective-permute-start(bf16[160,256]{1,0:T(8,128)(2,1)S(1)} %get-tuple-element.164), channel_id=1, source_target_pairs={{0,4},{1,5},{2,6},{3,7},{4,0},{5,1},{6,2},{7,3},{8,12},{9,13},{10,... | collective-permute-start | bytes 245768 | tf_op jit(solution)/shard_map/ppermute | solution.py:804
  39.1 2.1 %collective-permute-start.19 = (bf16[160,256]{1,0:T(8,128)(2,1)S(1)}, bf16[160,256]{1,0:T(8,128)(2,1)S(1)}, u32[]{:S(2)}, u32[]{:S(2)}) collective-permute-start(bf16[160,256]{1,0:T(8,128)(2,1)S(1)} %get-tuple-element.165), channel_id=1, source_target_pairs={{0,6},{1,7},{2,4},{3,5},{4,2},{5,3},{6,0},{7,1},{8,14},{9,15},{10,... | collective-permute-start | bytes 245768 | tf_op jit(solution)/shard_map/ppermute | solution.py:804
  41.2 1.6 %next_gradients.1 = (bf16[1152,128]{1,0:T(8,128)(2,1)S(1)}, bf16[1152,128]{1,0:T(8,128)(2,1)S(1)}) custom-call(bf16[1168,128]{1,0:T(8,128)(2,1)S(1)} %get-tuple-element.92.own, bf16[1168,128]{1,0:T(8,128)(2,1)S(1)} %collective-permute-done.partner, bf16[1152,128]{1,0:T(8,128)(2,1)S(1)} %collective-permute-done.7.both_own, ...), custom_call_target="tpu_custom_call" | custom-call | flops 4000000000 | bytes 10000 | tf_op jit(solution)/shard_map/next_gradients/pallas_call | solution.py:624
  42.8 1.1 %collective-permute-start.20 = (bf16[1152,128]{1,0:T(8,128)(2,1)S(1)}, bf16[1152,128]{1,0:T(8,128)(2,1)S(1)}, u32[]{:S(2)}, u32[]{:S(2)}) collective-permute-start(bf16[1152,128]{1,0:T(8,128)(2,1)S(1)} %get-tuple-element.169), channel_id=1, source_target_pairs={{0,1},{1,0},{2,3},{3,2},{4,5},{5,4},{6,7},{7,6},{8,9},{9,8},{10,11... | collective-permute-start | bytes 884744 | tf_op jit(solution)/shard_map/ppermute | solution.py:804
  44.0 2.4 %output.1 = (bf16[128,1024]{1,0:T(8,128)(2,1)}, bf16[128,1152]{1,0:T(8,128)(2,1)}, bf16[1152,128]{1,0:T(8,128)(2,1)}) custom-call(bf16[576,128]{1,0:T(8,128)(2,1)S(1)} %get-tuple-element.159.att_own, bf16[576,256]{1,0:T(8,128)(2,1)S(1)} %collective-permute-done.16.received, bf16[576,128]{1,0:T(8,128)(2,1)S(1)} %get-tuple-element.161.dq_mine, ...), custom_call_target="tpu_custom_call" | custom-call | flops 1000000 | bytes 10000 | tf_op jit(solution)/shard_map/output/pallas_call | solution.py:664
  47.1 1.3 %collective-permute-start.21 = (bf16[160,128]{1,0:T(8,128)(2,1)S(1)}, bf16[160,128]{1,0:T(8,128)(2,1)S(1)}, u32[]{:S(2)}, u32[]{:S(2)}) collective-permute-start(bf16[160,128]{1,0:T(8,128)(2,1)S(1)} %get-tuple-element.175), channel_id=1, source_target_pairs={{0,1},{1,0},{2,3},{3,2},{4,5},{5,4},{6,7},{7,6},{8,9},{9,8},{10,11... | collective-permute-start | bytes 122888 | tf_op jit(solution)/shard_map/ppermute | solution.py:804
  48.5 3.2 %collective-permute-done.21.arrived = bf16[160,128]{1,0:T(8,128)(2,1)S(1)} collective-permute-done((bf16[160,128]{1,0:T(8,128)(2,1)S(1)}, bf16[160,128]{1,0:T(8,128)(2,1)S(1)}, u32[]{:S(2)}, u32[]{:S(2)}) %collective-permute-start.21) | collective-permute-done | bytes 40992 | tf_op jit(solution)/shard_map/ppermute | solution.py:804
  51.7 1.1 %place.1 = (bf16[128,1152]{1,0:T(8,128)(2,1)}, bf16[128,1152]{1,0:T(8,128)(2,1)}, f32[288,128]{1,0:T(8,128)}) custom-call(bf16[1152,128]{1,0:T(8,128)(2,1)S(1)} %get-tuple-element.168.mine, bf16[1152,128]{1,0:T(8,128)(2,1)S(1)} %collective-permute-done.20.theirs, f32[160,128]{1,0:T(8,128)S(1)} %get-tuple-element.174.kept, ...), custom_call_target="tpu_custom_call" | custom-call | flops 1000000 | bytes 10000 | tf_op jit(solution)/shard_map/place/pallas_call | solution.py:716
  (34 shorter events, 5.6 us)
Async XLA Ops:
  0.6 14.0 %copy-start = (bf16[1,128,1024]{2,1,0:T(8,128)(2,1)S(1)}, bf16[1,128,1024]{2,1,0:T(8,128)(2,1)}, u32[]{:S(2)}) copy-start(bf16[1,128,1024]{2,1,0:T(8,128)(2,1)} %param.9) | copy-start | bytes 786436
  2.7 10.1 %collective-permute-start = (bf16[1168,128]{1,0:T(8,128)(2,1)S(1)}, bf16[1168,128]{1,0:T(8,128)(2,1)S(1)}, u32[]{:S(2)}, u32[]{:S(2)}) collective-permute-start(bf16[1168,128]{1,0:T(8,128)(2,1)S(1)} %get-tuple-element.94), channel_id=1, source_target_pairs={{0,1},{1,0},{2,3},{3,2},{4,5},{5,4},{6,7},{7,6},{8,9},{9,8},{10,11... | collective-permute-start | bytes 897032 | tf_op jit(solution)/shard_map/ppermute | solution.py:804
  5.7 10.4 %collective-permute-start.2 = (bf16[128,1024]{1,0:T(8,128)(2,1)}, bf16[128,1024]{1,0:T(8,128)(2,1)S(1)}, u32[]{:S(2)}, u32[]{:S(2)}) collective-permute-start(bf16[128,1024]{1,0:T(8,128)(2,1)} %bitcast.9), channel_id=1, source_target_pairs={{0,8},{8,0},{16,24},{24,16},{1,9},{9,1},{17,25},{25,17},{2,10},{10... | collective-permute-start | bytes 786440 | tf_op jit(solution)/shard_map/ppermute | solution.py:804
  5.8 11.7 %collective-permute-start.1 = (bf16[1168,128]{1,0:T(8,128)(2,1)S(1)}, bf16[1168,128]{1,0:T(8,128)(2,1)S(1)}, u32[]{:S(2)}, u32[]{:S(2)}) collective-permute-start(bf16[1168,128]{1,0:T(8,128)(2,1)S(1)} %get-tuple-element.92.own), channel_id=1, source_target_pairs={{0,2},{1,3},{2,4},{3,5},{4,6},{5,7},{6,0},{7,1},{8,10},{9,11},{10,... | collective-permute-start | bytes 897032 | tf_op jit(solution)/shard_map/ppermute | solution.py:809
  7.3 9.4 %collective-permute-start.3 = (bf16[128,1024]{1,0:T(8,128)(2,1)}, bf16[128,1024]{1,0:T(8,128)(2,1)S(1)}, u32[]{:S(2)}, u32[]{:S(2)}) collective-permute-start(bf16[128,1024]{1,0:T(8,128)(2,1)} %bitcast.10), channel_id=1, source_target_pairs={{0,16},{8,24},{16,0},{24,8},{1,17},{9,25},{17,1},{25,9},{2,18},{10... | collective-permute-start | bytes 786440 | tf_op jit(solution)/shard_map/ppermute | solution.py:804
  12.8 11.9 %collective-permute-start.4 = (bf16[1168,128]{1,0:T(8,128)(2,1)S(1)}, bf16[1168,128]{1,0:T(8,128)(2,1)S(1)}, u32[]{:S(2)}, u32[]{:S(2)}) collective-permute-start(bf16[1168,128]{1,0:T(8,128)(2,1)S(1)} %collective-permute-done.partner), channel_id=1, source_target_pairs={{0,2},{1,3},{2,4},{3,5},{4,6},{5,7},{6,0},{7,1},{8,10},{9,11},{10,... | collective-permute-start | bytes 897032 | tf_op jit(solution)/shard_map/ppermute | solution.py:809
  14.7 8.5 %collective-permute-start.6 = (bf16[128,1024]{1,0:T(8,128)(2,1)S(1)}, bf16[128,1024]{1,0:T(8,128)(2,1)S(1)}, u32[]{:S(2)}, u32[]{:S(2)}) collective-permute-start(bf16[128,1024]{1,0:T(8,128)(2,1)S(1)} %bitcast.12), channel_id=1, source_target_pairs={{0,1},{1,0},{2,3},{3,2},{4,5},{5,4},{6,7},{7,6},{8,9},{9,8},{10,11... | collective-permute-start | bytes 786440 | tf_op jit(solution)/shard_map/ppermute | solution.py:804
  16.2 8.6 %collective-permute-start.5 = (bf16[576,128]{1,0:T(8,128)(2,1)S(1)}, bf16[576,128]{1,0:T(8,128)(2,1)S(1)}, u32[]{:S(2)}, u32[]{:S(2)}) collective-permute-start(bf16[576,128]{1,0:T(8,128)(2,1)S(1)} %get-tuple-element.102), channel_id=1, source_target_pairs={{0,1},{1,0},{2,3},{3,2},{4,5},{5,4},{6,7},{7,6},{8,9},{9,8},{10,11... | collective-permute-start | bytes 442376 | tf_op jit(solution)/shard_map/ppermute | solution.py:804
  17.4 12.5 %collective-permute-start.7 = (bf16[1152,128]{1,0:T(8,128)(2,1)S(1)}, bf16[1152,128]{1,0:T(8,128)(2,1)S(1)}, u32[]{:S(2)}, u32[]{:S(2)}) collective-permute-start(bf16[1152,128]{1,0:T(8,128)(2,1)S(1)} %get-tuple-element.104.both_own), channel_id=1, source_target_pairs={{2,0},{3,1},{4,2},{5,3},{6,4},{7,5},{10,8},{11,9},{12,10},{13,11},... | collective-permute-start | bytes 884744 | tf_op jit(solution)/shard_map/ppermute | solution.py:817
  18.7 9.9 %collective-permute-start.8 = (bf16[128,1024]{1,0:T(8,128)(2,1)S(1)}, bf16[128,1024]{1,0:T(8,128)(2,1)S(1)}, u32[]{:S(2)}, u32[]{:S(2)}) collective-permute-start(bf16[128,1024]{1,0:T(8,128)(2,1)S(1)} %collective-permute-done.3.refs_6_), channel_id=1, source_target_pairs={{0,8},{8,0},{16,24},{24,16},{1,9},{9,1},{17,25},{25,17},{2,10},{10... | collective-permute-start | bytes 786440 | tf_op jit(solution)/shard_map/ppermute | solution.py:804
  23.1 10.8 %collective-permute-start.12 = (bf16[128,1024]{1,0:T(8,128)(2,1)S(1)}, bf16[128,1024]{1,0:T(8,128)(2,1)S(1)}, u32[]{:S(2)}, u32[]{:S(2)}) collective-permute-start(bf16[128,1024]{1,0:T(8,128)(2,1)S(1)} %collective-permute-done.6.cotangent.refs_4_), channel_id=1, source_target_pairs={{0,16},{8,24},{16,0},{24,8},{1,17},{9,25},{17,1},{25,9},{2,18},{10... | collective-permute-start | bytes 786440 | tf_op jit(solution)/shard_map/ppermute | solution.py:804
  26.8 7.1 %collective-permute-start.10 = (bf16[160,256]{1,0:T(8,128)(2,1)S(1)}, bf16[160,256]{1,0:T(8,128)(2,1)S(1)}, u32[]{:S(2)}, u32[]{:S(2)}) collective-permute-start(bf16[160,256]{1,0:T(8,128)(2,1)S(1)} %get-tuple-element.132), channel_id=1, source_target_pairs={{0,16},{8,24},{16,0},{24,8},{1,17},{9,25},{17,1},{25,9},{2,18},{10... | collective-permute-start | bytes 245768 | tf_op jit(solution)/shard_map/ppermute | solution.py:804
  28.6 5.3 %collective-permute-start.11 = (bf16[160,256]{1,0:T(8,128)(2,1)S(1)}, bf16[160,256]{1,0:T(8,128)(2,1)S(1)}, u32[]{:S(2)}, u32[]{:S(2)}) collective-permute-start(bf16[160,256]{1,0:T(8,128)(2,1)S(1)} %get-tuple-element.133), channel_id=1, source_target_pairs={{0,24},{8,16},{16,8},{24,0},{1,25},{9,17},{17,9},{25,1},{2,26},{10... | collective-permute-start | bytes 245768 | tf_op jit(solution)/shard_map/ppermute | solution.py:804
  28.6 5.3 %collective-permute-start.9 = (bf16[160,256]{1,0:T(8,128)(2,1)S(1)}, bf16[160,256]{1,0:T(8,128)(2,1)S(1)}, u32[]{:S(2)}, u32[]{:S(2)}) collective-permute-start(bf16[160,256]{1,0:T(8,128)(2,1)S(1)} %get-tuple-element.131), channel_id=1, source_target_pairs={{0,8},{8,0},{16,24},{24,16},{1,9},{9,1},{17,25},{25,17},{2,10},{10... | collective-permute-start | bytes 245768 | tf_op jit(solution)/shard_map/ppermute | solution.py:804
  29.9 11.3 %collective-permute-start.15 = (bf16[1296,128]{1,0:T(8,128)(2,1)S(1)}, bf16[1296,128]{1,0:T(8,128)(2,1)S(1)}, u32[]{:S(2)}, u32[]{:S(2)}) collective-permute-start(bf16[1296,128]{1,0:T(8,128)(2,1)S(1)} %get-tuple-element.123.both_partner), channel_id=1, source_target_pairs={{0,6},{1,7},{2,0},{3,1},{4,2},{5,3},{6,4},{7,5},{8,14},{9,15},{10,... | collective-permute-start | bytes 995336 | tf_op jit(solution)/shard_map/ppermute | solution.py:809
  33.9 2.4 %collective-permute-start.13 = (bf16[128,1024]{1,0:T(8,128)(2,1)S(1)}, bf16[128,1024]{1,0:T(8,128)(2,1)S(1)}, u32[]{:S(2)}, u32[]{:S(2)}) collective-permute-start(bf16[128,1024]{1,0:T(8,128)(2,1)S(1)} %collective-permute-done.6.cotangent.refs_4_), channel_id=1, source_target_pairs={{0,8},{8,0},{16,24},{24,16},{1,9},{9,1},{17,25},{25,17},{2,10},{10... | collective-permute-start | bytes 786440 | tf_op jit(solution)/shard_map/ppermute | solution.py:804
  34.0 2.3 %collective-permute-start.14 = (bf16[128,1024]{1,0:T(8,128)(2,1)S(1)}, bf16[128,1024]{1,0:T(8,128)(2,1)S(1)}, u32[]{:S(2)}, u32[]{:S(2)}) collective-permute-start(bf16[128,1024]{1,0:T(8,128)(2,1)S(1)} %collective-permute-done.12.refs_6_), channel_id=1, source_target_pairs={{0,8},{8,0},{16,24},{24,16},{1,9},{9,1},{17,25},{25,17},{2,10},{10... | collective-permute-start | bytes 786440 | tf_op jit(solution)/shard_map/ppermute | solution.py:804
  34.5 9.5 %collective-permute-start.16 = (bf16[576,256]{1,0:T(8,128)(2,1)S(1)}, bf16[576,256]{1,0:T(8,128)(2,1)S(1)}, u32[]{:S(2)}, u32[]{:S(2)}) collective-permute-start(bf16[576,256]{1,0:T(8,128)(2,1)S(1)} %get-tuple-element.157), channel_id=1, source_target_pairs={{0,1},{1,0},{2,3},{3,2},{4,5},{5,4},{6,7},{7,6},{8,9},{9,8},{10,11... | collective-permute-start | bytes 884744 | tf_op jit(solution)/shard_map/ppermute | solution.py:804
  36.7 9.7 %collective-permute-start.17 = (bf16[160,256]{1,0:T(8,128)(2,1)S(1)}, bf16[160,256]{1,0:T(8,128)(2,1)S(1)}, u32[]{:S(2)}, u32[]{:S(2)}) collective-permute-start(bf16[160,256]{1,0:T(8,128)(2,1)S(1)} %get-tuple-element.163), channel_id=1, source_target_pairs={{0,2},{1,3},{2,0},{3,1},{4,6},{5,7},{6,4},{7,5},{8,10},{9,11},{10,... | collective-permute-start | bytes 245768 | tf_op jit(solution)/shard_map/ppermute | solution.py:804
  37.5 9.6 %collective-permute-start.18 = (bf16[160,256]{1,0:T(8,128)(2,1)S(1)}, bf16[160,256]{1,0:T(8,128)(2,1)S(1)}, u32[]{:S(2)}, u32[]{:S(2)}) collective-permute-start(bf16[160,256]{1,0:T(8,128)(2,1)S(1)} %get-tuple-element.164), channel_id=1, source_target_pairs={{0,4},{1,5},{2,6},{3,7},{4,0},{5,1},{6,2},{7,3},{8,12},{9,13},{10,... | collective-permute-start | bytes 245768 | tf_op jit(solution)/shard_map/ppermute | solution.py:804
  39.1 8.0 %collective-permute-start.19 = (bf16[160,256]{1,0:T(8,128)(2,1)S(1)}, bf16[160,256]{1,0:T(8,128)(2,1)S(1)}, u32[]{:S(2)}, u32[]{:S(2)}) collective-permute-start(bf16[160,256]{1,0:T(8,128)(2,1)S(1)} %get-tuple-element.165), channel_id=1, source_target_pairs={{0,6},{1,7},{2,4},{3,5},{4,2},{5,3},{6,0},{7,1},{8,14},{9,15},{10,... | collective-permute-start | bytes 245768 | tf_op jit(solution)/shard_map/ppermute | solution.py:804
  42.8 8.8 %collective-permute-start.20 = (bf16[1152,128]{1,0:T(8,128)(2,1)S(1)}, bf16[1152,128]{1,0:T(8,128)(2,1)S(1)}, u32[]{:S(2)}, u32[]{:S(2)}) collective-permute-start(bf16[1152,128]{1,0:T(8,128)(2,1)S(1)} %get-tuple-element.169), channel_id=1, source_target_pairs={{0,1},{1,0},{2,3},{3,2},{4,5},{5,4},{6,7},{7,6},{8,9},{9,8},{10,11... | collective-permute-start | bytes 884744 | tf_op jit(solution)/shard_map/ppermute | solution.py:804
  47.1 4.6 %collective-permute-start.21 = (bf16[160,128]{1,0:T(8,128)(2,1)S(1)}, bf16[160,128]{1,0:T(8,128)(2,1)S(1)}, u32[]{:S(2)}, u32[]{:S(2)}) collective-permute-start(bf16[160,128]{1,0:T(8,128)(2,1)S(1)} %get-tuple-element.175), channel_id=1, source_target_pairs={{0,1},{1,0},{2,3},{3,2},{4,5},{5,4},{6,7},{7,6},{8,9},{9,8},{10,11... | collective-permute-start | bytes 122888 | tf_op jit(solution)/shard_map/ppermute | solution.py:804

commit v6 on v5

--- a/solution.py
+++ b/solution.py
@@ -121,7 +121,7 @@
     return pltpu.roll(value, HDIM, 1)
 
 
-def pack_kernel(clip, query, key, value, swap_kv, own_kv, swap_query, own_query, *scratch):
+def pack_kernel(query, key, value, swap_kv, own_kv, swap_query, own_query, *scratch):
     query_all, key_all, value_all, mixed, single, sems = scratch
     half = my_half()
     pairs = ((key, key_all), (value, value_all), (query, query_all))
@@ -131,12 +131,10 @@
     shared = slice(SHARED, SHARED + PAIR)
     for copy in copies:
         copy.wait()
-    clip_rows = jnp.broadcast_to(clip[...].astype(f32), (CLIP_ROWS, PAIR)).astype(bf16)
     for side, target in ((1 - half, swap_kv), (half, own_kv)):
         for pair in range(PAIRS):
             target[rows_of(pair)] = key_all[:, columns_of(side, pair)]
             target[rows_of(PAIRS + pair)] = value_all[:, columns_of(side, pair)]
-        target[ROWS:] = clip_rows
     key_shared = key_all[:, shared].astype(f32)
     value_shared = value_all[:, shared].astype(f32)
     mixed[0] = low_or_high(key_shared, turned(value_shared)).astype(bf16)
@@ -154,13 +152,13 @@
     swap_query[SHARED:] = low_or_high(theirs[:HDIM], turned(theirs[HDIM:])).astype(bf16)
 
 
-def pack(clip, query, key, value):
+def pack(query, key, value):
     wide = pltpu.VMEM((BLOCK, WIDTH), bf16)
     return kernel(
         pack_kernel,
         "pack",
-        [VMEM, HBM, HBM, HBM],
-        [shaped((ROWS + CLIP_ROWS, PAIR), bf16)] * 2
+        [HBM] * 3,
+        [shaped((ROWS, PAIR), bf16)] * 2
         + [shaped((HALF, PAIR), bf16), shaped((SHARED + PAIR, PAIR), bf16)],
         [
             wide,
@@ -170,7 +168,37 @@
             pltpu.VMEM((2, BLOCK, PAIR), f32),
             pltpu.SemaphoreType.DMA((3,)),
         ],
-    )(clip, in_hbm(query), in_hbm(key), in_hbm(value))
+    )(in_hbm(query), in_hbm(key), in_hbm(value))
+
+
+def label_kernel(clip, own_kv, out):
+    out[:ROWS] = own_kv[...]
+    clip_rows = jnp.broadcast_to(clip[...].astype(f32), (CLIP_ROWS, PAIR))
+    out[ROWS:] = clip_rows.astype(bf16)
+
+
+def label(clip, own_kv):
+    return kernel(
+        label_kernel,
+        "label",
+        [VMEM] * 2,
+        [shaped((ROWS + CLIP_ROWS, PAIR), bf16)],
+    )(clip, own_kv)[0]
+
+
+def label_query_kernel(query, own, halo, out):
+    out[:HALF] = query[...]
+    out[HALF : HALF + CLIP_ROWS] = own[ROWS:]
+    out[HALF + CLIP_ROWS :] = halo[ROWS:]
+
+
+def label_query(query, own, halo):
+    return kernel(
+        label_query_kernel,
+        "label_query",
+        [VMEM] * 3,
+        [shaped((HALF + 2 * CLIP_ROWS, PAIR), bf16)],
+    )(query, own, halo)[0]
 
 
 def unpacked_single(packed):
@@ -237,7 +265,7 @@
     columns = [weight[:, columns_of(half, pair)] for pair in range(PAIRS)]
     pairs = times(rows, jnp.concatenate(columns, axis=1), ((1,), (0,)))
     shared = times(rows, weight[:, SHARED : SHARED + PAIR], ((1,), (0,)))
-    query_single = unpacked_single(query[SHARED:])
+    query_single = unpacked_single(query[SHARED:HALF])
     join_query(both, d_turned, single, query, query_single, pairs, shared)
     d_all[:, at(half, BLOCK)] = d_turned_own[...]
     d_all[:, at(1 - half, BLOCK)] = d_turned[...]
@@ -325,10 +353,11 @@
         query_all[pair, at(half, BLOCK)] = query_own[rows_of(pair)]
         query_all[pair, at(1 - half, BLOCK)] = query_partner[rows_of(pair)]
     query_all[PAIRS, at(half, BLOCK)] = query_own[rows_of(PAIRS)]
-    query_all[PAIRS, at(1 - half, BLOCK)] = unpacked_single(query_partner[SHARED:])
-    for offset, mine, theirs in ((0, halo, halo_other), (2, own, partner)):
-        clips[at(offset + half, CLIP_ROWS)] = mine[ROWS:]
-        clips[at(offset + 1 - half, CLIP_ROWS)] = theirs[ROWS:]
+    query_all[PAIRS, at(1 - half, BLOCK)] = unpacked_single(query_partner[SHARED:HALF])
+    clips[at(half, CLIP_ROWS)] = halo[ROWS:]
+    clips[at(1 - half, CLIP_ROWS)] = query_partner[HALF + CLIP_ROWS :]
+    clips[at(2 + half, CLIP_ROWS)] = own[ROWS:]
+    clips[at(3 - half, CLIP_ROWS)] = query_partner[HALF : HALF + CLIP_ROWS]
 
     def clip_of(block):
         return clips[block * CLIP_ROWS : (block + 1) * CLIP_ROWS].astype(f32)[0:1]
@@ -353,8 +382,8 @@
             shaped((PAIRS + 1, 2 * BLOCK, PAIR), bf16),
             shaped((2, WIN + BLOCK, BLOCK), f32),
             shaped((1, 2 * BLOCK), f32),
+            shaped((4 * CLIP_ROWS, PAIR), bf16),
         ],
-        [pltpu.VMEM((4 * CLIP_ROWS, PAIR), bf16)],
         flops=COST_GATHER,
     )(*sources)
 
@@ -550,13 +579,13 @@
     both_partner,
     own_grads,
     partner_grads,
+    clips,
     mine,
     swap,
     keys_all,
     query_all,
     mask,
     grads,
-    clips,
     stats,
 ):
     half = my_half()
@@ -566,13 +595,11 @@
     for block in range(MIXED + 1):
         grads[block, at(half, BLOCK)] = own_grads[rows_of(block)]
         grads[block, at(1 - half, BLOCK)] = partner_grads[rows_of(block)]
-    clips[at(half, CLIP_ROWS)] = own[ROWS:]
-    clips[at(1 - half, CLIP_ROWS)] = partner[ROWS:]
     present = jnp.where(my_group() < groups - 1, 1.0, 0.0)
     older, every, _ = triangles()
     for query_block, block, shape in ((0, 0, older), (0, 1, every), (1, 1, older)):
         query_clip = stats[CLIP_STAT : CLIP_STAT + 1, rows_of(query_block)]
-        key_clip = clips[block * CLIP_ROWS : (block + 1) * CLIP_ROWS].astype(f32)[0:1]
+        key_clip = clips[(2 + block) * CLIP_ROWS : (3 + block) * CLIP_ROWS].astype(f32)[0:1]
         same = jnp.where(key_clip == query_clip, 1.0, 0.0)
         mask[query_block, rows_of(block)] = shape * same * present
 
@@ -624,14 +651,13 @@
     return kernel(
         functools.partial(next_kernel, groups),
         "next_gradients",
-        [VMEM] * 6,
+        [VMEM] * 7,
         [shaped((ROWS, PAIR), bf16)] * 2,
         [
             pltpu.VMEM((MIXED + 1, 2 * BLOCK, PAIR), bf16),
             pltpu.VMEM((MIXED + 1, 2 * BLOCK, PAIR), bf16),
             pltpu.VMEM((2, 2 * BLOCK, BLOCK), f32),
             pltpu.VMEM((MIXED + 1, 2 * BLOCK, PAIR), f32),
-            pltpu.VMEM((2 * CLIP_ROWS, PAIR), bf16),
             pltpu.VMEM((STAT_ROWS, 2 * BLOCK), f32),
         ],
         flops=COST_NEXT,
@@ -827,10 +853,9 @@
     short = sequences == 4 and groups in (2, 4)
     cotangent = out_cotangent[0]
 
-    swap_kv, own, swap_query, query = pack(
-        block_clip, queries[0], key_states[0], value_states[0]
-    )
-    swap_kv, cot_early = after(swap_kv, cotangent)
+    swap_kv, own_kv, swap_query, query = pack(queries[0], key_states[0], value_states[0])
+    swap_kv, cot_early, clip = after(swap_kv, cotangent, block_clip)
+    own = label(clip, own_kv)
     partner = swapped(swap_kv, "ctx", 1)
     halo = rotated(own, "ctx", 2)
     both_own, d_turned_own, weight = own_cotangents(cotangent, out_weight, query)
@@ -841,12 +866,12 @@
     partner, both_own, swap_query, cot_late = after(partner, both_own, swap_query, cotangent)
     cot_partner = swapped(cot_late, "ctx", 1)
     halo_other = rotated(partner, "ctx", 2)
-    query_partner = swapped(swap_query, "ctx", 1)
+    query_partner = swapped(label_query(swap_query, own, halo), "ctx", 1)
     halo, both_own, *cots = after(halo, both_own, *cots)
     next_own = moved(both_own, "ctx", -2)
     if short:
         cots.append(swapped(cots[2], "dp", 1))
-    keys_all, query_all, mask, clip_row = gathered(
+    keys_all, query_all, mask, clip_row, clips = gathered(
         own, partner, halo, halo_other, query, query_partner
     )
     weights, single, totals, att, att_own, att_swap, *pieces = forward(
@@ -873,13 +898,13 @@
         later = [cot_partner, swapped(cot_partner, "dp", 1), cot_across]
         later.append(swapped(cot_across, "dp", 1))
         products = weight_products(pieces, cots)
-        products, *later = after(products, *later)
+        products, swap = after(products, swap)
         kept, *sent = weight_rest(products, pieces, later, groups)
         arrived = [swapped(part, "ctx", 2 * (n + 1)) for n, part in enumerate(sent)]
         kept, own_grads = after(kept, own_grads)
     received = swapped(swap, "ctx", 1)
     kv_own, kv_swap = next_gradients(
-        groups, own, partner, next_own, next_partner, own_grads, partner_grads
+        groups, own, partner, next_own, next_partner, own_grads, partner_grads, clips
     )
     kv_rest = swapped(kv_swap, "ctx", 1)
     kv_own, received = after(kv_own, received)

time: 53 us -> 52.4 us (0.989)
    ppermute x18, starting transfers between devices: 19.3 us -> 18.7 us  [swapped(): lax.ppermute(value, axis, [(source, source ^ bits) for source in range(co...]
    pallas_call x1 -> x3, Pallas kernels: 1.4 us -> 1.53 us  [the longest x1 1.44 us: pack(): kernel(pack_kernel, 'pack', [HBM] * 3, [shaped((ROWS, PAIR), bf16)] * 2 +...]
  transfers between devices with their start and end apart: 22 -> 22, of which waited for: 7 -> 6; matrix products, arithmetic and copies ran while one was open for 0% -> 0% of each run, Pallas kernels for 22% -> 23%
where the time goes in v6:
time: 52.4 us; the launch traced here: 52.2 us
  starting transfers between devices  25.7 us (49%)
  Pallas kernels  14.3 us (27%)
  waiting for transfers between devices  10.8 us (21%)
  between operations  1.44 us (3%)
    ppermute x18, starting transfers between devices, swapped(): lax.ppermute(value, axis, [(source, source ^ bits) for source in range(co...  18.7 us
    ppermute x18, waiting for transfers between devices, swapped(): lax.ppermute(value, axis, [(source, source ^ bits) for source in range(co...  9.62 us
    ppermute x3, starting transfers between devices, rotated(): lax.ppermute(value, axis, [(source, (source + steps) % count) for source...  5.7 us
    pallas_call x1, Pallas kernels, output_rows(): kernel(output_kernel, 'output', [VMEM] * 4, [shaped((BLOCK, weight.shape[...  2.44 us
    pallas_call x1, Pallas kernels, own_cotangents(): kernel(own_cotangent_kernel, 'own_cotangents', [HBM, HBM, VMEM], [shaped(...  2.24 us
    pallas_call x1, Pallas kernels, forward(): kernel(functools.partial(forward_kernel, pieces_wanted), 'forward', [VMEM...  1.91 us
    pallas_call x1, Pallas kernels, own_gradients(): kernel(own_kernel, 'own_gradients', [VMEM] * 7, [shaped((HALF, BLOCK), bf...  1.83 us
    pallas_call x1, Pallas kernels, next_gradients(): kernel(functools.partial(next_kernel, groups), 'next_gradients', [VMEM] *...  1.65 us
  transfers between devices with their start and end apart: 22, of which 6 were waited for; matrix products, arithmetic and copies ran while one was open for 0% of the time, Pallas kernels for 23%

profile of v6, /device:TPU:0, one launch (start us, length us, event | category | flops | bytes accessed | tf_op | source)
XLA Modules:
  0.0 52.2 jit_solution(129257828527929713)
XLA Ops:
  0.6 1.4 %pack.1 = (bf16[1152,128]{1,0:T(8,128)(2,1)S(1)}, bf16[1152,128]{1,0:T(8,128)(2,1)S(1)}, bf16[576,128]{1,0:T(8,128)(2,1)S(1)}, bf16[640,128]{1,0:T(8,128)(2,1)S(1)}) custom-call(bf16[128,1152]{1,0:T(8,128)(2,1)} %bitcast.14, bf16[128,1152]{1,0:T(8,128)(2,1)} %bitcast.15, bf16[128,1152]{1,0:T(8,128)(2,1)} %bitcast.16), custom_call_target="tpu_custom_call" | custom-call | flops 1000000 | bytes 10000 | tf_op jit(solution)/shard_map/pack/pallas_call | solution.py:157
  2.1 3.0 %collective-permute-start = (bf16[1152,128]{1,0:T(8,128)(2,1)S(1)}, bf16[1152,128]{1,0:T(8,128)(2,1)S(1)}, u32[]{:S(2)}, u32[]{:S(2)}) collective-permute-start(bf16[1152,128]{1,0:T(8,128)(2,1)S(1)} %get-tuple-element.94), channel_id=1, source_target_pairs={{0,1},{1,0},{2,3},{3,2},{4,5},{5,4},{6,7},{7,6},{8,9},{9,8},{10,11... | collective-permute-start | bytes 884744 | tf_op jit(solution)/shard_map/ppermute | solution.py:830
  5.8 1.6 %collective-permute-start.1 = (bf16[1168,128]{1,0:T(8,128)(2,1)S(1)}, bf16[1168,128]{1,0:T(8,128)(2,1)S(1)}, u32[]{:S(2)}, u32[]{:S(2)}) collective-permute-start(bf16[1168,128]{1,0:T(8,128)(2,1)S(1)} %label.1.own), channel_id=1, source_target_pairs={{0,2},{1,3},{2,4},{3,5},{4,6},{5,7},{6,0},{7,1},{8,10},{9,11},{10,... | collective-permute-start | bytes 897032 | tf_op jit(solution)/shard_map/ppermute | solution.py:835
  7.4 1.5 %collective-permute-start.3 = (bf16[128,1024]{1,0:T(8,128)(2,1)}, bf16[128,1024]{1,0:T(8,128)(2,1)S(1)}, u32[]{:S(2)}, u32[]{:S(2)}) collective-permute-start(bf16[128,1024]{1,0:T(8,128)(2,1)} %bitcast.10), channel_id=1, source_target_pairs={{0,16},{8,24},{16,0},{24,8},{1,17},{9,25},{17,1},{25,9},{2,18},{10... | collective-permute-start | bytes 786440 | tf_op jit(solution)/shard_map/ppermute | solution.py:830
  8.9 2.2 %own_cotangents.1 = (bf16[1152,128]{1,0:T(8,128)(2,1)S(1)}, bf16[576,128]{1,0:T(8,128)(2,1)S(1)}, bf16[1024,1152]{1,0:T(8,128)(2,1)S(1)}) custom-call(bf16[128,1024]{1,0:T(8,128)(2,1)} %bitcast.11, bf16[1024,1152]{1,0:T(8,128)(2,1)} %weight.1, bf16[640,128]{1,0:T(8,128)(2,1)S(1)} %get-tuple-element.95.query.query_own), custom_call_target="tpu_custom_call" | custom-call | flops 1000000 | bytes 10000 | tf_op jit(solution)/shard_map/own_cotangents/pallas_call | solution.py:247
  12.1 1.8 %collective-permute-start.4 = (bf16[1152,128]{1,0:T(8,128)(2,1)S(1)}, bf16[1152,128]{1,0:T(8,128)(2,1)S(1)}, u32[]{:S(2)}, u32[]{:S(2)}) collective-permute-start(bf16[1152,128]{1,0:T(8,128)(2,1)S(1)} %collective-permute-done.partner), channel_id=1, source_target_pairs={{0,2},{1,3},{2,4},{3,5},{4,6},{5,7},{6,0},{7,1},{8,10},{9,11},{10,... | collective-permute-start | bytes 884744 | tf_op jit(solution)/shard_map/ppermute | solution.py:835
  13.9 1.5 %collective-permute-start.6 = (bf16[128,1024]{1,0:T(8,128)(2,1)S(1)}, bf16[128,1024]{1,0:T(8,128)(2,1)S(1)}, u32[]{:S(2)}, u32[]{:S(2)}) collective-permute-start(bf16[128,1024]{1,0:T(8,128)(2,1)S(1)} %bitcast.12), channel_id=1, source_target_pairs={{0,1},{1,0},{2,3},{3,2},{4,5},{5,4},{6,7},{7,6},{8,9},{9,8},{10,11... | collective-permute-start | bytes 786440 | tf_op jit(solution)/shard_map/ppermute | solution.py:830
  15.4 1.2 %collective-permute-done.1.halo = bf16[1168,128]{1,0:T(8,128)(2,1)S(1)} collective-permute-done((bf16[1168,128]{1,0:T(8,128)(2,1)S(1)}, bf16[1168,128]{1,0:T(8,128)(2,1)S(1)}, u32[]{:S(2)}, u32[]{:S(2)}) %collective-permute-start.1) | collective-permute-done | bytes 299040 | tf_op jit(solution)/shard_map/ppermute | solution.py:835
  16.9 1.3 %collective-permute-start.7 = (bf16[1152,128]{1,0:T(8,128)(2,1)S(1)}, bf16[1152,128]{1,0:T(8,128)(2,1)S(1)}, u32[]{:S(2)}, u32[]{:S(2)}) collective-permute-start(bf16[1152,128]{1,0:T(8,128)(2,1)S(1)} %get-tuple-element.104.both_own), channel_id=1, source_target_pairs={{2,0},{3,1},{4,2},{5,3},{6,4},{7,5},{10,8},{11,9},{12,10},{13,11},... | collective-permute-start | bytes 884744 | tf_op jit(solution)/shard_map/ppermute | solution.py:843
  18.2 4.4 %collective-permute-done.6.cotangent.refs_4_ = bf16[128,1024]{1,0:T(8,128)(2,1)S(1)} collective-permute-done((bf16[128,1024]{1,0:T(8,128)(2,1)S(1)}, bf16[128,1024]{1,0:T(8,128)(2,1)S(1)}, u32[]{:S(2)}, u32[]{:S(2)}) %collective-permute-start.6) | collective-permute-done | bytes 262176 | tf_op jit(solution)/shard_map/ppermute | solution.py:830
  22.6 1.4 %collective-permute-start.12 = (bf16[128,1024]{1,0:T(8,128)(2,1)S(1)}, bf16[128,1024]{1,0:T(8,128)(2,1)S(1)}, u32[]{:S(2)}, u32[]{:S(2)}) collective-permute-start(bf16[128,1024]{1,0:T(8,128)(2,1)S(1)} %collective-permute-done.6.cotangent.refs_4_), channel_id=1, source_target_pairs={{0,16},{8,24},{16,0},{24,8},{1,17},{9,25},{17,1},{25,9},{2,18},{10... | collective-permute-start | bytes 786440 | tf_op jit(solution)/shard_map/ppermute | solution.py:830
  24.5 1.9 %forward.1 = (bf16[4,2,384,256]{3,2,1,0:T(8,128)(2,1)S(1)}, bf16[2,384,128]{2,1,0:T(8,128)(2,1)S(1)}, f32[24,256]{1,0:T(8,128)S(1)}, bf16[608,256]{1,0:T(8,128)(...) custom-call(bf16[9,512,128]{2,1,0:T(8,128)(2,1)S(1)} %get-tuple-elem, ...), custom_call_target="tpu_custom_call" | custom-call | flops 1000000 | bytes 10000 | tf_op jit(solution)/shard_map/forward/pallas_call | solution.py:466
  26.4 1.4 %collective-permute-start.10 = (bf16[160,256]{1,0:T(8,128)(2,1)S(1)}, bf16[160,256]{1,0:T(8,128)(2,1)S(1)}, u32[]{:S(2)}, u32[]{:S(2)}) collective-permute-start(bf16[160,256]{1,0:T(8,128)(2,1)S(1)} %get-tuple-element.132), channel_id=1, source_target_pairs={{0,16},{8,24},{16,0},{24,8},{1,17},{9,25},{17,1},{25,9},{2,18},{10... | collective-permute-start | bytes 245768 | tf_op jit(solution)/shard_map/ppermute | solution.py:830
  29.3 2.3 %collective-permute-start.15 = (bf16[1296,128]{1,0:T(8,128)(2,1)S(1)}, bf16[1296,128]{1,0:T(8,128)(2,1)S(1)}, u32[]{:S(2)}, u32[]{:S(2)}) collective-permute-start(bf16[1296,128]{1,0:T(8,128)(2,1)S(1)} %get-tuple-element.123.both_partner), channel_id=1, source_target_pairs={{0,6},{1,7},{2,0},{3,1},{4,2},{5,3},{6,4},{7,5},{8,14},{9,15},{10,... | collective-permute-start | bytes 995336 | tf_op jit(solution)/shard_map/ppermute | solution.py:835
  31.6 1.8 %own_gradients.1 = (bf16[576,128]{1,0:T(8,128)(2,1)S(1)}, bf16[576,256]{1,0:T(8,128)(2,1)S(1)}, f32[1152,128]{1,0:T(8,128)S(1)}, f32[1152,128]{1,0:T(8,128)S(1)}) custom-call(bf16[9,512,128]{2,1,0:T(8,128)(2,1)S(1)} %get-tuple-element.103.keys_all, bf16[1152,128]{1,0:T(8,128)(2,1)S(1)} %get-tuple-element.104.both_own, ...), custom_call_target="tpu_custom_call" | custom-call | flops 1000000 | bytes 10000 | tf_op jit(solution)/shard_map/own_gradients/pallas_call | solution.py:560
  34.4 1.4 %collective-permute-start.16 = (bf16[576,256]{1,0:T(8,128)(2,1)S(1)}, bf16[576,256]{1,0:T(8,128)(2,1)S(1)}, u32[]{:S(2)}, u32[]{:S(2)}) collective-permute-start(bf16[576,256]{1,0:T(8,128)(2,1)S(1)} %get-tuple-element.155), channel_id=1, source_target_pairs={{0,1},{1,0},{2,3},{3,2},{4,5},{5,4},{6,7},{7,6},{8,9},{9,8},{10,11... | collective-permute-start | bytes 884744 | tf_op jit(solution)/shard_map/ppermute | solution.py:830
  37.0 1.6 %collective-permute-start.18 = (bf16[160,256]{1,0:T(8,128)(2,1)S(1)}, bf16[160,256]{1,0:T(8,128)(2,1)S(1)}, u32[]{:S(2)}, u32[]{:S(2)}) collective-permute-start(bf16[160,256]{1,0:T(8,128)(2,1)S(1)} %get-tuple-element.162), channel_id=1, source_target_pairs={{0,4},{1,5},{2,6},{3,7},{4,0},{5,1},{6,2},{7,3},{8,12},{9,13},{10,... | collective-permute-start | bytes 245768 | tf_op jit(solution)/shard_map/ppermute | solution.py:830
  38.6 2.1 %collective-permute-start.19 = (bf16[160,256]{1,0:T(8,128)(2,1)S(1)}, bf16[160,256]{1,0:T(8,128)(2,1)S(1)}, u32[]{:S(2)}, u32[]{:S(2)}) collective-permute-start(bf16[160,256]{1,0:T(8,128)(2,1)S(1)} %get-tuple-element.163), channel_id=1, source_target_pairs={{0,6},{1,7},{2,4},{3,5},{4,2},{5,3},{6,0},{7,1},{8,14},{9,15},{10,... | collective-permute-start | bytes 245768 | tf_op jit(solution)/shard_map/ppermute | solution.py:830
  40.7 1.6 %next_gradients.1 = (bf16[1152,128]{1,0:T(8,128)(2,1)S(1)}, bf16[1152,128]{1,0:T(8,128)(2,1)S(1)}) custom-call(bf16[1168,128]{1,0:T(8,128)(2,1)S(1)} %label.1.own, bf16[1152,128]{1,0:T(8,128)(2,1)S(1)} %collective-permute-done.partner, bf16[1152,128]{1,0:T(8,128)(2,1)S(1)} %collective-permute-done.7.both_own, ...), custom_call_target="tpu_custom_call" | custom-call | flops 4000000000 | bytes 10000 | tf_op jit(solution)/shard_map/next_gradients/pallas_call | solution.py:651
  42.3 1.0 %collective-permute-start.20 = (bf16[1152,128]{1,0:T(8,128)(2,1)S(1)}, bf16[1152,128]{1,0:T(8,128)(2,1)S(1)}, u32[]{:S(2)}, u32[]{:S(2)}) collective-permute-start(bf16[1152,128]{1,0:T(8,128)(2,1)S(1)} %get-tuple-element.167), channel_id=1, source_target_pairs={{0,1},{1,0},{2,3},{3,2},{4,5},{5,4},{6,7},{7,6},{8,9},{9,8},{10,11... | collective-permute-start | bytes 884744 | tf_op jit(solution)/shard_map/ppermute | solution.py:830
  43.4 2.4 %output.1 = (bf16[128,1024]{1,0:T(8,128)(2,1)}, bf16[128,1152]{1,0:T(8,128)(2,1)}, bf16[1152,128]{1,0:T(8,128)(2,1)}) custom-call(bf16[576,128]{1,0:T(8,128)(2,1)S(1)} %get-tuple-element.157.att_own, bf16[576,256]{1,0:T(8,128)(2,1)S(1)} %collective-permute-done.16.received, bf16[576,128]{1,0:T(8,128)(2,1)S(1)} %get-tuple-element.159.dq_mine, ...), custom_call_target="tpu_custom_call" | custom-call | flops 1000000 | bytes 10000 | tf_op jit(solution)/shard_map/output/pallas_call | solution.py:690
  46.6 1.3 %collective-permute-start.21 = (bf16[160,128]{1,0:T(8,128)(2,1)S(1)}, bf16[160,128]{1,0:T(8,128)(2,1)S(1)}, u32[]{:S(2)}, u32[]{:S(2)}) collective-permute-start(bf16[160,128]{1,0:T(8,128)(2,1)S(1)} %get-tuple-element.173), channel_id=1, source_target_pairs={{0,1},{1,0},{2,3},{3,2},{4,5},{5,4},{6,7},{7,6},{8,9},{9,8},{10,11... | collective-permute-start | bytes 122888 | tf_op jit(solution)/shard_map/ppermute | solution.py:830
  47.9 3.3 %collective-permute-done.21.arrived = bf16[160,128]{1,0:T(8,128)(2,1)S(1)} collective-permute-done((bf16[160,128]{1,0:T(8,128)(2,1)S(1)}, bf16[160,128]{1,0:T(8,128)(2,1)S(1)}, u32[]{:S(2)}, u32[]{:S(2)}) %collective-permute-start.21) | collective-permute-done | bytes 40992 | tf_op jit(solution)/shard_map/ppermute | solution.py:830
  51.1 1.1 %place.1 = (bf16[128,1152]{1,0:T(8,128)(2,1)}, bf16[128,1152]{1,0:T(8,128)(2,1)}, f32[288,128]{1,0:T(8,128)}) custom-call(bf16[1152,128]{1,0:T(8,128)(2,1)S(1)} %get-tuple-element.166.mine, bf16[1152,128]{1,0:T(8,128)(2,1)S(1)} %collective-permute-done.20.theirs, f32[160,128]{1,0:T(8,128)S(1)} %get-tuple-element.172.kept, ...), custom_call_target="tpu_custom_call" | custom-call | flops 1000000 | bytes 10000 | tf_op jit(solution)/shard_map/place/pallas_call | solution.py:742
  (36 shorter events, 6.1 us)
Async XLA Ops:
  0.6 13.3 %copy-start = (bf16[1,128,1024]{2,1,0:T(8,128)(2,1)S(1)}, bf16[1,128,1024]{2,1,0:T(8,128)(2,1)}, u32[]{:S(2)}) copy-start(bf16[1,128,1024]{2,1,0:T(8,128)(2,1)} %param.9) | copy-start | bytes 786436
  2.1 10.0 %collective-permute-start = (bf16[1152,128]{1,0:T(8,128)(2,1)S(1)}, bf16[1152,128]{1,0:T(8,128)(2,1)S(1)}, u32[]{:S(2)}, u32[]{:S(2)}) collective-permute-start(bf16[1152,128]{1,0:T(8,128)(2,1)S(1)} %get-tuple-element.94), channel_id=1, source_target_pairs={{0,1},{1,0},{2,3},{3,2},{4,5},{5,4},{6,7},{7,6},{8,9},{9,8},{10,11... | collective-permute-start | bytes 884744 | tf_op jit(solution)/shard_map/ppermute | solution.py:830
  5.8 10.8 %collective-permute-start.1 = (bf16[1168,128]{1,0:T(8,128)(2,1)S(1)}, bf16[1168,128]{1,0:T(8,128)(2,1)S(1)}, u32[]{:S(2)}, u32[]{:S(2)}) collective-permute-start(bf16[1168,128]{1,0:T(8,128)(2,1)S(1)} %label.1.own), channel_id=1, source_target_pairs={{0,2},{1,3},{2,4},{3,5},{4,6},{5,7},{6,0},{7,1},{8,10},{9,11},{10,... | collective-permute-start | bytes 897032 | tf_op jit(solution)/shard_map/ppermute | solution.py:835
  7.4 9.5 %collective-permute-start.2 = (bf16[128,1024]{1,0:T(8,128)(2,1)}, bf16[128,1024]{1,0:T(8,128)(2,1)S(1)}, u32[]{:S(2)}, u32[]{:S(2)}) collective-permute-start(bf16[128,1024]{1,0:T(8,128)(2,1)} %bitcast.9), channel_id=1, source_target_pairs={{0,8},{8,0},{16,24},{24,16},{1,9},{9,1},{17,25},{25,17},{2,10},{10... | collective-permute-start | bytes 786440 | tf_op jit(solution)/shard_map/ppermute | solution.py:830
  7.4 9.5 %collective-permute-start.3 = (bf16[128,1024]{1,0:T(8,128)(2,1)}, bf16[128,1024]{1,0:T(8,128)(2,1)S(1)}, u32[]{:S(2)}, u32[]{:S(2)}) collective-permute-start(bf16[128,1024]{1,0:T(8,128)(2,1)} %bitcast.10), channel_id=1, source_target_pairs={{0,16},{8,24},{16,0},{24,8},{1,17},{9,25},{17,1},{25,9},{2,18},{10... | collective-permute-start | bytes 786440 | tf_op jit(solution)/shard_map/ppermute | solution.py:830
  12.1 12.2 %collective-permute-start.4 = (bf16[1152,128]{1,0:T(8,128)(2,1)S(1)}, bf16[1152,128]{1,0:T(8,128)(2,1)S(1)}, u32[]{:S(2)}, u32[]{:S(2)}) collective-permute-start(bf16[1152,128]{1,0:T(8,128)(2,1)S(1)} %collective-permute-done.partner), channel_id=1, source_target_pairs={{0,2},{1,3},{2,4},{3,5},{4,6},{5,7},{6,0},{7,1},{8,10},{9,11},{10,... | collective-permute-start | bytes 884744 | tf_op jit(solution)/shard_map/ppermute | solution.py:835
  13.9 8.7 %collective-permute-start.6 = (bf16[128,1024]{1,0:T(8,128)(2,1)S(1)}, bf16[128,1024]{1,0:T(8,128)(2,1)S(1)}, u32[]{:S(2)}, u32[]{:S(2)}) collective-permute-start(bf16[128,1024]{1,0:T(8,128)(2,1)S(1)} %bitcast.12), channel_id=1, source_target_pairs={{0,1},{1,0},{2,3},{3,2},{4,5},{5,4},{6,7},{7,6},{8,9},{9,8},{10,11... | collective-permute-start | bytes 786440 | tf_op jit(solution)/shard_map/ppermute | solution.py:830
  16.6 7.7 %collective-permute-start.5 = (bf16[608,128]{1,0:T(8,128)(2,1)S(1)}, bf16[608,128]{1,0:T(8,128)(2,1)S(1)}, u32[]{:S(2)}, u32[]{:S(2)}) collective-permute-start(bf16[608,128]{1,0:T(8,128)(2,1)S(1)} %label_query.1), channel_id=1, source_target_pairs={{0,1},{1,0},{2,3},{3,2},{4,5},{5,4},{6,7},{7,6},{8,9},{9,8},{10,11... | collective-permute-start | bytes 466952 | tf_op jit(solution)/shard_map/ppermute | solution.py:830
  16.9 12.4 %collective-permute-start.7 = (bf16[1152,128]{1,0:T(8,128)(2,1)S(1)}, bf16[1152,128]{1,0:T(8,128)(2,1)S(1)}, u32[]{:S(2)}, u32[]{:S(2)}) collective-permute-start(bf16[1152,128]{1,0:T(8,128)(2,1)S(1)} %get-tuple-element.104.both_own), channel_id=1, source_target_pairs={{2,0},{3,1},{4,2},{5,3},{6,4},{7,5},{10,8},{11,9},{12,10},{13,11},... | collective-permute-start | bytes 884744 | tf_op jit(solution)/shard_map/ppermute | solution.py:843
  18.2 9.7 %collective-permute-start.8 = (bf16[128,1024]{1,0:T(8,128)(2,1)S(1)}, bf16[128,1024]{1,0:T(8,128)(2,1)S(1)}, u32[]{:S(2)}, u32[]{:S(2)}) collective-permute-start(bf16[128,1024]{1,0:T(8,128)(2,1)S(1)} %collective-permute-done.3.refs_6_), channel_id=1, source_target_pairs={{0,8},{8,0},{16,24},{24,16},{1,9},{9,1},{17,25},{25,17},{2,10},{10... | collective-permute-start | bytes 786440 | tf_op jit(solution)/shard_map/ppermute | solution.py:830
  22.6 10.8 %collective-permute-start.12 = (bf16[128,1024]{1,0:T(8,128)(2,1)S(1)}, bf16[128,1024]{1,0:T(8,128)(2,1)S(1)}, u32[]{:S(2)}, u32[]{:S(2)}) collective-permute-start(bf16[128,1024]{1,0:T(8,128)(2,1)S(1)} %collective-permute-done.6.cotangent.refs_4_), channel_id=1, source_target_pairs={{0,16},{8,24},{16,0},{24,8},{1,17},{9,25},{17,1},{25,9},{2,18},{10... | collective-permute-start | bytes 786440 | tf_op jit(solution)/shard_map/ppermute | solution.py:830
  26.4 7.0 %collective-permute-start.10 = (bf16[160,256]{1,0:T(8,128)(2,1)S(1)}, bf16[160,256]{1,0:T(8,128)(2,1)S(1)}, u32[]{:S(2)}, u32[]{:S(2)}) collective-permute-start(bf16[160,256]{1,0:T(8,128)(2,1)S(1)} %get-tuple-element.132), channel_id=1, source_target_pairs={{0,16},{8,24},{16,0},{24,8},{1,17},{9,25},{17,1},{25,9},{2,18},{10... | collective-permute-start | bytes 245768 | tf_op jit(solution)/shard_map/ppermute | solution.py:830
  27.8 5.6 %collective-permute-start.11 = (bf16[160,256]{1,0:T(8,128)(2,1)S(1)}, bf16[160,256]{1,0:T(8,128)(2,1)S(1)}, u32[]{:S(2)}, u32[]{:S(2)}) collective-permute-start(bf16[160,256]{1,0:T(8,128)(2,1)S(1)} %get-tuple-element.133), channel_id=1, source_target_pairs={{0,24},{8,16},{16,8},{24,0},{1,25},{9,17},{17,9},{25,1},{2,26},{10... | collective-permute-start | bytes 245768 | tf_op jit(solution)/shard_map/ppermute | solution.py:830
  27.8 5.6 %collective-permute-start.9 = (bf16[160,256]{1,0:T(8,128)(2,1)S(1)}, bf16[160,256]{1,0:T(8,128)(2,1)S(1)}, u32[]{:S(2)}, u32[]{:S(2)}) collective-permute-start(bf16[160,256]{1,0:T(8,128)(2,1)S(1)} %get-tuple-element.131), channel_id=1, source_target_pairs={{0,8},{8,0},{16,24},{24,16},{1,9},{9,1},{17,25},{25,17},{2,10},{10... | collective-permute-start | bytes 245768 | tf_op jit(solution)/shard_map/ppermute | solution.py:830
  29.3 11.4 %collective-permute-start.15 = (bf16[1296,128]{1,0:T(8,128)(2,1)S(1)}, bf16[1296,128]{1,0:T(8,128)(2,1)S(1)}, u32[]{:S(2)}, u32[]{:S(2)}) collective-permute-start(bf16[1296,128]{1,0:T(8,128)(2,1)S(1)} %get-tuple-element.123.both_partner), channel_id=1, source_target_pairs={{0,6},{1,7},{2,0},{3,1},{4,2},{5,3},{6,4},{7,5},{8,14},{9,15},{10,... | collective-permute-start | bytes 995336 | tf_op jit(solution)/shard_map/ppermute | solution.py:835
  33.4 2.4 %collective-permute-start.13 = (bf16[128,1024]{1,0:T(8,128)(2,1)S(1)}, bf16[128,1024]{1,0:T(8,128)(2,1)S(1)}, u32[]{:S(2)}, u32[]{:S(2)}) collective-permute-start(bf16[128,1024]{1,0:T(8,128)(2,1)S(1)} %collective-permute-done.6.cotangent.refs_4_), channel_id=1, source_target_pairs={{0,8},{8,0},{16,24},{24,16},{1,9},{9,1},{17,25},{25,17},{2,10},{10... | collective-permute-start | bytes 786440 | tf_op jit(solution)/shard_map/ppermute | solution.py:830
  33.5 2.3 %collective-permute-start.14 = (bf16[128,1024]{1,0:T(8,128)(2,1)S(1)}, bf16[128,1024]{1,0:T(8,128)(2,1)S(1)}, u32[]{:S(2)}, u32[]{:S(2)}) collective-permute-start(bf16[128,1024]{1,0:T(8,128)(2,1)S(1)} %collective-permute-done.12.refs_6_), channel_id=1, source_target_pairs={{0,8},{8,0},{16,24},{24,16},{1,9},{9,1},{17,25},{25,17},{2,10},{10... | collective-permute-start | bytes 786440 | tf_op jit(solution)/shard_map/ppermute | solution.py:830
  34.4 9.1 %collective-permute-start.16 = (bf16[576,256]{1,0:T(8,128)(2,1)S(1)}, bf16[576,256]{1,0:T(8,128)(2,1)S(1)}, u32[]{:S(2)}, u32[]{:S(2)}) collective-permute-start(bf16[576,256]{1,0:T(8,128)(2,1)S(1)} %get-tuple-element.155), channel_id=1, source_target_pairs={{0,1},{1,0},{2,3},{3,2},{4,5},{5,4},{6,7},{7,6},{8,9},{9,8},{10,11... | collective-permute-start | bytes 884744 | tf_op jit(solution)/shard_map/ppermute | solution.py:830
  36.2 9.6 %collective-permute-start.17 = (bf16[160,256]{1,0:T(8,128)(2,1)S(1)}, bf16[160,256]{1,0:T(8,128)(2,1)S(1)}, u32[]{:S(2)}, u32[]{:S(2)}) collective-permute-start(bf16[160,256]{1,0:T(8,128)(2,1)S(1)} %get-tuple-element.161), channel_id=1, source_target_pairs={{0,2},{1,3},{2,0},{3,1},{4,6},{5,7},{6,4},{7,5},{8,10},{9,11},{10,... | collective-permute-start | bytes 245768 | tf_op jit(solution)/shard_map/ppermute | solution.py:830
  37.0 9.6 %collective-permute-start.18 = (bf16[160,256]{1,0:T(8,128)(2,1)S(1)}, bf16[160,256]{1,0:T(8,128)(2,1)S(1)}, u32[]{:S(2)}, u32[]{:S(2)}) collective-permute-start(bf16[160,256]{1,0:T(8,128)(2,1)S(1)} %get-tuple-element.162), channel_id=1, source_target_pairs={{0,4},{1,5},{2,6},{3,7},{4,0},{5,1},{6,2},{7,3},{8,12},{9,13},{10,... | collective-permute-start | bytes 245768 | tf_op jit(solution)/shard_map/ppermute | solution.py:830
  38.6 7.9 %collective-permute-start.19 = (bf16[160,256]{1,0:T(8,128)(2,1)S(1)}, bf16[160,256]{1,0:T(8,128)(2,1)S(1)}, u32[]{:S(2)}, u32[]{:S(2)}) collective-permute-start(bf16[160,256]{1,0:T(8,128)(2,1)S(1)} %get-tuple-element.163), channel_id=1, source_target_pairs={{0,6},{1,7},{2,4},{3,5},{4,2},{5,3},{6,0},{7,1},{8,14},{9,15},{10,... | collective-permute-start | bytes 245768 | tf_op jit(solution)/shard_map/ppermute | solution.py:830
  42.3 8.8 %collective-permute-start.20 = (bf16[1152,128]{1,0:T(8,128)(2,1)S(1)}, bf16[1152,128]{1,0:T(8,128)(2,1)S(1)}, u32[]{:S(2)}, u32[]{:S(2)}) collective-permute-start(bf16[1152,128]{1,0:T(8,128)(2,1)S(1)} %get-tuple-element.167), channel_id=1, source_target_pairs={{0,1},{1,0},{2,3},{3,2},{4,5},{5,4},{6,7},{7,6},{8,9},{9,8},{10,11... | collective-permute-start | bytes 884744 | tf_op jit(solution)/shard_map/ppermute | solution.py:830
  46.6 4.5 %collective-permute-start.21 = (bf16[160,128]{1,0:T(8,128)(2,1)S(1)}, bf16[160,128]{1,0:T(8,128)(2,1)S(1)}, u32[]{:S(2)}, u32[]{:S(2)}) collective-permute-start(bf16[160,128]{1,0:T(8,128)(2,1)S(1)} %get-tuple-element.173), channel_id=1, source_target_pairs={{0,1},{1,0},{2,3},{3,2},{4,5},{5,4},{6,7},{7,6},{8,9},{9,8},{10,11... | collective-permute-start | bytes 122888 | tf_op jit(solution)/shard_map/ppermute | solution.py:830

commit v7 on v6

--- a/solution.py
+++ b/solution.py
@@ -37,7 +37,7 @@
 SENT_ROWS = ROWS + 6 * STAT_ROWS
 CHUNKS = 4
 SCALING = 1.0 / math.sqrt(HDIM)
-COST_GATHER = 2_000_000_000
+COST_GATHER = 1_500_000_000
 COST_KEYS = 1_000_000
 COST_FIRST = 2_000_000_000
 COST_NEXT = 4_000_000_000

time: 52.4 us -> 52.4 us (level)
    ppermute x18, waiting for transfers between devices: 9.62 us -> 8.12 us  [swapped(): lax.ppermute(value, axis, [(source, source ^ bits) for source in range(co...]
    ppermute x18, starting transfers between devices: 18.7 us -> 19.5 us  [swapped(): lax.ppermute(value, axis, [(source, source ^ bits) for source in range(co...]
    ppermute x1, waiting for transfers between devices: 0.01 us -> 0.71 us  [moved(): lax.ppermute(value, axis, [(source, source + steps) for source in range(f...]
    ppermute x3, waiting for transfers between devices: 1.16 us -> 1.86 us  [rotated(): lax.ppermute(value, axis, [(source, (source + steps) % count) for source...]
    ppermute x3, starting transfers between devices: 5.7 us -> 5 us  [rotated(): lax.ppermute(value, axis, [(source, (source + steps) % count) for source...]
  transfers between devices with their start and end apart: 22 -> 22, of which waited for: 6 -> 8; matrix products, arithmetic and copies ran while one was open for 0% -> 0% of each run, Pallas kernels for 23% -> 23%
where the time goes in v7:
time: 52.4 us; the launch traced here: 52.2 us
  starting transfers between devices  25.8 us (49%)
  Pallas kernels  14.3 us (27%)
  waiting for transfers between devices  10.7 us (20%)
  between operations  1.46 us (3%)
    ppermute x18, starting transfers between devices, swapped(): lax.ppermute(value, axis, [(source, source ^ bits) for source in range(co...  19.5 us
    ppermute x18, waiting for transfers between devices, swapped(): lax.ppermute(value, axis, [(source, source ^ bits) for source in range(co...  8.12 us
    ppermute x3, starting transfers between devices, rotated(): lax.ppermute(value, axis, [(source, (source + steps) % count) for source...  5 us
    pallas_call x1, Pallas kernels, output_rows(): kernel(output_kernel, 'output', [VMEM] * 4, [shaped((BLOCK, weight.shape[...  2.44 us
    pallas_call x1, Pallas kernels, own_cotangents(): kernel(own_cotangent_kernel, 'own_cotangents', [HBM, HBM, VMEM], [shaped(...  2.24 us
    pallas_call x1, Pallas kernels, forward(): kernel(functools.partial(forward_kernel, pieces_wanted), 'forward', [VMEM...  1.9 us
    ppermute x3, waiting for transfers between devices, rotated(): lax.ppermute(value, axis, [(source, (source + steps) % count) for source...  1.86 us
    pallas_call x1, Pallas kernels, own_gradients(): kernel(own_kernel, 'own_gradients', [VMEM] * 7, [shaped((HALF, BLOCK), bf...  1.82 us
  transfers between devices with their start and end apart: 22, of which 8 were waited for; matrix products, arithmetic and copies ran while one was open for 0% of the time, Pallas kernels for 23%

profile of v7, /device:TPU:0, one launch (start us, length us, event | category | flops | bytes accessed | tf_op | source)
XLA Modules:
  0.0 52.2 jit_solution(16595596924403696684)
XLA Ops:
  0.6 1.4 %pack.1 = (bf16[1152,128]{1,0:T(8,128)(2,1)S(1)}, bf16[1152,128]{1,0:T(8,128)(2,1)S(1)}, bf16[576,128]{1,0:T(8,128)(2,1)S(1)}, bf16[640,128]{1,0:T(8,128)(2,1)S(1)}) custom-call(bf16[128,1152]{1,0:T(8,128)(2,1)} %bitcast.14, bf16[128,1152]{1,0:T(8,128)(2,1)} %bitcast.15, bf16[128,1152]{1,0:T(8,128)(2,1)} %bitcast.16), custom_call_target="tpu_custom_call" | custom-call | flops 1000000 | bytes 10000 | tf_op jit(solution)/shard_map/pack/pallas_call | solution.py:157
  2.1 3.0 %collective-permute-start = (bf16[1152,128]{1,0:T(8,128)(2,1)S(1)}, bf16[1152,128]{1,0:T(8,128)(2,1)S(1)}, u32[]{:S(2)}, u32[]{:S(2)}) collective-permute-start(bf16[1152,128]{1,0:T(8,128)(2,1)S(1)} %get-tuple-element.94), channel_id=1, source_target_pairs={{0,1},{1,0},{2,3},{3,2},{4,5},{5,4},{6,7},{7,6},{8,9},{9,8},{10,11... | collective-permute-start | bytes 884744 | tf_op jit(solution)/shard_map/ppermute | solution.py:830
  5.8 1.6 %collective-permute-start.1 = (bf16[1168,128]{1,0:T(8,128)(2,1)S(1)}, bf16[1168,128]{1,0:T(8,128)(2,1)S(1)}, u32[]{:S(2)}, u32[]{:S(2)}) collective-permute-start(bf16[1168,128]{1,0:T(8,128)(2,1)S(1)} %label.1.own), channel_id=1, source_target_pairs={{0,2},{1,3},{2,4},{3,5},{4,6},{5,7},{6,0},{7,1},{8,10},{9,11},{10,... | collective-permute-start | bytes 897032 | tf_op jit(solution)/shard_map/ppermute | solution.py:835
  7.4 1.5 %collective-permute-start.3 = (bf16[128,1024]{1,0:T(8,128)(2,1)}, bf16[128,1024]{1,0:T(8,128)(2,1)S(1)}, u32[]{:S(2)}, u32[]{:S(2)}) collective-permute-start(bf16[128,1024]{1,0:T(8,128)(2,1)} %bitcast.10), channel_id=1, source_target_pairs={{0,16},{8,24},{16,0},{24,8},{1,17},{9,25},{17,1},{25,9},{2,18},{10... | collective-permute-start | bytes 786440 | tf_op jit(solution)/shard_map/ppermute | solution.py:830
  8.9 2.2 %own_cotangents.1 = (bf16[1152,128]{1,0:T(8,128)(2,1)S(1)}, bf16[576,128]{1,0:T(8,128)(2,1)S(1)}, bf16[1024,1152]{1,0:T(8,128)(2,1)S(1)}) custom-call(bf16[128,1024]{1,0:T(8,128)(2,1)} %bitcast.11, bf16[1024,1152]{1,0:T(8,128)(2,1)} %weight.1, bf16[640,128]{1,0:T(8,128)(2,1)S(1)} %get-tuple-element.95.query.query_own), custom_call_target="tpu_custom_call" | custom-call | flops 1000000 | bytes 10000 | tf_op jit(solution)/shard_map/own_cotangents/pallas_call | solution.py:247
  12.1 1.7 %collective-permute-start.6 = (bf16[128,1024]{1,0:T(8,128)(2,1)S(1)}, bf16[128,1024]{1,0:T(8,128)(2,1)S(1)}, u32[]{:S(2)}, u32[]{:S(2)}) collective-permute-start(bf16[128,1024]{1,0:T(8,128)(2,1)S(1)} %bitcast.12), channel_id=1, source_target_pairs={{0,1},{1,0},{2,3},{3,2},{4,5},{5,4},{6,7},{7,6},{8,9},{9,8},{10,11... | collective-permute-start | bytes 786440 | tf_op jit(solution)/shard_map/ppermute | solution.py:830
  13.9 1.6 %collective-permute-start.4 = (bf16[1152,128]{1,0:T(8,128)(2,1)S(1)}, bf16[1152,128]{1,0:T(8,128)(2,1)S(1)}, u32[]{:S(2)}, u32[]{:S(2)}) collective-permute-start(bf16[1152,128]{1,0:T(8,128)(2,1)S(1)} %collective-permute-done.partner), channel_id=1, source_target_pairs={{0,2},{1,3},{2,4},{3,5},{4,6},{5,7},{6,0},{7,1},{8,10},{9,11},{10,... | collective-permute-start | bytes 884744 | tf_op jit(solution)/shard_map/ppermute | solution.py:835
  16.9 1.3 %collective-permute-start.7 = (bf16[1152,128]{1,0:T(8,128)(2,1)S(1)}, bf16[1152,128]{1,0:T(8,128)(2,1)S(1)}, u32[]{:S(2)}, u32[]{:S(2)}) collective-permute-start(bf16[1152,128]{1,0:T(8,128)(2,1)S(1)} %get-tuple-element.104.both_own), channel_id=1, source_target_pairs={{2,0},{3,1},{4,2},{5,3},{6,4},{7,5},{10,8},{11,9},{12,10},{13,11},... | collective-permute-start | bytes 884744 | tf_op jit(solution)/shard_map/ppermute | solution.py:843
  18.2 3.1 %collective-permute-done.6.cotangent.refs_4_ = bf16[128,1024]{1,0:T(8,128)(2,1)S(1)} collective-permute-done((bf16[128,1024]{1,0:T(8,128)(2,1)S(1)}, bf16[128,1024]{1,0:T(8,128)(2,1)S(1)}, u32[]{:S(2)}, u32[]{:S(2)}) %collective-permute-start.6) | collective-permute-done | bytes 262176 | tf_op jit(solution)/shard_map/ppermute | solution.py:830
  21.4 1.4 %collective-permute-start.12 = (bf16[128,1024]{1,0:T(8,128)(2,1)S(1)}, bf16[128,1024]{1,0:T(8,128)(2,1)S(1)}, u32[]{:S(2)}, u32[]{:S(2)}) collective-permute-start(bf16[128,1024]{1,0:T(8,128)(2,1)S(1)} %collective-permute-done.6.cotangent.refs_4_), channel_id=1, source_target_pairs={{0,16},{8,24},{16,0},{24,8},{1,17},{9,25},{17,1},{25,9},{2,18},{10... | collective-permute-start | bytes 786440 | tf_op jit(solution)/shard_map/ppermute | solution.py:830
  23.0 0.9 %collective-permute-done.4.halo_other = bf16[1152,128]{1,0:T(8,128)(2,1)S(1)} collective-permute-done((bf16[1152,128]{1,0:T(8,128)(2,1)S(1)}, bf16[1152,128]{1,0:T(8,128)(2,1)S(1)}, u32[]{:S(2)}, u32[]{:S(2)}) %collective-permute-start.4) | collective-permute-done | bytes 294944 | tf_op jit(solution)/shard_map/ppermute | solution.py:835
  24.1 1.9 %forward.1 = (bf16[4,2,384,256]{3,2,1,0:T(8,128)(2,1)S(1)}, bf16[2,384,128]{2,1,0:T(8,128)(2,1)S(1)}, f32[24,256]{1,0:T(8,128)S(1)}, bf16[608,256]{1,0:T(8,128)(...) custom-call(bf16[9,512,128]{2,1,0:T(8,128)(2,1)S(1)} %get-tuple-elem, ...), custom_call_target="tpu_custom_call" | custom-call | flops 1000000 | bytes 10000 | tf_op jit(solution)/shard_map/forward/pallas_call | solution.py:466
  26.0 1.6 %collective-permute-start.10 = (bf16[160,256]{1,0:T(8,128)(2,1)S(1)}, bf16[160,256]{1,0:T(8,128)(2,1)S(1)}, u32[]{:S(2)}, u32[]{:S(2)}) collective-permute-start(bf16[160,256]{1,0:T(8,128)(2,1)S(1)} %get-tuple-element.132), channel_id=1, source_target_pairs={{0,16},{8,24},{16,0},{24,8},{1,17},{9,25},{17,1},{25,9},{2,18},{10... | collective-permute-start | bytes 245768 | tf_op jit(solution)/shard_map/ppermute | solution.py:830
  29.6 1.8 %collective-permute-start.15 = (bf16[1296,128]{1,0:T(8,128)(2,1)S(1)}, bf16[1296,128]{1,0:T(8,128)(2,1)S(1)}, u32[]{:S(2)}, u32[]{:S(2)}) collective-permute-start(bf16[1296,128]{1,0:T(8,128)(2,1)S(1)} %get-tuple-element.123.both_partner), channel_id=1, source_target_pairs={{0,6},{1,7},{2,0},{3,1},{4,2},{5,3},{6,4},{7,5},{8,14},{9,15},{10,... | collective-permute-start | bytes 995336 | tf_op jit(solution)/shard_map/ppermute | solution.py:835
  31.5 1.8 %own_gradients.1 = (bf16[576,128]{1,0:T(8,128)(2,1)S(1)}, bf16[576,256]{1,0:T(8,128)(2,1)S(1)}, f32[1152,128]{1,0:T(8,128)S(1)}, f32[1152,128]{1,0:T(8,128)S(1)}) custom-call(bf16[9,512,128]{2,1,0:T(8,128)(2,1)S(1)} %get-tuple-element.103.keys_all, bf16[1152,128]{1,0:T(8,128)(2,1)S(1)} %get-tuple-element.104.both_own, ...), custom_call_target="tpu_custom_call" | custom-call | flops 1000000 | bytes 10000 | tf_op jit(solution)/shard_map/own_gradients/pallas_call | solution.py:560
  34.3 1.6 %collective-permute-start.16 = (bf16[576,256]{1,0:T(8,128)(2,1)S(1)}, bf16[576,256]{1,0:T(8,128)(2,1)S(1)}, u32[]{:S(2)}, u32[]{:S(2)}) collective-permute-start(bf16[576,256]{1,0:T(8,128)(2,1)S(1)} %get-tuple-element.155), channel_id=1, source_target_pairs={{0,1},{1,0},{2,3},{3,2},{4,5},{5,4},{6,7},{7,6},{8,9},{9,8},{10,11... | collective-permute-start | bytes 884744 | tf_op jit(solution)/shard_map/ppermute | solution.py:830
  36.3 2.0 %collective-permute-start.18 = (bf16[160,256]{1,0:T(8,128)(2,1)S(1)}, bf16[160,256]{1,0:T(8,128)(2,1)S(1)}, u32[]{:S(2)}, u32[]{:S(2)}) collective-permute-start(bf16[160,256]{1,0:T(8,128)(2,1)S(1)} %get-tuple-element.162), channel_id=1, source_target_pairs={{0,4},{1,5},{2,6},{3,7},{4,0},{5,1},{6,2},{7,3},{8,12},{9,13},{10,... | collective-permute-start | bytes 245768 | tf_op jit(solution)/shard_map/ppermute | solution.py:830
  38.3 2.4 %collective-permute-start.19 = (bf16[160,256]{1,0:T(8,128)(2,1)S(1)}, bf16[160,256]{1,0:T(8,128)(2,1)S(1)}, u32[]{:S(2)}, u32[]{:S(2)}) collective-permute-start(bf16[160,256]{1,0:T(8,128)(2,1)S(1)} %get-tuple-element.163), channel_id=1, source_target_pairs={{0,6},{1,7},{2,4},{3,5},{4,2},{5,3},{6,0},{7,1},{8,14},{9,15},{10,... | collective-permute-start | bytes 245768 | tf_op jit(solution)/shard_map/ppermute | solution.py:830
  40.8 1.6 %next_gradients.1 = (bf16[1152,128]{1,0:T(8,128)(2,1)S(1)}, bf16[1152,128]{1,0:T(8,128)(2,1)S(1)}) custom-call(bf16[1168,128]{1,0:T(8,128)(2,1)S(1)} %label.1.own, bf16[1152,128]{1,0:T(8,128)(2,1)S(1)} %collective-permute-done.partner, bf16[1152,128]{1,0:T(8,128)(2,1)S(1)} %collective-permute-done.7.both_own, ...), custom_call_target="tpu_custom_call" | custom-call | flops 4000000000 | bytes 10000 | tf_op jit(solution)/shard_map/next_gradients/pallas_call | solution.py:651
  42.4 1.0 %collective-permute-start.20 = (bf16[1152,128]{1,0:T(8,128)(2,1)S(1)}, bf16[1152,128]{1,0:T(8,128)(2,1)S(1)}, u32[]{:S(2)}, u32[]{:S(2)}) collective-permute-start(bf16[1152,128]{1,0:T(8,128)(2,1)S(1)} %get-tuple-element.167), channel_id=1, source_target_pairs={{0,1},{1,0},{2,3},{3,2},{4,5},{5,4},{6,7},{7,6},{8,9},{9,8},{10,11... | collective-permute-start | bytes 884744 | tf_op jit(solution)/shard_map/ppermute | solution.py:830
  43.4 2.4 %output.1 = (bf16[128,1024]{1,0:T(8,128)(2,1)}, bf16[128,1152]{1,0:T(8,128)(2,1)}, bf16[1152,128]{1,0:T(8,128)(2,1)}) custom-call(bf16[576,128]{1,0:T(8,128)(2,1)S(1)} %get-tuple-element.157.att_own, bf16[576,256]{1,0:T(8,128)(2,1)S(1)} %collective-permute-done.16.received, bf16[576,128]{1,0:T(8,128)(2,1)S(1)} %get-tuple-element.159.dq_mine, ...), custom_call_target="tpu_custom_call" | custom-call | flops 1000000 | bytes 10000 | tf_op jit(solution)/shard_map/output/pallas_call | solution.py:690
  45.9 1.5 %collective-permute-start.21 = (bf16[160,128]{1,0:T(8,128)(2,1)S(1)}, bf16[160,128]{1,0:T(8,128)(2,1)S(1)}, u32[]{:S(2)}, u32[]{:S(2)}) collective-permute-start(bf16[160,128]{1,0:T(8,128)(2,1)S(1)} %get-tuple-element.173), channel_id=1, source_target_pairs={{0,1},{1,0},{2,3},{3,2},{4,5},{5,4},{6,7},{7,6},{8,9},{9,8},{10,11... | collective-permute-start | bytes 122888 | tf_op jit(solution)/shard_map/ppermute | solution.py:830
  47.4 3.7 %collective-permute-done.21.arrived = bf16[160,128]{1,0:T(8,128)(2,1)S(1)} collective-permute-done((bf16[160,128]{1,0:T(8,128)(2,1)S(1)}, bf16[160,128]{1,0:T(8,128)(2,1)S(1)}, u32[]{:S(2)}, u32[]{:S(2)}) %collective-permute-start.21) | collective-permute-done | bytes 40992 | tf_op jit(solution)/shard_map/ppermute | solution.py:830
  51.2 1.1 %place.1 = (bf16[128,1152]{1,0:T(8,128)(2,1)}, bf16[128,1152]{1,0:T(8,128)(2,1)}, f32[288,128]{1,0:T(8,128)}) custom-call(bf16[1152,128]{1,0:T(8,128)(2,1)S(1)} %get-tuple-element.166.mine, bf16[1152,128]{1,0:T(8,128)(2,1)S(1)} %collective-permute-done.20.theirs, f32[160,128]{1,0:T(8,128)S(1)} %get-tuple-element.172.kept, ...), custom_call_target="tpu_custom_call" | custom-call | flops 1000000 | bytes 10000 | tf_op jit(solution)/shard_map/place/pallas_call | solution.py:742
  (36 shorter events, 6.6 us)
Async XLA Ops:
  0.6 11.5 %copy-start = (bf16[1,128,1024]{2,1,0:T(8,128)(2,1)S(1)}, bf16[1,128,1024]{2,1,0:T(8,128)(2,1)}, u32[]{:S(2)}) copy-start(bf16[1,128,1024]{2,1,0:T(8,128)(2,1)} %param.9) | copy-start | bytes 786436
  2.1 10.0 %collective-permute-start = (bf16[1152,128]{1,0:T(8,128)(2,1)S(1)}, bf16[1152,128]{1,0:T(8,128)(2,1)S(1)}, u32[]{:S(2)}, u32[]{:S(2)}) collective-permute-start(bf16[1152,128]{1,0:T(8,128)(2,1)S(1)} %get-tuple-element.94), channel_id=1, source_target_pairs={{0,1},{1,0},{2,3},{3,2},{4,5},{5,4},{6,7},{7,6},{8,9},{9,8},{10,11... | collective-permute-start | bytes 884744 | tf_op jit(solution)/shard_map/ppermute | solution.py:830
  5.8 10.4 %collective-permute-start.1 = (bf16[1168,128]{1,0:T(8,128)(2,1)S(1)}, bf16[1168,128]{1,0:T(8,128)(2,1)S(1)}, u32[]{:S(2)}, u32[]{:S(2)}) collective-permute-start(bf16[1168,128]{1,0:T(8,128)(2,1)S(1)} %label.1.own), channel_id=1, source_target_pairs={{0,2},{1,3},{2,4},{3,5},{4,6},{5,7},{6,0},{7,1},{8,10},{9,11},{10,... | collective-permute-start | bytes 897032 | tf_op jit(solution)/shard_map/ppermute | solution.py:835
  7.4 9.5 %collective-permute-start.2 = (bf16[128,1024]{1,0:T(8,128)(2,1)}, bf16[128,1024]{1,0:T(8,128)(2,1)S(1)}, u32[]{:S(2)}, u32[]{:S(2)}) collective-permute-start(bf16[128,1024]{1,0:T(8,128)(2,1)} %bitcast.9), channel_id=1, source_target_pairs={{0,8},{8,0},{16,24},{24,16},{1,9},{9,1},{17,25},{25,17},{2,10},{10... | collective-permute-start | bytes 786440 | tf_op jit(solution)/shard_map/ppermute | solution.py:830
  7.4 9.5 %collective-permute-start.3 = (bf16[128,1024]{1,0:T(8,128)(2,1)}, bf16[128,1024]{1,0:T(8,128)(2,1)S(1)}, u32[]{:S(2)}, u32[]{:S(2)}) collective-permute-start(bf16[128,1024]{1,0:T(8,128)(2,1)} %bitcast.10), channel_id=1, source_target_pairs={{0,16},{8,24},{16,0},{24,8},{1,17},{9,25},{17,1},{25,9},{2,18},{10... | collective-permute-start | bytes 786440 | tf_op jit(solution)/shard_map/ppermute | solution.py:830
  12.1 9.2 %collective-permute-start.6 = (bf16[128,1024]{1,0:T(8,128)(2,1)S(1)}, bf16[128,1024]{1,0:T(8,128)(2,1)S(1)}, u32[]{:S(2)}, u32[]{:S(2)}) collective-permute-start(bf16[128,1024]{1,0:T(8,128)(2,1)S(1)} %bitcast.12), channel_id=1, source_target_pairs={{0,1},{1,0},{2,3},{3,2},{4,5},{5,4},{6,7},{7,6},{8,9},{9,8},{10,11... | collective-permute-start | bytes 786440 | tf_op jit(solution)/shard_map/ppermute | solution.py:830
  13.9 10.1 %collective-permute-start.4 = (bf16[1152,128]{1,0:T(8,128)(2,1)S(1)}, bf16[1152,128]{1,0:T(8,128)(2,1)S(1)}, u32[]{:S(2)}, u32[]{:S(2)}) collective-permute-start(bf16[1152,128]{1,0:T(8,128)(2,1)S(1)} %collective-permute-done.partner), channel_id=1, source_target_pairs={{0,2},{1,3},{2,4},{3,5},{4,6},{5,7},{6,0},{7,1},{8,10},{9,11},{10,... | collective-permute-start | bytes 884744 | tf_op jit(solution)/shard_map/ppermute | solution.py:835
  16.3 6.8 %collective-permute-start.5 = (bf16[608,128]{1,0:T(8,128)(2,1)S(1)}, bf16[608,128]{1,0:T(8,128)(2,1)S(1)}, u32[]{:S(2)}, u32[]{:S(2)}) collective-permute-start(bf16[608,128]{1,0:T(8,128)(2,1)S(1)} %label_query.1), channel_id=1, source_target_pairs={{0,1},{1,0},{2,3},{3,2},{4,5},{5,4},{6,7},{7,6},{8,9},{9,8},{10,11... | collective-permute-start | bytes 466952 | tf_op jit(solution)/shard_map/ppermute | solution.py:830
  16.9 12.8 %collective-permute-start.7 = (bf16[1152,128]{1,0:T(8,128)(2,1)S(1)}, bf16[1152,128]{1,0:T(8,128)(2,1)S(1)}, u32[]{:S(2)}, u32[]{:S(2)}) collective-permute-start(bf16[1152,128]{1,0:T(8,128)(2,1)S(1)} %get-tuple-element.104.both_own), channel_id=1, source_target_pairs={{2,0},{3,1},{4,2},{5,3},{6,4},{7,5},{10,8},{11,9},{12,10},{13,11},... | collective-permute-start | bytes 884744 | tf_op jit(solution)/shard_map/ppermute | solution.py:843
  18.2 9.5 %collective-permute-start.8 = (bf16[128,1024]{1,0:T(8,128)(2,1)S(1)}, bf16[128,1024]{1,0:T(8,128)(2,1)S(1)}, u32[]{:S(2)}, u32[]{:S(2)}) collective-permute-start(bf16[128,1024]{1,0:T(8,128)(2,1)S(1)} %collective-permute-done.3.refs_6_), channel_id=1, source_target_pairs={{0,8},{8,0},{16,24},{24,16},{1,9},{9,1},{17,25},{25,17},{2,10},{10... | collective-permute-start | bytes 786440 | tf_op jit(solution)/shard_map/ppermute | solution.py:830
  21.4 12.0 %collective-permute-start.12 = (bf16[128,1024]{1,0:T(8,128)(2,1)S(1)}, bf16[128,1024]{1,0:T(8,128)(2,1)S(1)}, u32[]{:S(2)}, u32[]{:S(2)}) collective-permute-start(bf16[128,1024]{1,0:T(8,128)(2,1)S(1)} %collective-permute-done.6.cotangent.refs_4_), channel_id=1, source_target_pairs={{0,16},{8,24},{16,0},{24,8},{1,17},{9,25},{17,1},{25,9},{2,18},{10... | collective-permute-start | bytes 786440 | tf_op jit(solution)/shard_map/ppermute | solution.py:830
  26.0 7.3 %collective-permute-start.10 = (bf16[160,256]{1,0:T(8,128)(2,1)S(1)}, bf16[160,256]{1,0:T(8,128)(2,1)S(1)}, u32[]{:S(2)}, u32[]{:S(2)}) collective-permute-start(bf16[160,256]{1,0:T(8,128)(2,1)S(1)} %get-tuple-element.132), channel_id=1, source_target_pairs={{0,16},{8,24},{16,0},{24,8},{1,17},{9,25},{17,1},{25,9},{2,18},{10... | collective-permute-start | bytes 245768 | tf_op jit(solution)/shard_map/ppermute | solution.py:830
  27.6 5.7 %collective-permute-start.11 = (bf16[160,256]{1,0:T(8,128)(2,1)S(1)}, bf16[160,256]{1,0:T(8,128)(2,1)S(1)}, u32[]{:S(2)}, u32[]{:S(2)}) collective-permute-start(bf16[160,256]{1,0:T(8,128)(2,1)S(1)} %get-tuple-element.133), channel_id=1, source_target_pairs={{0,24},{8,16},{16,8},{24,0},{1,25},{9,17},{17,9},{25,1},{2,26},{10... | collective-permute-start | bytes 245768 | tf_op jit(solution)/shard_map/ppermute | solution.py:830
  27.6 5.7 %collective-permute-start.9 = (bf16[160,256]{1,0:T(8,128)(2,1)S(1)}, bf16[160,256]{1,0:T(8,128)(2,1)S(1)}, u32[]{:S(2)}, u32[]{:S(2)}) collective-permute-start(bf16[160,256]{1,0:T(8,128)(2,1)S(1)} %get-tuple-element.131), channel_id=1, source_target_pairs={{0,8},{8,0},{16,24},{24,16},{1,9},{9,1},{17,25},{25,17},{2,10},{10... | collective-permute-start | bytes 245768 | tf_op jit(solution)/shard_map/ppermute | solution.py:830
  29.6 11.2 %collective-permute-start.15 = (bf16[1296,128]{1,0:T(8,128)(2,1)S(1)}, bf16[1296,128]{1,0:T(8,128)(2,1)S(1)}, u32[]{:S(2)}, u32[]{:S(2)}) collective-permute-start(bf16[1296,128]{1,0:T(8,128)(2,1)S(1)} %get-tuple-element.123.both_partner), channel_id=1, source_target_pairs={{0,6},{1,7},{2,0},{3,1},{4,2},{5,3},{6,4},{7,5},{8,14},{9,15},{10,... | collective-permute-start | bytes 995336 | tf_op jit(solution)/shard_map/ppermute | solution.py:835
  33.3 2.5 %collective-permute-start.13 = (bf16[128,1024]{1,0:T(8,128)(2,1)S(1)}, bf16[128,1024]{1,0:T(8,128)(2,1)S(1)}, u32[]{:S(2)}, u32[]{:S(2)}) collective-permute-start(bf16[128,1024]{1,0:T(8,128)(2,1)S(1)} %collective-permute-done.6.cotangent.refs_4_), channel_id=1, source_target_pairs={{0,8},{8,0},{16,24},{24,16},{1,9},{9,1},{17,25},{25,17},{2,10},{10... | collective-permute-start | bytes 786440 | tf_op jit(solution)/shard_map/ppermute | solution.py:830
  33.4 2.4 %collective-permute-start.14 = (bf16[128,1024]{1,0:T(8,128)(2,1)S(1)}, bf16[128,1024]{1,0:T(8,128)(2,1)S(1)}, u32[]{:S(2)}, u32[]{:S(2)}) collective-permute-start(bf16[128,1024]{1,0:T(8,128)(2,1)S(1)} %collective-permute-done.12.refs_6_), channel_id=1, source_target_pairs={{0,8},{8,0},{16,24},{24,16},{1,9},{9,1},{17,25},{25,17},{2,10},{10... | collective-permute-start | bytes 786440 | tf_op jit(solution)/shard_map/ppermute | solution.py:830
  34.3 9.1 %collective-permute-start.16 = (bf16[576,256]{1,0:T(8,128)(2,1)S(1)}, bf16[576,256]{1,0:T(8,128)(2,1)S(1)}, u32[]{:S(2)}, u32[]{:S(2)}) collective-permute-start(bf16[576,256]{1,0:T(8,128)(2,1)S(1)} %get-tuple-element.155), channel_id=1, source_target_pairs={{0,1},{1,0},{2,3},{3,2},{4,5},{5,4},{6,7},{7,6},{8,9},{9,8},{10,11... | collective-permute-start | bytes 884744 | tf_op jit(solution)/shard_map/ppermute | solution.py:830
  36.2 9.6 %collective-permute-start.17 = (bf16[160,256]{1,0:T(8,128)(2,1)S(1)}, bf16[160,256]{1,0:T(8,128)(2,1)S(1)}, u32[]{:S(2)}, u32[]{:S(2)}) collective-permute-start(bf16[160,256]{1,0:T(8,128)(2,1)S(1)} %get-tuple-element.161), channel_id=1, source_target_pairs={{0,2},{1,3},{2,0},{3,1},{4,6},{5,7},{6,4},{7,5},{8,10},{9,11},{10,... | collective-permute-start | bytes 245768 | tf_op jit(solution)/shard_map/ppermute | solution.py:830
  36.3 9.5 %collective-permute-start.18 = (bf16[160,256]{1,0:T(8,128)(2,1)S(1)}, bf16[160,256]{1,0:T(8,128)(2,1)S(1)}, u32[]{:S(2)}, u32[]{:S(2)}) collective-permute-start(bf16[160,256]{1,0:T(8,128)(2,1)S(1)} %get-tuple-element.162), channel_id=1, source_target_pairs={{0,4},{1,5},{2,6},{3,7},{4,0},{5,1},{6,2},{7,3},{8,12},{9,13},{10,... | collective-permute-start | bytes 245768 | tf_op jit(solution)/shard_map/ppermute | solution.py:830
  38.3 7.6 %collective-permute-start.19 = (bf16[160,256]{1,0:T(8,128)(2,1)S(1)}, bf16[160,256]{1,0:T(8,128)(2,1)S(1)}, u32[]{:S(2)}, u32[]{:S(2)}) collective-permute-start(bf16[160,256]{1,0:T(8,128)(2,1)S(1)} %get-tuple-element.163), channel_id=1, source_target_pairs={{0,6},{1,7},{2,4},{3,5},{4,2},{5,3},{6,0},{7,1},{8,14},{9,15},{10,... | collective-permute-start | bytes 245768 | tf_op jit(solution)/shard_map/ppermute | solution.py:830
  42.4 8.7 %collective-permute-start.20 = (bf16[1152,128]{1,0:T(8,128)(2,1)S(1)}, bf16[1152,128]{1,0:T(8,128)(2,1)S(1)}, u32[]{:S(2)}, u32[]{:S(2)}) collective-permute-start(bf16[1152,128]{1,0:T(8,128)(2,1)S(1)} %get-tuple-element.167), channel_id=1, source_target_pairs={{0,1},{1,0},{2,3},{3,2},{4,5},{5,4},{6,7},{7,6},{8,9},{9,8},{10,11... | collective-permute-start | bytes 884744 | tf_op jit(solution)/shard_map/ppermute | solution.py:830
  45.9 5.2 %collective-permute-start.21 = (bf16[160,128]{1,0:T(8,128)(2,1)S(1)}, bf16[160,128]{1,0:T(8,128)(2,1)S(1)}, u32[]{:S(2)}, u32[]{:S(2)}) collective-permute-start(bf16[160,128]{1,0:T(8,128)(2,1)S(1)} %get-tuple-element.173), channel_id=1, source_target_pairs={{0,1},{1,0},{2,3},{3,2},{4,5},{5,4},{6,7},{7,6},{8,9},{9,8},{10,11... | collective-permute-start | bytes 122888 | tf_op jit(solution)/shard_map/ppermute | solution.py:830

commit v8 on v7

--- a/solution.py
+++ b/solution.py
@@ -129,7 +129,7 @@
     for copy in copies:
         copy.start()
     shared = slice(SHARED, SHARED + PAIR)
-    for copy in copies:
+    for copy in copies[:2]:
         copy.wait()
     for side, target in ((1 - half, swap_kv), (half, own_kv)):
         for pair in range(PAIRS):
@@ -141,6 +141,7 @@
     mixed[1] = low_or_high(turned(key_shared), value_shared).astype(bf16)
     swap_kv[rows_of(MIXED)] = mixed[1 - half]
     own_kv[rows_of(MIXED)] = mixed[half]
+    copies[2].wait()
     for pair in range(PAIRS):
         swap_query[rows_of(pair)] = query_all[:, columns_of(1 - half, pair)]
         own_query[rows_of(pair)] = query_all[:, columns_of(half, pair)]
@@ -388,11 +389,11 @@
     )(*sources)
 
 
-def staggered(items, *stages):
+def staggered(items, apart, *stages):
     values = [None] * len(items)
-    for step in range(len(items) + 2 * len(stages) - 2):
+    for step in range(len(items) + apart * (len(stages) - 1)):
         for number, stage in enumerate(stages):
-            index = step - 2 * number
+            index = step - apart * number
             if 0 <= index < len(items):
                 values[index] = stage(*items[index], values[index])
 
@@ -449,7 +450,7 @@
             att[single_rows(), steps] = mixed[HDIM:].astype(bf16)
 
     items = [(pair, query_block) for pair in range(PAIRS + 1) for query_block in range(2)]
-    staggered(items, score, weigh, mix)
+    staggered(items, 3, score, weigh, mix)
 
     att[HALF:] = jnp.zeros((ATT_ROWS - HALF, 2 * BLOCK), bf16)
     att_own[...] = att[:HALF, at(half, BLOCK)]
@@ -547,7 +548,7 @@
             accumulate(MIXED, query_block, dk + dv)
 
     items = [(pair, query_block) for pair in range(PAIRS + 1) for query_block in (1, 0)]
-    staggered(items, d_weights_of, d_scores_of, products)
+    staggered(items, 2, d_weights_of, d_scores_of, products)
     dq_own[...] = dq_all[:, at(half, BLOCK)]
     swap[:, :BLOCK] = att_swap[...]
     swap[:, BLOCK:] = dq_all[:, at(1 - half, BLOCK)]
@@ -641,7 +642,7 @@
             grads[MIXED, keys] += dk + dv
 
     items = [(pair, query_block) for pair in range(PAIRS + 1) for query_block in range(2)]
-    staggered(items, score, weigh, products)
+    staggered(items, 2, score, weigh, products)
     for block in range(MIXED + 1):
         mine[rows_of(block)] = grads[block, at(half, BLOCK)].astype(bf16)
         swap[rows_of(block)] = grads[block, at(1 - half, BLOCK)].astype(bf16)

time: 52.4 us -> 52.4 us (level)
  transfers between devices with their start and end apart: 22 -> 22, of which waited for: 8 -> 8; matrix products, arithmetic and copies ran while one was open for 0% -> 0% of each run, Pallas kernels for 23% -> 22%
where the time goes in v8:
time: 52.4 us; the launch traced here: 52.2 us
  starting transfers between devices  25.7 us (49%)
  Pallas kernels  14.3 us (27%)
  waiting for transfers between devices  10.8 us (21%)
  between operations  1.46 us (3%)
    ppermute x18, starting transfers between devices, swapped(): lax.ppermute(value, axis, [(source, source ^ bits) for source in range(co...  19.4 us
    ppermute x18, waiting for transfers between devices, swapped(): lax.ppermute(value, axis, [(source, source ^ bits) for source in range(co...  8.11 us
    ppermute x3, starting transfers between devices, rotated(): lax.ppermute(value, axis, [(source, (source + steps) % count) for source...  4.97 us
    pallas_call x1, Pallas kernels, output_rows(): kernel(output_kernel, 'output', [VMEM] * 4, [shaped((BLOCK, weight.shape[...  2.44 us
    pallas_call x1, Pallas kernels, own_cotangents(): kernel(own_cotangent_kernel, 'own_cotangents', [HBM, HBM, VMEM], [shaped(...  2.24 us
    ppermute x3, waiting for transfers between devices, rotated(): lax.ppermute(value, axis, [(source, (source + steps) % count) for source...  1.94 us
    pallas_call x1, Pallas kernels, forward(): kernel(functools.partial(forward_kernel, pieces_wanted), 'forward', [VMEM...  1.87 us
    pallas_call x1, Pallas kernels, own_gradients(): kernel(own_kernel, 'own_gradients', [VMEM] * 7, [shaped((HALF, BLOCK), bf...  1.82 us
  transfers between devices with their start and end apart: 22, of which 8 were waited for; matrix products, arithmetic and copies ran while one was open for 0% of the time, Pallas kernels for 22%

profile of v8, /device:TPU:0, one launch (start us, length us, event | category | flops | bytes accessed | tf_op | source)
XLA Modules:
  0.0 52.2 jit_solution(3599365553019910061)
XLA Ops:
  0.6 1.5 %pack.1 = (bf16[1152,128]{1,0:T(8,128)(2,1)S(1)}, bf16[1152,128]{1,0:T(8,128)(2,1)S(1)}, bf16[576,128]{1,0:T(8,128)(2,1)S(1)}, bf16[640,128]{1,0:T(8,128)(2,1)S(1)}) custom-call(bf16[128,1152]{1,0:T(8,128)(2,1)} %bitcast.14, bf16[128,1152]{1,0:T(8,128)(2,1)} %bitcast.15, bf16[128,1152]{1,0:T(8,128)(2,1)} %bitcast.16), custom_call_target="tpu_custom_call" | custom-call | flops 1000000 | bytes 10000 | tf_op jit(solution)/shard_map/pack/pallas_call | solution.py:158
  2.1 3.0 %collective-permute-start = (bf16[1152,128]{1,0:T(8,128)(2,1)S(1)}, bf16[1152,128]{1,0:T(8,128)(2,1)S(1)}, u32[]{:S(2)}, u32[]{:S(2)}) collective-permute-start(bf16[1152,128]{1,0:T(8,128)(2,1)S(1)} %get-tuple-element.94), channel_id=1, source_target_pairs={{0,1},{1,0},{2,3},{3,2},{4,5},{5,4},{6,7},{7,6},{8,9},{9,8},{10,11... | collective-permute-start | bytes 884744 | tf_op jit(solution)/shard_map/ppermute | solution.py:831
  5.9 1.6 %collective-permute-start.1 = (bf16[1168,128]{1,0:T(8,128)(2,1)S(1)}, bf16[1168,128]{1,0:T(8,128)(2,1)S(1)}, u32[]{:S(2)}, u32[]{:S(2)}) collective-permute-start(bf16[1168,128]{1,0:T(8,128)(2,1)S(1)} %label.1.own), channel_id=1, source_target_pairs={{0,2},{1,3},{2,4},{3,5},{4,6},{5,7},{6,0},{7,1},{8,10},{9,11},{10,... | collective-permute-start | bytes 897032 | tf_op jit(solution)/shard_map/ppermute | solution.py:836
  7.5 1.5 %collective-permute-start.3 = (bf16[128,1024]{1,0:T(8,128)(2,1)}, bf16[128,1024]{1,0:T(8,128)(2,1)S(1)}, u32[]{:S(2)}, u32[]{:S(2)}) collective-permute-start(bf16[128,1024]{1,0:T(8,128)(2,1)} %bitcast.10), channel_id=1, source_target_pairs={{0,16},{8,24},{16,0},{24,8},{1,17},{9,25},{17,1},{25,9},{2,18},{10... | collective-permute-start | bytes 786440 | tf_op jit(solution)/shard_map/ppermute | solution.py:831
  9.0 2.2 %own_cotangents.1 = (bf16[1152,128]{1,0:T(8,128)(2,1)S(1)}, bf16[576,128]{1,0:T(8,128)(2,1)S(1)}, bf16[1024,1152]{1,0:T(8,128)(2,1)S(1)}) custom-call(bf16[128,1024]{1,0:T(8,128)(2,1)} %bitcast.11, bf16[1024,1152]{1,0:T(8,128)(2,1)} %weight.1, bf16[640,128]{1,0:T(8,128)(2,1)S(1)} %get-tuple-element.95.query.query_own), custom_call_target="tpu_custom_call" | custom-call | flops 1000000 | bytes 10000 | tf_op jit(solution)/shard_map/own_cotangents/pallas_call | solution.py:248
  11.2 0.9 %collective-permute-done.partner = bf16[1152,128]{1,0:T(8,128)(2,1)S(1)} collective-permute-done((bf16[1152,128]{1,0:T(8,128)(2,1)S(1)}, bf16[1152,128]{1,0:T(8,128)(2,1)S(1)}, u32[]{:S(2)}, u32[]{:S(2)}) %collective-permute-start) | collective-permute-done | bytes 294944 | tf_op jit(solution)/shard_map/ppermute | solution.py:831
  12.2 1.7 %collective-permute-start.6 = (bf16[128,1024]{1,0:T(8,128)(2,1)S(1)}, bf16[128,1024]{1,0:T(8,128)(2,1)S(1)}, u32[]{:S(2)}, u32[]{:S(2)}) collective-permute-start(bf16[128,1024]{1,0:T(8,128)(2,1)S(1)} %bitcast.12), channel_id=1, source_target_pairs={{0,1},{1,0},{2,3},{3,2},{4,5},{5,4},{6,7},{7,6},{8,9},{9,8},{10,11... | collective-permute-start | bytes 786440 | tf_op jit(solution)/shard_map/ppermute | solution.py:831
  13.9 1.6 %collective-permute-start.4 = (bf16[1152,128]{1,0:T(8,128)(2,1)S(1)}, bf16[1152,128]{1,0:T(8,128)(2,1)S(1)}, u32[]{:S(2)}, u32[]{:S(2)}) collective-permute-start(bf16[1152,128]{1,0:T(8,128)(2,1)S(1)} %collective-permute-done.partner), channel_id=1, source_target_pairs={{0,2},{1,3},{2,4},{3,5},{4,6},{5,7},{6,0},{7,1},{8,10},{9,11},{10,... | collective-permute-start | bytes 884744 | tf_op jit(solution)/shard_map/ppermute | solution.py:836
  16.9 1.3 %collective-permute-start.7 = (bf16[1152,128]{1,0:T(8,128)(2,1)S(1)}, bf16[1152,128]{1,0:T(8,128)(2,1)S(1)}, u32[]{:S(2)}, u32[]{:S(2)}) collective-permute-start(bf16[1152,128]{1,0:T(8,128)(2,1)S(1)} %get-tuple-element.104.both_own), channel_id=1, source_target_pairs={{2,0},{3,1},{4,2},{5,3},{6,4},{7,5},{10,8},{11,9},{12,10},{13,11},... | collective-permute-start | bytes 884744 | tf_op jit(solution)/shard_map/ppermute | solution.py:844
  18.3 3.1 %collective-permute-done.6.cotangent.refs_4_ = bf16[128,1024]{1,0:T(8,128)(2,1)S(1)} collective-permute-done((bf16[128,1024]{1,0:T(8,128)(2,1)S(1)}, bf16[128,1024]{1,0:T(8,128)(2,1)S(1)}, u32[]{:S(2)}, u32[]{:S(2)}) %collective-permute-start.6) | collective-permute-done | bytes 262176 | tf_op jit(solution)/shard_map/ppermute | solution.py:831
  21.4 1.4 %collective-permute-start.12 = (bf16[128,1024]{1,0:T(8,128)(2,1)S(1)}, bf16[128,1024]{1,0:T(8,128)(2,1)S(1)}, u32[]{:S(2)}, u32[]{:S(2)}) collective-permute-start(bf16[128,1024]{1,0:T(8,128)(2,1)S(1)} %collective-permute-done.6.cotangent.refs_4_), channel_id=1, source_target_pairs={{0,16},{8,24},{16,0},{24,8},{1,17},{9,25},{17,1},{25,9},{2,18},{10... | collective-permute-start | bytes 786440 | tf_op jit(solution)/shard_map/ppermute | solution.py:831
  23.1 0.9 %collective-permute-done.4.halo_other = bf16[1152,128]{1,0:T(8,128)(2,1)S(1)} collective-permute-done((bf16[1152,128]{1,0:T(8,128)(2,1)S(1)}, bf16[1152,128]{1,0:T(8,128)(2,1)S(1)}, u32[]{:S(2)}, u32[]{:S(2)}) %collective-permute-start.4) | collective-permute-done | bytes 294944 | tf_op jit(solution)/shard_map/ppermute | solution.py:836
  24.2 1.9 %forward.1 = (bf16[4,2,384,256]{3,2,1,0:T(8,128)(2,1)S(1)}, bf16[2,384,128]{2,1,0:T(8,128)(2,1)S(1)}, f32[24,256]{1,0:T(8,128)S(1)}, bf16[608,256]{1,0:T(8,128)(...) custom-call(bf16[9,512,128]{2,1,0:T(8,128)(2,1)S(1)} %get-tuple-elem, ...), custom_call_target="tpu_custom_call" | custom-call | flops 1000000 | bytes 10000 | tf_op jit(solution)/shard_map/forward/pallas_call | solution.py:467
  26.0 1.6 %collective-permute-start.10 = (bf16[160,256]{1,0:T(8,128)(2,1)S(1)}, bf16[160,256]{1,0:T(8,128)(2,1)S(1)}, u32[]{:S(2)}, u32[]{:S(2)}) collective-permute-start(bf16[160,256]{1,0:T(8,128)(2,1)S(1)} %get-tuple-element.132), channel_id=1, source_target_pairs={{0,16},{8,24},{16,0},{24,8},{1,17},{9,25},{17,1},{25,9},{2,18},{10... | collective-permute-start | bytes 245768 | tf_op jit(solution)/shard_map/ppermute | solution.py:831
  29.7 1.8 %collective-permute-start.15 = (bf16[1296,128]{1,0:T(8,128)(2,1)S(1)}, bf16[1296,128]{1,0:T(8,128)(2,1)S(1)}, u32[]{:S(2)}, u32[]{:S(2)}) collective-permute-start(bf16[1296,128]{1,0:T(8,128)(2,1)S(1)} %get-tuple-element.123.both_partner), channel_id=1, source_target_pairs={{0,6},{1,7},{2,0},{3,1},{4,2},{5,3},{6,4},{7,5},{8,14},{9,15},{10,... | collective-permute-start | bytes 995336 | tf_op jit(solution)/shard_map/ppermute | solution.py:836
  31.5 1.8 %own_gradients.1 = (bf16[576,128]{1,0:T(8,128)(2,1)S(1)}, bf16[576,256]{1,0:T(8,128)(2,1)S(1)}, f32[1152,128]{1,0:T(8,128)S(1)}, f32[1152,128]{1,0:T(8,128)S(1)}) custom-call(bf16[9,512,128]{2,1,0:T(8,128)(2,1)S(1)} %get-tuple-element.103.keys_all, bf16[1152,128]{1,0:T(8,128)(2,1)S(1)} %get-tuple-element.104.both_own, ...), custom_call_target="tpu_custom_call" | custom-call | flops 1000000 | bytes 10000 | tf_op jit(solution)/shard_map/own_gradients/pallas_call | solution.py:561
  34.3 1.5 %collective-permute-start.16 = (bf16[576,256]{1,0:T(8,128)(2,1)S(1)}, bf16[576,256]{1,0:T(8,128)(2,1)S(1)}, u32[]{:S(2)}, u32[]{:S(2)}) collective-permute-start(bf16[576,256]{1,0:T(8,128)(2,1)S(1)} %get-tuple-element.155), channel_id=1, source_target_pairs={{0,1},{1,0},{2,3},{3,2},{4,5},{5,4},{6,7},{7,6},{8,9},{9,8},{10,11... | collective-permute-start | bytes 884744 | tf_op jit(solution)/shard_map/ppermute | solution.py:831
  36.3 2.0 %collective-permute-start.18 = (bf16[160,256]{1,0:T(8,128)(2,1)S(1)}, bf16[160,256]{1,0:T(8,128)(2,1)S(1)}, u32[]{:S(2)}, u32[]{:S(2)}) collective-permute-start(bf16[160,256]{1,0:T(8,128)(2,1)S(1)} %get-tuple-element.162), channel_id=1, source_target_pairs={{0,4},{1,5},{2,6},{3,7},{4,0},{5,1},{6,2},{7,3},{8,12},{9,13},{10,... | collective-permute-start | bytes 245768 | tf_op jit(solution)/shard_map/ppermute | solution.py:831
  38.3 2.4 %collective-permute-start.19 = (bf16[160,256]{1,0:T(8,128)(2,1)S(1)}, bf16[160,256]{1,0:T(8,128)(2,1)S(1)}, u32[]{:S(2)}, u32[]{:S(2)}) collective-permute-start(bf16[160,256]{1,0:T(8,128)(2,1)S(1)} %get-tuple-element.163), channel_id=1, source_target_pairs={{0,6},{1,7},{2,4},{3,5},{4,2},{5,3},{6,0},{7,1},{8,14},{9,15},{10,... | collective-permute-start | bytes 245768 | tf_op jit(solution)/shard_map/ppermute | solution.py:831
  40.9 1.6 %next_gradients.1 = (bf16[1152,128]{1,0:T(8,128)(2,1)S(1)}, bf16[1152,128]{1,0:T(8,128)(2,1)S(1)}) custom-call(bf16[1168,128]{1,0:T(8,128)(2,1)S(1)} %label.1.own, bf16[1152,128]{1,0:T(8,128)(2,1)S(1)} %collective-permute-done.partner, bf16[1152,128]{1,0:T(8,128)(2,1)S(1)} %collective-permute-done.7.both_own, ...), custom_call_target="tpu_custom_call" | custom-call | flops 4000000000 | bytes 10000 | tf_op jit(solution)/shard_map/next_gradients/pallas_call | solution.py:652
  43.4 2.4 %output.1 = (bf16[128,1024]{1,0:T(8,128)(2,1)}, bf16[128,1152]{1,0:T(8,128)(2,1)}, bf16[1152,128]{1,0:T(8,128)(2,1)}) custom-call(bf16[576,128]{1,0:T(8,128)(2,1)S(1)} %get-tuple-element.157.att_own, bf16[576,256]{1,0:T(8,128)(2,1)S(1)} %collective-permute-done.16.received, bf16[576,128]{1,0:T(8,128)(2,1)S(1)} %get-tuple-element.159.dq_mine, ...), custom_call_target="tpu_custom_call" | custom-call | flops 1000000 | bytes 10000 | tf_op jit(solution)/shard_map/output/pallas_call | solution.py:691
  45.9 1.5 %collective-permute-start.21 = (bf16[160,128]{1,0:T(8,128)(2,1)S(1)}, bf16[160,128]{1,0:T(8,128)(2,1)S(1)}, u32[]{:S(2)}, u32[]{:S(2)}) collective-permute-start(bf16[160,128]{1,0:T(8,128)(2,1)S(1)} %get-tuple-element.173), channel_id=1, source_target_pairs={{0,1},{1,0},{2,3},{3,2},{4,5},{5,4},{6,7},{7,6},{8,9},{9,8},{10,11... | collective-permute-start | bytes 122888 | tf_op jit(solution)/shard_map/ppermute | solution.py:831
  47.4 3.7 %collective-permute-done.21.arrived = bf16[160,128]{1,0:T(8,128)(2,1)S(1)} collective-permute-done((bf16[160,128]{1,0:T(8,128)(2,1)S(1)}, bf16[160,128]{1,0:T(8,128)(2,1)S(1)}, u32[]{:S(2)}, u32[]{:S(2)}) %collective-permute-start.21) | collective-permute-done | bytes 40992 | tf_op jit(solution)/shard_map/ppermute | solution.py:831
  51.2 1.1 %place.1 = (bf16[128,1152]{1,0:T(8,128)(2,1)}, bf16[128,1152]{1,0:T(8,128)(2,1)}, f32[288,128]{1,0:T(8,128)}) custom-call(bf16[1152,128]{1,0:T(8,128)(2,1)S(1)} %get-tuple-element.166.mine, bf16[1152,128]{1,0:T(8,128)(2,1)S(1)} %collective-permute-done.20.theirs, f32[160,128]{1,0:T(8,128)S(1)} %get-tuple-element.172.kept, ...), custom_call_target="tpu_custom_call" | custom-call | flops 1000000 | bytes 10000 | tf_op jit(solution)/shard_map/place/pallas_call | solution.py:743
  (36 shorter events, 6.6 us)
Async XLA Ops:
  0.6 11.5 %copy-start = (bf16[1,128,1024]{2,1,0:T(8,128)(2,1)S(1)}, bf16[1,128,1024]{2,1,0:T(8,128)(2,1)}, u32[]{:S(2)}) copy-start(bf16[1,128,1024]{2,1,0:T(8,128)(2,1)} %param.9) | copy-start | bytes 786436
  2.1 10.0 %collective-permute-start = (bf16[1152,128]{1,0:T(8,128)(2,1)S(1)}, bf16[1152,128]{1,0:T(8,128)(2,1)S(1)}, u32[]{:S(2)}, u32[]{:S(2)}) collective-permute-start(bf16[1152,128]{1,0:T(8,128)(2,1)S(1)} %get-tuple-element.94), channel_id=1, source_target_pairs={{0,1},{1,0},{2,3},{3,2},{4,5},{5,4},{6,7},{7,6},{8,9},{9,8},{10,11... | collective-permute-start | bytes 884744 | tf_op jit(solution)/shard_map/ppermute | solution.py:831
  5.9 10.4 %collective-permute-start.1 = (bf16[1168,128]{1,0:T(8,128)(2,1)S(1)}, bf16[1168,128]{1,0:T(8,128)(2,1)S(1)}, u32[]{:S(2)}, u32[]{:S(2)}) collective-permute-start(bf16[1168,128]{1,0:T(8,128)(2,1)S(1)} %label.1.own), channel_id=1, source_target_pairs={{0,2},{1,3},{2,4},{3,5},{4,6},{5,7},{6,0},{7,1},{8,10},{9,11},{10,... | collective-permute-start | bytes 897032 | tf_op jit(solution)/shard_map/ppermute | solution.py:836
  7.5 9.5 %collective-permute-start.2 = (bf16[128,1024]{1,0:T(8,128)(2,1)}, bf16[128,1024]{1,0:T(8,128)(2,1)S(1)}, u32[]{:S(2)}, u32[]{:S(2)}) collective-permute-start(bf16[128,1024]{1,0:T(8,128)(2,1)} %bitcast.9), channel_id=1, source_target_pairs={{0,8},{8,0},{16,24},{24,16},{1,9},{9,1},{17,25},{25,17},{2,10},{10... | collective-permute-start | bytes 786440 | tf_op jit(solution)/shard_map/ppermute | solution.py:831
  7.5 9.5 %collective-permute-start.3 = (bf16[128,1024]{1,0:T(8,128)(2,1)}, bf16[128,1024]{1,0:T(8,128)(2,1)S(1)}, u32[]{:S(2)}, u32[]{:S(2)}) collective-permute-start(bf16[128,1024]{1,0:T(8,128)(2,1)} %bitcast.10), channel_id=1, source_target_pairs={{0,16},{8,24},{16,0},{24,8},{1,17},{9,25},{17,1},{25,9},{2,18},{10... | collective-permute-start | bytes 786440 | tf_op jit(solution)/shard_map/ppermute | solution.py:831
  12.2 9.2 %collective-permute-start.6 = (bf16[128,1024]{1,0:T(8,128)(2,1)S(1)}, bf16[128,1024]{1,0:T(8,128)(2,1)S(1)}, u32[]{:S(2)}, u32[]{:S(2)}) collective-permute-start(bf16[128,1024]{1,0:T(8,128)(2,1)S(1)} %bitcast.12), channel_id=1, source_target_pairs={{0,1},{1,0},{2,3},{3,2},{4,5},{5,4},{6,7},{7,6},{8,9},{9,8},{10,11... | collective-permute-start | bytes 786440 | tf_op jit(solution)/shard_map/ppermute | solution.py:831
  13.9 10.1 %collective-permute-start.4 = (bf16[1152,128]{1,0:T(8,128)(2,1)S(1)}, bf16[1152,128]{1,0:T(8,128)(2,1)S(1)}, u32[]{:S(2)}, u32[]{:S(2)}) collective-permute-start(bf16[1152,128]{1,0:T(8,128)(2,1)S(1)} %collective-permute-done.partner), channel_id=1, source_target_pairs={{0,2},{1,3},{2,4},{3,5},{4,6},{5,7},{6,0},{7,1},{8,10},{9,11},{10,... | collective-permute-start | bytes 884744 | tf_op jit(solution)/shard_map/ppermute | solution.py:836
  16.3 6.8 %collective-permute-start.5 = (bf16[608,128]{1,0:T(8,128)(2,1)S(1)}, bf16[608,128]{1,0:T(8,128)(2,1)S(1)}, u32[]{:S(2)}, u32[]{:S(2)}) collective-permute-start(bf16[608,128]{1,0:T(8,128)(2,1)S(1)} %label_query.1), channel_id=1, source_target_pairs={{0,1},{1,0},{2,3},{3,2},{4,5},{5,4},{6,7},{7,6},{8,9},{9,8},{10,11... | collective-permute-start | bytes 466952 | tf_op jit(solution)/shard_map/ppermute | solution.py:831
  16.9 12.8 %collective-permute-start.7 = (bf16[1152,128]{1,0:T(8,128)(2,1)S(1)}, bf16[1152,128]{1,0:T(8,128)(2,1)S(1)}, u32[]{:S(2)}, u32[]{:S(2)}) collective-permute-start(bf16[1152,128]{1,0:T(8,128)(2,1)S(1)} %get-tuple-element.104.both_own), channel_id=1, source_target_pairs={{2,0},{3,1},{4,2},{5,3},{6,4},{7,5},{10,8},{11,9},{12,10},{13,11},... | collective-permute-start | bytes 884744 | tf_op jit(solution)/shard_map/ppermute | solution.py:844
  18.2 9.4 %collective-permute-start.8 = (bf16[128,1024]{1,0:T(8,128)(2,1)S(1)}, bf16[128,1024]{1,0:T(8,128)(2,1)S(1)}, u32[]{:S(2)}, u32[]{:S(2)}) collective-permute-start(bf16[128,1024]{1,0:T(8,128)(2,1)S(1)} %collective-permute-done.3.refs_6_), channel_id=1, source_target_pairs={{0,8},{8,0},{16,24},{24,16},{1,9},{9,1},{17,25},{25,17},{2,10},{10... | collective-permute-start | bytes 786440 | tf_op jit(solution)/shard_map/ppermute | solution.py:831
  21.4 11.9 %collective-permute-start.12 = (bf16[128,1024]{1,0:T(8,128)(2,1)S(1)}, bf16[128,1024]{1,0:T(8,128)(2,1)S(1)}, u32[]{:S(2)}, u32[]{:S(2)}) collective-permute-start(bf16[128,1024]{1,0:T(8,128)(2,1)S(1)} %collective-permute-done.6.cotangent.refs_4_), channel_id=1, source_target_pairs={{0,16},{8,24},{16,0},{24,8},{1,17},{9,25},{17,1},{25,9},{2,18},{10... | collective-permute-start | bytes 786440 | tf_op jit(solution)/shard_map/ppermute | solution.py:831
  26.0 7.3 %collective-permute-start.10 = (bf16[160,256]{1,0:T(8,128)(2,1)S(1)}, bf16[160,256]{1,0:T(8,128)(2,1)S(1)}, u32[]{:S(2)}, u32[]{:S(2)}) collective-permute-start(bf16[160,256]{1,0:T(8,128)(2,1)S(1)} %get-tuple-element.132), channel_id=1, source_target_pairs={{0,16},{8,24},{16,0},{24,8},{1,17},{9,25},{17,1},{25,9},{2,18},{10... | collective-permute-start | bytes 245768 | tf_op jit(solution)/shard_map/ppermute | solution.py:831
  27.6 5.7 %collective-permute-start.11 = (bf16[160,256]{1,0:T(8,128)(2,1)S(1)}, bf16[160,256]{1,0:T(8,128)(2,1)S(1)}, u32[]{:S(2)}, u32[]{:S(2)}) collective-permute-start(bf16[160,256]{1,0:T(8,128)(2,1)S(1)} %get-tuple-element.133), channel_id=1, source_target_pairs={{0,24},{8,16},{16,8},{24,0},{1,25},{9,17},{17,9},{25,1},{2,26},{10... | collective-permute-start | bytes 245768 | tf_op jit(solution)/shard_map/ppermute | solution.py:831
  27.6 5.7 %collective-permute-start.9 = (bf16[160,256]{1,0:T(8,128)(2,1)S(1)}, bf16[160,256]{1,0:T(8,128)(2,1)S(1)}, u32[]{:S(2)}, u32[]{:S(2)}) collective-permute-start(bf16[160,256]{1,0:T(8,128)(2,1)S(1)} %get-tuple-element.131), channel_id=1, source_target_pairs={{0,8},{8,0},{16,24},{24,16},{1,9},{9,1},{17,25},{25,17},{2,10},{10... | collective-permute-start | bytes 245768 | tf_op jit(solution)/shard_map/ppermute | solution.py:831
  29.7 11.2 %collective-permute-start.15 = (bf16[1296,128]{1,0:T(8,128)(2,1)S(1)}, bf16[1296,128]{1,0:T(8,128)(2,1)S(1)}, u32[]{:S(2)}, u32[]{:S(2)}) collective-permute-start(bf16[1296,128]{1,0:T(8,128)(2,1)S(1)} %get-tuple-element.123.both_partner), channel_id=1, source_target_pairs={{0,6},{1,7},{2,0},{3,1},{4,2},{5,3},{6,4},{7,5},{8,14},{9,15},{10,... | collective-permute-start | bytes 995336 | tf_op jit(solution)/shard_map/ppermute | solution.py:836
  33.3 2.5 %collective-permute-start.13 = (bf16[128,1024]{1,0:T(8,128)(2,1)S(1)}, bf16[128,1024]{1,0:T(8,128)(2,1)S(1)}, u32[]{:S(2)}, u32[]{:S(2)}) collective-permute-start(bf16[128,1024]{1,0:T(8,128)(2,1)S(1)} %collective-permute-done.6.cotangent.refs_4_), channel_id=1, source_target_pairs={{0,8},{8,0},{16,24},{24,16},{1,9},{9,1},{17,25},{25,17},{2,10},{10... | collective-permute-start | bytes 786440 | tf_op jit(solution)/shard_map/ppermute | solution.py:831
  33.4 2.4 %collective-permute-start.14 = (bf16[128,1024]{1,0:T(8,128)(2,1)S(1)}, bf16[128,1024]{1,0:T(8,128)(2,1)S(1)}, u32[]{:S(2)}, u32[]{:S(2)}) collective-permute-start(bf16[128,1024]{1,0:T(8,128)(2,1)S(1)} %collective-permute-done.12.refs_6_), channel_id=1, source_target_pairs={{0,8},{8,0},{16,24},{24,16},{1,9},{9,1},{17,25},{25,17},{2,10},{10... | collective-permute-start | bytes 786440 | tf_op jit(solution)/shard_map/ppermute | solution.py:831
  34.3 9.1 %collective-permute-start.16 = (bf16[576,256]{1,0:T(8,128)(2,1)S(1)}, bf16[576,256]{1,0:T(8,128)(2,1)S(1)}, u32[]{:S(2)}, u32[]{:S(2)}) collective-permute-start(bf16[576,256]{1,0:T(8,128)(2,1)S(1)} %get-tuple-element.155), channel_id=1, source_target_pairs={{0,1},{1,0},{2,3},{3,2},{4,5},{5,4},{6,7},{7,6},{8,9},{9,8},{10,11... | collective-permute-start | bytes 884744 | tf_op jit(solution)/shard_map/ppermute | solution.py:831
  36.2 9.6 %collective-permute-start.17 = (bf16[160,256]{1,0:T(8,128)(2,1)S(1)}, bf16[160,256]{1,0:T(8,128)(2,1)S(1)}, u32[]{:S(2)}, u32[]{:S(2)}) collective-permute-start(bf16[160,256]{1,0:T(8,128)(2,1)S(1)} %get-tuple-element.161), channel_id=1, source_target_pairs={{0,2},{1,3},{2,0},{3,1},{4,6},{5,7},{6,4},{7,5},{8,10},{9,11},{10,... | collective-permute-start | bytes 245768 | tf_op jit(solution)/shard_map/ppermute | solution.py:831
  36.3 9.5 %collective-permute-start.18 = (bf16[160,256]{1,0:T(8,128)(2,1)S(1)}, bf16[160,256]{1,0:T(8,128)(2,1)S(1)}, u32[]{:S(2)}, u32[]{:S(2)}) collective-permute-start(bf16[160,256]{1,0:T(8,128)(2,1)S(1)} %get-tuple-element.162), channel_id=1, source_target_pairs={{0,4},{1,5},{2,6},{3,7},{4,0},{5,1},{6,2},{7,3},{8,12},{9,13},{10,... | collective-permute-start | bytes 245768 | tf_op jit(solution)/shard_map/ppermute | solution.py:831
  38.3 7.6 %collective-permute-start.19 = (bf16[160,256]{1,0:T(8,128)(2,1)S(1)}, bf16[160,256]{1,0:T(8,128)(2,1)S(1)}, u32[]{:S(2)}, u32[]{:S(2)}) collective-permute-start(bf16[160,256]{1,0:T(8,128)(2,1)S(1)} %get-tuple-element.163), channel_id=1, source_target_pairs={{0,6},{1,7},{2,4},{3,5},{4,2},{5,3},{6,0},{7,1},{8,14},{9,15},{10,... | collective-permute-start | bytes 245768 | tf_op jit(solution)/shard_map/ppermute | solution.py:831
  42.5 8.6 %collective-permute-start.20 = (bf16[1152,128]{1,0:T(8,128)(2,1)S(1)}, bf16[1152,128]{1,0:T(8,128)(2,1)S(1)}, u32[]{:S(2)}, u32[]{:S(2)}) collective-permute-start(bf16[1152,128]{1,0:T(8,128)(2,1)S(1)} %get-tuple-element.167), channel_id=1, source_target_pairs={{0,1},{1,0},{2,3},{3,2},{4,5},{5,4},{6,7},{7,6},{8,9},{9,8},{10,11... | collective-permute-start | bytes 884744 | tf_op jit(solution)/shard_map/ppermute | solution.py:831
  45.9 5.2 %collective-permute-start.21 = (bf16[160,128]{1,0:T(8,128)(2,1)S(1)}, bf16[160,128]{1,0:T(8,128)(2,1)S(1)}, u32[]{:S(2)}, u32[]{:S(2)}) collective-permute-start(bf16[160,128]{1,0:T(8,128)(2,1)S(1)} %get-tuple-element.173), channel_id=1, source_target_pairs={{0,1},{1,0},{2,3},{3,2},{4,5},{5,4},{6,7},{7,6},{8,9},{9,8},{10,11... | collective-permute-start | bytes 122888 | tf_op jit(solution)/shard_map/ppermute | solution.py:831

commit v9 on v8

--- a/solution.py
+++ b/solution.py
@@ -450,7 +450,7 @@
             att[single_rows(), steps] = mixed[HDIM:].astype(bf16)
 
     items = [(pair, query_block) for pair in range(PAIRS + 1) for query_block in range(2)]
-    staggered(items, 3, score, weigh, mix)
+    staggered(items, 4, score, weigh, mix)
 
     att[HALF:] = jnp.zeros((ATT_ROWS - HALF, 2 * BLOCK), bf16)
     att_own[...] = att[:HALF, at(half, BLOCK)]

time: 52.4 us -> 52.4 us (level)
  no operation moved by 1% of the time
where the time goes in v9:
time: 52.4 us; the launch traced here: 52.2 us
  starting transfers between devices  25.7 us (49%)
  Pallas kernels  14.3 us (27%)
  waiting for transfers between devices  10.8 us (21%)
  between operations  1.46 us (3%)
    ppermute x18, starting transfers between devices, swapped(): lax.ppermute(value, axis, [(source, source ^ bits) for source in range(co...  19.4 us
    ppermute x18, waiting for transfers between devices, swapped(): lax.ppermute(value, axis, [(source, source ^ bits) for source in range(co...  8.11 us
    ppermute x3, starting transfers between devices, rotated(): lax.ppermute(value, axis, [(source, (source + steps) % count) for source...  4.96 us
    pallas_call x1, Pallas kernels, output_rows(): kernel(output_kernel, 'output', [VMEM] * 4, [shaped((BLOCK, weight.shape[...  2.44 us
    pallas_call x1, Pallas kernels, own_cotangents(): kernel(own_cotangent_kernel, 'own_cotangents', [HBM, HBM, VMEM], [shaped(...  2.24 us
    ppermute x3, waiting for transfers between devices, rotated(): lax.ppermute(value, axis, [(source, (source + steps) % count) for source...  1.95 us
    pallas_call x1, Pallas kernels, forward(): kernel(functools.partial(forward_kernel, pieces_wanted), 'forward', [VMEM...  1.85 us
    pallas_call x1, Pallas kernels, own_gradients(): kernel(own_kernel, 'own_gradients', [VMEM] * 7, [shaped((HALF, BLOCK), bf...  1.82 us
  transfers between devices with their start and end apart: 22, of which 8 were waited for; matrix products, arithmetic and copies ran while one was open for 0% of the time, Pallas kernels for 22%

profile of v9, /device:TPU:0, one launch (start us, length us, event | category | flops | bytes accessed | tf_op | source)
XLA Modules:
  0.0 52.2 jit_solution(12891815197375046327)
XLA Ops:
  0.6 1.5 %pack.1 = (bf16[1152,128]{1,0:T(8,128)(2,1)S(1)}, bf16[1152,128]{1,0:T(8,128)(2,1)S(1)}, bf16[576,128]{1,0:T(8,128)(2,1)S(1)}, bf16[640,128]{1,0:T(8,128)(2,1)S(1)}) custom-call(bf16[128,1152]{1,0:T(8,128)(2,1)} %bitcast.14, bf16[128,1152]{1,0:T(8,128)(2,1)} %bitcast.15, bf16[128,1152]{1,0:T(8,128)(2,1)} %bitcast.16), custom_call_target="tpu_custom_call" | custom-call | flops 1000000 | bytes 10000 | tf_op jit(solution)/shard_map/pack/pallas_call | solution.py:158
  2.1 3.0 %collective-permute-start = (bf16[1152,128]{1,0:T(8,128)(2,1)S(1)}, bf16[1152,128]{1,0:T(8,128)(2,1)S(1)}, u32[]{:S(2)}, u32[]{:S(2)}) collective-permute-start(bf16[1152,128]{1,0:T(8,128)(2,1)S(1)} %get-tuple-element.94), channel_id=1, source_target_pairs={{0,1},{1,0},{2,3},{3,2},{4,5},{5,4},{6,7},{7,6},{8,9},{9,8},{10,11... | collective-permute-start | bytes 884744 | tf_op jit(solution)/shard_map/ppermute | solution.py:831
  5.9 1.6 %collective-permute-start.1 = (bf16[1168,128]{1,0:T(8,128)(2,1)S(1)}, bf16[1168,128]{1,0:T(8,128)(2,1)S(1)}, u32[]{:S(2)}, u32[]{:S(2)}) collective-permute-start(bf16[1168,128]{1,0:T(8,128)(2,1)S(1)} %label.1.own), channel_id=1, source_target_pairs={{0,2},{1,3},{2,4},{3,5},{4,6},{5,7},{6,0},{7,1},{8,10},{9,11},{10,... | collective-permute-start | bytes 897032 | tf_op jit(solution)/shard_map/ppermute | solution.py:836
  7.5 1.5 %collective-permute-start.3 = (bf16[128,1024]{1,0:T(8,128)(2,1)}, bf16[128,1024]{1,0:T(8,128)(2,1)S(1)}, u32[]{:S(2)}, u32[]{:S(2)}) collective-permute-start(bf16[128,1024]{1,0:T(8,128)(2,1)} %bitcast.10), channel_id=1, source_target_pairs={{0,16},{8,24},{16,0},{24,8},{1,17},{9,25},{17,1},{25,9},{2,18},{10... | collective-permute-start | bytes 786440 | tf_op jit(solution)/shard_map/ppermute | solution.py:831
  9.0 2.2 %own_cotangents.1 = (bf16[1152,128]{1,0:T(8,128)(2,1)S(1)}, bf16[576,128]{1,0:T(8,128)(2,1)S(1)}, bf16[1024,1152]{1,0:T(8,128)(2,1)S(1)}) custom-call(bf16[128,1024]{1,0:T(8,128)(2,1)} %bitcast.11, bf16[1024,1152]{1,0:T(8,128)(2,1)} %weight.1, bf16[640,128]{1,0:T(8,128)(2,1)S(1)} %get-tuple-element.95.query.query_own), custom_call_target="tpu_custom_call" | custom-call | flops 1000000 | bytes 10000 | tf_op jit(solution)/shard_map/own_cotangents/pallas_call | solution.py:248
  11.2 0.9 %collective-permute-done.partner = bf16[1152,128]{1,0:T(8,128)(2,1)S(1)} collective-permute-done((bf16[1152,128]{1,0:T(8,128)(2,1)S(1)}, bf16[1152,128]{1,0:T(8,128)(2,1)S(1)}, u32[]{:S(2)}, u32[]{:S(2)}) %collective-permute-start) | collective-permute-done | bytes 294944 | tf_op jit(solution)/shard_map/ppermute | solution.py:831
  12.2 1.7 %collective-permute-start.6 = (bf16[128,1024]{1,0:T(8,128)(2,1)S(1)}, bf16[128,1024]{1,0:T(8,128)(2,1)S(1)}, u32[]{:S(2)}, u32[]{:S(2)}) collective-permute-start(bf16[128,1024]{1,0:T(8,128)(2,1)S(1)} %bitcast.12), channel_id=1, source_target_pairs={{0,1},{1,0},{2,3},{3,2},{4,5},{5,4},{6,7},{7,6},{8,9},{9,8},{10,11... | collective-permute-start | bytes 786440 | tf_op jit(solution)/shard_map/ppermute | solution.py:831
  13.9 1.6 %collective-permute-start.4 = (bf16[1152,128]{1,0:T(8,128)(2,1)S(1)}, bf16[1152,128]{1,0:T(8,128)(2,1)S(1)}, u32[]{:S(2)}, u32[]{:S(2)}) collective-permute-start(bf16[1152,128]{1,0:T(8,128)(2,1)S(1)} %collective-permute-done.partner), channel_id=1, source_target_pairs={{0,2},{1,3},{2,4},{3,5},{4,6},{5,7},{6,0},{7,1},{8,10},{9,11},{10,... | collective-permute-start | bytes 884744 | tf_op jit(solution)/shard_map/ppermute | solution.py:836
  16.9 1.3 %collective-permute-start.7 = (bf16[1152,128]{1,0:T(8,128)(2,1)S(1)}, bf16[1152,128]{1,0:T(8,128)(2,1)S(1)}, u32[]{:S(2)}, u32[]{:S(2)}) collective-permute-start(bf16[1152,128]{1,0:T(8,128)(2,1)S(1)} %get-tuple-element.104.both_own), channel_id=1, source_target_pairs={{2,0},{3,1},{4,2},{5,3},{6,4},{7,5},{10,8},{11,9},{12,10},{13,11},... | collective-permute-start | bytes 884744 | tf_op jit(solution)/shard_map/ppermute | solution.py:844
  18.3 3.1 %collective-permute-done.6.cotangent.refs_4_ = bf16[128,1024]{1,0:T(8,128)(2,1)S(1)} collective-permute-done((bf16[128,1024]{1,0:T(8,128)(2,1)S(1)}, bf16[128,1024]{1,0:T(8,128)(2,1)S(1)}, u32[]{:S(2)}, u32[]{:S(2)}) %collective-permute-start.6) | collective-permute-done | bytes 262176 | tf_op jit(solution)/shard_map/ppermute | solution.py:831
  21.4 1.4 %collective-permute-start.12 = (bf16[128,1024]{1,0:T(8,128)(2,1)S(1)}, bf16[128,1024]{1,0:T(8,128)(2,1)S(1)}, u32[]{:S(2)}, u32[]{:S(2)}) collective-permute-start(bf16[128,1024]{1,0:T(8,128)(2,1)S(1)} %collective-permute-done.6.cotangent.refs_4_), channel_id=1, source_target_pairs={{0,16},{8,24},{16,0},{24,8},{1,17},{9,25},{17,1},{25,9},{2,18},{10... | collective-permute-start | bytes 786440 | tf_op jit(solution)/shard_map/ppermute | solution.py:831
  23.1 0.9 %collective-permute-done.4.halo_other = bf16[1152,128]{1,0:T(8,128)(2,1)S(1)} collective-permute-done((bf16[1152,128]{1,0:T(8,128)(2,1)S(1)}, bf16[1152,128]{1,0:T(8,128)(2,1)S(1)}, u32[]{:S(2)}, u32[]{:S(2)}) %collective-permute-start.4) | collective-permute-done | bytes 294944 | tf_op jit(solution)/shard_map/ppermute | solution.py:836
  24.2 1.9 %forward.1 = (bf16[4,2,384,256]{3,2,1,0:T(8,128)(2,1)S(1)}, bf16[2,384,128]{2,1,0:T(8,128)(2,1)S(1)}, f32[24,256]{1,0:T(8,128)S(1)}, bf16[608,256]{1,0:T(8,128)(...) custom-call(bf16[9,512,128]{2,1,0:T(8,128)(2,1)S(1)} %get-tuple-elem, ...), custom_call_target="tpu_custom_call" | custom-call | flops 1000000 | bytes 10000 | tf_op jit(solution)/shard_map/forward/pallas_call | solution.py:467
  26.0 1.6 %collective-permute-start.10 = (bf16[160,256]{1,0:T(8,128)(2,1)S(1)}, bf16[160,256]{1,0:T(8,128)(2,1)S(1)}, u32[]{:S(2)}, u32[]{:S(2)}) collective-permute-start(bf16[160,256]{1,0:T(8,128)(2,1)S(1)} %get-tuple-element.132), channel_id=1, source_target_pairs={{0,16},{8,24},{16,0},{24,8},{1,17},{9,25},{17,1},{25,9},{2,18},{10... | collective-permute-start | bytes 245768 | tf_op jit(solution)/shard_map/ppermute | solution.py:831
  29.7 1.8 %collective-permute-start.15 = (bf16[1296,128]{1,0:T(8,128)(2,1)S(1)}, bf16[1296,128]{1,0:T(8,128)(2,1)S(1)}, u32[]{:S(2)}, u32[]{:S(2)}) collective-permute-start(bf16[1296,128]{1,0:T(8,128)(2,1)S(1)} %get-tuple-element.123.both_partner), channel_id=1, source_target_pairs={{0,6},{1,7},{2,0},{3,1},{4,2},{5,3},{6,4},{7,5},{8,14},{9,15},{10,... | collective-permute-start | bytes 995336 | tf_op jit(solution)/shard_map/ppermute | solution.py:836
  31.5 1.8 %own_gradients.1 = (bf16[576,128]{1,0:T(8,128)(2,1)S(1)}, bf16[576,256]{1,0:T(8,128)(2,1)S(1)}, f32[1152,128]{1,0:T(8,128)S(1)}, f32[1152,128]{1,0:T(8,128)S(1)}) custom-call(bf16[9,512,128]{2,1,0:T(8,128)(2,1)S(1)} %get-tuple-element.103.keys_all, bf16[1152,128]{1,0:T(8,128)(2,1)S(1)} %get-tuple-element.104.both_own, ...), custom_call_target="tpu_custom_call" | custom-call | flops 1000000 | bytes 10000 | tf_op jit(solution)/shard_map/own_gradients/pallas_call | solution.py:561
  34.3 1.6 %collective-permute-start.16 = (bf16[576,256]{1,0:T(8,128)(2,1)S(1)}, bf16[576,256]{1,0:T(8,128)(2,1)S(1)}, u32[]{:S(2)}, u32[]{:S(2)}) collective-permute-start(bf16[576,256]{1,0:T(8,128)(2,1)S(1)} %get-tuple-element.155), channel_id=1, source_target_pairs={{0,1},{1,0},{2,3},{3,2},{4,5},{5,4},{6,7},{7,6},{8,9},{9,8},{10,11... | collective-permute-start | bytes 884744 | tf_op jit(solution)/shard_map/ppermute | solution.py:831
  36.3 2.0 %collective-permute-start.18 = (bf16[160,256]{1,0:T(8,128)(2,1)S(1)}, bf16[160,256]{1,0:T(8,128)(2,1)S(1)}, u32[]{:S(2)}, u32[]{:S(2)}) collective-permute-start(bf16[160,256]{1,0:T(8,128)(2,1)S(1)} %get-tuple-element.162), channel_id=1, source_target_pairs={{0,4},{1,5},{2,6},{3,7},{4,0},{5,1},{6,2},{7,3},{8,12},{9,13},{10,... | collective-permute-start | bytes 245768 | tf_op jit(solution)/shard_map/ppermute | solution.py:831
  38.3 2.4 %collective-permute-start.19 = (bf16[160,256]{1,0:T(8,128)(2,1)S(1)}, bf16[160,256]{1,0:T(8,128)(2,1)S(1)}, u32[]{:S(2)}, u32[]{:S(2)}) collective-permute-start(bf16[160,256]{1,0:T(8,128)(2,1)S(1)} %get-tuple-element.163), channel_id=1, source_target_pairs={{0,6},{1,7},{2,4},{3,5},{4,2},{5,3},{6,0},{7,1},{8,14},{9,15},{10,... | collective-permute-start | bytes 245768 | tf_op jit(solution)/shard_map/ppermute | solution.py:831
  40.9 1.6 %next_gradients.1 = (bf16[1152,128]{1,0:T(8,128)(2,1)S(1)}, bf16[1152,128]{1,0:T(8,128)(2,1)S(1)}) custom-call(bf16[1168,128]{1,0:T(8,128)(2,1)S(1)} %label.1.own, bf16[1152,128]{1,0:T(8,128)(2,1)S(1)} %collective-permute-done.partner, bf16[1152,128]{1,0:T(8,128)(2,1)S(1)} %collective-permute-done.7.both_own, ...), custom_call_target="tpu_custom_call" | custom-call | flops 4000000000 | bytes 10000 | tf_op jit(solution)/shard_map/next_gradients/pallas_call | solution.py:652
  43.4 2.4 %output.1 = (bf16[128,1024]{1,0:T(8,128)(2,1)}, bf16[128,1152]{1,0:T(8,128)(2,1)}, bf16[1152,128]{1,0:T(8,128)(2,1)}) custom-call(bf16[576,128]{1,0:T(8,128)(2,1)S(1)} %get-tuple-element.157.att_own, bf16[576,256]{1,0:T(8,128)(2,1)S(1)} %collective-permute-done.16.received, bf16[576,128]{1,0:T(8,128)(2,1)S(1)} %get-tuple-element.159.dq_mine, ...), custom_call_target="tpu_custom_call" | custom-call | flops 1000000 | bytes 10000 | tf_op jit(solution)/shard_map/output/pallas_call | solution.py:691
  45.9 1.5 %collective-permute-start.21 = (bf16[160,128]{1,0:T(8,128)(2,1)S(1)}, bf16[160,128]{1,0:T(8,128)(2,1)S(1)}, u32[]{:S(2)}, u32[]{:S(2)}) collective-permute-start(bf16[160,128]{1,0:T(8,128)(2,1)S(1)} %get-tuple-element.173), channel_id=1, source_target_pairs={{0,1},{1,0},{2,3},{3,2},{4,5},{5,4},{6,7},{7,6},{8,9},{9,8},{10,11... | collective-permute-start | bytes 122888 | tf_op jit(solution)/shard_map/ppermute | solution.py:831
  47.4 3.7 %collective-permute-done.21.arrived = bf16[160,128]{1,0:T(8,128)(2,1)S(1)} collective-permute-done((bf16[160,128]{1,0:T(8,128)(2,1)S(1)}, bf16[160,128]{1,0:T(8,128)(2,1)S(1)}, u32[]{:S(2)}, u32[]{:S(2)}) %collective-permute-start.21) | collective-permute-done | bytes 40992 | tf_op jit(solution)/shard_map/ppermute | solution.py:831
  51.2 1.1 %place.1 = (bf16[128,1152]{1,0:T(8,128)(2,1)}, bf16[128,1152]{1,0:T(8,128)(2,1)}, f32[288,128]{1,0:T(8,128)}) custom-call(bf16[1152,128]{1,0:T(8,128)(2,1)S(1)} %get-tuple-element.166.mine, bf16[1152,128]{1,0:T(8,128)(2,1)S(1)} %collective-permute-done.20.theirs, f32[160,128]{1,0:T(8,128)S(1)} %get-tuple-element.172.kept, ...), custom_call_target="tpu_custom_call" | custom-call | flops 1000000 | bytes 10000 | tf_op jit(solution)/shard_map/place/pallas_call | solution.py:743
  (36 shorter events, 6.6 us)
Async XLA Ops:
  0.6 11.5 %copy-start = (bf16[1,128,1024]{2,1,0:T(8,128)(2,1)S(1)}, bf16[1,128,1024]{2,1,0:T(8,128)(2,1)}, u32[]{:S(2)}) copy-start(bf16[1,128,1024]{2,1,0:T(8,128)(2,1)} %param.9) | copy-start | bytes 786436
  2.1 10.0 %collective-permute-start = (bf16[1152,128]{1,0:T(8,128)(2,1)S(1)}, bf16[1152,128]{1,0:T(8,128)(2,1)S(1)}, u32[]{:S(2)}, u32[]{:S(2)}) collective-permute-start(bf16[1152,128]{1,0:T(8,128)(2,1)S(1)} %get-tuple-element.94), channel_id=1, source_target_pairs={{0,1},{1,0},{2,3},{3,2},{4,5},{5,4},{6,7},{7,6},{8,9},{9,8},{10,11... | collective-permute-start | bytes 884744 | tf_op jit(solution)/shard_map/ppermute | solution.py:831
  5.9 10.4 %collective-permute-start.1 = (bf16[1168,128]{1,0:T(8,128)(2,1)S(1)}, bf16[1168,128]{1,0:T(8,128)(2,1)S(1)}, u32[]{:S(2)}, u32[]{:S(2)}) collective-permute-start(bf16[1168,128]{1,0:T(8,128)(2,1)S(1)} %label.1.own), channel_id=1, source_target_pairs={{0,2},{1,3},{2,4},{3,5},{4,6},{5,7},{6,0},{7,1},{8,10},{9,11},{10,... | collective-permute-start | bytes 897032 | tf_op jit(solution)/shard_map/ppermute | solution.py:836
  7.5 9.5 %collective-permute-start.2 = (bf16[128,1024]{1,0:T(8,128)(2,1)}, bf16[128,1024]{1,0:T(8,128)(2,1)S(1)}, u32[]{:S(2)}, u32[]{:S(2)}) collective-permute-start(bf16[128,1024]{1,0:T(8,128)(2,1)} %bitcast.9), channel_id=1, source_target_pairs={{0,8},{8,0},{16,24},{24,16},{1,9},{9,1},{17,25},{25,17},{2,10},{10... | collective-permute-start | bytes 786440 | tf_op jit(solution)/shard_map/ppermute | solution.py:831
  7.5 9.5 %collective-permute-start.3 = (bf16[128,1024]{1,0:T(8,128)(2,1)}, bf16[128,1024]{1,0:T(8,128)(2,1)S(1)}, u32[]{:S(2)}, u32[]{:S(2)}) collective-permute-start(bf16[128,1024]{1,0:T(8,128)(2,1)} %bitcast.10), channel_id=1, source_target_pairs={{0,16},{8,24},{16,0},{24,8},{1,17},{9,25},{17,1},{25,9},{2,18},{10... | collective-permute-start | bytes 786440 | tf_op jit(solution)/shard_map/ppermute | solution.py:831
  12.2 9.2 %collective-permute-start.6 = (bf16[128,1024]{1,0:T(8,128)(2,1)S(1)}, bf16[128,1024]{1,0:T(8,128)(2,1)S(1)}, u32[]{:S(2)}, u32[]{:S(2)}) collective-permute-start(bf16[128,1024]{1,0:T(8,128)(2,1)S(1)} %bitcast.12), channel_id=1, source_target_pairs={{0,1},{1,0},{2,3},{3,2},{4,5},{5,4},{6,7},{7,6},{8,9},{9,8},{10,11... | collective-permute-start | bytes 786440 | tf_op jit(solution)/shard_map/ppermute | solution.py:831
  13.9 10.1 %collective-permute-start.4 = (bf16[1152,128]{1,0:T(8,128)(2,1)S(1)}, bf16[1152,128]{1,0:T(8,128)(2,1)S(1)}, u32[]{:S(2)}, u32[]{:S(2)}) collective-permute-start(bf16[1152,128]{1,0:T(8,128)(2,1)S(1)} %collective-permute-done.partner), channel_id=1, source_target_pairs={{0,2},{1,3},{2,4},{3,5},{4,6},{5,7},{6,0},{7,1},{8,10},{9,11},{10,... | collective-permute-start | bytes 884744 | tf_op jit(solution)/shard_map/ppermute | solution.py:836
  16.3 6.8 %collective-permute-start.5 = (bf16[608,128]{1,0:T(8,128)(2,1)S(1)}, bf16[608,128]{1,0:T(8,128)(2,1)S(1)}, u32[]{:S(2)}, u32[]{:S(2)}) collective-permute-start(bf16[608,128]{1,0:T(8,128)(2,1)S(1)} %label_query.1), channel_id=1, source_target_pairs={{0,1},{1,0},{2,3},{3,2},{4,5},{5,4},{6,7},{7,6},{8,9},{9,8},{10,11... | collective-permute-start | bytes 466952 | tf_op jit(solution)/shard_map/ppermute | solution.py:831
  16.9 12.8 %collective-permute-start.7 = (bf16[1152,128]{1,0:T(8,128)(2,1)S(1)}, bf16[1152,128]{1,0:T(8,128)(2,1)S(1)}, u32[]{:S(2)}, u32[]{:S(2)}) collective-permute-start(bf16[1152,128]{1,0:T(8,128)(2,1)S(1)} %get-tuple-element.104.both_own), channel_id=1, source_target_pairs={{2,0},{3,1},{4,2},{5,3},{6,4},{7,5},{10,8},{11,9},{12,10},{13,11},... | collective-permute-start | bytes 884744 | tf_op jit(solution)/shard_map/ppermute | solution.py:844
  18.2 9.4 %collective-permute-start.8 = (bf16[128,1024]{1,0:T(8,128)(2,1)S(1)}, bf16[128,1024]{1,0:T(8,128)(2,1)S(1)}, u32[]{:S(2)}, u32[]{:S(2)}) collective-permute-start(bf16[128,1024]{1,0:T(8,128)(2,1)S(1)} %collective-permute-done.3.refs_6_), channel_id=1, source_target_pairs={{0,8},{8,0},{16,24},{24,16},{1,9},{9,1},{17,25},{25,17},{2,10},{10... | collective-permute-start | bytes 786440 | tf_op jit(solution)/shard_map/ppermute | solution.py:831
  21.4 11.9 %collective-permute-start.12 = (bf16[128,1024]{1,0:T(8,128)(2,1)S(1)}, bf16[128,1024]{1,0:T(8,128)(2,1)S(1)}, u32[]{:S(2)}, u32[]{:S(2)}) collective-permute-start(bf16[128,1024]{1,0:T(8,128)(2,1)S(1)} %collective-permute-done.6.cotangent.refs_4_), channel_id=1, source_target_pairs={{0,16},{8,24},{16,0},{24,8},{1,17},{9,25},{17,1},{25,9},{2,18},{10... | collective-permute-start | bytes 786440 | tf_op jit(solution)/shard_map/ppermute | solution.py:831
  26.0 7.3 %collective-permute-start.10 = (bf16[160,256]{1,0:T(8,128)(2,1)S(1)}, bf16[160,256]{1,0:T(8,128)(2,1)S(1)}, u32[]{:S(2)}, u32[]{:S(2)}) collective-permute-start(bf16[160,256]{1,0:T(8,128)(2,1)S(1)} %get-tuple-element.132), channel_id=1, source_target_pairs={{0,16},{8,24},{16,0},{24,8},{1,17},{9,25},{17,1},{25,9},{2,18},{10... | collective-permute-start | bytes 245768 | tf_op jit(solution)/shard_map/ppermute | solution.py:831
  27.6 5.7 %collective-permute-start.11 = (bf16[160,256]{1,0:T(8,128)(2,1)S(1)}, bf16[160,256]{1,0:T(8,128)(2,1)S(1)}, u32[]{:S(2)}, u32[]{:S(2)}) collective-permute-start(bf16[160,256]{1,0:T(8,128)(2,1)S(1)} %get-tuple-element.133), channel_id=1, source_target_pairs={{0,24},{8,16},{16,8},{24,0},{1,25},{9,17},{17,9},{25,1},{2,26},{10... | collective-permute-start | bytes 245768 | tf_op jit(solution)/shard_map/ppermute | solution.py:831
  27.6 5.7 %collective-permute-start.9 = (bf16[160,256]{1,0:T(8,128)(2,1)S(1)}, bf16[160,256]{1,0:T(8,128)(2,1)S(1)}, u32[]{:S(2)}, u32[]{:S(2)}) collective-permute-start(bf16[160,256]{1,0:T(8,128)(2,1)S(1)} %get-tuple-element.131), channel_id=1, source_target_pairs={{0,8},{8,0},{16,24},{24,16},{1,9},{9,1},{17,25},{25,17},{2,10},{10... | collective-permute-start | bytes 245768 | tf_op jit(solution)/shard_map/ppermute | solution.py:831
  29.7 11.2 %collective-permute-start.15 = (bf16[1296,128]{1,0:T(8,128)(2,1)S(1)}, bf16[1296,128]{1,0:T(8,128)(2,1)S(1)}, u32[]{:S(2)}, u32[]{:S(2)}) collective-permute-start(bf16[1296,128]{1,0:T(8,128)(2,1)S(1)} %get-tuple-element.123.both_partner), channel_id=1, source_target_pairs={{0,6},{1,7},{2,0},{3,1},{4,2},{5,3},{6,4},{7,5},{8,14},{9,15},{10,... | collective-permute-start | bytes 995336 | tf_op jit(solution)/shard_map/ppermute | solution.py:836
  33.3 2.5 %collective-permute-start.13 = (bf16[128,1024]{1,0:T(8,128)(2,1)S(1)}, bf16[128,1024]{1,0:T(8,128)(2,1)S(1)}, u32[]{:S(2)}, u32[]{:S(2)}) collective-permute-start(bf16[128,1024]{1,0:T(8,128)(2,1)S(1)} %collective-permute-done.6.cotangent.refs_4_), channel_id=1, source_target_pairs={{0,8},{8,0},{16,24},{24,16},{1,9},{9,1},{17,25},{25,17},{2,10},{10... | collective-permute-start | bytes 786440 | tf_op jit(solution)/shard_map/ppermute | solution.py:831
  33.4 2.4 %collective-permute-start.14 = (bf16[128,1024]{1,0:T(8,128)(2,1)S(1)}, bf16[128,1024]{1,0:T(8,128)(2,1)S(1)}, u32[]{:S(2)}, u32[]{:S(2)}) collective-permute-start(bf16[128,1024]{1,0:T(8,128)(2,1)S(1)} %collective-permute-done.12.refs_6_), channel_id=1, source_target_pairs={{0,8},{8,0},{16,24},{24,16},{1,9},{9,1},{17,25},{25,17},{2,10},{10... | collective-permute-start | bytes 786440 | tf_op jit(solution)/shard_map/ppermute | solution.py:831
  34.3 9.1 %collective-permute-start.16 = (bf16[576,256]{1,0:T(8,128)(2,1)S(1)}, bf16[576,256]{1,0:T(8,128)(2,1)S(1)}, u32[]{:S(2)}, u32[]{:S(2)}) collective-permute-start(bf16[576,256]{1,0:T(8,128)(2,1)S(1)} %get-tuple-element.155), channel_id=1, source_target_pairs={{0,1},{1,0},{2,3},{3,2},{4,5},{5,4},{6,7},{7,6},{8,9},{9,8},{10,11... | collective-permute-start | bytes 884744 | tf_op jit(solution)/shard_map/ppermute | solution.py:831
  36.2 9.6 %collective-permute-start.17 = (bf16[160,256]{1,0:T(8,128)(2,1)S(1)}, bf16[160,256]{1,0:T(8,128)(2,1)S(1)}, u32[]{:S(2)}, u32[]{:S(2)}) collective-permute-start(bf16[160,256]{1,0:T(8,128)(2,1)S(1)} %get-tuple-element.161), channel_id=1, source_target_pairs={{0,2},{1,3},{2,0},{3,1},{4,6},{5,7},{6,4},{7,5},{8,10},{9,11},{10,... | collective-permute-start | bytes 245768 | tf_op jit(solution)/shard_map/ppermute | solution.py:831
  36.3 9.5 %collective-permute-start.18 = (bf16[160,256]{1,0:T(8,128)(2,1)S(1)}, bf16[160,256]{1,0:T(8,128)(2,1)S(1)}, u32[]{:S(2)}, u32[]{:S(2)}) collective-permute-start(bf16[160,256]{1,0:T(8,128)(2,1)S(1)} %get-tuple-element.162), channel_id=1, source_target_pairs={{0,4},{1,5},{2,6},{3,7},{4,0},{5,1},{6,2},{7,3},{8,12},{9,13},{10,... | collective-permute-start | bytes 245768 | tf_op jit(solution)/shard_map/ppermute | solution.py:831
  38.3 7.6 %collective-permute-start.19 = (bf16[160,256]{1,0:T(8,128)(2,1)S(1)}, bf16[160,256]{1,0:T(8,128)(2,1)S(1)}, u32[]{:S(2)}, u32[]{:S(2)}) collective-permute-start(bf16[160,256]{1,0:T(8,128)(2,1)S(1)} %get-tuple-element.163), channel_id=1, source_target_pairs={{0,6},{1,7},{2,4},{3,5},{4,2},{5,3},{6,0},{7,1},{8,14},{9,15},{10,... | collective-permute-start | bytes 245768 | tf_op jit(solution)/shard_map/ppermute | solution.py:831
  42.5 8.6 %collective-permute-start.20 = (bf16[1152,128]{1,0:T(8,128)(2,1)S(1)}, bf16[1152,128]{1,0:T(8,128)(2,1)S(1)}, u32[]{:S(2)}, u32[]{:S(2)}) collective-permute-start(bf16[1152,128]{1,0:T(8,128)(2,1)S(1)} %get-tuple-element.167), channel_id=1, source_target_pairs={{0,1},{1,0},{2,3},{3,2},{4,5},{5,4},{6,7},{7,6},{8,9},{9,8},{10,11... | collective-permute-start | bytes 884744 | tf_op jit(solution)/shard_map/ppermute | solution.py:831
  45.9 5.2 %collective-permute-start.21 = (bf16[160,128]{1,0:T(8,128)(2,1)S(1)}, bf16[160,128]{1,0:T(8,128)(2,1)S(1)}, u32[]{:S(2)}, u32[]{:S(2)}) collective-permute-start(bf16[160,128]{1,0:T(8,128)(2,1)S(1)} %get-tuple-element.173), channel_id=1, source_target_pairs={{0,1},{1,0},{2,3},{3,2},{4,5},{5,4},{6,7},{7,6},{8,9},{9,8},{10,11... | collective-permute-start | bytes 122888 | tf_op jit(solution)/shard_map/ppermute | solution.py:831
